TPU v7x, 32 devices: a whole 2x2x4 slice. The times are simulated.
32 devices in a mesh: sec: 2 (over core), blk: 16 (over z, y, x).
Axes of the slice: x: 2, y: 2, z: 4, core: 2. Of those that a mesh axis runs over, the one named last changes fastest.
Arguments:
- surface_fields: bfloat16 [2, 3, 1024, 128], P('sec', None, 'blk'), may hold values from -6 to 6
- source_blocks: int32 [2, 1024, 4], P('sec', 'blk'), may hold values from 0 to 15, all different within a row; in each aligned block of 64 rows (0 to 63, 64 to 127, ..., all dimensions but the last counted through in order) at most 16 rows name the same one
- source_columns: int32 [2, 1024, 4], P('sec', 'blk'), may hold values from 0 to 63
- remap_weights: bfloat16 [2, 1024, 4, 128, 128], P('sec', 'blk'), may hold values from -0.25 to 0.25
- ocean_state: float32 [2, 80, 1024, 128], P(None, None, 'blk'), may hold values from -6 to 6
- bathymetry: int32 [1024, 128], P('blk'), may hold values from 1 to 80
Outputs:
- coupled_surface: float32 [2, 3, 1024, 128], P('sec', None, 'blk')
- ocean_tracers: float32 [2, 80, 1024, 128], P(None, None, 'blk')
Inputs may be any that keep to these rules, and one draw needn't show every extreme that they name: `source_blocks`: A destination column's 4 sources lie in different blocks; among the 64 destination columns of one block, no block is named more than 16 times, and that count is reached.
All inputs are finite; a program needn't handle non-finite values.
Results may differ from a plain program's by a relative error of at most 0.00094.
Values may be sent and summed in bfloat16 or wider, within the bound.
No kernel may reach another device: no remote copies, remote signals or barrier semaphores. Data moves between devices by JAX's collectives and lax.ppermute only.
A program may use at most 128 MiB of HBM per device.

v0:
```python
import jax
import jax.numpy as jnp
from jax import lax
from jax.sharding import PartitionSpec as P

NSUB = 2


FLUX_GAIN = 0.5
SIDE_MIX = 0.2
TOP_MIX = 1.0
DEEP_MIX = 2.0


def extended(block, sides, width):
    for axis, dim in sides:
        count = lax.axis_size(axis)
        forward = [(i, i + 1) for i in range(count - 1)]
        forward.append((count - 1, 0))
        backward = [(target, source) for source, target in forward]
        low = lax.ppermute(
            lax.slice_in_dim(block, block.shape[dim] - width, None, axis=dim), axis, forward
        )
        high = lax.ppermute(lax.slice_in_dim(block, 0, width, axis=dim), axis, backward)
        block = jnp.concatenate([low, block, high], axis=dim)
    return block


def from_partner(value, axis, bit):
    mask = 2**bit
    pairs = [(source, source ^ mask) for source in range(lax.axis_size(axis))]
    return lax.ppermute(value, axis, pairs)


def remap_local(fields, block_map, column_map, weight_table):
    column_count = fields.shape[1]
    columns = jnp.transpose(fields, (1, 0, 2))
    gathered = lax.all_gather(columns, "blk", axis=0, tiled=True)
    picked = gathered[(block_map * column_count + column_map).reshape(-1)]
    picked = picked.reshape(column_count, block_map.shape[1], picked.shape[1], picked.shape[2])
    return jnp.einsum("xkij,xkfj->fxi", weight_table, picked, preferred_element_type=jnp.float32)


def side_mix(tracers, wet_mask):
    stacked = jnp.concatenate([tracers * wet_mask[None], wet_mask[None]], axis=0)
    padded = extended(stacked.astype(jnp.bfloat16), (("blk", 2),), 1).astype(stacked.dtype)
    sideways = padded[:, :, 2:] + padded[:, :, :-2]
    edged = jnp.pad(stacked, ((0, 0), (0, 0), (0, 0), (1, 1)))
    sideways = sideways + edged[:, :, :, 2:] + edged[:, :, :, :-2]
    return tracers + SIDE_MIX * wet_mask[None] * (sideways[:2] - sideways[2:3] * tracers)


def column_mix(tracers, wet_mask, heat_flux, fresh_flux, top_mix):
    levels = tracers.shape[1]
    forcing = jnp.stack([heat_flux, fresh_flux])
    links = []
    for layer_index in range(levels - 1):
        strength = top_mix if layer_index == 0 else DEEP_MIX
        links.append(strength * wet_mask[layer_index] * wet_mask[layer_index + 1])
    zero_field = jnp.zeros_like(heat_flux)
    ratios = []
    partials = []
    for layer_index in range(levels):
        upper_link = links[layer_index - 1] if layer_index > 0 else zero_field
        lower_link = links[layer_index] if layer_index < levels - 1 else zero_field
        source_term = tracers[:, layer_index]
        if layer_index == 0:
            source_term = source_term + FLUX_GAIN * forcing
            divisor = 1.0 + lower_link
            partial_value = source_term / divisor
        else:
            divisor = 1.0 + upper_link + lower_link - upper_link * ratios[-1]
            partial_value = (source_term + upper_link * partials[-1]) / divisor
        ratios.append(lower_link / divisor)
        partials.append(partial_value)
    solved = [partials[-1]]
    for layer_index in range(levels - 2, -1, -1):
        solved.append(partials[layer_index] + ratios[layer_index] * solved[-1])
    solved = solved[::-1]
    return jnp.stack(solved, axis=1)


def per_device(
    surface_fields, source_blocks, source_columns, remap_weights, ocean_state, bathymetry
):
    section = lax.axis_index("sec")
    on_ocean = section == 1
    fields = surface_fields[0]
    start_stack = jnp.concatenate([ocean_state[:, 0].astype(jnp.bfloat16), fields[2:3]], axis=0)
    to_remap = jnp.where(on_ocean, start_stack, fields)
    remapped = remap_local(to_remap, source_blocks[0], source_columns[0], remap_weights[0])
    own_fields = fields.astype(jnp.float32)
    outgoing = jnp.concatenate([remapped, own_fields], axis=0)
    partner = from_partner(outgoing, "sec", 0)
    fluxes = jnp.where(on_ocean, partner[:3], remapped)
    ice_fluxes = jnp.where(on_ocean, own_fields, partner[3:])
    returned = jnp.where(on_ocean, remapped, partner[:3])
    heat_flux = fluxes[0] + ice_fluxes[0]
    fresh_flux = fluxes[1] + ice_fluxes[1]
    top_mix = TOP_MIX * (1.0 + fluxes[2] * fluxes[2] + ice_fluxes[2] * ice_fluxes[2])
    levels = ocean_state.shape[1]
    wet_mask = (jnp.arange(levels, dtype=jnp.int32)[:, None, None] < bathymetry[None]).astype(
        jnp.float32
    )
    tracers = ocean_state
    for substep in range(NSUB):
        tracers = side_mix(tracers, wet_mask)
        tracers = column_mix(tracers, wet_mask, heat_flux, fresh_flux, top_mix)
    ocean_side = jnp.stack([tracers[0, 0], tracers[1, 0], top_mix])
    result = jnp.where(on_ocean, ocean_side, returned)
    return (result[None], tracers)


def solution(mesh):
    return jax.shard_map(
        per_device,
        mesh=mesh,
        in_specs=(
            P("sec", None, "blk", None),
            P("sec", "blk", None),
            P("sec", "blk", None),
            P("sec", "blk", None, None, None),
            P(None, None, "blk", None),
            P("blk", None),
        ),
        out_specs=(P("sec", None, "blk", None), P(None, None, "blk", None)),
        check_vma=False,
    )
```

profile of v0, /device:TPU:0, one launch (start us, length us, event | category | flops | bytes accessed | tf_op | source)
XLA Modules:
  0.0 195.9 jit_solution(8031989508527581046)
XLA Ops:
  4.8 47.0 %all_gather.3 = bf16[1024,3,128]{2,0,1:T(8,128)(2,1)S(1)} all-gather(bf16[64,3,128]{2,0,1:T(8,128)(2,1)S(1)} %fusion.217), channel_id=1, replica_groups=mesh['sec'=2,'blk'=16] {'blk'}, dimensions={0}, use_global_device_ids=true | all-gather | bytes 835584 | tf_op jit(solution)/shard_map/all_gather | solution.py:38
  52.4 1.0 gather_fusion
  53.5 5.8 %fusion.13 = f32[64,3,128]{2,1,0:T(4,128)S(1)} fusion(bf16[64,4,3,128]{3,2,1,0:T(4,128)(2,1)S(1)} %bitcast.3636, bf16[1,64,4,128,128]{4,3,2,1,0:T(8,128)(2,1)} %param.9), kind=kOutput, calls=%fused_computation.32 | convolution fusion | flops 25165824 | bytes 8683520 | tf_op jit(solution)/shard_map/xkij,xkfj->fxi/dot_general | solution.py:41
  61.8 5.6 %collective-permute-start.1 = (bf16[3,80,1,128]{3,2,0,1:T(2,128)(2,1)S(1)}, bf16[3,80,1,128]{3,2,0,1:T(2,128)(2,1)S(1)}, u32[]{:S(2)}, u32[]{:S(2)}) collective-permute-start(bf16[3,80,1,128]{3,2,0,1:T(2,128)(2,1)S(1)} %get-tuple-element.327), channel_id=1, source_target_pairs={{1,0},{2,1},{3,2},{4,3},{5,4},{6,5},{7,6},{8,7},{9,8},{10,9},{11,1... | collective-permute-start | bytes 184328 | tf_op jit(solution)/shard_map/ppermute | solution.py:24
  69.6 1.8 fusion.11
  71.4 4.2 %pad_maximum_fusion.1 = f32[3,80,64,128]{3,2,0,1:T(8,128)} fusion(f32[1,80,64,128]{3,2,0,1:T(8,128)S(1)} %fusion.12, f32[2,80,64,128]{3,2,0,1:T(8,128)S(1)} %broadcast_multiply_fusion.1), kind=kLoop, calls=%fused_computation.6 | loop fusion | flops 1966080 | bytes 15728640 | tf_op jit(solution)/shard_map/concatenate | solution.py:45
  76.3 2.7 %maximum_convert_fusion = f32[3,80,66,128]{3,2,0,1:T(8,128)S(1)} fusion(bf16[3,80,1,128]{3,2,0,1:T(2,128)(2,1)S(1)} %collective-permute-done.1, bf16[3,80,64,128]{3,2,0,1:T(8,128)(2,1)S(1)} %fusion.341, bf16[3,80,1,128]{3,2,0,1:T(2,128)(2,1)S(1)} %collective-permute-done), kind=kLoop, calls=%fused_computation.21 | loop fusion | flops 12165120 | bytes 12165120 | tf_op jit(solution)/shard_map/convert_element_type | solution.py:46
  79.0 11.9 %fusion.3 = f32[3,80,64,128]{3,2,0,1:T(8,128)} fusion(f32[3,80,64,128]{3,2,0,1:T(8,128)} %pad_maximum_fusion.1, f32[3,80,66,128]{3,2,0,1:T(8,128)S(1)} %maximum_convert_fusion), kind=kLoop, calls=%fused_computation.10 | loop fusion | flops 5898240 | bytes 31457280 | tf_op jit(solution)/shard_map/add | solution.py:49
  90.9 2.1 %slice_bitcast_fusion.1 = f32[80,64,128]{2,1,0:T(8,128)S(1)} fusion(f32[3,80,64,128]{3,2,0,1:T(8,128)} %fusion.3), kind=kLoop, calls=%fused_computation.24 | loop fusion | bytes 5242880 | tf_op jit(solution)/shard_map/mul | solution.py:50
  93.4 5.1 %fusion.9 = f32[2,80,64,128]{3,2,0,1:T(8,128)S(1)} fusion(f32[3,80,64,128]{3,2,0,1:T(8,128)} %fusion.3, f32[80,64,128]{2,1,0:T(8,128)S(1)} %slice_bitcast_fusion.1, f32[80,64,128]{2,1,0:T(8,128)S(1)} %copy-done, f32[2,80,64,128]{3,2,1,0:T(8,128)} %param.10), kind=kLoop, calls=%fused_computation.20 | loop fusion | flops 5242880 | bytes 20971520 | tf_op jit(solution)/shard_map/add | solution.py:50
  102.5 1.1 fusion.288
  104.3 1.2 multiply_subtract_fusion
  105.6 1.5 divide_bitcast_fusion.26
  108.5 1.6 fusion.282
  110.0 1.4 divide_bitcast_fusion.1
  111.5 1.4 divide_bitcast_fusion.24
  114.9 1.4 divide_bitcast_fusion.16
  116.3 1.5 divide_bitcast_fusion.20
  117.8 1.5 fusion.178
  119.7 3.6 %constant_dynamic-update-slice_fusion.79 = (f32[2,80,64,128]{3,2,0,1:T(8,128)S(1)}, f32[2,64,128]{2,1,0:T(8,128)S(1)}, f32[2,64,128]{2,1,0:T(8,128)S(1)}, f32[2,...) fusion(f32[64,128]{1,0:T(8,128)} %get-tuple-element.423, ...), kind=kLoop, calls=%fused_computation.112 | loop fusion | flops 5849087 | bytes 15204352
  129.7 4.3 %constant_dynamic-update-slice_fusion.62 = (f32[2,80,64,128]{3,2,0,1:T(8,128)S(1)}, f32[2,1,64,128]{3,2,0,1:T(8,128)S(1)}, f32[2,1,64,128]{3,2,0,1:T(8,128)S(1)}...) fusion(f32[2,80,64,128]{3,2,0,1:T(8,128)S(1)} %constant_dynamic, ...), kind=kLoop, calls=%fused_computation.95 | loop fusion | flops 5980160 | bytes 14188544
  135.4 2.3 %copy-done.2 = f32[2,80,64,128]{3,2,0,1:T(8,128)} copy-done((f32[2,80,64,128]{3,2,0,1:T(8,128)}, f32[2,80,64,128]{3,2,0,1:T(8,128)S(1)}, u32[]{:S(2)}) %copy-start.2) | copy-done | bytes 5242904
  139.5 5.6 %collective-permute-start.4 = (bf16[3,80,1,128]{3,2,0,1:T(2,128)(2,1)S(1)}, bf16[3,80,1,128]{3,2,0,1:T(2,128)(2,1)S(1)}, u32[]{:S(2)}, u32[]{:S(2)}) collective-permute-start(bf16[3,80,1,128]{3,2,0,1:T(2,128)(2,1)S(1)} %get-tuple-element.325), channel_id=1, source_target_pairs={{1,0},{2,1},{3,2},{4,3},{5,4},{6,5},{7,6},{8,7},{9,8},{10,9},{11,1... | collective-permute-start | bytes 184328 | tf_op jit(solution)/shard_map/ppermute | solution.py:24
  145.1 4.2 %pad_maximum_fusion = f32[3,80,64,128]{3,2,0,1:T(8,128)} fusion(f32[1,80,64,128]{3,2,0,1:T(8,128)S(1)} %fusion.12, f32[2,80,64,128]{3,2,0,1:T(8,128)S(1)} %broadcast_multiply_fusion), kind=kLoop, calls=%fused_computation.5 | loop fusion | flops 1966080 | bytes 15728640 | tf_op jit(solution)/shard_map/concatenate | solution.py:45
  149.2 2.5 %maximum_convert_fusion.1 = f32[3,80,66,128]{3,2,0,1:T(8,128)S(1)} fusion(bf16[3,80,1,128]{3,2,0,1:T(2,128)(2,1)S(1)} %collective-permute-done.4, bf16[3,80,64,128]{3,2,0,1:T(8,128)(2,1)S(1)} %fusion.342, bf16[3,80,1,128]{3,2,0,1:T(2,128)(2,1)S(1)} %collective-permute-done.3), kind=kLoop, calls=%fused_computation.22 | loop fusion | flops 12165120 | bytes 12165120 | tf_op jit(solution)/shard_map/convert_element_type | solution.py:46
  151.8 11.9 %fusion.5 = f32[3,80,64,128]{3,2,0,1:T(8,128)} fusion(f32[3,80,64,128]{3,2,0,1:T(8,128)} %pad_maximum_fusion, f32[3,80,66,128]{3,2,0,1:T(8,128)S(1)} %maximum_convert_fusion.1), kind=kLoop, calls=%fused_computation.12 | loop fusion | flops 5898240 | bytes 31457280 | tf_op jit(solution)/shard_map/add | solution.py:49
  163.7 3.8 %slice_bitcast_fusion = f32[80,64,128]{2,1,0:T(8,128)} fusion(f32[3,80,64,128]{3,2,0,1:T(8,128)} %fusion.5), kind=kLoop, calls=%fused_computation.23 | loop fusion | bytes 5242880 | tf_op jit(solution)/shard_map/mul | solution.py:50
  167.5 7.4 %fusion.7 = f32[2,80,64,128]{3,2,0,1:T(8,128)S(1)} fusion(f32[2,80,64,128]{3,2,0,1:T(8,128)} %copy-done.2, f32[3,80,64,128]{3,2,0,1:T(8,128)} %fusion.5, f32[80,64,128]{2,1,0:T(8,128)} %slice_bitcast_fusion, f32[80,64,128]{2,1,0:T(8,128)S(1)} %copy-done.1), kind=kLoop, calls=%fused_computation.17 | loop fusion | flops 5242880 | bytes 20971520 | tf_op jit(solution)/shard_map/add | solution.py:50
  175.1 1.8 fusion.94
  177.3 4.1 %constant_dynamic-update-slice_fusion.159 = (f32[2,80,64,128]{3,2,1,0:T(8,128)S(1)}, f32[2,64,128]{2,1,0:T(8,128)S(1)}, f32[2,64,128]{2,1,0:T(8,128)S(1)}, f32[2...) fusion(f32[2,64,128]{2,1,0:T(8,128)S(1)} %get-tuple-element.91,, ...), kind=kLoop, calls=%fused_computation.192 | loop fusion | flops 5849087 | bytes 15269888
  187.9 4.5 %constant_dynamic-update-slice_fusion.142 = (f32[2,80,64,128]{3,2,1,0:T(8,128)S(1)}, f32[2,1,64,128]{3,2,0,1:T(8,128)S(1)}, f32[2,1,64,128]{3,2,0,1:T(8,128)S(1)...) fusion(f32[2,80,64,128]{3,2,1,0:T(8,128)S(1)} %constant_dynamic, ...), kind=kLoop, calls=%fused_computation.175 | loop fusion | flops 5980160 | bytes 14188544
  194.3 1.6 copy-done.122
  (450 shorter events, 34.8 us)
Async XLA Ops:
  59.3 39.2 %collective-permute-start.2 = (f32[6,64,128]{2,1,0:T(8,128)S(1)}, f32[6,64,128]{2,1,0:T(8,128)S(1)}, u32[]{:S(2)}, u32[]{:S(2)}) collective-permute-start(f32[6,64,128]{2,1,0:T(8,128)S(1)} %pad_maximum_fusion.2), channel_id=1, source_target_pairs={{0,16},{16,0},{1,17},{17,1},{2,18},{18,2},{3,19},{19,3},{4,20},{20... | collective-permute-start | bytes 589832 | tf_op jit(solution)/shard_map/ppermute | solution.py:32
  61.7 14.6 %collective-permute-start = (bf16[3,80,1,128]{3,2,0,1:T(2,128)(2,1)S(1)}, bf16[3,80,1,128]{3,2,0,1:T(2,128)(2,1)S(1)}, u32[]{:S(2)}, u32[]{:S(2)}) collective-permute-start(bf16[3,80,1,128]{3,2,0,1:T(2,128)(2,1)S(1)} %get-tuple-element.326), channel_id=1, source_target_pairs={{0,1},{1,2},{2,3},{3,4},{4,5},{5,6},{6,7},{7,8},{8,9},{9,10},{10,1... | collective-permute-start | bytes 184328 | tf_op jit(solution)/shard_map/ppermute | solution.py:21
  61.8 14.5 %collective-permute-start.1 = (bf16[3,80,1,128]{3,2,0,1:T(2,128)(2,1)S(1)}, bf16[3,80,1,128]{3,2,0,1:T(2,128)(2,1)S(1)}, u32[]{:S(2)}, u32[]{:S(2)}) collective-permute-start(bf16[3,80,1,128]{3,2,0,1:T(2,128)(2,1)S(1)} %get-tuple-element.327), channel_id=1, source_target_pairs={{1,0},{2,1},{3,2},{4,3},{5,4},{6,5},{7,6},{8,7},{9,8},{10,9},{11,1... | collective-permute-start | bytes 184328 | tf_op jit(solution)/shard_map/ppermute | solution.py:24
  99.2 30.4 %copy-start.67 = (f32[1,64,128]{2,1,0:T(8,128)}, f32[1,64,128]{2,1,0:T(8,128)S(1)}, u32[]{:S(2)}) copy-start(f32[1,64,128]{2,1,0:T(8,128)S(1)} %get-tuple-element.165) | copy-start | bytes 98308
  99.9 29.7 %copy-start.57 = (f32[1,64,128]{2,1,0:T(8,128)}, f32[1,64,128]{2,1,0:T(8,128)S(1)}, u32[]{:S(2)}) copy-start(f32[1,64,128]{2,1,0:T(8,128)S(1)} %get-tuple-element.170) | copy-start | bytes 98308
  100.5 29.1 %copy-start.59 = (f32[1,64,128]{2,1,0:T(8,128)}, f32[1,64,128]{2,1,0:T(8,128)S(1)}, u32[]{:S(2)}) copy-start(f32[1,64,128]{2,1,0:T(8,128)S(1)} %get-tuple-element.174) | copy-start | bytes 98308
  101.2 28.4 %copy-start.61 = (f32[1,64,128]{2,1,0:T(8,128)}, f32[1,64,128]{2,1,0:T(8,128)S(1)}, u32[]{:S(2)}) copy-start(f32[1,64,128]{2,1,0:T(8,128)S(1)} %get-tuple-element.178) | copy-start | bytes 98308
  101.8 27.8 %copy-start.63 = (f32[1,64,128]{2,1,0:T(8,128)}, f32[1,64,128]{2,1,0:T(8,128)S(1)}, u32[]{:S(2)}) copy-start(f32[1,64,128]{2,1,0:T(8,128)S(1)} %get-tuple-element.182) | copy-start | bytes 98308
  102.5 27.2 %copy-start.65 = (f32[1,64,128]{2,1,0:T(8,128)}, f32[1,64,128]{2,1,0:T(8,128)S(1)}, u32[]{:S(2)}) copy-start(f32[1,64,128]{2,1,0:T(8,128)S(1)} %get-tuple-element.186) | copy-start | bytes 98308
  103.6 31.0 %copy-start.55 = (f32[64,128]{1,0:T(8,128)}, f32[64,128]{1,0:T(8,128)S(1)}, u32[]{:S(2)}) copy-start(f32[64,128]{1,0:T(8,128)S(1)} %get-tuple-element.268) | copy-start | bytes 98308
  103.6 31.0 %copy-start.53 = (f32[64,128]{1,0:T(8,128)}, f32[64,128]{1,0:T(8,128)S(1)}, u32[]{:S(2)}) copy-start(f32[64,128]{1,0:T(8,128)S(1)} %get-tuple-element.264) | copy-start | bytes 98308
  105.5 29.2 %copy-start.25 = (f32[64,128]{1,0:T(8,128)}, f32[64,128]{1,0:T(8,128)S(1)}, u32[]{:S(2)}) copy-start(f32[64,128]{1,0:T(8,128)S(1)} %get-tuple-element.256) | copy-start | bytes 98308
  105.5 29.2 %copy-start.23 = (f32[64,128]{1,0:T(8,128)}, f32[64,128]{1,0:T(8,128)S(1)}, u32[]{:S(2)}) copy-start(f32[64,128]{1,0:T(8,128)S(1)} %get-tuple-element.252) | copy-start | bytes 98308
  105.5 29.2 %copy-start.21 = (f32[64,128]{1,0:T(8,128)}, f32[64,128]{1,0:T(8,128)S(1)}, u32[]{:S(2)}) copy-start(f32[64,128]{1,0:T(8,128)S(1)} %get-tuple-element.248) | copy-start | bytes 98308
  105.6 29.3 %copy-start.19 = (f32[64,128]{1,0:T(8,128)}, f32[64,128]{1,0:T(8,128)S(1)}, u32[]{:S(2)}) copy-start(f32[64,128]{1,0:T(8,128)S(1)} %get-tuple-element.244) | copy-start | bytes 98308
  105.6 29.3 %copy-start.17 = (f32[64,128]{1,0:T(8,128)}, f32[64,128]{1,0:T(8,128)S(1)}, u32[]{:S(2)}) copy-start(f32[64,128]{1,0:T(8,128)S(1)} %get-tuple-element.240) | copy-start | bytes 98308
  105.6 29.3 %copy-start.15 = (f32[64,128]{1,0:T(8,128)}, f32[64,128]{1,0:T(8,128)S(1)}, u32[]{:S(2)}) copy-start(f32[64,128]{1,0:T(8,128)S(1)} %get-tuple-element.236) | copy-start | bytes 98308
  105.6 29.4 %copy-start.13 = (f32[64,128]{1,0:T(8,128)}, f32[64,128]{1,0:T(8,128)S(1)}, u32[]{:S(2)}) copy-start(f32[64,128]{1,0:T(8,128)S(1)} %get-tuple-element.232) | copy-start | bytes 98308
  105.6 29.4 %copy-start.11 = (f32[64,128]{1,0:T(8,128)}, f32[64,128]{1,0:T(8,128)S(1)}, u32[]{:S(2)}) copy-start(f32[64,128]{1,0:T(8,128)S(1)} %get-tuple-element.228) | copy-start | bytes 98308
  105.6 29.5 %copy-start.9 = (f32[64,128]{1,0:T(8,128)}, f32[64,128]{1,0:T(8,128)S(1)}, u32[]{:S(2)}) copy-start(f32[64,128]{1,0:T(8,128)S(1)} %get-tuple-element.224) | copy-start | bytes 98308
  105.6 29.5 %copy-start.7 = (f32[64,128]{1,0:T(8,128)}, f32[64,128]{1,0:T(8,128)S(1)}, u32[]{:S(2)}) copy-start(f32[64,128]{1,0:T(8,128)S(1)} %get-tuple-element.220) | copy-start | bytes 98308
  105.6 29.5 %copy-start.5 = (f32[64,128]{1,0:T(8,128)}, f32[64,128]{1,0:T(8,128)S(1)}, u32[]{:S(2)}) copy-start(f32[64,128]{1,0:T(8,128)S(1)} %get-tuple-element.216) | copy-start | bytes 98308
  105.6 29.6 %copy-start.3 = (f32[64,128]{1,0:T(8,128)}, f32[64,128]{1,0:T(8,128)S(1)}, u32[]{:S(2)}) copy-start(f32[64,128]{1,0:T(8,128)S(1)} %get-tuple-element.212) | copy-start | bytes 98308
  107.1 22.6 %copy-start.27 = (f32[1,64,128]{2,1,0:T(8,128)}, f32[1,64,128]{2,1,0:T(8,128)S(1)}, u32[]{:S(2)}) copy-start(f32[1,64,128]{2,1,0:T(8,128)S(1)} %get-tuple-element.194) | copy-start | bytes 98308
  108.1 21.6 %copy-start.73 = (f32[1,64,128]{2,1,0:T(8,128)}, f32[1,64,128]{2,1,0:T(8,128)S(1)}, u32[]{:S(2)}) copy-start(f32[1,64,128]{2,1,0:T(8,128)S(1)} %get-tuple-element.283) | copy-start | bytes 98308
  108.1 21.6 %copy-start.75 = (f32[1,64,128]{2,1,0:T(8,128)}, f32[1,64,128]{2,1,0:T(8,128)S(1)}, u32[]{:S(2)}) copy-start(f32[1,64,128]{2,1,0:T(8,128)S(1)} %get-tuple-element.284) | copy-start | bytes 98308
  108.1 21.6 %copy-start.77 = (f32[1,64,128]{2,1,0:T(8,128)}, f32[1,64,128]{2,1,0:T(8,128)S(1)}, u32[]{:S(2)}) copy-start(f32[1,64,128]{2,1,0:T(8,128)S(1)} %get-tuple-element.289) | copy-start | bytes 98308
  108.1 21.6 %copy-start.79 = (f32[1,64,128]{2,1,0:T(8,128)}, f32[1,64,128]{2,1,0:T(8,128)S(1)}, u32[]{:S(2)}) copy-start(f32[1,64,128]{2,1,0:T(8,128)S(1)} %get-tuple-element.290) | copy-start | bytes 98308
  110.0 24.4 %copy-start.51 = (f32[64,128]{1,0:T(8,128)}, f32[64,128]{1,0:T(8,128)S(1)}, u32[]{:S(2)}) copy-start(f32[64,128]{1,0:T(8,128)S(1)} %get-tuple-element.411) | copy-start | bytes 98308
  111.4 23.1 %copy-start.49 = (f32[64,128]{1,0:T(8,128)}, f32[64,128]{1,0:T(8,128)S(1)}, u32[]{:S(2)}) copy-start(f32[64,128]{1,0:T(8,128)S(1)} %get-tuple-element.412) | copy-start | bytes 98308
  139.4 9.8 %collective-permute-start.3 = (bf16[3,80,1,128]{3,2,0,1:T(2,128)(2,1)S(1)}, bf16[3,80,1,128]{3,2,0,1:T(2,128)(2,1)S(1)}, u32[]{:S(2)}, u32[]{:S(2)}) collective-permute-start(bf16[3,80,1,128]{3,2,0,1:T(2,128)(2,1)S(1)} %get-tuple-element.324), channel_id=1, source_target_pairs={{0,1},{1,2},{2,3},{3,4},{4,5},{5,6},{6,7},{7,8},{8,9},{9,10},{10,1... | collective-permute-start | bytes 184328 | tf_op jit(solution)/shard_map/ppermute | solution.py:21
  139.5 9.8 %collective-permute-start.4 = (bf16[3,80,1,128]{3,2,0,1:T(2,128)(2,1)S(1)}, bf16[3,80,1,128]{3,2,0,1:T(2,128)(2,1)S(1)}, u32[]{:S(2)}, u32[]{:S(2)}) collective-permute-start(bf16[3,80,1,128]{3,2,0,1:T(2,128)(2,1)S(1)} %get-tuple-element.325), channel_id=1, source_target_pairs={{1,0},{2,1},{3,2},{4,3},{5,4},{6,5},{7,6},{8,7},{9,8},{10,9},{11,1... | collective-permute-start | bytes 184328 | tf_op jit(solution)/shard_map/ppermute | solution.py:24
  (98 other events, 864.1 us)
where the time goes:
time: 198 us; the launch traced here: 196 us
  other arithmetic  113 us (57%)
  blocking collectives  47 us (24%)
  local copies, waits for them, and re-layouts  15.1 us (8%)
  starting transfers between devices  11.4 us (6%)
  matrix products  5.8 us (3%)
  between operations  3.67 us (2%)
    all_gather x1, blocking collectives, remap_local(): gathered = lax.all_gather(columns, 'blk', axis=0, tiled=True)  47 us
    unnamed x83, other arithmetic  29.7 us
    add x2, other arithmetic, side_mix(): sideways = sideways + edged[:, :, :, 2:] + edged[:, :, :, :-2]  23.8 us
    mul x15, other arithmetic, column_mix(): solved.append(partials[layer_index] + ratios[layer_index] * solved[-1])  13.8 us
    add x2, other arithmetic, side_mix(): tracers + SIDE_MIX * wet_mask[None] * (sideways[:2] - sideways[2:3] * tra...  12.5 us
    ppermute x2, starting transfers between devices, extended(): lax.ppermute(lax.slice_in_dim(block, 0, width, axis=dim), axis, backward)  11.2 us
    concatenate x2, other arithmetic, side_mix(): jnp.concatenate([tracers * wet_mask[None], wet_mask[None]], axis=0)  8.32 us
    div x4, other arithmetic, column_mix(): partial_value = (source_term + upper_link * partials[-1]) / divisor  5.84 us
  transfers between devices with their start and end apart: 5, of which 0 were waited for; matrix products, arithmetic and copies ran while one was open for 19% of the time, Pallas kernels for 0%

commit v1 on v0

v1 whole, which is shorter than its diff:
```python
import functools

import jax
import jax.numpy as jnp
from jax import lax
from jax.experimental import pallas as pl
from jax.experimental.pallas import tpu as pltpu
from jax.sharding import PartitionSpec as P

FLUX_GAIN = 0.5
SIDE_MIX = 0.2
TOP_MIX = 1.0
DEEP_MIX = 2.0

EDGE = 8
MIB = 2**20


def neighbour_sum(h, lane):
    rows, lanes = h.shape
    total = pltpu.roll(h, 1, 0) + pltpu.roll(h, rows - 1, 0)
    total = total + jnp.where(lane == 0, 0.0, pltpu.roll(h, 1, 1))
    return total + jnp.where(lane == lanes - 1, 0.0, pltpu.roll(h, lanes - 1, 1))


def chunks_of(levels):
    size = 10 if levels % 10 == 0 else levels
    return [(start, size) for start in range(0, levels, size)]


def start_kernel(state, halo, bath, q_out, rho_out, side_out, held, near, sems):
    tracers, levels, columns, lanes = state.shape
    rows = columns + EDGE
    chunks = chunks_of(levels)
    copies = []
    for n, (low, size) in enumerate(chunks):
        copies.append(
            pltpu.make_async_copy(
                state.at[:, pl.ds(low, size)], held.at[:, pl.ds(low, size)], sems.at[n]
            )
        )
    for copy in reversed(copies):
        copy.start()
    lane = lax.broadcasted_iota(jnp.int32, (rows, lanes), 1)
    depth = bath[...]
    near[0] = pltpu.roll(depth, 1, 0)
    near[1] = pltpu.roll(depth, rows - 1, 0)
    near[2] = jnp.where(lane == 0, 0, pltpu.roll(depth, 1, 1))
    near[3] = jnp.where(lane == lanes - 1, 0, pltpu.roll(depth, lanes - 1, 1))

    def side(level):
        wet = level < bath[...]
        count = jnp.where(level < near[0], 1.0, 0.0)
        for n in range(1, 4):
            count = count + jnp.where(level < near[n], 1.0, 0.0)
        own = 0.5 - 0.5 * SIDE_MIX * count
        side_out[level] = own[:columns]
        halves = []
        for n in range(tracers):
            full = jnp.concatenate([held[n, level], halo[n, level]], axis=0)
            h = jnp.where(wet, full, 0.0)
            halves.append(own * h + 0.5 * SIDE_MIX * neighbour_sum(h, lane))
        return wet, halves

    def deep(step, carry, top):
        level = top - step
        rho_below, *below = carry
        wet, halves = side(level)
        linked = jnp.where(level + 1 < bath[...], DEEP_MIX - DEEP_MIX * rho_below, 0.0)
        rho = jnp.where(wet, DEEP_MIX / (1.0 + DEEP_MIX + linked), 0.0)
        rho_out[level] = rho
        solved = []
        for n in range(tracers):
            q = rho * (halves[n] + below[n])
            q_out[n, level] = q
            solved.append(q)
        return (rho, *solved)

    carry = tuple(jnp.zeros((rows, lanes), jnp.float32) for _ in range(1 + tracers))
    for n in reversed(range(len(chunks))):
        low, size = chunks[n]
        copies[n].wait()
        first = max(low, 2)
        top = low + size - 1
        carry = lax.fori_loop(
            0, top - first + 1, functools.partial(deep, top=top), carry
        )
    for level in (1, 0):
        _, halves = side(level)
        rho_out[level] = jnp.zeros((rows, lanes), jnp.float32)
        for n in range(tracers):
            q_out[n, level] = halves[n]


def remap_kernel(
    section, table, index, edge_ice, edge_weights, weights, out, picked, solved, held, sems
):
    columns, slots, width, _ = weights.shape
    rows = columns + EDGE
    fields = out.shape[0]
    group = 8
    copies = []
    for n in range(columns // group):
        copies.append(
            pltpu.make_async_copy(
                weights.at[pl.ds(n * group, group)], held.at[pl.ds(n * group, group)], sems.at[n]
            )
        )
        copies[-1].start()
    spots = lax.broadcasted_iota(jnp.int32, (rows, table.shape[0]), 1)
    picked[...] = jnp.zeros_like(picked)
    for k in range(slots):
        chosen = (spots == index[k]).astype(jnp.bfloat16)
        found = jnp.dot(chosen, table[...], preferred_element_type=jnp.float32)
        for f in range(fields):
            picked[k, pl.ds(f, rows, stride=8), :] = found[
                :, f * width : (f + 1) * width
            ]
    solved[...] = jnp.zeros_like(solved)

    def one(row, table_of):
        spot = pl.ds(row * 8, 8)
        left = jnp.concatenate([picked[k, spot, :] for k in range(slots)], axis=1)
        left = left.astype(jnp.bfloat16)
        right = jnp.concatenate([table_of(k) for k in range(slots)], axis=1)
        solved[spot, :] = lax.dot_general(
            left, right, (((1,), (1,)), ((), ())), preferred_element_type=jnp.float32
        )

    one(columns, lambda k: edge_weights[1, k])
    one(rows - 1, lambda k: edge_weights[0, k])
    for n in range(columns // group):
        copies[n].wait()
        for m in range(group):
            row = n * group + m
            one(row, lambda k: held[row, k])
    on_ocean = section[0] == 1
    for f in range(fields):
        out[f, pl.ds(0, columns)] = solved[pl.ds(f, columns, stride=8), :]
        edge = solved[pl.ds(columns * 8 + f, EDGE, stride=8), :]
        out[f, pl.ds(columns, EDGE)] = jnp.where(on_ocean, edge_ice[f], edge)


def finish_kernel(
    section, mine, other, ice, bath, state, q_in, rho_in, side_in, surface, result,
    q, rho, side, held, done, sems_in, sems_state, sems_out,
):
    tracers, levels, columns, lanes = state.shape
    rows = columns + EDGE
    chunks = chunks_of(levels)
    arrivals = []
    for n, (low, size) in enumerate(chunks):
        part = pl.ds(low, size)
        arrivals.append(
            (
                pltpu.make_async_copy(q_in.at[:, part], q.at[:, part], sems_in.at[n, 0]),
                pltpu.make_async_copy(rho_in.at[part], rho.at[part], sems_in.at[n, 1]),
                pltpu.make_async_copy(side_in.at[part], side.at[part], sems_in.at[n, 2]),
            )
        )
        for copy in arrivals[-1]:
            copy.start()
    starts = []
    for n, (low, size) in enumerate(chunks):
        part = pl.ds(low, size)
        starts.append(
            pltpu.make_async_copy(state.at[:, part], held.at[:, part], sems_state.at[n])
        )
        starts[-1].start()

    on_ocean = section[0] == 1
    lane = lax.broadcasted_iota(jnp.int32, (rows, lanes), 1)
    flux = [jnp.where(on_ocean, other[f], mine[f]) for f in range(3)]
    own = []
    for f in range(3):
        edge = jnp.where(on_ocean, mine[f, pl.ds(columns, EDGE)], other[f, pl.ds(columns, EDGE)])
        own.append(jnp.concatenate([ice[f], edge], axis=0))
    forcing = [flux[0] + own[0], flux[1] + own[1]]
    top_mix = TOP_MIX * (1.0 + flux[2] * flux[2] + own[2] * own[2])
    depth = bath[...]

    def top_levels(count, halves, below, rho_below):
        wet = 1 < depth[:count]
        link = jnp.where(wet, top_mix[:count], 0.0)
        deeper = jnp.where(2 < depth[:count], DEEP_MIX - DEEP_MIX * rho_below, 0.0)
        second = 1.0 / (1.0 + link + deeper)
        rho_second = link * second
        first = 1.0 / (1.0 + link - link * rho_second)
        values = []
        for n in range(tracers):
            partial = 2.0 * (halves[n][1] + below[n]) * second
            source = 2.0 * halves[n][0] + FLUX_GAIN * forcing[n][:count]
            surface_value = (source + link * partial) * first
            next_value = jnp.where(wet, partial, 0.0) + rho_second * surface_value
            values.append((surface_value, next_value))
        return values

    for copy in arrivals[0]:
        copy.wait()
    values = top_levels(
        rows,
        [(q[n, 0], q[n, 1]) for n in range(tracers)],
        [q[n, 2] for n in range(tracers)],
        rho[2],
    )

    def store_half(n, level, h):
        q[n, level, pl.ds(0, columns)] = (
            side[level] * h[:columns]
            + 0.5 * SIDE_MIX * neighbour_sum(h, lane)[:columns]
        )

    for n in range(tracers):
        for level in (0, 1):
            store_half(n, level, values[n][level])

    def down(step, carry, low):
        level = low + step
        ratio = rho[level]
        out = []
        for n in range(tracers):
            h = q[n, level] + ratio * carry[n]
            store_half(n, level, h)
            out.append(h)
        return tuple(out)

    carry = tuple(values[n][1] for n in range(tracers))
    for n, (low, size) in enumerate(chunks):
        if n > 0:
            for copy in arrivals[n]:
                copy.wait()
        first = max(low, 2)
        carry = lax.fori_loop(
            0, low + size - first, functools.partial(down, low=first), carry
        )

    def up(step, carry):
        level = levels - 1 - step
        ratio = rho[level, pl.ds(0, columns)]
        out = []
        for n in range(tracers):
            value = ratio * (q[n, level, pl.ds(0, columns)] + carry[n])
            q[n, level, pl.ds(0, columns)] = value
            out.append(value)
        return tuple(out)

    zero = jnp.zeros((columns, lanes), jnp.float32)
    carry = lax.fori_loop(0, levels - 2, up, (zero,) * tracers)
    values = top_levels(
        columns,
        [(q[n, 0, pl.ds(0, columns)], q[n, 1, pl.ds(0, columns)]) for n in range(tracers)],
        carry,
        rho[2, pl.ds(0, columns)],
    )
    for n in range(tracers):
        surface[n] = jnp.where(on_ocean, values[n][0], other[n, pl.ds(0, columns)])
    surface[2] = jnp.where(on_ocean, top_mix[:columns], other[2, pl.ds(0, columns)])

    def last(step, carry, low):
        level = low + step
        ratio = rho[level, pl.ds(0, columns)]
        wet = level < bath[pl.ds(0, columns)]
        out = []
        for n in range(tracers):
            h = q[n, level, pl.ds(0, columns)] + ratio * carry[n]
            done[n, level] = jnp.where(wet, h, held[n, level])
            out.append(h)
        return tuple(out)

    carry = tuple(values[n][1] for n in range(tracers))
    leaving = []
    for n, (low, size) in enumerate(chunks):
        starts[n].wait()
        if n == 0:
            for m in range(tracers):
                done[m, 0] = values[m][0]
                done[m, 1] = jnp.where(1 < depth[:columns], values[m][1], held[m, 1])
        first = max(low, 2)
        carry = lax.fori_loop(
            0, low + size - first, functools.partial(last, low=first), carry
        )
        part = pl.ds(low, size)
        leaving.append(
            pltpu.make_async_copy(done.at[:, part], result.at[:, part], sems_out.at[n])
        )
        leaving[-1].start()
    for copy in leaving:
        copy.wait()


def shift(value, axis, by):
    count = lax.axis_size(axis)
    return lax.ppermute(value, axis, [(i, (i + by) % count) for i in range(count)])


def per_device(
    surface_fields, source_blocks, source_columns, remap_weights, ocean_state, bathymetry
):
    tracers, levels, columns, lanes = ocean_state.shape
    slots = source_blocks.shape[2]
    rows = columns + EDGE
    bf16, f32 = jnp.bfloat16, jnp.float32
    on_ocean = lax.axis_index("sec") == 1
    section = lax.axis_index("sec").astype(jnp.int32).reshape(1)
    fields = surface_fields[0]
    blocks, spots, weights = source_blocks[0], source_columns[0], remap_weights[0]

    start_stack = jnp.concatenate([ocean_state[:, 0].astype(bf16), fields[2:3]], axis=0)
    to_remap = jnp.where(on_ocean, start_stack, fields)
    table = jnp.concatenate([to_remap[f] for f in range(3)], axis=1)
    gathered = lax.all_gather(table, "blk", axis=0, tiled=True)

    def edge_of(low, at):
        rows_of = [
            ocean_state[:, :, low : low + 2].astype(bf16).reshape(tracers * levels * 2, lanes),
            bathymetry[low : low + 2].astype(bf16),
            fields[:, at],
            jnp.pad(blocks[at].astype(bf16), (0, lanes - slots))[None],
            jnp.pad(spots[at].astype(bf16), (0, lanes - slots))[None],
        ]
        return jnp.concatenate(rows_of, axis=0)

    from_left = shift(edge_of(columns - 2, columns - 1), "blk", 1)
    from_right = shift(edge_of(0, 0), "blk", -1)
    left_weights = shift(weights[columns - 1], "blk", 1)
    right_weights = shift(weights[0], "blk", -1)
    partner_fields = lax.ppermute(fields, "sec", [(0, 1), (1, 0)])

    many = tracers * levels * 2

    def edge_tile(right, left, dtype):
        gap = EDGE - right.shape[-2] - left.shape[-2]
        middle = jnp.zeros(right.shape[:-2] + (gap, lanes), dtype)
        return jnp.concatenate([right.astype(dtype), middle, left.astype(dtype)], axis=-2)

    halo = edge_tile(
        from_right[:many].reshape(tracers, levels, 2, lanes),
        from_left[:many].reshape(tracers, levels, 2, lanes),
        f32,
    )
    bath_edge = edge_tile(from_right[many : many + 2], from_left[many : many + 2], jnp.int32)
    bath = jnp.concatenate([bathymetry, bath_edge], axis=0)
    edge_ice = edge_tile(
        from_right[many + 2 : many + 5][:, None], from_left[many + 2 : many + 5][:, None], f32
    )

    def flat(block_row, spot_row):
        return block_row.astype(jnp.int32) * columns + spot_row.astype(jnp.int32)

    right_index = flat(from_right[many + 5, :slots], from_right[many + 6, :slots])
    left_index = flat(from_left[many + 5, :slots], from_left[many + 6, :slots])
    index = jnp.concatenate(
        [
            flat(blocks, spots),
            right_index[None],
            jnp.zeros((EDGE - 2, slots), jnp.int32),
            left_index[None],
        ],
        axis=0,
    )
    index = jnp.transpose(index)[:, :, None]
    edge_weights = jnp.stack([left_weights, right_weights])
    ice = jnp.where(on_ocean, fields, partner_fields).astype(f32)

    anywhere = pl.BlockSpec(memory_space=pl.ANY)
    vmem = pl.BlockSpec(memory_space=pltpu.VMEM)
    smem = pl.BlockSpec(memory_space=pltpu.SMEM)
    pieces = len(chunks_of(levels))
    cells = rows * lanes
    q, rho, side = pl.pallas_call(
        start_kernel,
        out_shape=(
            jax.ShapeDtypeStruct((tracers, levels, rows, lanes), f32),
            jax.ShapeDtypeStruct((levels, rows, lanes), f32),
            jax.ShapeDtypeStruct((levels, columns, lanes), f32),
        ),
        in_specs=[anywhere, vmem, vmem],
        out_specs=(vmem, vmem, vmem),
        scratch_shapes=[
            pltpu.VMEM((tracers, levels, columns, lanes), f32),
            pltpu.VMEM((4, rows, lanes), jnp.int32),
            pltpu.SemaphoreType.DMA((pieces,)),
        ],
        compiler_params=pltpu.CompilerParams(vmem_limit_bytes=28 * MIB),
        cost_estimate=pl.CostEstimate(
            flops=60 * levels * cells, bytes_accessed=20 * levels * cells, transcendentals=0
        ),
    )(ocean_state, halo, bath)

    mine = pl.pallas_call(
        remap_kernel,
        out_shape=jax.ShapeDtypeStruct((3, rows, lanes), f32),
        in_specs=[smem, vmem, vmem, vmem, vmem, anywhere],
        out_specs=vmem,
        scratch_shapes=[
            pltpu.VMEM((slots, rows * 8, lanes), f32),
            pltpu.VMEM((rows * 8, lanes), f32),
            pltpu.VMEM(weights.shape, bf16),
            pltpu.SemaphoreType.DMA((columns // 8,)),
        ],
        compiler_params=pltpu.CompilerParams(vmem_limit_bytes=24 * MIB),
        cost_estimate=pl.CostEstimate(
            flops=2 * weights.size * 8, bytes_accessed=2 * weights.size, transcendentals=0
        ),
    )(section, gathered, index, edge_ice, edge_weights, weights)
    other = lax.ppermute(mine, "sec", [(0, 1), (1, 0)])

    surface, result = pl.pallas_call(
        finish_kernel,
        out_shape=(
            jax.ShapeDtypeStruct((3, columns, lanes), f32),
            jax.ShapeDtypeStruct((tracers, levels, columns, lanes), f32),
        ),
        in_specs=[smem, vmem, vmem, vmem, vmem, anywhere, anywhere, anywhere, anywhere],
        out_specs=(vmem, anywhere),
        scratch_shapes=[
            pltpu.VMEM((tracers, levels, rows, lanes), f32),
            pltpu.VMEM((levels, rows, lanes), f32),
            pltpu.VMEM((levels, columns, lanes), f32),
            pltpu.VMEM((tracers, levels, columns, lanes), f32),
            pltpu.VMEM((tracers, levels, columns, lanes), f32),
            pltpu.SemaphoreType.DMA((pieces, 3)),
            pltpu.SemaphoreType.DMA((pieces,)),
            pltpu.SemaphoreType.DMA((pieces,)),
        ],
        compiler_params=pltpu.CompilerParams(vmem_limit_bytes=32 * MIB),
        cost_estimate=pl.CostEstimate(
            flops=60 * levels * cells, bytes_accessed=32 * levels * cells, transcendentals=0
        ),
    )(section, mine, other, ice, bath, ocean_state, q, rho, side)
    return (surface[None], result)


def solution(mesh):
    return jax.shard_map(
        per_device,
        mesh=mesh,
        in_specs=(
            P("sec", None, "blk", None),
            P("sec", "blk", None),
            P("sec", "blk", None),
            P("sec", "blk", None, None, None),
            P(None, None, "blk", None),
            P("blk", None),
        ),
        out_specs=(P("sec", None, "blk", None), P(None, None, "blk", None)),
        check_vma=False,
    )
```

time: 198 us -> 109 us (0.55)
  other arithmetic: 113 us -> 5.36 us
  Pallas kernels: 0 us -> 32.5 us
  blocking collectives: 47 us -> 40.2 us
  matrix products: 5.8 us -> 0 us
  between operations: 3.67 us -> 1.08 us
    add x5 -> x3, other arithmetic: 37 us -> 1.54 us  [flat(): return block_row.astype(jnp.int32) * columns + spot_row.astype(jnp.int32)]
    pallas_call x0 -> x3, Pallas kernels: none -> 32.5 us  [the longest x1 17.5 us: per_device(): pl.pallas_call(finish_kernel, out_shape=(jax.ShapeDtypeStruct((3, columns...]
    unnamed x83 -> x1, other arithmetic: 29.7 us -> 0.01 us
    mul x22 -> x0, other arithmetic: 20.4 us -> none  [the longest x15 13.8 us: column_mix(): solved.append(partials[layer_index] + ratios[layer_index] * solved[-1])]
    concatenate x3 -> x4, other arithmetic: 8.33 us -> 0.33 us  [the longest x2 0.24 us: edge_tile(): jnp.concatenate([right.astype(dtype), middle, left.astype(dtype)], axis=-2)]
    unnamed x326 -> x14, local copies, waits for them, and re-layouts: 5.47 us -> 12.6 us
    div x5 -> x0, other arithmetic: 6.95 us -> none  [the longest x4 5.84 us: column_mix(): partial_value = (source_term + upper_link * partials[-1]) / divisor]
    all_gather x1, blocking collectives: 47 us -> 40.2 us  [per_device(): gathered = lax.all_gather(table, 'blk', axis=0, tiled=True)]
  transfers between devices with their start and end apart: 5 -> 6, of which waited for: 0 -> 0; matrix products, arithmetic and copies ran while one was open for 19% -> 15% of each run, Pallas kernels for 0% -> 10%
where the time goes in v1:
time: 109 us
  blocking collectives  40.2 us (37%)
  Pallas kernels  32.5 us (30%)
  local copies, waits for them, and re-layouts  16.5 us (15%)
  starting transfers between devices  12.8 us (12%)
  other arithmetic  5.36 us (5%)
    all_gather x1, blocking collectives, per_device(): gathered = lax.all_gather(table, 'blk', axis=0, tiled=True)  40.2 us
    pallas_call x1, Pallas kernels, per_device(): pl.pallas_call(finish_kernel, out_shape=(jax.ShapeDtypeStruct((3, columns...  17.5 us
    unnamed x14, local copies, waits for them, and re-layouts  12.6 us
    ppermute x4, starting transfers between devices, shift(): lax.ppermute(value, axis, [(i, (i + by) % count) for i in range(count)])  12.3 us
    pallas_call x1, Pallas kernels, per_device(): pl.pallas_call(start_kernel, out_shape=(jax.ShapeDtypeStruct((tracers, le...  10.4 us
    pallas_call x1, Pallas kernels, per_device(): pl.pallas_call(remap_kernel, out_shape=jax.ShapeDtypeStruct((3, rows, lan...  4.69 us
  transfers between devices with their start and end apart: 6, of which 0 were waited for; matrix products, arithmetic and copies ran while one was open for 15% of the time, Pallas kernels for 10%

profile of v1, /device:TPU:0, one launch (start us, length us, event | category | flops | bytes accessed | tf_op | source)
XLA Modules:
  0.0 108.5 jit_solution(14897504491586103845)
XLA Ops:
  0.6 1.5 %copy.75 = bf16[1,3,64,128]{3,1,2,0:T(4,128)(2,1)} copy(bf16[1,3,64,128]{3,2,1,0:T(8,128)(2,1)} %param.6) | data formatting | bytes 98304 | tf_op args[0]
  2.2 0.5 collective-permute-start.5
  2.6 1.0 slice_bitcast_fusion.1
  3.6 2.5 %collective-permute-start.2 = (bf16[4,128,128]{2,1,0:T(8,128)(2,1)S(1)}, bf16[4,128,128]{2,1,0:T(8,128)(2,1)S(1)}, u32[]{:S(2)}, u32[]{:S(2)}) collective-permute-start(bf16[4,128,128]{2,1,0:T(8,128)(2,1)S(1)} %get-tuple-element.16), channel_id=1, source_target_pairs={{0,1},{1,2},{2,3},{3,4},{4,5},{5,6},{6,7},{7,8},{8,9},{9,10},{10,1... | collective-permute-start | bytes 393224 | tf_op jit(solution)/shard_map/ppermute | solution.py:293
  6.2 4.1 %collective-permute-start.3 = (bf16[4,128,128]{2,1,0:T(8,128)(2,1)S(1)}, bf16[4,128,128]{2,1,0:T(8,128)(2,1)S(1)}, u32[]{:S(2)}, u32[]{:S(2)}) collective-permute-start(bf16[4,128,128]{2,1,0:T(8,128)(2,1)S(1)} %get-tuple-element.17), channel_id=1, source_target_pairs={{0,15},{1,0},{2,1},{3,2},{4,3},{5,4},{6,5},{7,6},{8,7},{9,8},{10,9... | collective-permute-start | bytes 393224 | tf_op jit(solution)/shard_map/ppermute | solution.py:293
  10.2 0.7 slice_bitcast_fusion.7
  10.9 0.8 add_bitcast_fusion.1
  11.7 0.2 slice_reduce_fusion.2
  11.9 0.8 convert.22
  12.7 7.4 %copy.74 = bf16[2,80,64,128]{3,0,2,1:T(2,128)(2,1)S(1)} copy(f32[2,80,64,128]{3,2,1,0:T(8,128)} %state.3) | data formatting | bytes 7864320 | tf_op args[4]
  20.1 0.1 fusion.6
  20.5 5.6 %collective-permute-start = (bf16[327,128]{1,0:T(8,128)(2,1)S(1)}, bf16[327,128]{1,0:T(8,128)(2,1)S(1)}, u32[]{:S(2)}, u32[]{:S(2)}) collective-permute-start(bf16[327,128]{1,0:T(8,128)(2,1)S(1)} %concatenate.26), channel_id=1, source_target_pairs={{0,15},{1,0},{2,1},{3,2},{4,3},{5,4},{6,5},{7,6},{8,7},{9,8},{10,9... | collective-permute-start | bytes 251144 | tf_op jit(solution)/shard_map/ppermute | solution.py:293
  26.2 0.1 pad.22.clone
  26.3 0.1 pad.31.clone
  26.4 0.1 pad.18.clone
  26.5 0.1 pad.27.clone
  26.6 1.0 select_convert_fusion
  27.7 40.2 %all_gather.3.table = bf16[1024,384]{1,0:T(8,128)(2,1)S(1)} all-gather(bf16[64,384]{1,0:T(8,128)(2,1)S(1)} %pad_maximum_fusion.2), channel_id=1, replica_groups=mesh['sec'=2,'blk'=16] {'blk'}, dimensions={0}, use_global_device_ids=true | all-gather | bytes 835584 | tf_op jit(solution)/shard_map/all_gather | solution.py:311
  67.9 0.7 fusion
  68.6 0.8 fusion.2
  69.4 0.1 copy.57
  69.5 0.9 slice.146
  70.5 0.1 copy.56
  70.6 0.1 add_bitcast_fusion
  70.7 0.1 copy.60.index
  70.9 0.2 pad_maximum_fusion.halo
  71.1 0.8 slice_convert_fusion
  72.0 3.6 %copy-done = bf16[1,64,4,128,128]{4,3,2,1,0:T(8,128)(2,1)S(1)} copy-done((bf16[1,64,4,128,128]{4,3,2,1,0:T(8,128)(2,1)S(1)}, bf16[1,64,4,128,128]{4,3,2,1,0:T(8,128)(2,1)}, u32[]{:S(2)}) %copy-start) | copy-done | bytes 8388632
  75.6 4.7 %shard_map.77.mine = f32[3,72,128]{2,1,0:T(8,128)S(1)} custom-call(s32[1]{0:T(128)} %bitcast.section, bf16[1024,384]{1,0:T(8,128)(2,1)S(1)} %all_gather.3.table, s32[4,72,1]{2,1,0:T(8,128)S(1)} %copy.60.index, f32[3,8,128]{2,1,0:T(8,128)S(1)} %pad_maximum_fusion.3.edge_ice, bf16[2,4,128,128]{3,2,1,0:T(8,128)(2,1)S(1)} %pad_maximum_fusion.1.edge_weights, ...), custom_call_target="tpu_custom_call" | custom-call | flops 67108864 | bytes 8388608 | tf_op jit(solution)/shard_map/pallas_call | solution.py:390
  80.4 0.1 pad_add_fusion.bath
  80.5 10.4 %shard_map.78 = (f32[2,80,72,128]{3,2,1,0:T(8,128)S(1)}, f32[80,72,128]{2,1,0:T(8,128)S(1)}, f32[80,64,128]{2,1,0:T(8,128)S(1)}) custom-call(f32[2,80,64,128]{3,2,1,0:T(8,128)S(1)} %bitcast.62, f32[2,80,8,128]{3,2,1,0:T(8,128)S(1)} %pad_maximum_fusion.halo, s32[72,128]{1,0:T(8,128)S(1)} %pad_add_fusion.bath), custom_call_target="tpu_custom_call" | custom-call | flops 44236800 | bytes 14745600 | tf_op jit(solution)/shard_map/pallas_call | solution.py:370
  90.9 17.5 %shard_map.79 = (f32[3,64,128]{2,1,0:T(8,128)}, f32[2,80,64,128]{3,2,1,0:T(8,128)}) custom-call(s32[1]{0:T(128)} %bitcast.section, f32[3,72,128]{2,1,0:T(8,128)S(1)} %shard_map.77.mine, f32[3,72,128]{2,1,0:T(8,128)S(1)} %collective-permute-done.4.other, f32[3,64,128]{2,1,0:T(8,128)S(1)} %copy.61.ice, s32[72,128]{1,0:T(8,128)S(1)} %pad_add_fusion.bath, ...), custom_call_target="tpu_custom_call" | custom-call | flops 44236800 | bytes 23592960 | tf_op jit(solution)/shard_map/pallas_call | solution.py:408
  (49 shorter events, 0.8 us)
Async XLA Ops:
  0.6 25.6 %copy-start.1 = (bf16[1,3,64,128]{3,2,1,0:T(8,128)(2,1)S(1)}, bf16[1,3,64,128]{3,2,1,0:T(8,128)(2,1)}, u32[]{:S(2)}) copy-start(bf16[1,3,64,128]{3,2,1,0:T(8,128)(2,1)} %param.6) | copy-start | bytes 147460
  2.2 24.4 %collective-permute-start.5 = (bf16[3,64,128]{2,0,1:T(4,128)(2,1)}, bf16[3,64,128]{2,0,1:T(4,128)(2,1)}, u32[]{:S(2)}, u32[]{:S(2)}) collective-permute-start(bf16[3,64,128]{2,0,1:T(4,128)(2,1)} %bitcast.59), channel_id=1, source_target_pairs={{0,16},{16,0},{1,17},{17,1},{2,18},{18,2},{3,19},{19,3},{4,20},{20... | collective-permute-start | bytes 147464 | tf_op jit(solution)/shard_map/ppermute | solution.py:327
  3.6 68.3 %collective-permute-start.2 = (bf16[4,128,128]{2,1,0:T(8,128)(2,1)S(1)}, bf16[4,128,128]{2,1,0:T(8,128)(2,1)S(1)}, u32[]{:S(2)}, u32[]{:S(2)}) collective-permute-start(bf16[4,128,128]{2,1,0:T(8,128)(2,1)S(1)} %get-tuple-element.16), channel_id=1, source_target_pairs={{0,1},{1,2},{2,3},{3,4},{4,5},{5,6},{6,7},{7,8},{8,9},{9,10},{10,1... | collective-permute-start | bytes 393224 | tf_op jit(solution)/shard_map/ppermute | solution.py:293
  6.2 65.8 %collective-permute-start.3 = (bf16[4,128,128]{2,1,0:T(8,128)(2,1)S(1)}, bf16[4,128,128]{2,1,0:T(8,128)(2,1)S(1)}, u32[]{:S(2)}, u32[]{:S(2)}) collective-permute-start(bf16[4,128,128]{2,1,0:T(8,128)(2,1)S(1)} %get-tuple-element.17), channel_id=1, source_target_pairs={{0,15},{1,0},{2,1},{3,2},{4,3},{5,4},{6,5},{7,6},{8,7},{9,8},{10,9... | collective-permute-start | bytes 393224 | tf_op jit(solution)/shard_map/ppermute | solution.py:293
  20.3 47.6 %collective-permute-start.1 = (bf16[327,128]{1,0:T(8,128)(2,1)S(1)}, bf16[327,128]{1,0:T(8,128)(2,1)}, u32[]{:S(2)}, u32[]{:S(2)}) collective-permute-start(bf16[327,128]{1,0:T(8,128)(2,1)S(1)} %concatenate.27), channel_id=1, source_target_pairs={{0,1},{1,2},{2,3},{3,4},{4,5},{5,6},{6,7},{7,8},{8,9},{9,10},{10,1... | collective-permute-start | bytes 251144 | tf_op jit(solution)/shard_map/ppermute | solution.py:293
  20.5 49.9 %collective-permute-start = (bf16[327,128]{1,0:T(8,128)(2,1)S(1)}, bf16[327,128]{1,0:T(8,128)(2,1)S(1)}, u32[]{:S(2)}, u32[]{:S(2)}) collective-permute-start(bf16[327,128]{1,0:T(8,128)(2,1)S(1)} %concatenate.26), channel_id=1, source_target_pairs={{0,15},{1,0},{2,1},{3,2},{4,3},{5,4},{6,5},{7,6},{8,7},{9,8},{10,9... | collective-permute-start | bytes 251144 | tf_op jit(solution)/shard_map/ppermute | solution.py:293
  70.9 9.5 %copy-start.2 = (s32[64,128]{1,0:T(8,128)S(1)}, s32[64,128]{1,0:T(8,128)}, u32[]{:S(2)}) copy-start(s32[64,128]{1,0:T(8,128)} %param.11) | copy-start | bytes 98308
  71.1 9.4 %slice-start = ((s8[5242880]{0:T(1024)(128)(4,1)}), s8[4194304]{0:T(1024)(128)(4,1)S(1)}, s32[]{:S(2)}) async-start(s8[5242880]{0:T(1024)(128)(4,1)} %bitcast.61), calls=%async_computation | async-start | bytes 8388608
  72.0 3.6 %copy-start = (bf16[1,64,4,128,128]{4,3,2,1,0:T(8,128)(2,1)S(1)}, bf16[1,64,4,128,128]{4,3,2,1,0:T(8,128)(2,1)}, u32[]{:S(2)}) copy-start(bf16[1,64,4,128,128]{4,3,2,1,0:T(8,128)(2,1)} %param.9) | copy-start | bytes 25165828
  75.6 4.9 %slice-start.1 = ((s8[5242880]{0:T(1024)(128)(4,1)}), s8[1048576]{0:T(1024)(128)(4,1)S(1)}, s32[]{:S(2)}) async-start(s8[5242880]{0:T(1024)(128)(4,1)} %bitcast.61), calls=%async_computation.1 | async-start | bytes 2097152
  80.3 10.6 %collective-permute-start.4 = (f32[3,72,128]{2,1,0:T(8,128)S(1)}, f32[3,72,128]{2,1,0:T(8,128)S(1)}, u32[]{:S(2)}, u32[]{:S(2)}) collective-permute-start(f32[3,72,128]{2,1,0:T(8,128)S(1)} %shard_map.77.mine), channel_id=1, source_target_pairs={{0,16},{16,0},{1,17},{17,1},{2,18},{18,2},{3,19},{19,3},{4,20},{20... | collective-permute-start | bytes 331784 | tf_op jit(solution)/shard_map/ppermute | solution.py:406

commit v2 on v1

v2 whole, which is shorter than its diff:
```python
import functools

import jax
import jax.numpy as jnp
from jax import lax
from jax.experimental import pallas as pl
from jax.experimental.pallas import tpu as pltpu
from jax.sharding import PartitionSpec as P

FLUX_GAIN = 0.5
SIDE_MIX = 0.2
TOP_MIX = 1.0
DEEP_MIX = 2.0

MOST = 16
SLOTS = 24
EDGE = 8
EXTRA = 16
MIB = 2**20
bf16, f32, i32 = jnp.bfloat16, jnp.float32, jnp.int32


def iota(shape, axis):
    return lax.broadcasted_iota(i32, shape, axis)


def neighbour_sum(h, lane):
    rows, lanes = h.shape
    total = pltpu.roll(h, 1, 0) + pltpu.roll(h, rows - 1, 0)
    total = total + jnp.where(lane == 0, 0.0, pltpu.roll(h, 1, 1))
    return total + jnp.where(lane == lanes - 1, 0.0, pltpu.roll(h, lanes - 1, 1))


def edge_tile(right, left):
    row = iota((EDGE, right.shape[1]), 0)
    return jnp.where(row == 0, right, jnp.where(row == EDGE - 1, left, 0.0))


def chunks_of(levels):
    size = 10 if levels % 10 == 0 else levels
    return [(start, size) for start in range(0, levels, size)]


def sweep(count, body, carry, unroll):
    rounds = count // unroll

    def several(number, carry):
        for n in range(unroll):
            carry = body(number * unroll + n, carry)
        return carry

    carry = lax.fori_loop(0, rounds, several, carry)
    for step in range(rounds * unroll, count):
        carry = body(step, carry)
    return carry


def ask_kernel(blocks, spots, request, place):
    count, total = request.shape[0], blocks.shape[1]
    columns = place.shape[1]
    owner = iota((count, total), 0) == blocks[...]
    one_hot = jnp.where(owner, 1.0, 0.0)
    before = jnp.where(iota((total, total), 0) < iota((total, total), 1), 1.0, 0.0)
    earlier = jnp.dot(one_hot.astype(bf16), before.astype(bf16), preferred_element_type=f32)
    rank = jnp.sum(one_hot * earlier, axis=0, keepdims=True)
    slot = iota((128, total), 0)
    spot_in_block = lax.rem(iota((128, total), 1), total // 4)
    last = total // 4 - 1
    filled = (
        (slot == rank.astype(i32))
        | ((slot == MOST) & (spot_in_block == 0))
        | ((slot == MOST + 1) & (spot_in_block == last))
    )
    named = jnp.where(owner, spots[...].astype(f32), 0.0)
    request[...] = lax.dot_general(
        named.astype(bf16),
        jnp.where(filled, 1.0, 0.0).astype(bf16),
        (((1,), (1,)), ((), ())),
        preferred_element_type=f32,
    ).astype(i32)
    arrives = blocks[...].astype(f32) * SLOTS + rank
    place[...] = jnp.transpose(jnp.broadcast_to(arrives, (columns, total))).astype(i32)


def pack_kernel(
    section, state, bath, fields, blocks, weights, to_left, to_right, table,
    low, high, surface, extra, sems,
):
    tracers, levels, columns, lanes = state.shape
    many = tracers * levels
    wide = to_left.shape[0] - 2 * many - EXTRA
    below = pl.ds(2 * many + EXTRA, wide)
    copies = [
        pltpu.make_async_copy(state.at[:, 0], surface, sems.at[0]),
        pltpu.make_async_copy(state.at[:, :, pl.ds(0, 8)], low, sems.at[1]),
        pltpu.make_async_copy(state.at[:, :, pl.ds(columns - 8, 8)], high, sems.at[2]),
        pltpu.make_async_copy(weights.at[pl.ds(0, wide)], to_left.at[below], sems.at[3]),
        pltpu.make_async_copy(
            weights.at[pl.ds((columns - 1) * wide, wide)], to_right.at[below], sems.at[4]
        ),
    ]
    for copy in copies:
        copy.start()
    for out, first, at in ((to_left, 0, 0), (to_right, columns - 2, columns - 1)):
        extra[...] = jnp.zeros_like(extra)
        extra[0:2] = bath[first : first + 2].astype(f32)
        for f in range(3):
            extra[2 + f : 3 + f] = fields[f].astype(f32)[at : at + 1]
        slots = blocks.shape[0]
        extra[8 : 8 + slots] = jnp.broadcast_to(blocks[:, at : at + 1].astype(f32), (slots, lanes))
        out[pl.ds(2 * many, EXTRA)] = extra[...].astype(bf16)
    copies[0].wait()
    on_ocean = section[0] == 1
    for f in range(3):
        own = fields[f]
        if f < 2:
            own = jnp.where(on_ocean, surface[f], own.astype(f32)).astype(bf16)
        table[:, f * lanes : (f + 1) * lanes] = own
    copies[1].wait()
    copies[2].wait()
    for c in range(2):
        for n in range(tracers):
            part = pl.ds(c * many + n * levels, levels)
            tiles = low.at[n].reshape(levels * 8, lanes)
            to_left[part] = tiles[pl.ds(c, levels, stride=8), :].astype(bf16)
            tiles = high.at[n].reshape(levels * 8, lanes)
            to_right[part] = tiles[pl.ds(6 + c, levels, stride=8), :].astype(bf16)
    copies[3].wait()
    copies[4].wait()


def serve_kernel(asked, table, out):
    count = asked.shape[0]
    wanted = jnp.transpose(asked[...].astype(f32))[:SLOTS]
    columns = table.shape[0]
    slot = iota((SLOTS, 1), 0)
    parts = []
    for e in range(count):
        after, before = (e + 1) % count, (e - 1) % count
        spot = jnp.where(
            slot == MOST,
            wanted[:, after : after + 1],
            jnp.where(slot == MOST + 1, wanted[:, before : before + 1], wanted[:, e : e + 1]),
        )
        parts.append(jnp.where(iota((SLOTS, columns), 1) == spot.astype(i32), 1.0, 0.0))
    chosen = jnp.concatenate(parts, axis=0).astype(bf16)
    out[...] = jnp.dot(chosen, table[...], preferred_element_type=f32).astype(bf16)


def start_kernel(
    state, from_left, from_right, bath, q_out, rho_out, side_out, held, bath_out, halo, near, sems
):
    tracers, levels, columns, lanes = state.shape
    rows = columns + EDGE
    many = tracers * levels
    chunks = chunks_of(levels)
    copies = []
    for n, (low, size) in enumerate(chunks):
        copies.append(
            pltpu.make_async_copy(
                state.at[:, pl.ds(low, size)], held.at[:, pl.ds(low, size)], sems.at[n]
            )
        )
    for copy in reversed(copies):
        copy.start()
    for c in range(2):
        part = pl.ds(c * many, many)
        halo[pl.ds(c, many, stride=8), :] = from_right[part].astype(f32)
        halo[pl.ds(EDGE - 2 + c, many, stride=8), :] = from_left[part].astype(f32)
    right = from_right[pl.ds(2 * many, EXTRA)].astype(f32)
    left = from_left[pl.ds(2 * many, EXTRA)].astype(f32)
    row = iota((EDGE, lanes), 0)
    edge = jnp.where(
        row == 0,
        right[0:1],
        jnp.where(
            row == 1,
            right[1:2],
            jnp.where(row == EDGE - 2, left[0:1], jnp.where(row == EDGE - 1, left[1:2], 0.0)),
        ),
    )
    depth = jnp.concatenate([bath[...], edge.astype(i32)], axis=0)
    bath_out[...] = depth
    lane = iota((rows, lanes), 1)
    a = pltpu.roll(depth, 1, 0)
    b = pltpu.roll(depth, rows - 1, 0)
    c = jnp.where(lane == 0, 0, pltpu.roll(depth, 1, 1))
    d = jnp.where(lane == lanes - 1, 0, pltpu.roll(depth, lanes - 1, 1))
    a, b = jnp.maximum(a, b), jnp.minimum(a, b)
    c, d = jnp.maximum(c, d), jnp.minimum(c, d)
    a, c = jnp.maximum(a, c), jnp.minimum(a, c)
    b, d = jnp.maximum(b, d), jnp.minimum(b, d)
    near[0], near[1], near[2], near[3] = a, jnp.maximum(b, c), jnp.minimum(b, c), d

    def side(level):
        wet = level < bath_out[...]
        own = 0.5
        for n in range(4):
            own = jnp.where(level < near[n], 0.5 - 0.5 * SIDE_MIX * (n + 1), own)
        side_out[level] = own[:columns]
        halves = []
        for n in range(tracers):
            spot = (n * levels + level) * 8
            if not isinstance(level, int):
                spot = pl.multiple_of(spot, 8)
            full = jnp.concatenate([held[n, level], halo[pl.ds(spot, 8), :]], axis=0)
            h = jnp.where(wet, full, 0.0)
            halves.append(own * h + 0.5 * SIDE_MIX * neighbour_sum(h, lane))
        return wet, halves

    def deep(step, carry, top):
        level = top - step
        rho_below, *below = carry
        wet, halves = side(level)
        linked = jnp.where(level + 1 < bath_out[...], DEEP_MIX - DEEP_MIX * rho_below, 0.0)
        divisor = 1.0 + DEEP_MIX + linked
        inverse = pl.reciprocal(divisor, approx=True)
        inverse = inverse * (2.0 - divisor * inverse)
        inverse = inverse * (2.0 * DEEP_MIX - DEEP_MIX * divisor * inverse)
        rho = jnp.where(wet, inverse, 0.0)
        rho_out[level] = rho
        solved = []
        for n in range(tracers):
            q = rho * (halves[n] + below[n])
            q_out[n, level] = q
            solved.append(q)
        return (rho, *solved)

    carry = tuple(jnp.zeros((rows, lanes), f32) for _ in range(1 + tracers))
    for n in reversed(range(len(chunks))):
        low, size = chunks[n]
        copies[n].wait()
        first = max(low, 2)
        top = low + size - 1
        carry = sweep(top - first + 1, functools.partial(deep, top=top), carry, 2)
    for level in (1, 0):
        _, halves = side(level)
        rho_out[level] = jnp.zeros((rows, lanes), f32)
        for n in range(tracers):
            q_out[n, level] = halves[n]


def remap_kernel(
    section, columns_in, place, from_left, from_right, weights, out, picked, solved, held, sems
):
    fields, rows, width = out.shape
    columns = rows - EDGE
    slots = weights.shape[0] // (columns * width)
    tall = slots * width
    many = from_left.shape[0] - tall - EXTRA
    group = 8
    copies = []
    for n in range(columns // group):
        part = pl.ds(n * group * tall, group * tall)
        copies.append(pltpu.make_async_copy(weights.at[part], held.at[part], sems.at[n]))
        copies[-1].start()
    right = from_right[pl.ds(many, EXTRA)].astype(f32)
    left = from_left[pl.ds(many, EXTRA)].astype(f32)
    spots = iota((rows, columns_in.shape[0]), 1)
    row = iota((EDGE, 1), 0)
    picked[...] = jnp.zeros_like(picked)
    for k in range(slots):
        edge = jnp.where(
            row == 0,
            right[8 + k : 9 + k, 0:1] * SLOTS + MOST,
            jnp.where(row == EDGE - 1, left[8 + k : 9 + k, 0:1] * SLOTS + MOST + 1, -1.0),
        ).astype(i32)
        wanted = jnp.concatenate([place[k * columns : (k + 1) * columns, 0:1], edge], axis=0)
        chosen = jnp.where(spots == wanted, 1.0, 0.0).astype(bf16)
        found = jnp.dot(chosen, columns_in[...], preferred_element_type=f32)
        for f in range(fields):
            picked[k, pl.ds(f, rows, stride=8), :] = found[:, f * width : (f + 1) * width]

    def one(row, table_of):
        spot = pl.ds(row * 8, 8)
        vector = jnp.concatenate([picked[k, spot, :] for k in range(slots)], axis=1)
        matrix = jnp.concatenate([table_of(k) for k in range(slots)], axis=1)
        solved[spot, :] = lax.dot_general(
            vector.astype(bf16), matrix, (((1,), (1,)), ((), ())), preferred_element_type=f32
        )

    solved[...] = jnp.zeros_like(solved)
    below = many + EXTRA
    one(columns, lambda k: from_right[pl.ds(below + k * width, width)])
    one(rows - 1, lambda k: from_left[pl.ds(below + k * width, width)])
    for n in range(columns // group):
        copies[n].wait()
        for m in range(group):
            spot = n * group + m
            one(spot, lambda k: held[pl.ds((spot * slots + k) * width, width)])
    on_ocean = section[0] == 1
    for f in range(fields):
        out[f, pl.ds(0, columns)] = solved[pl.ds(f, columns, stride=8), :]
        edge = solved[pl.ds(columns * 8 + f, EDGE, stride=8), :]
        ice = edge_tile(right[2 + f : 3 + f], left[2 + f : 3 + f])
        out[f, pl.ds(columns, EDGE)] = jnp.where(on_ocean, ice, edge)


def finish_kernel(
    section, mine, other, fields, partner_fields, bath, q, rho, side, start, surface, result,
    half, done, sems,
):
    tracers, levels, columns, lanes = start.shape
    rows = columns + EDGE
    chunks = chunks_of(levels)
    on_ocean = section[0] == 1
    lane = iota((rows, lanes), 1)
    flux = [jnp.where(on_ocean, other[f], mine[f]) for f in range(3)]
    own = []
    for f in range(3):
        edge = jnp.where(on_ocean, mine[f, pl.ds(columns, EDGE)], other[f, pl.ds(columns, EDGE)])
        ice = jnp.where(on_ocean, fields[f].astype(f32), partner_fields[f].astype(f32))
        own.append(jnp.concatenate([ice, edge], axis=0))
    forcing = [flux[0] + own[0], flux[1] + own[1]]
    top_mix = TOP_MIX * (1.0 + flux[2] * flux[2] + own[2] * own[2])
    depth = bath[...]

    def top_levels(count, halves, below, rho_below):
        wet = 1 < depth[:count]
        link = jnp.where(wet, top_mix[:count], 0.0)
        deeper = jnp.where(2 < depth[:count], DEEP_MIX - DEEP_MIX * rho_below, 0.0)
        second = 1.0 / (1.0 + link + deeper)
        rho_second = link * second
        first = 1.0 / (1.0 + link - link * rho_second)
        values = []
        for n in range(tracers):
            partial = 2.0 * (halves[n][1] + below[n]) * second
            source = 2.0 * halves[n][0] + FLUX_GAIN * forcing[n][:count]
            surface_value = (source + link * partial) * first
            next_value = jnp.where(wet, partial, 0.0) + rho_second * surface_value
            values.append((surface_value, next_value))
        return values

    values = top_levels(
        rows,
        [(q[n, 0], q[n, 1]) for n in range(tracers)],
        [q[n, 2] for n in range(tracers)],
        rho[2],
    )

    def store_half(n, level, h):
        half[n, level] = (
            side[level] * h[:columns] + 0.5 * SIDE_MIX * neighbour_sum(h, lane)[:columns]
        )

    for n in range(tracers):
        for level in (0, 1):
            store_half(n, level, values[n][level])

    def down(step, carry):
        level = 2 + step
        ratio = rho[level]
        out = []
        for n in range(tracers):
            h = q[n, level] + ratio * carry[n]
            store_half(n, level, h)
            out.append(h)
        return tuple(out)

    carry = tuple(values[n][1] for n in range(tracers))
    sweep(levels - 2, down, carry, 2)

    def up(step, carry):
        level = levels - 1 - step
        ratio = rho[level, pl.ds(0, columns)]
        out = []
        for n in range(tracers):
            value = ratio * (half[n, level] + carry[n])
            half[n, level] = value
            out.append(value)
        return tuple(out)

    zero = jnp.zeros((columns, lanes), f32)
    carry = sweep(levels - 2, up, (zero,) * tracers, 6)
    values = top_levels(
        columns,
        [(half[n, 0], half[n, 1]) for n in range(tracers)],
        carry,
        rho[2, pl.ds(0, columns)],
    )
    for n in range(tracers):
        surface[n] = jnp.where(on_ocean, values[n][0], other[n, pl.ds(0, columns)])
    surface[2] = jnp.where(on_ocean, top_mix[:columns], other[2, pl.ds(0, columns)])

    def last(step, carry, low):
        level = low + step
        ratio = rho[level, pl.ds(0, columns)]
        wet = level < bath[pl.ds(0, columns)]
        out = []
        for n in range(tracers):
            h = half[n, level] + ratio * carry[n]
            done[n, level] = jnp.where(wet, h, start[n, level])
            out.append(h)
        return tuple(out)

    carry = tuple(values[n][1] for n in range(tracers))
    leaving = []
    for n, (low, size) in enumerate(chunks):
        if n == 0:
            for m in range(tracers):
                done[m, 0] = values[m][0]
                done[m, 1] = jnp.where(1 < depth[:columns], values[m][1], start[m, 1])
        first = max(low, 2)
        carry = sweep(low + size - first, functools.partial(last, low=first), carry, 4)
        part = pl.ds(low, size)
        leaving.append(
            pltpu.make_async_copy(done.at[:, part], result.at[:, part], sems.at[n])
        )
        leaving[-1].start()
    for copy in leaving:
        copy.wait()


def shift(value, axis, by):
    count = lax.axis_size(axis)
    return lax.ppermute(value, axis, [(i, (i + by) % count) for i in range(count)])


def per_device(
    surface_fields, source_blocks, source_columns, remap_weights, ocean_state, bathymetry
):
    tracers, levels, columns, lanes = ocean_state.shape
    slots = source_blocks.shape[2]
    count = lax.axis_size("blk")
    rows = columns + EDGE
    section = lax.axis_index("sec").astype(i32).reshape(1)
    fields = surface_fields[0]
    blocks = jnp.transpose(source_blocks[0])
    spots = jnp.transpose(source_columns[0])
    weights = remap_weights[0].reshape(columns * slots * lanes, lanes)
    tall = slots * lanes
    many = tracers * levels

    anywhere = pl.BlockSpec(memory_space=pl.ANY)
    vmem = pl.BlockSpec(memory_space=pltpu.VMEM)
    smem = pl.BlockSpec(memory_space=pltpu.SMEM)
    shaped = jax.ShapeDtypeStruct
    pieces = len(chunks_of(levels))
    cells = rows * lanes

    request, place = pl.pallas_call(
        ask_kernel,
        out_shape=(shaped((count, 128), i32), shaped((slots * columns, 128), i32)),
        in_specs=[vmem, vmem],
        out_specs=(vmem, vmem),
        compiler_params=pltpu.CompilerParams(vmem_limit_bytes=4 * MIB),
        cost_estimate=pl.CostEstimate(flops=10**6, bytes_accessed=10**5, transcendentals=0),
    )(blocks.reshape(1, slots * columns), spots.reshape(1, slots * columns))
    asked = lax.all_to_all(request, "blk", split_axis=0, concat_axis=0, tiled=True)

    payload = shaped((2 * many + EXTRA + tall, lanes), bf16)
    to_left, to_right, table = pl.pallas_call(
        pack_kernel,
        out_shape=(payload, payload, shaped((columns, 3 * lanes), bf16)),
        in_specs=[smem, anywhere, vmem, vmem, vmem, anywhere],
        out_specs=(vmem, vmem, vmem),
        scratch_shapes=[
            pltpu.VMEM((tracers, levels, 8, lanes), f32),
            pltpu.VMEM((tracers, levels, 8, lanes), f32),
            pltpu.VMEM((tracers, columns, lanes), f32),
            pltpu.VMEM((EXTRA, lanes), f32),
            pltpu.SemaphoreType.DMA((5,)),
        ],
        compiler_params=pltpu.CompilerParams(vmem_limit_bytes=8 * MIB),
        cost_estimate=pl.CostEstimate(
            flops=10**6, bytes_accessed=4 * 10**6, transcendentals=0
        ),
    )(section, ocean_state, bathymetry, fields, blocks, weights)
    from_left = shift(to_right, "blk", 1)
    from_right = shift(to_left, "blk", -1)
    partner_fields = lax.ppermute(fields, "sec", [(0, 1), (1, 0)])

    served = pl.pallas_call(
        serve_kernel,
        out_shape=shaped((count * SLOTS, 3 * lanes), bf16),
        in_specs=[vmem, vmem],
        out_specs=vmem,
        compiler_params=pltpu.CompilerParams(vmem_limit_bytes=8 * MIB),
        cost_estimate=pl.CostEstimate(
            flops=10**7, bytes_accessed=10**6, transcendentals=0
        ),
    )(asked, table)
    columns_in = lax.all_to_all(served, "blk", split_axis=0, concat_axis=0, tiled=True)

    q, rho, side, start, bath = pl.pallas_call(
        start_kernel,
        out_shape=(
            shaped((tracers, levels, rows, lanes), f32),
            shaped((levels, rows, lanes), f32),
            shaped((levels, columns, lanes), f32),
            shaped(ocean_state.shape, f32),
            shaped((rows, lanes), i32),
        ),
        in_specs=[anywhere, vmem, vmem, vmem],
        out_specs=(vmem,) * 5,
        scratch_shapes=[
            pltpu.VMEM((many * 8, lanes), f32),
            pltpu.VMEM((4, rows, lanes), i32),
            pltpu.SemaphoreType.DMA((pieces,)),
        ],
        compiler_params=pltpu.CompilerParams(vmem_limit_bytes=8 * MIB),
        cost_estimate=pl.CostEstimate(
            flops=60 * levels * cells, bytes_accessed=20 * levels * cells, transcendentals=0
        ),
    )(ocean_state, from_left, from_right, bathymetry)

    mine = pl.pallas_call(
        remap_kernel,
        out_shape=shaped((3, rows, lanes), f32),
        in_specs=[smem, vmem, vmem, vmem, vmem, anywhere],
        out_specs=vmem,
        scratch_shapes=[
            pltpu.VMEM((slots, rows * 8, lanes), f32),
            pltpu.VMEM((rows * 8, lanes), f32),
            pltpu.VMEM(weights.shape, bf16),
            pltpu.SemaphoreType.DMA((columns // 8,)),
        ],
        compiler_params=pltpu.CompilerParams(vmem_limit_bytes=16 * MIB),
        cost_estimate=pl.CostEstimate(
            flops=16 * weights.size, bytes_accessed=2 * weights.size, transcendentals=0
        ),
    )(section, columns_in, place, from_left, from_right, weights)
    other = lax.ppermute(mine, "sec", [(0, 1), (1, 0)])

    surface, result = pl.pallas_call(
        finish_kernel,
        out_shape=(shaped((3, columns, lanes), f32), shaped(ocean_state.shape, f32)),
        in_specs=[smem] + [vmem] * 9,
        out_specs=(vmem, anywhere),
        scratch_shapes=[
            pltpu.VMEM(ocean_state.shape, f32),
            pltpu.VMEM(ocean_state.shape, f32),
            pltpu.SemaphoreType.DMA((pieces,)),
        ],
        compiler_params=pltpu.CompilerParams(vmem_limit_bytes=16 * MIB),
        cost_estimate=pl.CostEstimate(
            flops=60 * levels * cells, bytes_accessed=32 * levels * cells, transcendentals=0
        ),
    )(section, mine, other, fields, partner_fields, bath, q, rho, side, start)
    return (surface[None], result)


def solution(mesh):
    return jax.shard_map(
        per_device,
        mesh=mesh,
        in_specs=(
            P("sec", None, "blk", None),
            P("sec", "blk", None),
            P("sec", "blk", None),
            P("sec", "blk", None, None, None),
            P(None, None, "blk", None),
            P("blk", None),
        ),
        out_specs=(P("sec", None, "blk", None), P(None, None, "blk", None)),
        check_vma=False,
    )
```

time: 109 us -> 69.1 us (0.63)
  blocking collectives: 40.2 us -> 0 us
  waiting for transfers between devices: 0.02 us -> 9.23 us
  starting transfers between devices: 12.8 us -> 21.4 us
  Pallas kernels: 32.5 us -> 24.1 us
  other arithmetic: 5.36 us -> 0 us
  local copies, waits for them, and re-layouts: 16.5 us -> 13 us
    all_gather x1 -> x0, blocking collectives: 40.2 us -> none  [per_device(): gathered = lax.all_gather(table, 'blk', axis=0, tiled=True)]
    all_to_all x0 -> x2, starting transfers between devices: none -> 15.2 us  [the longest x1 8.31 us: per_device(): lax.all_to_all(request, 'blk', split_axis=0, concat_axis=0, tiled=True)]
    ppermute x4 -> x2, waiting for transfers between devices: 0.01 us -> 9.22 us  [shift(): lax.ppermute(value, axis, [(i, (i + by) % count) for i in range(count)])]
    pallas_call x3 -> x6, Pallas kernels: 32.5 us -> 24.1 us  [the longest x1 9.53 us: per_device(): pl.pallas_call(finish_kernel, out_shape=(shaped((3, columns, lanes), f32)...]
    ppermute x4 -> x2, starting transfers between devices: 12.3 us -> 5.67 us  [shift(): lax.ppermute(value, axis, [(i, (i + by) % count) for i in range(count)])]
    convert_element_type x7 -> x0, other arithmetic: 2.62 us -> none  [the longest x3 1.58 us: edge_tile(): left.astype(dtype)]
    squeeze x2 -> x0, local copies, waits for them, and re-layouts: 1.68 us -> none  [the longest x1 0.99 us: per_device(): left_weights = shift(weights[columns - 1], 'blk', 1)]
    add x3 -> x0, other arithmetic: 1.54 us -> none  [flat(): return block_row.astype(jnp.int32) * columns + spot_row.astype(jnp.int32)]
  transfers between devices with their start and end apart: 6 -> 6, of which waited for: 0 -> 2; matrix products, arithmetic and copies ran while one was open for 15% -> 0% of each run, Pallas kernels for 10% -> 12%
where the time goes in v2:
time: 69.1 us; the launch traced here: 68.5 us
  Pallas kernels  24.1 us (35%)
  starting transfers between devices  21.4 us (31%)
  local copies, waits for them, and re-layouts  13 us (19%)
  waiting for transfers between devices  9.23 us (13%)
  between operations  0.75 us (1%)
    unnamed x18, local copies, waits for them, and re-layouts  11.5 us
    pallas_call x1, Pallas kernels, per_device(): pl.pallas_call(finish_kernel, out_shape=(shaped((3, columns, lanes), f32)...  9.53 us
    ppermute x2, waiting for transfers between devices, shift(): lax.ppermute(value, axis, [(i, (i + by) % count) for i in range(count)])  9.22 us
    all_to_all x1, starting transfers between devices, per_device(): lax.all_to_all(request, 'blk', split_axis=0, concat_axis=0, tiled=True)  8.31 us
    pallas_call x1, Pallas kernels, per_device(): pl.pallas_call(start_kernel, out_shape=(shaped((tracers, levels, rows, la...  7.37 us
    all_to_all x1, starting transfers between devices, per_device(): lax.all_to_all(served, 'blk', split_axis=0, concat_axis=0, tiled=True)  6.9 us
    ppermute x2, starting transfers between devices, shift(): lax.ppermute(value, axis, [(i, (i + by) % count) for i in range(count)])  5.67 us
    pallas_call x1, Pallas kernels, per_device(): pl.pallas_call(remap_kernel, out_shape=shaped((3, rows, lanes), f32), in_...  4.32 us
  transfers between devices with their start and end apart: 6, of which 2 were waited for; matrix products, arithmetic and copies ran while one was open for 0% of the time, Pallas kernels for 12%

profile of v2, /device:TPU:0, one launch (start us, length us, event | category | flops | bytes accessed | tf_op | source)
XLA Modules:
  0.0 68.5 jit_solution(1122017172632230211)
XLA Ops:
  0.6 0.8 %reshape.18.blocks = s32[1,256]{1,0:T(1,128)S(1)} reshape(s32[4,64]{1,0:T(4,128)} %bitcast.23) | data formatting | bytes 2048 | tf_op jit(solution)/shard_map/reshape | solution.py:448
  1.4 0.8 %reshape.19.spots = s32[1,256]{1,0:T(1,128)S(1)} reshape(s32[4,64]{1,0:T(4,128)} %bitcast.25) | data formatting | bytes 2048 | tf_op jit(solution)/shard_map/reshape | solution.py:448
  2.2 0.9 %shard_map.77 = (s32[16,128]{1,0:T(8,128)}, s32[256,128]{1,0:T(8,128)S(1)}) custom-call(s32[1,256]{1,0:T(1,128)S(1)} %reshape.18.blocks, s32[1,256]{1,0:T(1,128)S(1)} %reshape.19.spots), custom_call_target="tpu_custom_call" | custom-call | flops 1000000 | bytes 100000 | tf_op jit(solution)/shard_map/pallas_call | solution.py:441
  3.1 8.3 %all-to-all-start = ((s32[16,1,128]{2,1,0:T(1,128)}), s32[16,1,128]{2,1,0:T(1,128)S(1)}, u32[]{:S(2)}, u32[]{:S(2)}) async-start(s32[16,1,128]{2,1,0:T(1,128)} %bitcast.6), calls=%async_computation | async-start | bytes 16384 | tf_op jit(solution)/shard_map/all_to_all | solution.py:449
  11.4 0.0 copy-start
  11.4 3.4 %copy-done = bf16[1,64,4,128,128]{4,3,2,1,0:T(8,128)(2,1)S(1)} copy-done((bf16[1,64,4,128,128]{4,3,2,1,0:T(8,128)(2,1)S(1)}, bf16[1,64,4,128,128]{4,3,2,1,0:T(8,128)(2,1)}, u32[]{:S(2)}) %copy-start) | copy-done | bytes 8388632
  14.8 2.5 %copy-done.2 = f32[2,80,64,128]{3,2,1,0:T(8,128)S(1)} copy-done((f32[2,80,64,128]{3,2,1,0:T(8,128)S(1)}, f32[2,80,64,128]{3,2,1,0:T(8,128)}, u32[]{:S(2)}) %copy-start.2) | copy-done | bytes 5242904
  17.3 0.8 %copy-done.4 = bf16[1,3,64,128]{3,2,1,0:T(8,128)(2,1)S(1)} copy-done((bf16[1,3,64,128]{3,2,1,0:T(8,128)(2,1)S(1)}, bf16[1,3,64,128]{3,2,1,0:T(8,128)(2,1)}, u32[]{:S(2)}) %copy-start.4) | copy-done | bytes 49176
  18.1 0.8 %copy-done.6 = s32[64,128]{1,0:T(8,128)S(1)} copy-done((s32[64,128]{1,0:T(8,128)S(1)}, s32[64,128]{1,0:T(8,128)}, u32[]{:S(2)}) %copy-start.6) | copy-done | bytes 32792
  18.8 0.7 copy-done.8
  19.5 0.7 %shard_map.78 = (bf16[848,128]{1,0:T(8,128)(2,1)S(1)}, bf16[848,128]{1,0:T(8,128)(2,1)S(1)}, bf16[64,384]{1,0:T(8,128)(2,1)S(1)}) custom-call(s32[1]{0:T(128)} %bitcast.section, f32[2,80,64,128]{3,2,1,0:T(8,128)S(1)} %copy-done.2, s32[64,128]{1,0:T(8,128)S(1)} %copy-done.6, bf16[3,64,128]{2,1,0:T(8,128)(2,1)S(1)} %bitcast.19, s32[4,64]{1,0:T(4,128)S(1)} %bitcast.24, ...), custom_call_target="tpu_custom_call" | custom-call | flops 1000000 | bytes 4000000 | tf_op jit(solution)/shard_map/pallas_call | solution.py:452
  20.3 0.0 copy-start.5
  20.3 0.0 copy-start.7
  20.3 0.0 all-to-all-done
  20.3 1.2 %shard_map.79 = bf16[384,384]{1,0:T(8,128)(2,1)} custom-call(s32[16,128]{1,0:T(8,128)S(1)} %bitcast.22, bf16[64,384]{1,0:T(8,128)(2,1)S(1)} %get-tuple-element.15.table), custom_call_target="tpu_custom_call" | custom-call | flops 10000000 | bytes 1000000 | tf_op jit(solution)/shard_map/pallas_call | solution.py:473
  21.5 6.9 %all-to-all-start.1 = ((bf16[16,24,384]{2,1,0:T(8,128)(2,1)}), bf16[16,24,384]{2,1,0:T(8,128)(2,1)S(1)}, u32[]{:S(2)}, u32[]{:S(2)}) async-start(bf16[16,24,384]{2,1,0:T(8,128)(2,1)} %bitcast.11), calls=%async_computation.1 | async-start | bytes 589824 | tf_op jit(solution)/shard_map/all_to_all | solution.py:483
  28.4 1.9 %collective-permute-start = (bf16[848,128]{1,0:T(8,128)(2,1)S(1)}, bf16[848,128]{1,0:T(8,128)(2,1)S(1)}, u32[]{:S(2)}, u32[]{:S(2)}) collective-permute-start(bf16[848,128]{1,0:T(8,128)(2,1)S(1)} %get-tuple-element.17), channel_id=1, source_target_pairs={{0,1},{1,2},{2,3},{3,4},{4,5},{5,6},{6,7},{7,8},{8,9},{9,10},{10,1... | collective-permute-start | bytes 651272 | tf_op jit(solution)/shard_map/ppermute | solution.py:416
  30.3 3.7 %collective-permute-start.1 = (bf16[848,128]{1,0:T(8,128)(2,1)S(1)}, bf16[848,128]{1,0:T(8,128)(2,1)S(1)}, u32[]{:S(2)}, u32[]{:S(2)}) collective-permute-start(bf16[848,128]{1,0:T(8,128)(2,1)S(1)} %get-tuple-element.18), channel_id=1, source_target_pairs={{0,15},{1,0},{2,1},{3,2},{4,3},{5,4},{6,5},{7,6},{8,7},{9,8},{10,9... | collective-permute-start | bytes 651272 | tf_op jit(solution)/shard_map/ppermute | solution.py:416
  34.1 9.1 %collective-permute-done.from_left = bf16[848,128]{1,0:T(8,128)(2,1)S(1)} collective-permute-done((bf16[848,128]{1,0:T(8,128)(2,1)S(1)}, bf16[848,128]{1,0:T(8,128)(2,1)S(1)}, u32[]{:S(2)}, u32[]{:S(2)}) %collective-permute-start) | collective-permute-done | bytes 217120 | tf_op jit(solution)/shard_map/ppermute | solution.py:416
  43.2 0.1 collective-permute-done.1.from_right
  43.3 0.0 all-to-all-done.1
  43.3 3.4 %copy-done.1 = bf16[1,64,4,128,128]{4,3,2,1,0:T(8,128)(2,1)S(1)} copy-done((bf16[1,64,4,128,128]{4,3,2,1,0:T(8,128)(2,1)S(1)}, bf16[1,64,4,128,128]{4,3,2,1,0:T(8,128)(2,1)}, u32[]{:S(2)}) %copy-start.1) | copy-done | bytes 8388632
  46.7 4.3 %shard_map.80.mine = f32[3,72,128]{2,1,0:T(8,128)S(1)} custom-call(s32[1]{0:T(128)} %bitcast.section, bf16[384,384]{1,0:T(8,128)(2,1)S(1)} %bitcast.18, s32[256,128]{1,0:T(8,128)S(1)} %get-tuple-element.16.place, bf16[848,128]{1,0:T(8,128)(2,1)S(1)} %collective-permute-done.from_left, bf16[848,128]{1,0:T(8,128)(2,1)S(1)} %collective-permute-done.1.from_right, ...), custom_call_target="tpu_custom_call" | custom-call | flops 67108864 | bytes 8388608 | tf_op jit(solution)/shard_map/pallas_call | solution.py:507
  51.0 0.1 collective-permute-start.2
  51.1 0.0 copy-done.5
  51.1 0.5 collective-permute-start.3
  51.6 0.0 copy-done.7
  51.6 0.0 copy-done.3
  51.6 7.4 %shard_map.81 = (f32[2,80,72,128]{3,2,1,0:T(8,128)S(1)}, f32[80,72,128]{2,1,0:T(8,128)S(1)}, f32[80,64,128]{2,1,0:T(8,128)S(1)}, f32[2,80,64,128]{3,2,1,0:T(8,128)S(1)}, s32[72,128]{1,0:T(8,128)S(1)}) custom-call(f32[2,80,64,128]{3,2,1,0:T(8,128)S(1)} %copy-done.3, bf16[848,128]{1,0:T(8,128)(2,1)S(1)} %collective-permute-done.from_left, ...), custom_call_target="tpu_custom_call" | custom-call | flops 44236800 | bytes 14745600 | tf_op jit(solution)/shard_map/pallas_call | solution.py:485
  59.0 0.0 collective-permute-done.3.partner_fields
  59.0 0.0 collective-permute-done.2.other
  59.0 9.5 %shard_map.82 = (f32[3,64,128]{2,1,0:T(8,128)}, f32[2,80,64,128]{3,2,1,0:T(8,128)}) custom-call(s32[1]{0:T(128)} %bitcast.section, f32[3,72,128]{2,1,0:T(8,128)S(1)} %shard_map.80.mine, f32[3,72,128]{2,1,0:T(8,128)S(1)} %collective-permute-done.2.other, bf16[3,64,128]{2,1,0:T(8,128)(2,1)S(1)} %bitcast.21, ...), custom_call_target="tpu_custom_call" | custom-call | flops 44236800 | bytes 23592960 | tf_op jit(solution)/shard_map/pallas_call | solution.py:525
  (6 shorter events, 0.0 us)
Async XLA Ops:
  3.1 17.2 %all-to-all-start = ((s32[16,1,128]{2,1,0:T(1,128)}), s32[16,1,128]{2,1,0:T(1,128)S(1)}, u32[]{:S(2)}, u32[]{:S(2)}) async-start(s32[16,1,128]{2,1,0:T(1,128)} %bitcast.6), calls=%async_computation | async-start | bytes 16384 | tf_op jit(solution)/shard_map/all_to_all | solution.py:449
  11.4 3.4 %copy-start = (bf16[1,64,4,128,128]{4,3,2,1,0:T(8,128)(2,1)S(1)}, bf16[1,64,4,128,128]{4,3,2,1,0:T(8,128)(2,1)}, u32[]{:S(2)}) copy-start(bf16[1,64,4,128,128]{4,3,2,1,0:T(8,128)(2,1)} %param.9) | copy-start | bytes 25165828
  14.8 2.5 %copy-start.2 = (f32[2,80,64,128]{3,2,1,0:T(8,128)S(1)}, f32[2,80,64,128]{3,2,1,0:T(8,128)}, u32[]{:S(2)}) copy-start(f32[2,80,64,128]{3,2,1,0:T(8,128)} %state.3) | copy-start | bytes 15728644
  17.3 0.8 %copy-start.4 = (bf16[1,3,64,128]{3,2,1,0:T(8,128)(2,1)S(1)}, bf16[1,3,64,128]{3,2,1,0:T(8,128)(2,1)}, u32[]{:S(2)}) copy-start(bf16[1,3,64,128]{3,2,1,0:T(8,128)(2,1)} %param.6) | copy-start | bytes 147460
  18.1 0.8 %copy-start.6 = (s32[64,128]{1,0:T(8,128)S(1)}, s32[64,128]{1,0:T(8,128)}, u32[]{:S(2)}) copy-start(s32[64,128]{1,0:T(8,128)} %bath.3) | copy-start | bytes 98308
  18.8 0.7 copy-start.8
  20.3 30.8 %copy-start.5 = (bf16[1,3,64,128]{3,2,1,0:T(8,128)(2,1)S(1)}, bf16[1,3,64,128]{3,2,1,0:T(8,128)(2,1)}, u32[]{:S(2)}) copy-start(bf16[1,3,64,128]{3,2,1,0:T(8,128)(2,1)} %param.6) | copy-start | bytes 147460
  20.3 31.3 %copy-start.7 = (s32[64,128]{1,0:T(8,128)S(1)}, s32[64,128]{1,0:T(8,128)}, u32[]{:S(2)}) copy-start(s32[64,128]{1,0:T(8,128)} %bath.3) | copy-start | bytes 98308
  21.5 21.8 %all-to-all-start.1 = ((bf16[16,24,384]{2,1,0:T(8,128)(2,1)}), bf16[16,24,384]{2,1,0:T(8,128)(2,1)S(1)}, u32[]{:S(2)}, u32[]{:S(2)}) async-start(bf16[16,24,384]{2,1,0:T(8,128)(2,1)} %bitcast.11), calls=%async_computation.1 | async-start | bytes 589824 | tf_op jit(solution)/shard_map/all_to_all | solution.py:483
  28.4 14.7 %collective-permute-start = (bf16[848,128]{1,0:T(8,128)(2,1)S(1)}, bf16[848,128]{1,0:T(8,128)(2,1)S(1)}, u32[]{:S(2)}, u32[]{:S(2)}) collective-permute-start(bf16[848,128]{1,0:T(8,128)(2,1)S(1)} %get-tuple-element.17), channel_id=1, source_target_pairs={{0,1},{1,2},{2,3},{3,4},{4,5},{5,6},{6,7},{7,8},{8,9},{9,10},{10,1... | collective-permute-start | bytes 651272 | tf_op jit(solution)/shard_map/ppermute | solution.py:416
  30.3 13.0 %collective-permute-start.1 = (bf16[848,128]{1,0:T(8,128)(2,1)S(1)}, bf16[848,128]{1,0:T(8,128)(2,1)S(1)}, u32[]{:S(2)}, u32[]{:S(2)}) collective-permute-start(bf16[848,128]{1,0:T(8,128)(2,1)S(1)} %get-tuple-element.18), channel_id=1, source_target_pairs={{0,15},{1,0},{2,1},{3,2},{4,3},{5,4},{6,5},{7,6},{8,7},{9,8},{10,9... | collective-permute-start | bytes 651272 | tf_op jit(solution)/shard_map/ppermute | solution.py:416
  43.3 3.4 %copy-start.1 = (bf16[1,64,4,128,128]{4,3,2,1,0:T(8,128)(2,1)S(1)}, bf16[1,64,4,128,128]{4,3,2,1,0:T(8,128)(2,1)}, u32[]{:S(2)}) copy-start(bf16[1,64,4,128,128]{4,3,2,1,0:T(8,128)(2,1)} %param.9) | copy-start | bytes 25165828
  46.7 4.9 %copy-start.3 = (f32[2,80,64,128]{3,2,1,0:T(8,128)S(1)}, f32[2,80,64,128]{3,2,1,0:T(8,128)}, u32[]{:S(2)}) copy-start(f32[2,80,64,128]{3,2,1,0:T(8,128)} %state.3) | copy-start | bytes 15728644
  51.0 8.0 %collective-permute-start.2 = (f32[3,72,128]{2,1,0:T(8,128)S(1)}, f32[3,72,128]{2,1,0:T(8,128)S(1)}, u32[]{:S(2)}, u32[]{:S(2)}) collective-permute-start(f32[3,72,128]{2,1,0:T(8,128)S(1)} %shard_map.80.mine), channel_id=1, source_target_pairs={{0,16},{16,0},{1,17},{17,1},{2,18},{18,2},{3,19},{19,3},{4,20},{20... | collective-permute-start | bytes 331784 | tf_op jit(solution)/shard_map/ppermute | solution.py:523
  51.1 7.9 %collective-permute-start.3 = (bf16[3,64,128]{2,1,0:T(8,128)(2,1)S(1)}, bf16[3,64,128]{2,1,0:T(8,128)(2,1)S(1)}, u32[]{:S(2)}, u32[]{:S(2)}) collective-permute-start(bf16[3,64,128]{2,1,0:T(8,128)(2,1)S(1)} %bitcast.20), channel_id=1, source_target_pairs={{0,16},{16,0},{1,17},{17,1},{2,18},{18,2},{3,19},{19,3},{4,20},{20... | collective-permute-start | bytes 147464 | tf_op jit(solution)/shard_map/ppermute | solution.py:471

commit v3 on v2

--- a/solution.py
+++ b/solution.py
@@ -2,6 +2,7 @@
 
 import jax
 import jax.numpy as jnp
+import numpy as np
 from jax import lax
 from jax.experimental import pallas as pl
 from jax.experimental.pallas import tpu as pltpu
@@ -11,6 +12,7 @@
 SIDE_MIX = 0.2
 TOP_MIX = 1.0
 DEEP_MIX = 2.0
+SCALE = 1.0 / (0.5 * SIDE_MIX)
 
 MOST = 16
 SLOTS = 24
@@ -55,69 +57,77 @@
     return carry
 
 
-def ask_kernel(blocks, spots, request, place):
-    count, total = request.shape[0], blocks.shape[1]
-    columns = place.shape[1]
-    owner = iota((count, total), 0) == blocks[...]
-    one_hot = jnp.where(owner, 1.0, 0.0)
-    before = jnp.where(iota((total, total), 0) < iota((total, total), 1), 1.0, 0.0)
-    earlier = jnp.dot(one_hot.astype(bf16), before.astype(bf16), preferred_element_type=f32)
-    rank = jnp.sum(one_hot * earlier, axis=0, keepdims=True)
-    slot = iota((128, total), 0)
-    spot_in_block = lax.rem(iota((128, total), 1), total // 4)
-    last = total // 4 - 1
-    filled = (
-        (slot == rank.astype(i32))
-        | ((slot == MOST) & (spot_in_block == 0))
-        | ((slot == MOST + 1) & (spot_in_block == last))
-    )
-    named = jnp.where(owner, spots[...].astype(f32), 0.0)
-    request[...] = lax.dot_general(
-        named.astype(bf16),
-        jnp.where(filled, 1.0, 0.0).astype(bf16),
-        (((1,), (1,)), ((), ())),
-        preferred_element_type=f32,
-    ).astype(i32)
-    arrives = blocks[...].astype(f32) * SLOTS + rank
-    place[...] = jnp.transpose(jnp.broadcast_to(arrives, (columns, total))).astype(i32)
-
-
-def pack_kernel(
-    section, state, bath, fields, blocks, weights, to_left, to_right, table,
-    low, high, surface, extra, sems,
+def prepare_kernel(
+    section, state, bath, fields, blocks, spots, weights,
+    request, place, to_left, to_right, table,
+    low, high, surface, bath_in, fields_in, blocks_in, spots_in, extra, sems,
 ):
     tracers, levels, columns, lanes = state.shape
     many = tracers * levels
     wide = to_left.shape[0] - 2 * many - EXTRA
     below = pl.ds(2 * many + EXTRA, wide)
-    copies = [
-        pltpu.make_async_copy(state.at[:, 0], surface, sems.at[0]),
-        pltpu.make_async_copy(state.at[:, :, pl.ds(0, 8)], low, sems.at[1]),
-        pltpu.make_async_copy(state.at[:, :, pl.ds(columns - 8, 8)], high, sems.at[2]),
-        pltpu.make_async_copy(weights.at[pl.ds(0, wide)], to_left.at[below], sems.at[3]),
-        pltpu.make_async_copy(
-            weights.at[pl.ds((columns - 1) * wide, wide)], to_right.at[below], sems.at[4]
-        ),
+    pairs = [
+        (blocks, blocks_in),
+        (spots, spots_in),
+        (bath, bath_in),
+        (fields, fields_in),
+        (state.at[:, 0], surface),
+        (state.at[:, :, pl.ds(0, 8)], low),
+        (state.at[:, :, pl.ds(columns - 8, 8)], high),
+        (weights.at[pl.ds(0, wide)], to_left.at[below]),
+        (weights.at[pl.ds((columns - 1) * wide, wide)], to_right.at[below]),
     ]
+    copies = [pltpu.make_async_copy(src, dst, sems.at[n]) for n, (src, dst) in enumerate(pairs)]
     for copy in copies:
         copy.start()
+    copies[0].wait()
+    copies[1].wait()
+
+    count, slots = request.shape[0], blocks.shape[0]
+    before = jnp.where(iota((columns, columns), 0) < iota((columns, columns), 1), 1.0, 0.0)
+    before = before.astype(bf16)
+    slot = iota((128, columns), 0)
+    here = iota((128, columns), 1)
+    marks = ((slot == MOST) & (here == 0)) | ((slot == MOST + 1) & (here == columns - 1))
+    used = jnp.zeros((count, 1), f32)
+    asked = jnp.zeros(request.shape, f32)
+    for k in range(slots):
+        block = blocks_in[k : k + 1, :]
+        owner = iota((count, columns), 0) == block
+        one_hot = jnp.where(owner, 1.0, 0.0)
+        earlier = used + jnp.dot(one_hot.astype(bf16), before, preferred_element_type=f32)
+        rank = jnp.sum(one_hot * earlier, axis=0, keepdims=True)
+        used = used + jnp.sum(one_hot, axis=1, keepdims=True)
+        filled = jnp.where((slot == rank.astype(i32)) | marks, 1.0, 0.0).astype(bf16)
+        named = jnp.where(owner, spots_in[k : k + 1, :].astype(f32), 0.0).astype(bf16)
+        asked = asked + lax.dot_general(
+            named, filled, (((1,), (1,)), ((), ())), preferred_element_type=f32
+        )
+        arrives = block.astype(f32) * SLOTS + rank
+        spread = jnp.transpose(jnp.broadcast_to(arrives, (128, columns)))
+        place[k * columns : (k + 1) * columns, :] = spread.astype(i32)
+    request[...] = asked.astype(i32)
+
+    copies[2].wait()
+    copies[3].wait()
     for out, first, at in ((to_left, 0, 0), (to_right, columns - 2, columns - 1)):
         extra[...] = jnp.zeros_like(extra)
-        extra[0:2] = bath[first : first + 2].astype(f32)
+        extra[0:2] = bath_in[first : first + 2].astype(f32)
         for f in range(3):
-            extra[2 + f : 3 + f] = fields[f].astype(f32)[at : at + 1]
-        slots = blocks.shape[0]
-        extra[8 : 8 + slots] = jnp.broadcast_to(blocks[:, at : at + 1].astype(f32), (slots, lanes))
+            extra[2 + f : 3 + f] = fields_in[f].astype(f32)[at : at + 1]
+        extra[8 : 8 + slots] = jnp.broadcast_to(
+            blocks_in[:, at : at + 1].astype(f32), (slots, lanes)
+        )
         out[pl.ds(2 * many, EXTRA)] = extra[...].astype(bf16)
-    copies[0].wait()
+    copies[4].wait()
     on_ocean = section[0] == 1
     for f in range(3):
-        own = fields[f]
+        own = fields_in[f]
         if f < 2:
             own = jnp.where(on_ocean, surface[f], own.astype(f32)).astype(bf16)
         table[:, f * lanes : (f + 1) * lanes] = own
-    copies[1].wait()
-    copies[2].wait()
+    copies[5].wait()
+    copies[6].wait()
     for c in range(2):
         for n in range(tracers):
             part = pl.ds(c * many + n * levels, levels)
@@ -125,8 +135,8 @@
             to_left[part] = tiles[pl.ds(c, levels, stride=8), :].astype(bf16)
             tiles = high.at[n].reshape(levels * 8, lanes)
             to_right[part] = tiles[pl.ds(6 + c, levels, stride=8), :].astype(bf16)
-    copies[3].wait()
-    copies[4].wait()
+    copies[7].wait()
+    copies[8].wait()
 
 
 def serve_kernel(asked, table, out):
@@ -148,7 +158,8 @@
 
 
 def start_kernel(
-    state, from_left, from_right, bath, q_out, rho_out, side_out, held, bath_out, halo, near, sems
+    state, from_left, from_right, bath, weights, ratios,
+    q_out, rho_out, side_out, held, bath_out, weights_out, halo, near, bath_in, sems,
 ):
     tracers, levels, columns, lanes = state.shape
     rows = columns + EDGE
@@ -161,8 +172,12 @@
                 state.at[:, pl.ds(low, size)], held.at[:, pl.ds(low, size)], sems.at[n]
             )
         )
+    bath_copy = pltpu.make_async_copy(bath, bath_in, sems.at[len(chunks)])
+    weights_copy = pltpu.make_async_copy(weights, weights_out, sems.at[len(chunks) + 1])
+    bath_copy.start()
     for copy in reversed(copies):
         copy.start()
+    weights_copy.start()
     for c in range(2):
         part = pl.ds(c * many, many)
         halo[pl.ds(c, many, stride=8), :] = from_right[part].astype(f32)
@@ -179,7 +194,8 @@
             jnp.where(row == EDGE - 2, left[0:1], jnp.where(row == EDGE - 1, left[1:2], 0.0)),
         ),
     )
-    depth = jnp.concatenate([bath[...], edge.astype(i32)], axis=0)
+    bath_copy.wait()
+    depth = jnp.concatenate([bath_in[...], edge.astype(i32)], axis=0)
     bath_out[...] = depth
     lane = iota((rows, lanes), 1)
     a = pltpu.roll(depth, 1, 0)
@@ -192,11 +208,13 @@
     b, d = jnp.maximum(b, d), jnp.minimum(b, d)
     near[0], near[1], near[2], near[3] = a, jnp.maximum(b, c), jnp.minimum(b, c), d
 
+    lookup = jnp.broadcast_to(ratios[0:1], (rows, lanes))
+
     def side(level):
         wet = level < bath_out[...]
-        own = 0.5
+        own = 0.5 * SCALE
         for n in range(4):
-            own = jnp.where(level < near[n], 0.5 - 0.5 * SIDE_MIX * (n + 1), own)
+            own = jnp.where(level < near[n], 0.5 * SCALE - (n + 1), own)
         side_out[level] = own[:columns]
         halves = []
         for n in range(tracers):
@@ -205,55 +223,55 @@
                 spot = pl.multiple_of(spot, 8)
             full = jnp.concatenate([held[n, level], halo[pl.ds(spot, 8), :]], axis=0)
             h = jnp.where(wet, full, 0.0)
-            halves.append(own * h + 0.5 * SIDE_MIX * neighbour_sum(h, lane))
-        return wet, halves
-
-    def deep(step, carry, top):
+            halves.append(own * h + neighbour_sum(h, lane))
+        return halves
+
+    def deep(step, below, top):
         level = top - step
-        rho_below, *below = carry
-        wet, halves = side(level)
-        linked = jnp.where(level + 1 < bath_out[...], DEEP_MIX - DEEP_MIX * rho_below, 0.0)
-        divisor = 1.0 + DEEP_MIX + linked
-        inverse = pl.reciprocal(divisor, approx=True)
-        inverse = inverse * (2.0 - divisor * inverse)
-        inverse = inverse * (2.0 * DEEP_MIX - DEEP_MIX * divisor * inverse)
-        rho = jnp.where(wet, inverse, 0.0)
+        halves = side(level)
+        above_floor = jnp.maximum(bath_out[...] - level, 0)
+        rho = jnp.take_along_axis(lookup, above_floor, axis=1, mode="promise_in_bounds")
         rho_out[level] = rho
         solved = []
         for n in range(tracers):
             q = rho * (halves[n] + below[n])
             q_out[n, level] = q
             solved.append(q)
-        return (rho, *solved)
-
-    carry = tuple(jnp.zeros((rows, lanes), f32) for _ in range(1 + tracers))
+        return tuple(solved)
+
+    carry = tuple(jnp.zeros((rows, lanes), f32) for _ in range(tracers))
     for n in reversed(range(len(chunks))):
         low, size = chunks[n]
         copies[n].wait()
         first = max(low, 2)
         top = low + size - 1
-        carry = sweep(top - first + 1, functools.partial(deep, top=top), carry, 2)
+        carry = sweep(top - first + 1, functools.partial(deep, top=top), carry, 5)
     for level in (1, 0):
-        _, halves = side(level)
+        halves = side(level)
         rho_out[level] = jnp.zeros((rows, lanes), f32)
         for n in range(tracers):
             q_out[n, level] = halves[n]
+    weights_copy.wait()
+
+
+def ratios_by_height(levels, lanes):
+    values = [0.0]
+    ratio = DEEP_MIX / (1.0 + DEEP_MIX)
+    for _ in range(levels):
+        values.append(ratio)
+        ratio = DEEP_MIX / (1.0 + DEEP_MIX + DEEP_MIX - DEEP_MIX * ratio)
+    values += [0.0] * (lanes - len(values))
+    return jnp.broadcast_to(jnp.asarray(np.array(values, np.float32)), (8, lanes))
 
 
 def remap_kernel(
-    section, columns_in, place, from_left, from_right, weights, out, picked, solved, held, sems
+    section, columns_in, place, from_left, from_right, weights, out, picked, solved
 ):
     fields, rows, width = out.shape
     columns = rows - EDGE
     slots = weights.shape[0] // (columns * width)
     tall = slots * width
     many = from_left.shape[0] - tall - EXTRA
-    group = 8
-    copies = []
-    for n in range(columns // group):
-        part = pl.ds(n * group * tall, group * tall)
-        copies.append(pltpu.make_async_copy(weights.at[part], held.at[part], sems.at[n]))
-        copies[-1].start()
     right = from_right[pl.ds(many, EXTRA)].astype(f32)
     left = from_left[pl.ds(many, EXTRA)].astype(f32)
     spots = iota((rows, columns_in.shape[0]), 1)
@@ -283,11 +301,8 @@
     below = many + EXTRA
     one(columns, lambda k: from_right[pl.ds(below + k * width, width)])
     one(rows - 1, lambda k: from_left[pl.ds(below + k * width, width)])
-    for n in range(columns // group):
-        copies[n].wait()
-        for m in range(group):
-            spot = n * group + m
-            one(spot, lambda k: held[pl.ds((spot * slots + k) * width, width)])
+    for spot in range(columns):
+        one(spot, lambda k: weights[pl.ds((spot * slots + k) * width, width)])
     on_ocean = section[0] == 1
     for f in range(fields):
         out[f, pl.ds(0, columns)] = solved[pl.ds(f, columns, stride=8), :]
@@ -315,7 +330,7 @@
     top_mix = TOP_MIX * (1.0 + flux[2] * flux[2] + own[2] * own[2])
     depth = bath[...]
 
-    def top_levels(count, halves, below, rho_below):
+    def top_levels(count, halves, below, rho_below, scale):
         wet = 1 < depth[:count]
         link = jnp.where(wet, top_mix[:count], 0.0)
         deeper = jnp.where(2 < depth[:count], DEEP_MIX - DEEP_MIX * rho_below, 0.0)
@@ -325,7 +340,7 @@
         values = []
         for n in range(tracers):
             partial = 2.0 * (halves[n][1] + below[n]) * second
-            source = 2.0 * halves[n][0] + FLUX_GAIN * forcing[n][:count]
+            source = 2.0 * halves[n][0] + scale * FLUX_GAIN * forcing[n][:count]
             surface_value = (source + link * partial) * first
             next_value = jnp.where(wet, partial, 0.0) + rho_second * surface_value
             values.append((surface_value, next_value))
@@ -336,12 +351,11 @@
         [(q[n, 0], q[n, 1]) for n in range(tracers)],
         [q[n, 2] for n in range(tracers)],
         rho[2],
+        SCALE,
     )
 
     def store_half(n, level, h):
-        half[n, level] = (
-            side[level] * h[:columns] + 0.5 * SIDE_MIX * neighbour_sum(h, lane)[:columns]
-        )
+        half[n, level] = side[level] * h[:columns] + neighbour_sum(h, lane)[:columns]
 
     for n in range(tracers):
         for level in (0, 1):
@@ -358,7 +372,7 @@
         return tuple(out)
 
     carry = tuple(values[n][1] for n in range(tracers))
-    sweep(levels - 2, down, carry, 2)
+    sweep(levels - 2, down, carry, 6)
 
     def up(step, carry):
         level = levels - 1 - step
@@ -371,15 +385,17 @@
         return tuple(out)
 
     zero = jnp.zeros((columns, lanes), f32)
-    carry = sweep(levels - 2, up, (zero,) * tracers, 6)
+    carry = sweep(levels - 2, up, (zero,) * tracers, 13)
     values = top_levels(
         columns,
         [(half[n, 0], half[n, 1]) for n in range(tracers)],
         carry,
         rho[2, pl.ds(0, columns)],
+        SCALE * SCALE,
     )
+    unscale = 1.0 / (SCALE * SCALE)
     for n in range(tracers):
-        surface[n] = jnp.where(on_ocean, values[n][0], other[n, pl.ds(0, columns)])
+        surface[n] = jnp.where(on_ocean, values[n][0] * unscale, other[n, pl.ds(0, columns)])
     surface[2] = jnp.where(on_ocean, top_mix[:columns], other[2, pl.ds(0, columns)])
 
     def last(step, carry, low):
@@ -389,7 +405,7 @@
         out = []
         for n in range(tracers):
             h = half[n, level] + ratio * carry[n]
-            done[n, level] = jnp.where(wet, h, start[n, level])
+            done[n, level] = jnp.where(wet, h * unscale, start[n, level])
             out.append(h)
         return tuple(out)
 
@@ -398,10 +414,12 @@
     for n, (low, size) in enumerate(chunks):
         if n == 0:
             for m in range(tracers):
-                done[m, 0] = values[m][0]
-                done[m, 1] = jnp.where(1 < depth[:columns], values[m][1], start[m, 1])
+                done[m, 0] = values[m][0] * unscale
+                done[m, 1] = jnp.where(
+                    1 < depth[:columns], values[m][1] * unscale, start[m, 1]
+                )
         first = max(low, 2)
-        carry = sweep(low + size - first, functools.partial(last, low=first), carry, 4)
+        carry = sweep(low + size - first, functools.partial(last, low=first), carry, 10)
         part = pl.ds(low, size)
         leaving.append(
             pltpu.make_async_copy(done.at[:, part], result.at[:, part], sems.at[n])
@@ -431,41 +449,42 @@
     tall = slots * lanes
     many = tracers * levels
 
-    anywhere = pl.BlockSpec(memory_space=pl.ANY)
+    hbm = pl.BlockSpec(memory_space=pltpu.HBM)
     vmem = pl.BlockSpec(memory_space=pltpu.VMEM)
     smem = pl.BlockSpec(memory_space=pltpu.SMEM)
     shaped = jax.ShapeDtypeStruct
     pieces = len(chunks_of(levels))
     cells = rows * lanes
 
-    request, place = pl.pallas_call(
-        ask_kernel,
-        out_shape=(shaped((count, 128), i32), shaped((slots * columns, 128), i32)),
-        in_specs=[vmem, vmem],
-        out_specs=(vmem, vmem),
-        compiler_params=pltpu.CompilerParams(vmem_limit_bytes=4 * MIB),
-        cost_estimate=pl.CostEstimate(flops=10**6, bytes_accessed=10**5, transcendentals=0),
-    )(blocks.reshape(1, slots * columns), spots.reshape(1, slots * columns))
-    asked = lax.all_to_all(request, "blk", split_axis=0, concat_axis=0, tiled=True)
-
     payload = shaped((2 * many + EXTRA + tall, lanes), bf16)
-    to_left, to_right, table = pl.pallas_call(
-        pack_kernel,
-        out_shape=(payload, payload, shaped((columns, 3 * lanes), bf16)),
-        in_specs=[smem, anywhere, vmem, vmem, vmem, anywhere],
-        out_specs=(vmem, vmem, vmem),
+    request, place, to_left, to_right, table = pl.pallas_call(
+        prepare_kernel,
+        out_shape=(
+            shaped((count, 128), i32),
+            shaped((slots * columns, 128), i32),
+            payload,
+            payload,
+            shaped((columns, 3 * lanes), bf16),
+        ),
+        in_specs=[smem] + [hbm] * 6,
+        out_specs=(vmem,) * 5,
         scratch_shapes=[
             pltpu.VMEM((tracers, levels, 8, lanes), f32),
             pltpu.VMEM((tracers, levels, 8, lanes), f32),
             pltpu.VMEM((tracers, columns, lanes), f32),
+            pltpu.VMEM(bathymetry.shape, i32),
+            pltpu.VMEM(fields.shape, bf16),
+            pltpu.VMEM(blocks.shape, i32),
+            pltpu.VMEM(spots.shape, i32),
             pltpu.VMEM((EXTRA, lanes), f32),
-            pltpu.SemaphoreType.DMA((5,)),
+            pltpu.SemaphoreType.DMA((9,)),
         ],
         compiler_params=pltpu.CompilerParams(vmem_limit_bytes=8 * MIB),
         cost_estimate=pl.CostEstimate(
             flops=10**6, bytes_accessed=4 * 10**6, transcendentals=0
         ),
-    )(section, ocean_state, bathymetry, fields, blocks, weights)
+    )(section, ocean_state, bathymetry, fields, blocks, spots, weights)
+    asked = lax.all_to_all(request, "blk", split_axis=0, concat_axis=0, tiled=True)
     from_left = shift(to_right, "blk", 1)
     from_right = shift(to_left, "blk", -1)
     partner_fields = lax.ppermute(fields, "sec", [(0, 1), (1, 0)])
@@ -482,7 +501,7 @@
     )(asked, table)
     columns_in = lax.all_to_all(served, "blk", split_axis=0, concat_axis=0, tiled=True)
 
-    q, rho, side, start, bath = pl.pallas_call(
+    q, rho, side, start, bath, near_weights = pl.pallas_call(
         start_kernel,
         out_shape=(
             shaped((tracers, levels, rows, lanes), f32),
@@ -490,43 +509,43 @@
             shaped((levels, columns, lanes), f32),
             shaped(ocean_state.shape, f32),
             shaped((rows, lanes), i32),
-        ),
-        in_specs=[anywhere, vmem, vmem, vmem],
-        out_specs=(vmem,) * 5,
+            shaped(weights.shape, bf16),
+        ),
+        in_specs=[hbm, vmem, vmem, hbm, hbm, vmem],
+        out_specs=(vmem,) * 6,
         scratch_shapes=[
             pltpu.VMEM((many * 8, lanes), f32),
             pltpu.VMEM((4, rows, lanes), i32),
-            pltpu.SemaphoreType.DMA((pieces,)),
+            pltpu.VMEM(bathymetry.shape, i32),
+            pltpu.SemaphoreType.DMA((pieces + 2,)),
         ],
         compiler_params=pltpu.CompilerParams(vmem_limit_bytes=8 * MIB),
         cost_estimate=pl.CostEstimate(
             flops=60 * levels * cells, bytes_accessed=20 * levels * cells, transcendentals=0
         ),
-    )(ocean_state, from_left, from_right, bathymetry)
+    )(ocean_state, from_left, from_right, bathymetry, weights, ratios_by_height(levels, lanes))
 
     mine = pl.pallas_call(
         remap_kernel,
         out_shape=shaped((3, rows, lanes), f32),
-        in_specs=[smem, vmem, vmem, vmem, vmem, anywhere],
+        in_specs=[smem] + [vmem] * 5,
         out_specs=vmem,
         scratch_shapes=[
             pltpu.VMEM((slots, rows * 8, lanes), f32),
             pltpu.VMEM((rows * 8, lanes), f32),
-            pltpu.VMEM(weights.shape, bf16),
-            pltpu.SemaphoreType.DMA((columns // 8,)),
         ],
-        compiler_params=pltpu.CompilerParams(vmem_limit_bytes=16 * MIB),
+        compiler_params=pltpu.CompilerParams(vmem_limit_bytes=8 * MIB),
         cost_estimate=pl.CostEstimate(
             flops=16 * weights.size, bytes_accessed=2 * weights.size, transcendentals=0
         ),
-    )(section, columns_in, place, from_left, from_right, weights)
+    )(section, columns_in, place, from_left, from_right, near_weights)
     other = lax.ppermute(mine, "sec", [(0, 1), (1, 0)])
 
     surface, result = pl.pallas_call(
         finish_kernel,
         out_shape=(shaped((3, columns, lanes), f32), shaped(ocean_state.shape, f32)),
         in_specs=[smem] + [vmem] * 9,
-        out_specs=(vmem, anywhere),
+        out_specs=(vmem, hbm),
         scratch_shapes=[
             pltpu.VMEM(ocean_state.shape, f32),
             pltpu.VMEM(ocean_state.shape, f32),

time: 69.1 us -> 91.2 us (1.32)
  local copies, waits for them, and re-layouts: 13 us -> 34 us
  blocking collectives: 0 us -> 15.4 us
  starting transfers between devices: 21.4 us -> 9.72 us
  Pallas kernels: 24.1 us -> 21.3 us
    unnamed x18 -> x50, local copies, waits for them, and re-layouts: 11.5 us -> 34 us
    all_to_all x0 -> x1, blocking collectives: none -> 15.4 us  [per_device(): lax.all_to_all(request, 'blk', split_axis=0, concat_axis=0, tiled=True)]
    all_to_all x1 -> x0, starting transfers between devices: 8.31 us -> none  [per_device(): lax.all_to_all(request, 'blk', split_axis=0, concat_axis=0, tiled=True)]
    all_to_all x1, starting transfers between devices: 6.9 us -> 3.54 us  [per_device(): lax.all_to_all(served, 'blk', split_axis=0, concat_axis=0, tiled=True)]
    pallas_call x1, Pallas kernels: 9.53 us -> 7.74 us  [per_device(): pl.pallas_call(finish_kernel, out_shape=(shaped((3, columns, lanes), f32)...]
    pallas_call x1, Pallas kernels: 4.32 us -> 2.71 us  [per_device(): pl.pallas_call(remap_kernel, out_shape=shaped((3, rows, lanes), f32), in_...]
    reshape x2 -> x0, local copies, waits for them, and re-layouts: 1.53 us -> none  [the longest x1 0.76 us: per_device(): blocks.reshape(1, slots * columns)]
  transfers between devices with their start and end apart: 6 -> 5, of which waited for: 2 -> 2; matrix products, arithmetic and copies ran while one was open for 0% -> 0% of each run, Pallas kernels for 12% -> 9%
where the time goes in v3:
time: 91.2 us; the launch traced here: 90.5 us
  local copies, waits for them, and re-layouts  34 us (37%)
  Pallas kernels  21.3 us (23%)
  blocking collectives  15.4 us (17%)
  starting transfers between devices  9.72 us (11%)
  waiting for transfers between devices  9.33 us (10%)
    unnamed x50, local copies, waits for them, and re-layouts  34 us
    all_to_all x1, blocking collectives, per_device(): lax.all_to_all(request, 'blk', split_axis=0, concat_axis=0, tiled=True)  15.4 us
    ppermute x2, waiting for transfers between devices, shift(): lax.ppermute(value, axis, [(i, (i + by) % count) for i in range(count)])  8.45 us
    pallas_call x1, Pallas kernels, per_device(): pl.pallas_call(start_kernel, out_shape=(shaped((tracers, levels, rows, la...  8.18 us
    pallas_call x1, Pallas kernels, per_device(): pl.pallas_call(finish_kernel, out_shape=(shaped((3, columns, lanes), f32)...  7.74 us
    ppermute x2, starting transfers between devices, shift(): lax.ppermute(value, axis, [(i, (i + by) % count) for i in range(count)])  5.67 us
    all_to_all x1, starting transfers between devices, per_device(): lax.all_to_all(served, 'blk', split_axis=0, concat_axis=0, tiled=True)  3.54 us
    pallas_call x1, Pallas kernels, per_device(): pl.pallas_call(remap_kernel, out_shape=shaped((3, rows, lanes), f32), in_...  2.71 us
  transfers between devices with their start and end apart: 5, of which 2 were waited for; matrix products, arithmetic and copies ran while one was open for 0% of the time, Pallas kernels for 9%

profile of v3, /device:TPU:0, one launch (start us, length us, event | category | flops | bytes accessed | tf_op | source)
XLA Modules:
  0.0 90.5 jit_solution(5542463620427247353)
XLA Ops:
  0.6 3.4 %copy-done = bf16[1,64,4,128,128]{4,3,2,1,0:T(8,128)(2,1)S(1)} copy-done((bf16[1,64,4,128,128]{4,3,2,1,0:T(8,128)(2,1)S(1)}, bf16[1,64,4,128,128]{4,3,2,1,0:T(8,128)(2,1)}, u32[]{:S(2)}) %copy-start) | copy-done | bytes 8388632
  4.0 2.5 %copy-done.2 = f32[2,80,64,128]{3,2,1,0:T(8,128)S(1)} copy-done((f32[2,80,64,128]{3,2,1,0:T(8,128)S(1)}, f32[2,80,64,128]{3,2,1,0:T(8,128)}, u32[]{:S(2)}) %copy-start.2) | copy-done | bytes 5242904
  6.5 0.8 copy-done.14
  7.3 0.8 copy-done.18
  8.1 0.7 copy-done.22
  8.7 0.7 copy-done.23
  9.4 1.4 %shard_map.86 = (s32[16,128]{1,0:T(8,128)S(1)}, s32[256,128]{1,0:T(8,128)S(1)}, bf16[848,128]{1,0:T(8,128)(2,1)S(1)}, bf16[848,128]{1,0:T(8,128)(2,1)S(1)}, bf16[64,384]{1,0:T(8,128)(2,1)S(1)}) custom-call(s32[1]{0:T(128)} %bitcast.section, f32[2,80,64,128]{3,2,1,0:T(8,128)S(1)} %copy-done.2, s32[64,128]{1,0:T(8,128)S(1)} %copy-done.18, ...), custom_call_target="tpu_custom_call" | custom-call | flops 1000000 | bytes 4000000 | tf_op jit(solution)/shard_map/pallas_call | solution.py:460
  10.9 0.7 copy-done.16
  11.6 15.4 %all_to_all.22 = s32[16,1,128]{2,1,0:T(1,128)S(1)} all-to-all(s32[16,1,128]{2,1,0:T(1,128)S(1)} %bitcast.23), channel_id=1, replica_groups=mesh['sec'=2,'blk'=16] {'blk'}, dimensions={0} | all-to-all | bytes 16384 | tf_op jit(solution)/shard_map/all_to_all | solution.py:487
  26.9 1.2 %shard_map.87 = bf16[384,384]{1,0:T(8,128)(2,1)} custom-call(s32[16,128]{1,0:T(8,128)S(1)} %bitcast.22, bf16[64,384]{1,0:T(8,128)(2,1)S(1)} %get-tuple-element.16.table), custom_call_target="tpu_custom_call" | custom-call | flops 10000000 | bytes 1000000 | tf_op jit(solution)/shard_map/pallas_call | solution.py:492
  28.1 3.5 %all-to-all-start.1 = ((bf16[16,24,384]{2,1,0:T(8,128)(2,1)}), bf16[16,24,384]{2,1,0:T(8,128)(2,1)S(1)}, u32[]{:S(2)}, u32[]{:S(2)}) async-start(bf16[16,24,384]{2,1,0:T(8,128)(2,1)} %bitcast.10), calls=%async_computation.1 | async-start | bytes 589824 | tf_op jit(solution)/shard_map/all_to_all | solution.py:502
  31.7 1.8 %collective-permute-start = (bf16[848,128]{1,0:T(8,128)(2,1)S(1)}, bf16[848,128]{1,0:T(8,128)(2,1)S(1)}, u32[]{:S(2)}, u32[]{:S(2)}) collective-permute-start(bf16[848,128]{1,0:T(8,128)(2,1)S(1)} %get-tuple-element.18), channel_id=1, source_target_pairs={{0,1},{1,2},{2,3},{3,4},{4,5},{5,6},{6,7},{7,8},{8,9},{9,10},{10,1... | collective-permute-start | bytes 651272 | tf_op jit(solution)/shard_map/ppermute | solution.py:434
  33.5 3.9 %collective-permute-start.1 = (bf16[848,128]{1,0:T(8,128)(2,1)S(1)}, bf16[848,128]{1,0:T(8,128)(2,1)S(1)}, u32[]{:S(2)}, u32[]{:S(2)}) collective-permute-start(bf16[848,128]{1,0:T(8,128)(2,1)S(1)} %get-tuple-element.19), channel_id=1, source_target_pairs={{0,15},{1,0},{2,1},{3,2},{4,3},{5,4},{6,5},{7,6},{8,7},{9,8},{10,9... | collective-permute-start | bytes 651272 | tf_op jit(solution)/shard_map/ppermute | solution.py:434
  37.4 8.4 %collective-permute-done.from_left = bf16[848,128]{1,0:T(8,128)(2,1)S(1)} collective-permute-done((bf16[848,128]{1,0:T(8,128)(2,1)S(1)}, bf16[848,128]{1,0:T(8,128)(2,1)S(1)}, u32[]{:S(2)}, u32[]{:S(2)}) %collective-permute-start) | collective-permute-done | bytes 217120 | tf_op jit(solution)/shard_map/ppermute | solution.py:434
  45.8 3.4 %copy-done.1 = bf16[1,64,4,128,128]{4,3,2,1,0:T(8,128)(2,1)S(1)} copy-done((bf16[1,64,4,128,128]{4,3,2,1,0:T(8,128)(2,1)S(1)}, bf16[1,64,4,128,128]{4,3,2,1,0:T(8,128)(2,1)}, u32[]{:S(2)}) %copy-start.1) | copy-done | bytes 8388632
  49.2 2.5 %copy-done.3 = f32[2,80,64,128]{3,2,1,0:T(8,128)S(1)} copy-done((f32[2,80,64,128]{3,2,1,0:T(8,128)S(1)}, f32[2,80,64,128]{3,2,1,0:T(8,128)}, u32[]{:S(2)}) %copy-start.3) | copy-done | bytes 5242904
  51.7 8.2 %shard_map.88 = (f32[2,80,72,128]{3,2,1,0:T(8,128)S(1)}, f32[80,72,128]{2,1,0:T(8,128)S(1)}, f32[80,64,128]{2,1,0:T(8,128)S(1)}, f32[2,80,64,128]{3,2,1,0:T(8,12...) custom-call(f32[2,80,64,128]{3,2,1,0:T(8,128)S(1)} %copy-done.3, ...), custom_call_target="tpu_custom_call" | custom-call | flops 44236800 | bytes 14745600 | tf_op jit(solution)/shard_map/pallas_call | solution.py:504
  59.9 3.3 %copy-done.4 = bf16[32768,128]{1,0:T(8,128)(2,1)} copy-done((bf16[32768,128]{1,0:T(8,128)(2,1)}, bf16[32768,128]{1,0:T(8,128)(2,1)S(1)}, u32[]{:S(2)}) %copy-start.4) | copy-done | bytes 8388632
  63.2 2.6 %copy-done.6 = f32[2,80,72,128]{3,2,1,0:T(8,128)} copy-done((f32[2,80,72,128]{3,2,1,0:T(8,128)}, f32[2,80,72,128]{3,2,1,0:T(8,128)S(1)}, u32[]{:S(2)}) %copy-start.6) | copy-done | bytes 5898264
  65.7 2.4 %copy-done.8 = f32[2,80,64,128]{3,2,1,0:T(8,128)} copy-done((f32[2,80,64,128]{3,2,1,0:T(8,128)}, f32[2,80,64,128]{3,2,1,0:T(8,128)S(1)}, u32[]{:S(2)}) %copy-start.8) | copy-done | bytes 5242904
  68.1 1.5 %copy-done.10 = f32[80,64,128]{2,1,0:T(8,128)} copy-done((f32[80,64,128]{2,1,0:T(8,128)}, f32[80,64,128]{2,1,0:T(8,128)S(1)}, u32[]{:S(2)}) %copy-start.10) | copy-done | bytes 2621464
  69.6 0.7 copy-done.12
  70.3 0.6 copy-done.20
  70.9 3.4 %copy-done.5 = bf16[32768,128]{1,0:T(8,128)(2,1)S(1)} copy-done((bf16[32768,128]{1,0:T(8,128)(2,1)S(1)}, bf16[32768,128]{1,0:T(8,128)(2,1)}, u32[]{:S(2)}) %copy-start.5) | copy-done | bytes 8388632
  74.3 0.9 %copy-done.13 = bf16[848,128]{1,0:T(8,128)(2,1)S(1)} copy-done((bf16[848,128]{1,0:T(8,128)(2,1)S(1)}, bf16[848,128]{1,0:T(8,128)(2,1)}, u32[]{:S(2)}) %copy-start.13) | copy-done | bytes 217112
  75.2 0.9 copy-done.17
  76.1 2.7 %shard_map.89.mine = f32[3,72,128]{2,1,0:T(8,128)S(1)} custom-call(s32[1]{0:T(128)} %bitcast.section, bf16[384,384]{1,0:T(8,128)(2,1)S(1)} %bitcast.18, s32[256,128]{1,0:T(8,128)S(1)} %copy-done.17, bf16[848,128]{1,0:T(8,128)(2,1)S(1)} %collective-permute-done.from_left, bf16[848,128]{1,0:T(8,128)(2,1)S(1)} %copy-done.13, bf16[32768,128]{1,0:T(8,128)(2,1)S(1)} %copy-done.5), custom_call_target="tpu_custom_call" | custom-call | flops 67108864 | bytes 8388608 | tf_op jit(solution)/shard_map/pallas_call | solution.py:528
  78.8 0.0 copy-done.15
  78.8 0.5 collective-permute-start.3
  79.3 0.9 collective-permute-done.3.partner_fields
  80.3 2.5 %copy-done.9 = f32[2,80,64,128]{3,2,1,0:T(8,128)S(1)} copy-done((f32[2,80,64,128]{3,2,1,0:T(8,128)S(1)}, f32[2,80,64,128]{3,2,1,0:T(8,128)}, u32[]{:S(2)}) %copy-start.9) | copy-done | bytes 5242904
  82.7 7.7 %shard_map.90 = (f32[3,64,128]{2,1,0:T(8,128)}, f32[2,80,64,128]{3,2,1,0:T(8,128)}) custom-call(s32[1]{0:T(128)} %bitcast.section, f32[3,72,128]{2,1,0:T(8,128)S(1)} %shard_map.89.mine, f32[3,72,128]{2,1,0:T(8,128)S(1)} %collective-permute-done.2.other, bf16[3,64,128]{2,1,0:T(8,128)(2,1)S(1)} %bitcast.21, ...), custom_call_target="tpu_custom_call" | custom-call | flops 44236800 | bytes 23592960 | tf_op jit(solution)/shard_map/pallas_call | solution.py:544
  (35 shorter events, 0.1 us)
Async XLA Ops:
  0.6 3.4 %copy-start = (bf16[1,64,4,128,128]{4,3,2,1,0:T(8,128)(2,1)S(1)}, bf16[1,64,4,128,128]{4,3,2,1,0:T(8,128)(2,1)}, u32[]{:S(2)}) copy-start(bf16[1,64,4,128,128]{4,3,2,1,0:T(8,128)(2,1)} %param.10) | copy-start | bytes 25165828
  4.0 2.5 %copy-start.2 = (f32[2,80,64,128]{3,2,1,0:T(8,128)S(1)}, f32[2,80,64,128]{3,2,1,0:T(8,128)}, u32[]{:S(2)}) copy-start(f32[2,80,64,128]{3,2,1,0:T(8,128)} %state.3) | copy-start | bytes 15728644
  6.5 0.8 copy-start.14
  7.3 0.8 copy-start.18
  8.1 0.7 copy-start.22
  8.7 0.7 copy-start.23
  9.4 36.4 %copy-start.24 = (f32[128]{0:T(128)S(1)}, f32[128]{0:T(128)}, u32[]{:S(2)}) copy-start(f32[128]{0:T(128)} %constant.8.clone) | copy-start | bytes 1540
  9.4 36.4 %copy-start.19 = (s32[64,128]{1,0:T(8,128)S(1)}, s32[64,128]{1,0:T(8,128)}, u32[]{:S(2)}) copy-start(s32[64,128]{1,0:T(8,128)} %bath.3) | copy-start | bytes 98308
  10.9 0.7 copy-start.16
  28.1 42.7 %all-to-all-start.1 = ((bf16[16,24,384]{2,1,0:T(8,128)(2,1)}), bf16[16,24,384]{2,1,0:T(8,128)(2,1)S(1)}, u32[]{:S(2)}, u32[]{:S(2)}) async-start(bf16[16,24,384]{2,1,0:T(8,128)(2,1)} %bitcast.10), calls=%async_computation.1 | async-start | bytes 589824 | tf_op jit(solution)/shard_map/all_to_all | solution.py:502
  31.7 14.1 %collective-permute-start = (bf16[848,128]{1,0:T(8,128)(2,1)S(1)}, bf16[848,128]{1,0:T(8,128)(2,1)S(1)}, u32[]{:S(2)}, u32[]{:S(2)}) collective-permute-start(bf16[848,128]{1,0:T(8,128)(2,1)S(1)} %get-tuple-element.18), channel_id=1, source_target_pairs={{0,1},{1,2},{2,3},{3,4},{4,5},{5,6},{6,7},{7,8},{8,9},{9,10},{10,1... | collective-permute-start | bytes 651272 | tf_op jit(solution)/shard_map/ppermute | solution.py:434
  33.5 12.3 %collective-permute-start.1 = (bf16[848,128]{1,0:T(8,128)(2,1)S(1)}, bf16[848,128]{1,0:T(8,128)(2,1)S(1)}, u32[]{:S(2)}, u32[]{:S(2)}) collective-permute-start(bf16[848,128]{1,0:T(8,128)(2,1)S(1)} %get-tuple-element.19), channel_id=1, source_target_pairs={{0,15},{1,0},{2,1},{3,2},{4,3},{5,4},{6,5},{7,6},{8,7},{9,8},{10,9... | collective-permute-start | bytes 651272 | tf_op jit(solution)/shard_map/ppermute | solution.py:434
  45.8 3.4 %copy-start.1 = (bf16[1,64,4,128,128]{4,3,2,1,0:T(8,128)(2,1)S(1)}, bf16[1,64,4,128,128]{4,3,2,1,0:T(8,128)(2,1)}, u32[]{:S(2)}) copy-start(bf16[1,64,4,128,128]{4,3,2,1,0:T(8,128)(2,1)} %param.10) | copy-start | bytes 25165828
  49.2 2.5 %copy-start.3 = (f32[2,80,64,128]{3,2,1,0:T(8,128)S(1)}, f32[2,80,64,128]{3,2,1,0:T(8,128)}, u32[]{:S(2)}) copy-start(f32[2,80,64,128]{3,2,1,0:T(8,128)} %state.3) | copy-start | bytes 15728644
  51.7 27.1 %copy-start.15 = (bf16[1,3,64,128]{3,2,1,0:T(8,128)(2,1)S(1)}, bf16[1,3,64,128]{3,2,1,0:T(8,128)(2,1)}, u32[]{:S(2)}) copy-start(bf16[1,3,64,128]{3,2,1,0:T(8,128)(2,1)} %param.7) | copy-start | bytes 147460
  59.9 3.3 %copy-start.4 = (bf16[32768,128]{1,0:T(8,128)(2,1)}, bf16[32768,128]{1,0:T(8,128)(2,1)S(1)}, u32[]{:S(2)}) copy-start(bf16[32768,128]{1,0:T(8,128)(2,1)S(1)} %get-tuple-element.20.weights) | copy-start | bytes 25165828
  63.2 2.6 %copy-start.6 = (f32[2,80,72,128]{3,2,1,0:T(8,128)}, f32[2,80,72,128]{3,2,1,0:T(8,128)S(1)}, u32[]{:S(2)}) copy-start(f32[2,80,72,128]{3,2,1,0:T(8,128)S(1)} %get-tuple-element.22.q) | copy-start | bytes 17694724
  65.7 2.4 %copy-start.8 = (f32[2,80,64,128]{3,2,1,0:T(8,128)}, f32[2,80,64,128]{3,2,1,0:T(8,128)S(1)}, u32[]{:S(2)}) copy-start(f32[2,80,64,128]{3,2,1,0:T(8,128)S(1)} %get-tuple-element.25.start) | copy-start | bytes 15728644
  68.1 1.5 %copy-start.10 = (f32[80,64,128]{2,1,0:T(8,128)}, f32[80,64,128]{2,1,0:T(8,128)S(1)}, u32[]{:S(2)}) copy-start(f32[80,64,128]{2,1,0:T(8,128)S(1)} %get-tuple-element.24.side) | copy-start | bytes 7864324
  69.6 0.7 copy-start.12
  70.3 0.6 copy-start.20
  70.9 3.4 %copy-start.5 = (bf16[32768,128]{1,0:T(8,128)(2,1)S(1)}, bf16[32768,128]{1,0:T(8,128)(2,1)}, u32[]{:S(2)}) copy-start(bf16[32768,128]{1,0:T(8,128)(2,1)} %copy-done.4) | copy-start | bytes 25165828
  74.3 0.9 %copy-start.13 = (bf16[848,128]{1,0:T(8,128)(2,1)S(1)}, bf16[848,128]{1,0:T(8,128)(2,1)}, u32[]{:S(2)}) copy-start(bf16[848,128]{1,0:T(8,128)(2,1)} %copy-done.12) | copy-start | bytes 651268
  75.2 0.9 copy-start.17
  76.1 4.1 %copy-start.7 = (f32[2,80,72,128]{3,2,1,0:T(8,128)S(1)}, f32[2,80,72,128]{3,2,1,0:T(8,128)}, u32[]{:S(2)}) copy-start(f32[2,80,72,128]{3,2,1,0:T(8,128)} %copy-done.6) | copy-start | bytes 17694724
  76.1 4.1 %copy-start.11 = (f32[80,64,128]{2,1,0:T(8,128)S(1)}, f32[80,64,128]{2,1,0:T(8,128)}, u32[]{:S(2)}) copy-start(f32[80,64,128]{2,1,0:T(8,128)} %copy-done.10) | copy-start | bytes 7864324
  76.1 4.1 %copy-start.21 = (s32[72,128]{1,0:T(8,128)S(1)}, s32[72,128]{1,0:T(8,128)}, u32[]{:S(2)}) copy-start(s32[72,128]{1,0:T(8,128)} %copy-done.20) | copy-start | bytes 110596
  78.8 1.4 %collective-permute-start.2 = (f32[3,72,128]{2,1,0:T(8,128)S(1)}, f32[3,72,128]{2,1,0:T(8,128)S(1)}, u32[]{:S(2)}, u32[]{:S(2)}) collective-permute-start(f32[3,72,128]{2,1,0:T(8,128)S(1)} %shard_map.89.mine), channel_id=1, source_target_pairs={{0,16},{16,0},{1,17},{17,1},{2,18},{18,2},{3,19},{19,3},{4,20},{20... | collective-permute-start | bytes 331784 | tf_op jit(solution)/shard_map/ppermute | solution.py:542
  78.8 1.4 %collective-permute-start.3 = (bf16[3,64,128]{2,1,0:T(8,128)(2,1)S(1)}, bf16[3,64,128]{2,1,0:T(8,128)(2,1)S(1)}, u32[]{:S(2)}, u32[]{:S(2)}) collective-permute-start(bf16[3,64,128]{2,1,0:T(8,128)(2,1)S(1)} %bitcast.20), channel_id=1, source_target_pairs={{0,16},{16,0},{1,17},{17,1},{2,18},{18,2},{3,19},{19,3},{4,20},{20... | collective-permute-start | bytes 147464 | tf_op jit(solution)/shard_map/ppermute | solution.py:490
  80.2 2.5 %copy-start.9 = (f32[2,80,64,128]{3,2,1,0:T(8,128)S(1)}, f32[2,80,64,128]{3,2,1,0:T(8,128)}, u32[]{:S(2)}) copy-start(f32[2,80,64,128]{3,2,1,0:T(8,128)} %copy-done.8) | copy-start | bytes 15728644

commit v4 on v3

--- a/solution.py
+++ b/solution.py
@@ -59,13 +59,12 @@
 
 def prepare_kernel(
     section, state, bath, fields, blocks, spots, weights,
-    request, place, to_left, to_right, table,
+    request, place, to_left, to_right, left_weights, right_weights, table,
     low, high, surface, bath_in, fields_in, blocks_in, spots_in, extra, sems,
 ):
     tracers, levels, columns, lanes = state.shape
     many = tracers * levels
-    wide = to_left.shape[0] - 2 * many - EXTRA
-    below = pl.ds(2 * many + EXTRA, wide)
+    wide = left_weights.shape[0]
     pairs = [
         (blocks, blocks_in),
         (spots, spots_in),
@@ -74,8 +73,8 @@
         (state.at[:, 0], surface),
         (state.at[:, :, pl.ds(0, 8)], low),
         (state.at[:, :, pl.ds(columns - 8, 8)], high),
-        (weights.at[pl.ds(0, wide)], to_left.at[below]),
-        (weights.at[pl.ds((columns - 1) * wide, wide)], to_right.at[below]),
+        (weights.at[pl.ds(0, wide)], left_weights),
+        (weights.at[pl.ds((columns - 1) * wide, wide)], right_weights),
     ]
     copies = [pltpu.make_async_copy(src, dst, sems.at[n]) for n, (src, dst) in enumerate(pairs)]
     for copy in copies:
@@ -265,13 +264,13 @@
 
 
 def remap_kernel(
-    section, columns_in, place, from_left, from_right, weights, out, picked, solved
+    section, columns_in, place, from_left, from_right, left_weights, right_weights, weights,
+    out, picked, solved,
 ):
     fields, rows, width = out.shape
     columns = rows - EDGE
     slots = weights.shape[0] // (columns * width)
-    tall = slots * width
-    many = from_left.shape[0] - tall - EXTRA
+    many = from_left.shape[0] - EXTRA
     right = from_right[pl.ds(many, EXTRA)].astype(f32)
     left = from_left[pl.ds(many, EXTRA)].astype(f32)
     spots = iota((rows, columns_in.shape[0]), 1)
@@ -298,9 +297,8 @@
         )
 
     solved[...] = jnp.zeros_like(solved)
-    below = many + EXTRA
-    one(columns, lambda k: from_right[pl.ds(below + k * width, width)])
-    one(rows - 1, lambda k: from_left[pl.ds(below + k * width, width)])
+    one(columns, lambda k: right_weights[pl.ds(k * width, width)])
+    one(rows - 1, lambda k: left_weights[pl.ds(k * width, width)])
     for spot in range(columns):
         one(spot, lambda k: weights[pl.ds((spot * slots + k) * width, width)])
     on_ocean = section[0] == 1
@@ -434,6 +432,19 @@
     return lax.ppermute(value, axis, [(i, (i + by) % count) for i in range(count)])
 
 
+def shift_first_section(value, by):
+    count = lax.axis_size("blk")
+    return lax.ppermute(value, ("sec", "blk"), [(i, (i + by) % count) for i in range(count)])
+
+
+def in_hbm(value):
+    return pltpu.with_memory_space_constraint(value, pltpu.HBM)
+
+
+def in_vmem(value):
+    return pltpu.with_memory_space_constraint(value, pltpu.VMEM)
+
+
 def per_device(
     surface_fields, source_blocks, source_columns, remap_weights, ocean_state, bathymetry
 ):
@@ -456,18 +467,21 @@
     pieces = len(chunks_of(levels))
     cells = rows * lanes
 
-    payload = shaped((2 * many + EXTRA + tall, lanes), bf16)
-    request, place, to_left, to_right, table = pl.pallas_call(
+    payload = pltpu.VMEM((2 * many + EXTRA, lanes), bf16)
+    edge_weights = pltpu.VMEM((tall, lanes), bf16)
+    request, place, to_left, to_right, to_left_weights, to_right_weights, table = pl.pallas_call(
         prepare_kernel,
         out_shape=(
-            shaped((count, 128), i32),
-            shaped((slots * columns, 128), i32),
+            pltpu.VMEM((count, 128), i32),
+            pltpu.VMEM((slots * columns, 128), i32),
             payload,
             payload,
-            shaped((columns, 3 * lanes), bf16),
+            edge_weights,
+            edge_weights,
+            pltpu.VMEM((columns, 3 * lanes), bf16),
         ),
         in_specs=[smem] + [hbm] * 6,
-        out_specs=(vmem,) * 5,
+        out_specs=(vmem,) * 7,
         scratch_shapes=[
             pltpu.VMEM((tracers, levels, 8, lanes), f32),
             pltpu.VMEM((tracers, levels, 8, lanes), f32),
@@ -483,33 +497,43 @@
         cost_estimate=pl.CostEstimate(
             flops=10**6, bytes_accessed=4 * 10**6, transcendentals=0
         ),
-    )(section, ocean_state, bathymetry, fields, blocks, spots, weights)
+    )(
+        section,
+        in_hbm(ocean_state),
+        in_hbm(bathymetry),
+        in_hbm(fields),
+        in_hbm(blocks),
+        in_hbm(spots),
+        in_hbm(weights),
+    )
     asked = lax.all_to_all(request, "blk", split_axis=0, concat_axis=0, tiled=True)
     from_left = shift(to_right, "blk", 1)
     from_right = shift(to_left, "blk", -1)
+    left_weights = shift_first_section(to_right_weights, 1)
+    right_weights = shift_first_section(to_left_weights, -1)
     partner_fields = lax.ppermute(fields, "sec", [(0, 1), (1, 0)])
 
     served = pl.pallas_call(
         serve_kernel,
-        out_shape=shaped((count * SLOTS, 3 * lanes), bf16),
+        out_shape=pltpu.VMEM((count * SLOTS, 3 * lanes), bf16),
         in_specs=[vmem, vmem],
         out_specs=vmem,
         compiler_params=pltpu.CompilerParams(vmem_limit_bytes=8 * MIB),
         cost_estimate=pl.CostEstimate(
             flops=10**7, bytes_accessed=10**6, transcendentals=0
         ),
-    )(asked, table)
+    )(in_vmem(asked), in_vmem(table))
     columns_in = lax.all_to_all(served, "blk", split_axis=0, concat_axis=0, tiled=True)
 
     q, rho, side, start, bath, near_weights = pl.pallas_call(
         start_kernel,
         out_shape=(
-            shaped((tracers, levels, rows, lanes), f32),
-            shaped((levels, rows, lanes), f32),
-            shaped((levels, columns, lanes), f32),
-            shaped(ocean_state.shape, f32),
-            shaped((rows, lanes), i32),
-            shaped(weights.shape, bf16),
+            pltpu.VMEM((tracers, levels, rows, lanes), f32),
+            pltpu.VMEM((levels, rows, lanes), f32),
+            pltpu.VMEM((levels, columns, lanes), f32),
+            pltpu.VMEM(ocean_state.shape, f32),
+            pltpu.VMEM((rows, lanes), i32),
+            pltpu.VMEM(weights.shape, bf16),
         ),
         in_specs=[hbm, vmem, vmem, hbm, hbm, vmem],
         out_specs=(vmem,) * 6,
@@ -521,14 +545,21 @@
         ],
         compiler_params=pltpu.CompilerParams(vmem_limit_bytes=8 * MIB),
         cost_estimate=pl.CostEstimate(
-            flops=60 * levels * cells, bytes_accessed=20 * levels * cells, transcendentals=0
-        ),
-    )(ocean_state, from_left, from_right, bathymetry, weights, ratios_by_height(levels, lanes))
+            flops=60 * levels * cells, bytes_accessed=200 * levels * cells, transcendentals=0
+        ),
+    )(
+        in_hbm(ocean_state),
+        in_vmem(from_left),
+        in_vmem(from_right),
+        in_hbm(bathymetry),
+        in_hbm(weights),
+        ratios_by_height(levels, lanes),
+    )
 
     mine = pl.pallas_call(
         remap_kernel,
-        out_shape=shaped((3, rows, lanes), f32),
-        in_specs=[smem] + [vmem] * 5,
+        out_shape=pltpu.VMEM((3, rows, lanes), f32),
+        in_specs=[smem] + [vmem] * 7,
         out_specs=vmem,
         scratch_shapes=[
             pltpu.VMEM((slots, rows * 8, lanes), f32),
@@ -538,7 +569,16 @@
         cost_estimate=pl.CostEstimate(
             flops=16 * weights.size, bytes_accessed=2 * weights.size, transcendentals=0
         ),
-    )(section, columns_in, place, from_left, from_right, near_weights)
+    )(
+        section,
+        in_vmem(columns_in),
+        in_vmem(place),
+        in_vmem(from_left),
+        in_vmem(from_right),
+        in_vmem(left_weights),
+        in_vmem(right_weights),
+        in_vmem(near_weights),
+    )
     other = lax.ppermute(mine, "sec", [(0, 1), (1, 0)])
 
     surface, result = pl.pallas_call(
@@ -555,7 +595,18 @@
         cost_estimate=pl.CostEstimate(
             flops=60 * levels * cells, bytes_accessed=32 * levels * cells, transcendentals=0
         ),
-    )(section, mine, other, fields, partner_fields, bath, q, rho, side, start)
+    )(
+        section,
+        in_vmem(mine),
+        in_vmem(other),
+        fields,
+        partner_fields,
+        in_vmem(bath),
+        in_vmem(q),
+        in_vmem(rho),
+        in_vmem(side),
+        in_vmem(start),
+    )
     return (surface[None], result)
 
 

time: 91.2 us -> 80.8 us (0.89)
  local copies, waits for them, and re-layouts: 34 us -> 20.2 us
  starting transfers between devices: 9.72 us -> 19.2 us
  waiting for transfers between devices: 9.33 us -> 3.35 us
    unnamed x50 -> x32, local copies, waits for them, and re-layouts: 34 us -> 20.2 us
    ppermute x0 -> x2, starting transfers between devices: none -> 9.44 us  [shift_first_section(): lax.ppermute(value, ('sec', 'blk'), [(i, (i + by) % count) for i in range...]
    ppermute x2, waiting for transfers between devices: 8.45 us -> 2.46 us  [shift(): lax.ppermute(value, axis, [(i, (i + by) % count) for i in range(count)])]
  transfers between devices with their start and end apart: 5 -> 7, of which waited for: 2 -> 2; matrix products, arithmetic and copies ran while one was open for 0% -> 0% of each run, Pallas kernels for 9% -> 9%
where the time goes in v4:
time: 80.8 us; the launch traced here: 80.4 us
  Pallas kernels  21.5 us (27%)
  local copies, waits for them, and re-layouts  20.2 us (25%)
  starting transfers between devices  19.2 us (24%)
  blocking collectives  15.4 us (19%)
  waiting for transfers between devices  3.35 us (4%)
    unnamed x32, local copies, waits for them, and re-layouts  20.2 us
    all_to_all x1, blocking collectives, per_device(): lax.all_to_all(request, 'blk', split_axis=0, concat_axis=0, tiled=True)  15.4 us
    ppermute x2, starting transfers between devices, shift_first_section(): lax.ppermute(value, ('sec', 'blk'), [(i, (i + by) % count) for i in range...  9.44 us
    pallas_call x1, Pallas kernels, per_device(): pl.pallas_call(finish_kernel, out_shape=(shaped((3, columns, lanes), f32)...  7.74 us
    pallas_call x1, Pallas kernels, per_device(): pl.pallas_call(start_kernel, out_shape=(pltpu.VMEM((tracers, levels, rows...  7.57 us
    ppermute x2, starting transfers between devices, shift(): lax.ppermute(value, axis, [(i, (i + by) % count) for i in range(count)])  5.67 us
    all_to_all x1, starting transfers between devices, per_device(): lax.all_to_all(served, 'blk', split_axis=0, concat_axis=0, tiled=True)  3.54 us
    pallas_call x1, Pallas kernels, per_device(): pl.pallas_call(remap_kernel, out_shape=pltpu.VMEM((3, rows, lanes), f32),...  2.71 us
  transfers between devices with their start and end apart: 7, of which 2 were waited for; matrix products, arithmetic and copies ran while one was open for 0% of the time, Pallas kernels for 9%

profile of v4, /device:TPU:0, one launch (start us, length us, event | category | flops | bytes accessed | tf_op | source)
XLA Modules:
  0.0 80.4 jit_solution(4235024636949632604)
XLA Ops:
  0.6 0.0 copy-start.15
  0.6 2.3 %shard_map.86 = (s32[16,128]{1,0:T(8,128)S(1)}, s32[256,128]{1,0:T(8,128)S(1)}, bf16[336,128]{1,0:T(8,128)(2,1)S(1)}, bf16[336,128]{1,0:T(8,128)(2,1)S(1)}, bf16...) custom-call(s32[1]{0:T(128)} %bitcast.section, f32[2,80,64,128]{3,2,1,0:T(8,128)} %state.3, ...), custom_call_target="tpu_custom_call" | custom-call | flops 1000000 | bytes 4000000 | tf_op jit(solution)/shard_map/pallas_call | solution.py:472
  2.9 0.6 copy-done.9
  3.6 15.4 %all_to_all.22 = s32[16,1,128]{2,1,0:T(1,128)S(1)} all-to-all(s32[16,1,128]{2,1,0:T(1,128)S(1)} %bitcast.21), channel_id=1, replica_groups=mesh['sec'=2,'blk'=16] {'blk'}, dimensions={0} | all-to-all | bytes 16384 | tf_op jit(solution)/shard_map/all_to_all | solution.py:509
  19.0 1.2 %shard_map.87 = bf16[384,384]{1,0:T(8,128)(2,1)} custom-call(s32[16,128]{1,0:T(8,128)S(1)} %bitcast.20, bf16[64,384]{1,0:T(8,128)(2,1)S(1)} %get-tuple-element.18.table), custom_call_target="tpu_custom_call" | custom-call | flops 10000000 | bytes 1000000 | tf_op jit(solution)/shard_map/pallas_call | solution.py:516
  20.2 3.5 %all-to-all-start.1 = ((bf16[16,24,384]{2,1,0:T(8,128)(2,1)}), bf16[16,24,384]{2,1,0:T(8,128)(2,1)S(1)}, u32[]{:S(2)}, u32[]{:S(2)}) async-start(bf16[16,24,384]{2,1,0:T(8,128)(2,1)} %bitcast.10), calls=%async_computation.1 | async-start | bytes 589824 | tf_op jit(solution)/shard_map/all_to_all | solution.py:526
  23.7 3.7 %collective-permute-start.2 = (bf16[512,128]{1,0:T(8,128)(2,1)}, bf16[512,128]{1,0:T(8,128)(2,1)S(1)}, u32[]{:S(2)}, u32[]{:S(2)}) collective-permute-start(bf16[512,128]{1,0:T(8,128)(2,1)} %get-tuple-element.22), channel_id=1, source_target_pairs={{0,1},{1,2},{2,3},{3,4},{4,5},{5,6},{6,7},{7,8},{8,9},{9,10},{10,1... | collective-permute-start | bytes 393224 | tf_op jit(solution)/shard_map/ppermute | solution.py:437
  27.4 5.7 %collective-permute-start.3 = (bf16[512,128]{1,0:T(8,128)(2,1)}, bf16[512,128]{1,0:T(8,128)(2,1)S(1)}, u32[]{:S(2)}, u32[]{:S(2)}) collective-permute-start(bf16[512,128]{1,0:T(8,128)(2,1)} %get-tuple-element.23), channel_id=1, source_target_pairs={{0,15},{1,0},{2,1},{3,2},{4,3},{5,4},{6,5},{7,6},{8,7},{9,8},{10,9... | collective-permute-start | bytes 393224 | tf_op jit(solution)/shard_map/ppermute | solution.py:437
  33.1 0.1 collective-permute-start
  33.2 5.6 %collective-permute-start.1 = (bf16[336,128]{1,0:T(8,128)(2,1)S(1)}, bf16[336,128]{1,0:T(8,128)(2,1)S(1)}, u32[]{:S(2)}, u32[]{:S(2)}) collective-permute-start(bf16[336,128]{1,0:T(8,128)(2,1)S(1)} %get-tuple-element.21), channel_id=1, source_target_pairs={{0,15},{1,0},{2,1},{3,2},{4,3},{5,4},{6,5},{7,6},{8,7},{9,8},{10,9... | collective-permute-start | bytes 258056 | tf_op jit(solution)/shard_map/ppermute | solution.py:432
  38.8 2.5 %collective-permute-done.from_left = bf16[336,128]{1,0:T(8,128)(2,1)S(1)} collective-permute-done((bf16[336,128]{1,0:T(8,128)(2,1)S(1)}, bf16[336,128]{1,0:T(8,128)(2,1)S(1)}, u32[]{:S(2)}, u32[]{:S(2)}) %collective-permute-start) | collective-permute-done | bytes 86048 | tf_op jit(solution)/shard_map/ppermute | solution.py:432
  41.3 0.0 collective-permute-done.1.from_right
  41.3 0.0 copy-start.8
  41.3 7.6 %shard_map.88 = (f32[2,80,72,128]{3,2,1,0:T(8,128)S(1)}, f32[80,72,128]{2,1,0:T(8,128)S(1)}, f32[80,64,128]{2,1,0:T(8,128)S(1)}, f32[2,80,64,128]{3,2,1,0:T(8,12...) custom-call(f32[2,80,64,128]{3,2,1,0:T(8,128)} %state.3, ...), custom_call_target="tpu_custom_call" | custom-call | flops 44236800 | bytes 147456000 | tf_op jit(solution)/shard_map/pallas_call | solution.py:528
  48.9 3.3 %copy-done = bf16[32768,128]{1,0:T(8,128)(2,1)} copy-done((bf16[32768,128]{1,0:T(8,128)(2,1)}, bf16[32768,128]{1,0:T(8,128)(2,1)S(1)}, u32[]{:S(2)}) %copy-start) | copy-done | bytes 8388632
  52.2 2.6 %copy-done.2 = f32[2,80,72,128]{3,2,1,0:T(8,128)} copy-done((f32[2,80,72,128]{3,2,1,0:T(8,128)}, f32[2,80,72,128]{3,2,1,0:T(8,128)S(1)}, u32[]{:S(2)}) %copy-start.2) | copy-done | bytes 5898264
  54.7 2.4 %copy-done.4 = f32[2,80,64,128]{3,2,1,0:T(8,128)} copy-done((f32[2,80,64,128]{3,2,1,0:T(8,128)}, f32[2,80,64,128]{3,2,1,0:T(8,128)S(1)}, u32[]{:S(2)}) %copy-start.4) | copy-done | bytes 5242904
  57.1 1.5 %copy-done.6 = f32[80,64,128]{2,1,0:T(8,128)} copy-done((f32[80,64,128]{2,1,0:T(8,128)}, f32[80,64,128]{2,1,0:T(8,128)S(1)}, u32[]{:S(2)}) %copy-start.6) | copy-done | bytes 2621464
  58.6 0.0 collective-permute-done.2.left_weights
  58.6 0.7 copy-done.11
  59.2 0.0 collective-permute-done.3.right_weights
  59.2 0.7 copy-done.13
  59.9 3.4 %copy-done.1 = bf16[32768,128]{1,0:T(8,128)(2,1)S(1)} copy-done((bf16[32768,128]{1,0:T(8,128)(2,1)S(1)}, bf16[32768,128]{1,0:T(8,128)(2,1)}, u32[]{:S(2)}) %copy-start.1) | copy-done | bytes 8388632
  63.3 0.9 %copy-done.10 = s32[256,128]{1,0:T(8,128)S(1)} copy-done((s32[256,128]{1,0:T(8,128)S(1)}, s32[256,128]{1,0:T(8,128)}, u32[]{:S(2)}) %copy-start.10) | copy-done | bytes 131096
  64.2 0.9 %copy-done.12 = bf16[512,128]{1,0:T(8,128)(2,1)S(1)} copy-done((bf16[512,128]{1,0:T(8,128)(2,1)S(1)}, bf16[512,128]{1,0:T(8,128)(2,1)}, u32[]{:S(2)}) %copy-start.12) | copy-done | bytes 131096
  65.1 0.9 %copy-done.14 = bf16[512,128]{1,0:T(8,128)(2,1)S(1)} copy-done((bf16[512,128]{1,0:T(8,128)(2,1)S(1)}, bf16[512,128]{1,0:T(8,128)(2,1)}, u32[]{:S(2)}) %copy-start.14) | copy-done | bytes 131096
  66.0 2.7 %shard_map.89.mine = f32[3,72,128]{2,1,0:T(8,128)S(1)} custom-call(s32[1]{0:T(128)} %bitcast.section, bf16[384,384]{1,0:T(8,128)(2,1)S(1)} %bitcast.16, s32[256,128]{1,0:T(8,128)S(1)} %copy-done.10, bf16[336,128]{1,0:T(8,128)(2,1)S(1)} %collective-permute-done.from_left, bf16[336,128]{1,0:T(8,128)(2,1)S(1)} %collective-permute-done.1.from_right, ...), custom_call_target="tpu_custom_call" | custom-call | flops 67108864 | bytes 8388608 | tf_op jit(solution)/shard_map/pallas_call | solution.py:559
  68.7 0.0 copy-done.8
  68.7 0.5 collective-permute-start.5
  69.2 0.9 %collective-permute-done.5.partner_fields = bf16[3,64,128]{2,1,0:T(8,128)(2,1)S(1)} collective-permute-done((bf16[3,64,128]{2,1,0:T(8,128)(2,1)S(1)}, bf16[3,64,128]{2,1,0:T(8,128)(2,1)S(1)}, u32[]{:S(2)}, u32[]{:S(2)}) %collective-permute-start.5) | collective-permute-done | bytes 49184 | tf_op jit(solution)/shard_map/ppermute | solution.py:514
  70.1 2.5 %copy-done.5 = f32[2,80,64,128]{3,2,1,0:T(8,128)S(1)} copy-done((f32[2,80,64,128]{3,2,1,0:T(8,128)S(1)}, f32[2,80,64,128]{3,2,1,0:T(8,128)}, u32[]{:S(2)}) %copy-start.5) | copy-done | bytes 5242904
  72.6 7.7 %shard_map.90 = (f32[3,64,128]{2,1,0:T(8,128)}, f32[2,80,64,128]{3,2,1,0:T(8,128)}) custom-call(s32[1]{0:T(128)} %bitcast.section, f32[3,72,128]{2,1,0:T(8,128)S(1)} %shard_map.89.mine, f32[3,72,128]{2,1,0:T(8,128)S(1)} %collective-permute-done.4.other, bf16[3,64,128]{2,1,0:T(8,128)(2,1)S(1)} %bitcast.19, ...), custom_call_target="tpu_custom_call" | custom-call | flops 44236800 | bytes 23592960 | tf_op jit(solution)/shard_map/pallas_call | solution.py:584
  (21 shorter events, 0.0 us)
Async XLA Ops:
  0.6 40.7 %copy-start.15 = (f32[128]{0:T(128)S(1)}, f32[128]{0:T(128)}, u32[]{:S(2)}) copy-start(f32[128]{0:T(128)} %constant.8.clone) | copy-start | bytes 1540
  2.9 0.7 copy-start.9
  20.2 39.7 %all-to-all-start.1 = ((bf16[16,24,384]{2,1,0:T(8,128)(2,1)}), bf16[16,24,384]{2,1,0:T(8,128)(2,1)S(1)}, u32[]{:S(2)}, u32[]{:S(2)}) async-start(bf16[16,24,384]{2,1,0:T(8,128)(2,1)} %bitcast.10), calls=%async_computation.1 | async-start | bytes 589824 | tf_op jit(solution)/shard_map/all_to_all | solution.py:526
  23.7 34.9 %collective-permute-start.2 = (bf16[512,128]{1,0:T(8,128)(2,1)}, bf16[512,128]{1,0:T(8,128)(2,1)S(1)}, u32[]{:S(2)}, u32[]{:S(2)}) collective-permute-start(bf16[512,128]{1,0:T(8,128)(2,1)} %get-tuple-element.22), channel_id=1, source_target_pairs={{0,1},{1,2},{2,3},{3,4},{4,5},{5,6},{6,7},{7,8},{8,9},{9,10},{10,1... | collective-permute-start | bytes 393224 | tf_op jit(solution)/shard_map/ppermute | solution.py:437
  27.4 31.8 %collective-permute-start.3 = (bf16[512,128]{1,0:T(8,128)(2,1)}, bf16[512,128]{1,0:T(8,128)(2,1)S(1)}, u32[]{:S(2)}, u32[]{:S(2)}) collective-permute-start(bf16[512,128]{1,0:T(8,128)(2,1)} %get-tuple-element.23), channel_id=1, source_target_pairs={{0,15},{1,0},{2,1},{3,2},{4,3},{5,4},{6,5},{7,6},{8,7},{9,8},{10,9... | collective-permute-start | bytes 393224 | tf_op jit(solution)/shard_map/ppermute | solution.py:437
  33.1 8.1 %collective-permute-start = (bf16[336,128]{1,0:T(8,128)(2,1)S(1)}, bf16[336,128]{1,0:T(8,128)(2,1)S(1)}, u32[]{:S(2)}, u32[]{:S(2)}) collective-permute-start(bf16[336,128]{1,0:T(8,128)(2,1)S(1)} %get-tuple-element.20), channel_id=1, source_target_pairs={{0,1},{1,2},{2,3},{3,4},{4,5},{5,6},{6,7},{7,8},{8,9},{9,10},{10,1... | collective-permute-start | bytes 258056 | tf_op jit(solution)/shard_map/ppermute | solution.py:432
  33.2 8.1 %collective-permute-start.1 = (bf16[336,128]{1,0:T(8,128)(2,1)S(1)}, bf16[336,128]{1,0:T(8,128)(2,1)S(1)}, u32[]{:S(2)}, u32[]{:S(2)}) collective-permute-start(bf16[336,128]{1,0:T(8,128)(2,1)S(1)} %get-tuple-element.21), channel_id=1, source_target_pairs={{0,15},{1,0},{2,1},{3,2},{4,3},{5,4},{6,5},{7,6},{8,7},{9,8},{10,9... | collective-permute-start | bytes 258056 | tf_op jit(solution)/shard_map/ppermute | solution.py:432
  41.3 27.4 %copy-start.8 = (bf16[1,3,64,128]{3,2,1,0:T(8,128)(2,1)S(1)}, bf16[1,3,64,128]{3,2,1,0:T(8,128)(2,1)}, u32[]{:S(2)}) copy-start(bf16[1,3,64,128]{3,2,1,0:T(8,128)(2,1)} %param.7) | copy-start | bytes 147460
  48.9 3.3 %copy-start = (bf16[32768,128]{1,0:T(8,128)(2,1)}, bf16[32768,128]{1,0:T(8,128)(2,1)S(1)}, u32[]{:S(2)}) copy-start(bf16[32768,128]{1,0:T(8,128)(2,1)S(1)} %get-tuple-element.24.weights) | copy-start | bytes 25165828
  52.2 2.6 %copy-start.2 = (f32[2,80,72,128]{3,2,1,0:T(8,128)}, f32[2,80,72,128]{3,2,1,0:T(8,128)S(1)}, u32[]{:S(2)}) copy-start(f32[2,80,72,128]{3,2,1,0:T(8,128)S(1)} %get-tuple-element.26.q) | copy-start | bytes 17694724
  54.7 2.4 %copy-start.4 = (f32[2,80,64,128]{3,2,1,0:T(8,128)}, f32[2,80,64,128]{3,2,1,0:T(8,128)S(1)}, u32[]{:S(2)}) copy-start(f32[2,80,64,128]{3,2,1,0:T(8,128)S(1)} %get-tuple-element.29.start) | copy-start | bytes 15728644
  57.1 1.5 %copy-start.6 = (f32[80,64,128]{2,1,0:T(8,128)}, f32[80,64,128]{2,1,0:T(8,128)S(1)}, u32[]{:S(2)}) copy-start(f32[80,64,128]{2,1,0:T(8,128)S(1)} %get-tuple-element.28.side) | copy-start | bytes 7864324
  58.6 0.7 copy-start.11
  59.2 0.7 copy-start.13
  59.9 3.4 %copy-start.1 = (bf16[32768,128]{1,0:T(8,128)(2,1)S(1)}, bf16[32768,128]{1,0:T(8,128)(2,1)}, u32[]{:S(2)}) copy-start(bf16[32768,128]{1,0:T(8,128)(2,1)} %copy-done) | copy-start | bytes 25165828
  63.3 0.9 %copy-start.10 = (s32[256,128]{1,0:T(8,128)S(1)}, s32[256,128]{1,0:T(8,128)}, u32[]{:S(2)}) copy-start(s32[256,128]{1,0:T(8,128)} %copy-done.9) | copy-start | bytes 393220
  64.2 0.9 %copy-start.12 = (bf16[512,128]{1,0:T(8,128)(2,1)S(1)}, bf16[512,128]{1,0:T(8,128)(2,1)}, u32[]{:S(2)}) copy-start(bf16[512,128]{1,0:T(8,128)(2,1)} %copy-done.11) | copy-start | bytes 393220
  65.1 0.9 %copy-start.14 = (bf16[512,128]{1,0:T(8,128)(2,1)S(1)}, bf16[512,128]{1,0:T(8,128)(2,1)}, u32[]{:S(2)}) copy-start(bf16[512,128]{1,0:T(8,128)(2,1)} %copy-done.13) | copy-start | bytes 393220
  66.0 4.1 %copy-start.3 = (f32[2,80,72,128]{3,2,1,0:T(8,128)S(1)}, f32[2,80,72,128]{3,2,1,0:T(8,128)}, u32[]{:S(2)}) copy-start(f32[2,80,72,128]{3,2,1,0:T(8,128)} %copy-done.2) | copy-start | bytes 17694724
  66.0 4.1 %copy-start.7 = (f32[80,64,128]{2,1,0:T(8,128)S(1)}, f32[80,64,128]{2,1,0:T(8,128)}, u32[]{:S(2)}) copy-start(f32[80,64,128]{2,1,0:T(8,128)} %copy-done.6) | copy-start | bytes 7864324
  68.7 1.4 %collective-permute-start.4 = (f32[3,72,128]{2,1,0:T(8,128)S(1)}, f32[3,72,128]{2,1,0:T(8,128)S(1)}, u32[]{:S(2)}, u32[]{:S(2)}) collective-permute-start(f32[3,72,128]{2,1,0:T(8,128)S(1)} %shard_map.89.mine), channel_id=1, source_target_pairs={{0,16},{16,0},{1,17},{17,1},{2,18},{18,2},{3,19},{19,3},{4,20},{20... | collective-permute-start | bytes 331784 | tf_op jit(solution)/shard_map/ppermute | solution.py:582
  68.7 1.4 %collective-permute-start.5 = (bf16[3,64,128]{2,1,0:T(8,128)(2,1)S(1)}, bf16[3,64,128]{2,1,0:T(8,128)(2,1)S(1)}, u32[]{:S(2)}, u32[]{:S(2)}) collective-permute-start(bf16[3,64,128]{2,1,0:T(8,128)(2,1)S(1)} %bitcast.18), channel_id=1, source_target_pairs={{0,16},{16,0},{1,17},{17,1},{2,18},{18,2},{3,19},{19,3},{4,20},{20... | collective-permute-start | bytes 147464 | tf_op jit(solution)/shard_map/ppermute | solution.py:514
  70.1 2.5 %copy-start.5 = (f32[2,80,64,128]{3,2,1,0:T(8,128)S(1)}, f32[2,80,64,128]{3,2,1,0:T(8,128)}, u32[]{:S(2)}) copy-start(f32[2,80,64,128]{3,2,1,0:T(8,128)} %copy-done.4) | copy-start | bytes 15728644

commit v5 on v4

--- a/solution.py
+++ b/solution.py
@@ -57,58 +57,69 @@
     return carry
 
 
-def prepare_kernel(
-    section, state, bath, fields, blocks, spots, weights,
-    request, place, to_left, to_right, left_weights, right_weights, table,
-    low, high, surface, bath_in, fields_in, blocks_in, spots_in, extra, sems,
+def ranks(blocks, count):
+    slots, columns = blocks.shape
+    before = jnp.where(iota((columns, columns), 0) < iota((columns, columns), 1), 1.0, 0.0)
+    before = before.astype(bf16)
+    used = jnp.zeros((count, 1), f32)
+    result = []
+    for k in range(slots):
+        owner = iota((count, columns), 0) == blocks[k : k + 1, :]
+        one_hot = jnp.where(owner, 1.0, 0.0)
+        earlier = used + jnp.dot(one_hot.astype(bf16), before, preferred_element_type=f32)
+        rank = jnp.sum(one_hot * earlier, axis=0, keepdims=True)
+        used = used + jnp.sum(one_hot, axis=1, keepdims=True)
+        result.append((owner, rank))
+    return result
+
+
+def ask_kernel(blocks, spots, request, blocks_in, spots_in, sems):
+    copies = [
+        pltpu.make_async_copy(blocks, blocks_in, sems.at[0]),
+        pltpu.make_async_copy(spots, spots_in, sems.at[1]),
+    ]
+    for copy in copies:
+        copy.start()
+    for copy in copies:
+        copy.wait()
+    count, columns = request.shape[0], blocks.shape[1]
+    slot = iota((128, columns), 0)
+    here = iota((128, columns), 1)
+    marks = ((slot == MOST) & (here == 0)) | ((slot == MOST + 1) & (here == columns - 1))
+    asked = jnp.zeros(request.shape, f32)
+    for k, (owner, rank) in enumerate(ranks(blocks_in, count)):
+        filled = jnp.where((slot == rank.astype(i32)) | marks, 1.0, 0.0).astype(bf16)
+        named = jnp.where(owner, spots_in[k : k + 1, :].astype(f32), 0.0).astype(bf16)
+        asked = asked + lax.dot_general(
+            named, filled, (((1,), (1,)), ((), ())), preferred_element_type=f32
+        )
+    request[...] = asked.astype(i32)
+
+
+def pack_kernel(
+    section, state, bath, fields, blocks, weights,
+    to_left, to_right, table, left_weights, right_weights,
+    low, high, surface, bath_in, fields_in, blocks_in, extra, sems,
 ):
     tracers, levels, columns, lanes = state.shape
+    slots = blocks.shape[0]
     many = tracers * levels
     wide = left_weights.shape[0]
     pairs = [
+        (state.at[:, :, pl.ds(0, 8)], low),
+        (state.at[:, :, pl.ds(columns - 8, 8)], high),
         (blocks, blocks_in),
-        (spots, spots_in),
         (bath, bath_in),
         (fields, fields_in),
         (state.at[:, 0], surface),
-        (state.at[:, :, pl.ds(0, 8)], low),
-        (state.at[:, :, pl.ds(columns - 8, 8)], high),
         (weights.at[pl.ds(0, wide)], left_weights),
         (weights.at[pl.ds((columns - 1) * wide, wide)], right_weights),
     ]
     copies = [pltpu.make_async_copy(src, dst, sems.at[n]) for n, (src, dst) in enumerate(pairs)]
     for copy in copies:
         copy.start()
-    copies[0].wait()
-    copies[1].wait()
-
-    count, slots = request.shape[0], blocks.shape[0]
-    before = jnp.where(iota((columns, columns), 0) < iota((columns, columns), 1), 1.0, 0.0)
-    before = before.astype(bf16)
-    slot = iota((128, columns), 0)
-    here = iota((128, columns), 1)
-    marks = ((slot == MOST) & (here == 0)) | ((slot == MOST + 1) & (here == columns - 1))
-    used = jnp.zeros((count, 1), f32)
-    asked = jnp.zeros(request.shape, f32)
-    for k in range(slots):
-        block = blocks_in[k : k + 1, :]
-        owner = iota((count, columns), 0) == block
-        one_hot = jnp.where(owner, 1.0, 0.0)
-        earlier = used + jnp.dot(one_hot.astype(bf16), before, preferred_element_type=f32)
-        rank = jnp.sum(one_hot * earlier, axis=0, keepdims=True)
-        used = used + jnp.sum(one_hot, axis=1, keepdims=True)
-        filled = jnp.where((slot == rank.astype(i32)) | marks, 1.0, 0.0).astype(bf16)
-        named = jnp.where(owner, spots_in[k : k + 1, :].astype(f32), 0.0).astype(bf16)
-        asked = asked + lax.dot_general(
-            named, filled, (((1,), (1,)), ((), ())), preferred_element_type=f32
-        )
-        arrives = block.astype(f32) * SLOTS + rank
-        spread = jnp.transpose(jnp.broadcast_to(arrives, (128, columns)))
-        place[k * columns : (k + 1) * columns, :] = spread.astype(i32)
-    request[...] = asked.astype(i32)
-
-    copies[2].wait()
-    copies[3].wait()
+    for copy in copies[2:6]:
+        copy.wait()
     for out, first, at in ((to_left, 0, 0), (to_right, columns - 2, columns - 1)):
         extra[...] = jnp.zeros_like(extra)
         extra[0:2] = bath_in[first : first + 2].astype(f32)
@@ -118,15 +129,14 @@
             blocks_in[:, at : at + 1].astype(f32), (slots, lanes)
         )
         out[pl.ds(2 * many, EXTRA)] = extra[...].astype(bf16)
-    copies[4].wait()
     on_ocean = section[0] == 1
     for f in range(3):
         own = fields_in[f]
         if f < 2:
             own = jnp.where(on_ocean, surface[f], own.astype(f32)).astype(bf16)
         table[:, f * lanes : (f + 1) * lanes] = own
-    copies[5].wait()
-    copies[6].wait()
+    copies[0].wait()
+    copies[1].wait()
     for c in range(2):
         for n in range(tracers):
             part = pl.ds(c * many + n * levels, levels)
@@ -134,11 +144,11 @@
             to_left[part] = tiles[pl.ds(c, levels, stride=8), :].astype(bf16)
             tiles = high.at[n].reshape(levels * 8, lanes)
             to_right[part] = tiles[pl.ds(6 + c, levels, stride=8), :].astype(bf16)
+    copies[6].wait()
     copies[7].wait()
-    copies[8].wait()
-
-
-def serve_kernel(asked, table, out):
+
+
+def serve_kernel(asked, table, from_left, from_right, out):
     count = asked.shape[0]
     wanted = jnp.transpose(asked[...].astype(f32))[:SLOTS]
     columns = table.shape[0]
@@ -157,8 +167,10 @@
 
 
 def start_kernel(
-    state, from_left, from_right, bath, weights, ratios,
-    q_out, rho_out, side_out, held, bath_out, weights_out, halo, near, bath_in, sems,
+    state, from_left, from_right, bath, blocks, ratios,
+    q_result, rho_result, side_result, bath_result, place_result,
+    q_out, rho_out, side_out, held, bath_out, halo, near, bath_in, blocks_in, place, sems, sems_out,
+    *, count,
 ):
     tracers, levels, columns, lanes = state.shape
     rows = columns + EDGE
@@ -172,11 +184,18 @@
             )
         )
     bath_copy = pltpu.make_async_copy(bath, bath_in, sems.at[len(chunks)])
-    weights_copy = pltpu.make_async_copy(weights, weights_out, sems.at[len(chunks) + 1])
+    blocks_copy = pltpu.make_async_copy(blocks, blocks_in, sems.at[len(chunks) + 1])
+    blocks_copy.start()
     bath_copy.start()
     for copy in reversed(copies):
         copy.start()
-    weights_copy.start()
+    leaving = []
+
+    def send(source, target, number):
+        copy = pltpu.make_async_copy(source, target, sems_out.at[number])
+        copy.start()
+        leaving.append(copy)
+
     for c in range(2):
         part = pl.ds(c * many, many)
         halo[pl.ds(c, many, stride=8), :] = from_right[part].astype(f32)
@@ -196,6 +215,13 @@
     bath_copy.wait()
     depth = jnp.concatenate([bath_in[...], edge.astype(i32)], axis=0)
     bath_out[...] = depth
+    send(bath_out, bath_result, 3 * len(chunks))
+    blocks_copy.wait()
+    for k, (_, rank) in enumerate(ranks(blocks_in, count)):
+        arrives = blocks_in[k : k + 1, :].astype(f32) * SLOTS + rank
+        spread = jnp.transpose(jnp.broadcast_to(arrives, (128, columns)))
+        place[k * columns : (k + 1) * columns, :] = spread.astype(i32)
+    send(place, place_result, 3 * len(chunks) + 1)
     lane = iota((rows, lanes), 1)
     a = pltpu.roll(depth, 1, 0)
     b = pltpu.roll(depth, rows - 1, 0)
@@ -245,12 +271,18 @@
         first = max(low, 2)
         top = low + size - 1
         carry = sweep(top - first + 1, functools.partial(deep, top=top), carry, 5)
-    for level in (1, 0):
-        halves = side(level)
-        rho_out[level] = jnp.zeros((rows, lanes), f32)
-        for n in range(tracers):
-            q_out[n, level] = halves[n]
-    weights_copy.wait()
+        if n == 0:
+            for level in (1, 0):
+                halves = side(level)
+                rho_out[level] = jnp.zeros((rows, lanes), f32)
+                for m in range(tracers):
+                    q_out[m, level] = halves[m]
+        part = pl.ds(low, size)
+        send(q_out.at[:, part], q_result.at[:, part], 3 * n)
+        send(rho_out.at[part], rho_result.at[part], 3 * n + 1)
+        send(side_out.at[part], side_result.at[part], 3 * n + 2)
+    for copy in leaving:
+        copy.wait()
 
 
 def ratios_by_height(levels, lanes):
@@ -264,18 +296,32 @@
 
 
 def remap_kernel(
-    section, columns_in, place, from_left, from_right, left_weights, right_weights, weights,
-    out, picked, solved,
+    section, columns_in, place_from, from_left, from_right, left_weights, right_weights, weights,
+    out, picked, solved, held, held_left, held_right, place, sems,
 ):
     fields, rows, width = out.shape
     columns = rows - EDGE
     slots = weights.shape[0] // (columns * width)
     many = from_left.shape[0] - EXTRA
+    tall = slots * width
+    group = 8
+    place_copy = pltpu.make_async_copy(place_from, place, sems.at[0])
+    edge_copies = [
+        pltpu.make_async_copy(left_weights, held_left, sems.at[1]),
+        pltpu.make_async_copy(right_weights, held_right, sems.at[2]),
+    ]
+    copies = []
+    for n in range(columns // group):
+        part = pl.ds(n * group * tall, group * tall)
+        copies.append(pltpu.make_async_copy(weights.at[part], held.at[part], sems.at[3 + n]))
+    for copy in [place_copy] + copies + edge_copies:
+        copy.start()
     right = from_right[pl.ds(many, EXTRA)].astype(f32)
     left = from_left[pl.ds(many, EXTRA)].astype(f32)
     spots = iota((rows, columns_in.shape[0]), 1)
     row = iota((EDGE, 1), 0)
     picked[...] = jnp.zeros_like(picked)
+    place_copy.wait()
     for k in range(slots):
         edge = jnp.where(
             row == 0,
@@ -297,10 +343,15 @@
         )
 
     solved[...] = jnp.zeros_like(solved)
-    one(columns, lambda k: right_weights[pl.ds(k * width, width)])
-    one(rows - 1, lambda k: left_weights[pl.ds(k * width, width)])
-    for spot in range(columns):
-        one(spot, lambda k: weights[pl.ds((spot * slots + k) * width, width)])
+    for n in range(columns // group):
+        copies[n].wait()
+        for m in range(group):
+            spot = n * group + m
+            one(spot, lambda k: held[pl.ds((spot * slots + k) * width, width)])
+    for copy in edge_copies:
+        copy.wait()
+    one(columns, lambda k: held_right[pl.ds(k * width, width)])
+    one(rows - 1, lambda k: held_left[pl.ds(k * width, width)])
     on_ocean = section[0] == 1
     for f in range(fields):
         out[f, pl.ds(0, columns)] = solved[pl.ds(f, columns, stride=8), :]
@@ -310,12 +361,34 @@
 
 
 def finish_kernel(
-    section, mine, other, fields, partner_fields, bath, q, rho, side, start, surface, result,
-    half, done, sems,
+    section, mine, other, fields, partner_fields, bath_from, q_from, rho_from, side_from, state,
+    surface, result,
+    q, rho, side, held, bath, sems, sems_out,
 ):
-    tracers, levels, columns, lanes = start.shape
+    tracers, levels, columns, lanes = state.shape
     rows = columns + EDGE
     chunks = chunks_of(levels)
+    bath_copy = pltpu.make_async_copy(bath_from, bath, sems.at[len(chunks), 0])
+    bath_copy.start()
+    arrivals, starts = [], []
+    for n, (low, size) in enumerate(chunks):
+        part = pl.ds(low, size)
+        arrivals.append(
+            (
+                pltpu.make_async_copy(q_from.at[:, part], q.at[:, part], sems.at[n, 0]),
+                pltpu.make_async_copy(rho_from.at[part], rho.at[part], sems.at[n, 1]),
+                pltpu.make_async_copy(side_from.at[part], side.at[part], sems.at[n, 2]),
+            )
+        )
+        starts.append(pltpu.make_async_copy(state.at[:, part], held.at[:, part], sems.at[n, 3]))
+    for group in arrivals:
+        for copy in group:
+            copy.start()
+    for copy in starts:
+        copy.start()
+    bath_copy.wait()
+    for copy in arrivals[0]:
+        copy.wait()
     on_ocean = section[0] == 1
     lane = iota((rows, lanes), 1)
     flux = [jnp.where(on_ocean, other[f], mine[f]) for f in range(3)]
@@ -353,14 +426,14 @@
     )
 
     def store_half(n, level, h):
-        half[n, level] = side[level] * h[:columns] + neighbour_sum(h, lane)[:columns]
+        q[n, level, pl.ds(0, columns)] = side[level] * h[:columns] + neighbour_sum(h, lane)[:columns]
 
     for n in range(tracers):
         for level in (0, 1):
             store_half(n, level, values[n][level])
 
-    def down(step, carry):
-        level = 2 + step
+    def down(step, carry, low):
+        level = low + step
         ratio = rho[level]
         out = []
         for n in range(tracers):
@@ -370,15 +443,20 @@
         return tuple(out)
 
     carry = tuple(values[n][1] for n in range(tracers))
-    sweep(levels - 2, down, carry, 6)
+    for n, (low, size) in enumerate(chunks):
+        if n > 0:
+            for copy in arrivals[n]:
+                copy.wait()
+        first = max(low, 2)
+        carry = sweep(low + size - first, functools.partial(down, low=first), carry, 5)
 
     def up(step, carry):
         level = levels - 1 - step
         ratio = rho[level, pl.ds(0, columns)]
         out = []
         for n in range(tracers):
-            value = ratio * (half[n, level] + carry[n])
-            half[n, level] = value
+            value = ratio * (q[n, level, pl.ds(0, columns)] + carry[n])
+            q[n, level, pl.ds(0, columns)] = value
             out.append(value)
         return tuple(out)
 
@@ -386,7 +464,7 @@
     carry = sweep(levels - 2, up, (zero,) * tracers, 13)
     values = top_levels(
         columns,
-        [(half[n, 0], half[n, 1]) for n in range(tracers)],
+        [(q[n, 0, pl.ds(0, columns)], q[n, 1, pl.ds(0, columns)]) for n in range(tracers)],
         carry,
         rho[2, pl.ds(0, columns)],
         SCALE * SCALE,
@@ -402,25 +480,26 @@
         wet = level < bath[pl.ds(0, columns)]
         out = []
         for n in range(tracers):
-            h = half[n, level] + ratio * carry[n]
-            done[n, level] = jnp.where(wet, h * unscale, start[n, level])
+            h = q[n, level, pl.ds(0, columns)] + ratio * carry[n]
+            held[n, level] = jnp.where(wet, h * unscale, held[n, level])
             out.append(h)
         return tuple(out)
 
     carry = tuple(values[n][1] for n in range(tracers))
     leaving = []
     for n, (low, size) in enumerate(chunks):
+        starts[n].wait()
         if n == 0:
             for m in range(tracers):
-                done[m, 0] = values[m][0] * unscale
-                done[m, 1] = jnp.where(
-                    1 < depth[:columns], values[m][1] * unscale, start[m, 1]
+                held[m, 0] = values[m][0] * unscale
+                held[m, 1] = jnp.where(
+                    1 < depth[:columns], values[m][1] * unscale, held[m, 1]
                 )
         first = max(low, 2)
         carry = sweep(low + size - first, functools.partial(last, low=first), carry, 10)
         part = pl.ds(low, size)
         leaving.append(
-            pltpu.make_async_copy(done.at[:, part], result.at[:, part], sems.at[n])
+            pltpu.make_async_copy(held.at[:, part], result.at[:, part], sems_out.at[n])
         )
         leaving[-1].start()
     for copy in leaving:
@@ -439,10 +518,6 @@
 
 def in_hbm(value):
     return pltpu.with_memory_space_constraint(value, pltpu.HBM)
-
-
-def in_vmem(value):
-    return pltpu.with_memory_space_constraint(value, pltpu.VMEM)
 
 
 def per_device(
@@ -461,27 +536,41 @@
     many = tracers * levels
 
     hbm = pl.BlockSpec(memory_space=pltpu.HBM)
+    anywhere = pl.BlockSpec(memory_space=pl.ANY)
     vmem = pl.BlockSpec(memory_space=pltpu.VMEM)
     smem = pl.BlockSpec(memory_space=pltpu.SMEM)
     shaped = jax.ShapeDtypeStruct
     pieces = len(chunks_of(levels))
     cells = rows * lanes
 
-    payload = pltpu.VMEM((2 * many + EXTRA, lanes), bf16)
-    edge_weights = pltpu.VMEM((tall, lanes), bf16)
-    request, place, to_left, to_right, to_left_weights, to_right_weights, table = pl.pallas_call(
-        prepare_kernel,
+    request = pl.pallas_call(
+        ask_kernel,
+        out_shape=shaped((count, 128), i32),
+        in_specs=[hbm, hbm],
+        out_specs=vmem,
+        scratch_shapes=[
+            pltpu.VMEM(blocks.shape, i32),
+            pltpu.VMEM(spots.shape, i32),
+            pltpu.SemaphoreType.DMA((2,)),
+        ],
+        compiler_params=pltpu.CompilerParams(vmem_limit_bytes=4 * MIB),
+        cost_estimate=pl.CostEstimate(flops=10**6, bytes_accessed=10**5, transcendentals=0),
+    )(in_hbm(blocks), in_hbm(spots))
+    asked = lax.all_to_all(request, "blk", split_axis=0, concat_axis=0, tiled=True)
+
+    payload = shaped((2 * many + EXTRA, lanes), bf16)
+    edge_weights = pltpu.HBM((tall, lanes), bf16)
+    to_left, to_right, table, to_left_weights, to_right_weights = pl.pallas_call(
+        pack_kernel,
         out_shape=(
-            pltpu.VMEM((count, 128), i32),
-            pltpu.VMEM((slots * columns, 128), i32),
             payload,
             payload,
+            shaped((columns, 3 * lanes), bf16),
             edge_weights,
             edge_weights,
-            pltpu.VMEM((columns, 3 * lanes), bf16),
-        ),
-        in_specs=[smem] + [hbm] * 6,
-        out_specs=(vmem,) * 7,
+        ),
+        in_specs=[smem] + [hbm] * 5,
+        out_specs=(vmem, vmem, vmem, hbm, hbm),
         scratch_shapes=[
             pltpu.VMEM((tracers, levels, 8, lanes), f32),
             pltpu.VMEM((tracers, levels, 8, lanes), f32),
@@ -489,9 +578,8 @@
             pltpu.VMEM(bathymetry.shape, i32),
             pltpu.VMEM(fields.shape, bf16),
             pltpu.VMEM(blocks.shape, i32),
-            pltpu.VMEM(spots.shape, i32),
             pltpu.VMEM((EXTRA, lanes), f32),
-            pltpu.SemaphoreType.DMA((9,)),
+            pltpu.SemaphoreType.DMA((8,)),
         ],
         compiler_params=pltpu.CompilerParams(vmem_limit_bytes=8 * MIB),
         cost_estimate=pl.CostEstimate(
@@ -503,10 +591,8 @@
         in_hbm(bathymetry),
         in_hbm(fields),
         in_hbm(blocks),
-        in_hbm(spots),
         in_hbm(weights),
     )
-    asked = lax.all_to_all(request, "blk", split_axis=0, concat_axis=0, tiled=True)
     from_left = shift(to_right, "blk", 1)
     from_right = shift(to_left, "blk", -1)
     left_weights = shift_first_section(to_right_weights, 1)
@@ -515,97 +601,113 @@
 
     served = pl.pallas_call(
         serve_kernel,
-        out_shape=pltpu.VMEM((count * SLOTS, 3 * lanes), bf16),
-        in_specs=[vmem, vmem],
+        out_shape=shaped((count * SLOTS, 3 * lanes), bf16),
+        in_specs=[vmem] * 4,
         out_specs=vmem,
         compiler_params=pltpu.CompilerParams(vmem_limit_bytes=8 * MIB),
         cost_estimate=pl.CostEstimate(
             flops=10**7, bytes_accessed=10**6, transcendentals=0
         ),
-    )(in_vmem(asked), in_vmem(table))
+    )(asked, table, from_left, from_right)
     columns_in = lax.all_to_all(served, "blk", split_axis=0, concat_axis=0, tiled=True)
 
-    q, rho, side, start, bath, near_weights = pl.pallas_call(
-        start_kernel,
+    q, rho, side, bath, place = pl.pallas_call(
+        functools.partial(start_kernel, count=count),
         out_shape=(
+            pltpu.HBM((tracers, levels, rows, lanes), f32),
+            pltpu.HBM((levels, rows, lanes), f32),
+            pltpu.HBM((levels, columns, lanes), f32),
+            pltpu.HBM((rows, lanes), i32),
+            pltpu.HBM((slots * columns, 128), i32),
+        ),
+        in_specs=[hbm, vmem, vmem, hbm, hbm, vmem],
+        out_specs=(hbm,) * 5,
+        scratch_shapes=[
             pltpu.VMEM((tracers, levels, rows, lanes), f32),
             pltpu.VMEM((levels, rows, lanes), f32),
             pltpu.VMEM((levels, columns, lanes), f32),
             pltpu.VMEM(ocean_state.shape, f32),
             pltpu.VMEM((rows, lanes), i32),
-            pltpu.VMEM(weights.shape, bf16),
-        ),
-        in_specs=[hbm, vmem, vmem, hbm, hbm, vmem],
-        out_specs=(vmem,) * 6,
-        scratch_shapes=[
             pltpu.VMEM((many * 8, lanes), f32),
             pltpu.VMEM((4, rows, lanes), i32),
             pltpu.VMEM(bathymetry.shape, i32),
+            pltpu.VMEM(blocks.shape, i32),
+            pltpu.VMEM((slots * columns, 128), i32),
             pltpu.SemaphoreType.DMA((pieces + 2,)),
+            pltpu.SemaphoreType.DMA((3 * pieces + 2,)),
         ],
-        compiler_params=pltpu.CompilerParams(vmem_limit_bytes=8 * MIB),
+        compiler_params=pltpu.CompilerParams(vmem_limit_bytes=28 * MIB),
         cost_estimate=pl.CostEstimate(
             flops=60 * levels * cells, bytes_accessed=200 * levels * cells, transcendentals=0
         ),
     )(
         in_hbm(ocean_state),
-        in_vmem(from_left),
-        in_vmem(from_right),
+        from_left,
+        from_right,
         in_hbm(bathymetry),
-        in_hbm(weights),
+        in_hbm(blocks),
         ratios_by_height(levels, lanes),
     )
 
     mine = pl.pallas_call(
         remap_kernel,
-        out_shape=pltpu.VMEM((3, rows, lanes), f32),
-        in_specs=[smem] + [vmem] * 7,
+        out_shape=shaped((3, rows, lanes), f32),
+        in_specs=[smem, vmem, hbm, vmem, vmem, anywhere, anywhere, hbm],
         out_specs=vmem,
         scratch_shapes=[
             pltpu.VMEM((slots, rows * 8, lanes), f32),
             pltpu.VMEM((rows * 8, lanes), f32),
+            pltpu.VMEM(weights.shape, bf16),
+            pltpu.VMEM((tall, lanes), bf16),
+            pltpu.VMEM((tall, lanes), bf16),
+            pltpu.VMEM((slots * columns, 128), i32),
+            pltpu.SemaphoreType.DMA((3 + columns // 8,)),
         ],
-        compiler_params=pltpu.CompilerParams(vmem_limit_bytes=8 * MIB),
+        compiler_params=pltpu.CompilerParams(vmem_limit_bytes=20 * MIB),
         cost_estimate=pl.CostEstimate(
             flops=16 * weights.size, bytes_accessed=2 * weights.size, transcendentals=0
         ),
     )(
         section,
-        in_vmem(columns_in),
-        in_vmem(place),
-        in_vmem(from_left),
-        in_vmem(from_right),
-        in_vmem(left_weights),
-        in_vmem(right_weights),
-        in_vmem(near_weights),
+        columns_in,
+        in_hbm(place),
+        from_left,
+        from_right,
+        left_weights,
+        right_weights,
+        in_hbm(weights),
     )
     other = lax.ppermute(mine, "sec", [(0, 1), (1, 0)])
 
     surface, result = pl.pallas_call(
         finish_kernel,
         out_shape=(shaped((3, columns, lanes), f32), shaped(ocean_state.shape, f32)),
-        in_specs=[smem] + [vmem] * 9,
+        in_specs=[smem] + [vmem] * 4 + [hbm] * 5,
         out_specs=(vmem, hbm),
         scratch_shapes=[
+            pltpu.VMEM((tracers, levels, rows, lanes), f32),
+            pltpu.VMEM((levels, rows, lanes), f32),
+            pltpu.VMEM((levels, columns, lanes), f32),
             pltpu.VMEM(ocean_state.shape, f32),
-            pltpu.VMEM(ocean_state.shape, f32),
+            pltpu.VMEM((rows, lanes), i32),
+            pltpu.SemaphoreType.DMA((pieces + 1, 4)),
             pltpu.SemaphoreType.DMA((pieces,)),
         ],
-        compiler_params=pltpu.CompilerParams(vmem_limit_bytes=16 * MIB),
+        compiler_params=pltpu.CompilerParams(vmem_limit_bytes=28 * MIB),
         cost_estimate=pl.CostEstimate(
             flops=60 * levels * cells, bytes_accessed=32 * levels * cells, transcendentals=0
         ),
     )(
         section,
-        in_vmem(mine),
-        in_vmem(other),
+        mine,
+        other,
         fields,
         partner_fields,
-        in_vmem(bath),
-        in_vmem(q),
-        in_vmem(rho),
-        in_vmem(side),
-        in_vmem(start),
+        in_hbm(bath),
+        in_hbm(q),
+        in_hbm(rho),
+        in_hbm(side),
+        in_hbm(ocean_state),
     )
     return (surface[None], result)
 

time: 80.8 us -> 67.4 us (0.83)
  local copies, waits for them, and re-layouts: 20.2 us -> 0.02 us
  Pallas kernels: 21.5 us -> 34.3 us
  blocking collectives: 15.4 us -> 10.4 us
  waiting for transfers between devices: 3.35 us -> 0.9 us
  starting transfers between devices: 19.2 us -> 20.6 us
    unnamed x32 -> x4, local copies, waits for them, and re-layouts: 20.2 us -> 0.01 us
    pallas_call x4 -> x5, Pallas kernels: 13.7 us -> 24.9 us  [the longest x1 9.13 us: per_device(): pl.pallas_call(pack_kernel, out_shape=(payload, payload, shaped((columns,...]
    all_to_all x1, blocking collectives: 15.4 us -> 10.4 us  [per_device(): lax.all_to_all(request, 'blk', split_axis=0, concat_axis=0, tiled=True)]
    ppermute x2, waiting for transfers between devices: 2.46 us -> 0.01 us  [shift(): lax.ppermute(value, axis, [(i, (i + by) % count) for i in range(count)])]
    pallas_call x1, Pallas kernels: 7.74 us -> 9.42 us  [per_device(): pl.pallas_call(finish_kernel, out_shape=(shaped((3, columns, lanes), f32)...]
    ppermute x2, starting transfers between devices: 5.67 us -> 7.05 us  [shift(): lax.ppermute(value, axis, [(i, (i + by) % count) for i in range(count)])]
  transfers between devices with their start and end apart: 7 -> 7, of which waited for: 2 -> 1; matrix products, arithmetic and copies ran while one was open for 0% -> 0% of each run, Pallas kernels for 9% -> 15%
where the time goes in v5:
time: 67.4 us; the launch traced here: 67 us
  Pallas kernels  34.3 us (51%)
  starting transfers between devices  20.6 us (31%)
  blocking collectives  10.4 us (15%)
  waiting for transfers between devices  0.9 us (1%)
  between operations  0.76 us (1%)
    all_to_all x1, blocking collectives, per_device(): lax.all_to_all(request, 'blk', split_axis=0, concat_axis=0, tiled=True)  10.4 us
    ppermute x2, starting transfers between devices, shift_first_section(): lax.ppermute(value, ('sec', 'blk'), [(i, (i + by) % count) for i in range...  9.44 us
    pallas_call x1, Pallas kernels, per_device(): pl.pallas_call(finish_kernel, out_shape=(shaped((3, columns, lanes), f32)...  9.42 us
    pallas_call x1, Pallas kernels, per_device(): pl.pallas_call(pack_kernel, out_shape=(payload, payload, shaped((columns,...  9.13 us
    pallas_call x1, Pallas kernels, per_device(): pl.pallas_call(functools.partial(start_kernel, count=count), out_shape=(p...  8.83 us
    ppermute x2, starting transfers between devices, shift(): lax.ppermute(value, axis, [(i, (i + by) % count) for i in range(count)])  7.05 us
    pallas_call x1, Pallas kernels, per_device(): pl.pallas_call(remap_kernel, out_shape=shaped((3, rows, lanes), f32), in_...  4.72 us
    all_to_all x1, starting transfers between devices, per_device(): lax.all_to_all(served, 'blk', split_axis=0, concat_axis=0, tiled=True)  3.54 us
  transfers between devices with their start and end apart: 7, of which 1 were waited for; matrix products, arithmetic and copies ran while one was open for 0% of the time, Pallas kernels for 15%

profile of v5, /device:TPU:0, one launch (start us, length us, event | category | flops | bytes accessed | tf_op | source)
XLA Modules:
  0.0 67.0 jit_solution(16171124071774729970)
XLA Ops:
  0.6 0.0 copy-start.1
  0.6 9.1 %shard_map.87 = (bf16[336,128]{1,0:T(8,128)(2,1)S(1)}, bf16[336,128]{1,0:T(8,128)(2,1)S(1)}, bf16[64,384]{1,0:T(8,128)(2,1)S(1)}, bf16[512,128]{1,0:T(8,128)(2,1)}, bf16[512,128]{1,0:T(8,128)(2,1)}) custom-call(s32[1]{0:T(128)} %bitcast.section, f32[2,80,64,128]{3,2,1,0:T(8,128)} %state.5, s32[64,128]{1,0:T(8,128)} %bath.3, bf16[3,64,128]{2,1,0:T(8,128)(2,1)} %bitcast.17, ...), custom_call_target="tpu_custom_call" | custom-call | flops 1000000 | bytes 4000000 | tf_op jit(solution)/shard_map/pallas_call | solution.py:563
  9.8 3.0 %collective-permute-start = (bf16[336,128]{1,0:T(8,128)(2,1)S(1)}, bf16[336,128]{1,0:T(8,128)(2,1)S(1)}, u32[]{:S(2)}, u32[]{:S(2)}) collective-permute-start(bf16[336,128]{1,0:T(8,128)(2,1)S(1)} %get-tuple-element.15), channel_id=1, source_target_pairs={{0,1},{1,2},{2,3},{3,4},{4,5},{5,6},{6,7},{7,8},{8,9},{9,10},{10,1... | collective-permute-start | bytes 258056 | tf_op jit(solution)/shard_map/ppermute | solution.py:511
  12.8 4.1 %collective-permute-start.1 = (bf16[336,128]{1,0:T(8,128)(2,1)S(1)}, bf16[336,128]{1,0:T(8,128)(2,1)S(1)}, u32[]{:S(2)}, u32[]{:S(2)}) collective-permute-start(bf16[336,128]{1,0:T(8,128)(2,1)S(1)} %get-tuple-element.16), channel_id=1, source_target_pairs={{0,15},{1,0},{2,1},{3,2},{4,3},{5,4},{6,5},{7,6},{8,7},{9,8},{10,9... | collective-permute-start | bytes 258056 | tf_op jit(solution)/shard_map/ppermute | solution.py:511
  16.8 1.0 %shard_map.86 = s32[16,128]{1,0:T(8,128)S(1)} custom-call(s32[4,64]{1,0:T(4,128)} %bitcast.25, s32[4,64]{1,0:T(4,128)} %bitcast.27), custom_call_target="tpu_custom_call" | custom-call | flops 1000000 | bytes 100000 | tf_op jit(solution)/shard_map/pallas_call | solution.py:546
  17.9 10.4 %all_to_all.22 = s32[16,1,128]{2,1,0:T(1,128)S(1)} all-to-all(s32[16,1,128]{2,1,0:T(1,128)S(1)} %bitcast.21), channel_id=1, replica_groups=mesh['sec'=2,'blk'=16] {'blk'}, dimensions={0} | all-to-all | bytes 16384 | tf_op jit(solution)/shard_map/all_to_all | solution.py:559
  28.3 0.0 collective-permute-done.from_left
  28.3 0.0 collective-permute-done.1.from_right
  28.3 1.2 %shard_map.88 = bf16[384,384]{1,0:T(8,128)(2,1)} custom-call(s32[16,128]{1,0:T(8,128)S(1)} %bitcast.20, bf16[64,384]{1,0:T(8,128)(2,1)S(1)} %get-tuple-element.14.table, bf16[336,128]{1,0:T(8,128)(2,1)S(1)} %collective-permute-done.from_left, bf16[336,128]{1,0:T(8,128)(2,1)S(1)} %collective-permute-done.1.from_right), custom_call_target="tpu_custom_call" | custom-call | flops 10000000 | bytes 1000000 | tf_op jit(solution)/shard_map/pallas_call | solution.py:602
  29.5 3.5 %all-to-all-start.1 = ((bf16[16,24,384]{2,1,0:T(8,128)(2,1)}), bf16[16,24,384]{2,1,0:T(8,128)(2,1)S(1)}, u32[]{:S(2)}, u32[]{:S(2)}) async-start(bf16[16,24,384]{2,1,0:T(8,128)(2,1)} %bitcast.11), calls=%async_computation.1 | async-start | bytes 589824 | tf_op jit(solution)/shard_map/all_to_all | solution.py:612
  33.1 3.7 %collective-permute-start.2 = (bf16[512,128]{1,0:T(8,128)(2,1)}, bf16[512,128]{1,0:T(8,128)(2,1)S(1)}, u32[]{:S(2)}, u32[]{:S(2)}) collective-permute-start(bf16[512,128]{1,0:T(8,128)(2,1)} %get-tuple-element.18), channel_id=1, source_target_pairs={{0,1},{1,2},{2,3},{3,4},{4,5},{5,6},{6,7},{7,8},{8,9},{9,10},{10,1... | collective-permute-start | bytes 393224 | tf_op jit(solution)/shard_map/ppermute | solution.py:516
  36.8 5.7 %collective-permute-start.3 = (bf16[512,128]{1,0:T(8,128)(2,1)}, bf16[512,128]{1,0:T(8,128)(2,1)S(1)}, u32[]{:S(2)}, u32[]{:S(2)}) collective-permute-start(bf16[512,128]{1,0:T(8,128)(2,1)} %get-tuple-element.19), channel_id=1, source_target_pairs={{0,15},{1,0},{2,1},{3,2},{4,3},{5,4},{6,5},{7,6},{8,7},{9,8},{10,9... | collective-permute-start | bytes 393224 | tf_op jit(solution)/shard_map/ppermute | solution.py:516
  42.5 0.0 copy-done.1
  42.5 8.8 %shard_map.89 = (f32[2,80,72,128]{3,2,1,0:T(8,128)}, f32[80,72,128]{2,1,0:T(8,128)}, f32[80,64,128]{2,1,0:T(8,128)}, s32[72,128]{1,0:T(8,128)}, s32[256,128]{1,0:T(8,128)}) custom-call(f32[2,80,64,128]{3,2,1,0:T(8,128)} %state.5, bf16[336,128]{1,0:T(8,128)(2,1)S(1)} %collective-permute-done.from_left, ...), custom_call_target="tpu_custom_call" | custom-call | flops 44236800 | bytes 147456000 | tf_op jit(solution)/shard_map/pallas_call | solution.py:614
  51.4 0.0 copy-start
  51.4 0.0 collective-permute-done.2.left_weights
  51.4 0.0 collective-permute-done.3.right_weights
  51.4 0.0 all-to-all-done.1
  51.4 4.7 %shard_map.90.mine = f32[3,72,128]{2,1,0:T(8,128)S(1)} custom-call(s32[1]{0:T(128)} %bitcast.section, bf16[384,384]{1,0:T(8,128)(2,1)S(1)} %bitcast.16, s32[256,128]{1,0:T(8,128)} %get-tuple-element.17.place_from, bf16[336,128]{1,0:T(8,128)(2,1)S(1)} %collective-permute-done.from_left, bf16[336,128]{1,0:T(8,128)(2,1)S(1)} %collective-permute-done.1.from_right, ...), custom_call_target="tpu_custom_call" | custom-call | flops 67108864 | bytes 8388608 | tf_op jit(solution)/shard_map/pallas_call | solution.py:652
  56.1 0.1 collective-permute-start.4
  56.2 0.0 copy-done
  56.2 0.5 collective-permute-start.5
  56.7 0.9 %collective-permute-done.5.partner_fields = bf16[3,64,128]{2,1,0:T(8,128)(2,1)S(1)} collective-permute-done((bf16[3,64,128]{2,1,0:T(8,128)(2,1)S(1)}, bf16[3,64,128]{2,1,0:T(8,128)(2,1)S(1)}, u32[]{:S(2)}, u32[]{:S(2)}) %collective-permute-start.5) | collective-permute-done | bytes 49184 | tf_op jit(solution)/shard_map/ppermute | solution.py:600
  57.6 0.0 collective-permute-done.4.other
  57.6 9.4 %shard_map.91 = (f32[3,64,128]{2,1,0:T(8,128)}, f32[2,80,64,128]{3,2,1,0:T(8,128)}) custom-call(s32[1]{0:T(128)} %bitcast.section, f32[3,72,128]{2,1,0:T(8,128)S(1)} %shard_map.90.mine, f32[3,72,128]{2,1,0:T(8,128)S(1)} %collective-permute-done.4.other, bf16[3,64,128]{2,1,0:T(8,128)(2,1)S(1)} %bitcast.19, ...), custom_call_target="tpu_custom_call" | custom-call | flops 44236800 | bytes 23592960 | tf_op jit(solution)/shard_map/pallas_call | solution.py:682
  (1 shorter events, 0.0 us)
Async XLA Ops:
  0.6 41.9 %copy-start.1 = (f32[128]{0:T(128)S(1)}, f32[128]{0:T(128)}, u32[]{:S(2)}) copy-start(f32[128]{0:T(128)} %constant.8.clone) | copy-start | bytes 1540
  9.8 18.5 %collective-permute-start = (bf16[336,128]{1,0:T(8,128)(2,1)S(1)}, bf16[336,128]{1,0:T(8,128)(2,1)S(1)}, u32[]{:S(2)}, u32[]{:S(2)}) collective-permute-start(bf16[336,128]{1,0:T(8,128)(2,1)S(1)} %get-tuple-element.15), channel_id=1, source_target_pairs={{0,1},{1,2},{2,3},{3,4},{4,5},{5,6},{6,7},{7,8},{8,9},{9,10},{10,1... | collective-permute-start | bytes 258056 | tf_op jit(solution)/shard_map/ppermute | solution.py:511
  12.8 15.5 %collective-permute-start.1 = (bf16[336,128]{1,0:T(8,128)(2,1)S(1)}, bf16[336,128]{1,0:T(8,128)(2,1)S(1)}, u32[]{:S(2)}, u32[]{:S(2)}) collective-permute-start(bf16[336,128]{1,0:T(8,128)(2,1)S(1)} %get-tuple-element.16), channel_id=1, source_target_pairs={{0,15},{1,0},{2,1},{3,2},{4,3},{5,4},{6,5},{7,6},{8,7},{9,8},{10,9... | collective-permute-start | bytes 258056 | tf_op jit(solution)/shard_map/ppermute | solution.py:511
  29.5 21.9 %all-to-all-start.1 = ((bf16[16,24,384]{2,1,0:T(8,128)(2,1)}), bf16[16,24,384]{2,1,0:T(8,128)(2,1)S(1)}, u32[]{:S(2)}, u32[]{:S(2)}) async-start(bf16[16,24,384]{2,1,0:T(8,128)(2,1)} %bitcast.11), calls=%async_computation.1 | async-start | bytes 589824 | tf_op jit(solution)/shard_map/all_to_all | solution.py:612
  33.1 18.3 %collective-permute-start.2 = (bf16[512,128]{1,0:T(8,128)(2,1)}, bf16[512,128]{1,0:T(8,128)(2,1)S(1)}, u32[]{:S(2)}, u32[]{:S(2)}) collective-permute-start(bf16[512,128]{1,0:T(8,128)(2,1)} %get-tuple-element.18), channel_id=1, source_target_pairs={{0,1},{1,2},{2,3},{3,4},{4,5},{5,6},{6,7},{7,8},{8,9},{9,10},{10,1... | collective-permute-start | bytes 393224 | tf_op jit(solution)/shard_map/ppermute | solution.py:516
  36.8 14.6 %collective-permute-start.3 = (bf16[512,128]{1,0:T(8,128)(2,1)}, bf16[512,128]{1,0:T(8,128)(2,1)S(1)}, u32[]{:S(2)}, u32[]{:S(2)}) collective-permute-start(bf16[512,128]{1,0:T(8,128)(2,1)} %get-tuple-element.19), channel_id=1, source_target_pairs={{0,15},{1,0},{2,1},{3,2},{4,3},{5,4},{6,5},{7,6},{8,7},{9,8},{10,9... | collective-permute-start | bytes 393224 | tf_op jit(solution)/shard_map/ppermute | solution.py:516
  51.4 4.9 %copy-start = (bf16[1,3,64,128]{3,2,1,0:T(8,128)(2,1)S(1)}, bf16[1,3,64,128]{3,2,1,0:T(8,128)(2,1)}, u32[]{:S(2)}) copy-start(bf16[1,3,64,128]{3,2,1,0:T(8,128)(2,1)} %param.7) | copy-start | bytes 147460
  56.1 1.5 %collective-permute-start.4 = (f32[3,72,128]{2,1,0:T(8,128)S(1)}, f32[3,72,128]{2,1,0:T(8,128)S(1)}, u32[]{:S(2)}, u32[]{:S(2)}) collective-permute-start(f32[3,72,128]{2,1,0:T(8,128)S(1)} %shard_map.90.mine), channel_id=1, source_target_pairs={{0,16},{16,0},{1,17},{17,1},{2,18},{18,2},{3,19},{19,3},{4,20},{20... | collective-permute-start | bytes 331784 | tf_op jit(solution)/shard_map/ppermute | solution.py:680
  56.2 1.4 %collective-permute-start.5 = (bf16[3,64,128]{2,1,0:T(8,128)(2,1)S(1)}, bf16[3,64,128]{2,1,0:T(8,128)(2,1)S(1)}, u32[]{:S(2)}, u32[]{:S(2)}) collective-permute-start(bf16[3,64,128]{2,1,0:T(8,128)(2,1)S(1)} %bitcast.18), channel_id=1, source_target_pairs={{0,16},{16,0},{1,17},{17,1},{2,18},{18,2},{3,19},{19,3},{4,20},{20... | collective-permute-start | bytes 147464 | tf_op jit(solution)/shard_map/ppermute | solution.py:600

commit v6 on v5

--- a/solution.py
+++ b/solution.py
@@ -18,6 +18,7 @@
 SLOTS = 24
 EDGE = 8
 EXTRA = 16
+UNROLL = 5
 MIB = 2**20
 bf16, f32, i32 = jnp.bfloat16, jnp.float32, jnp.int32
 
@@ -26,11 +27,33 @@
     return lax.broadcasted_iota(i32, shape, axis)
 
 
-def neighbour_sum(h, lane):
-    rows, lanes = h.shape
-    total = pltpu.roll(h, 1, 0) + pltpu.roll(h, rows - 1, 0)
-    total = total + jnp.where(lane == 0, 0.0, pltpu.roll(h, 1, 1))
-    return total + jnp.where(lane == lanes - 1, 0.0, pltpu.roll(h, lanes - 1, 1))
+def band_matrix(lanes):
+    shape = (2 * lanes, lanes)
+    apart = lax.rem(iota(shape, 0), lanes) - iota(shape, 1)
+    return jnp.where(jnp.abs(apart) == 1, 1.0, 0.0).astype(bf16)
+
+
+def sums_along_lanes(arrays, band):
+    rows = arrays[0].shape[0]
+    stacked = jnp.concatenate(arrays, axis=0)
+    head = stacked.astype(bf16)
+    tail = (stacked - head.astype(f32)).astype(bf16)
+    sums = jnp.dot(
+        jnp.concatenate([head, tail], axis=1), band[...], preferred_element_type=f32
+    )
+    return [sums[n * rows : (n + 1) * rows] for n in range(len(arrays))]
+
+
+def sum_along_rows(h, columns, ring, with_edge):
+    edge = h[columns:]
+    ring[pl.ds(0, EDGE), :] = edge
+    ring[pl.ds(EDGE, columns), :] = h[:columns]
+    ring[pl.ds(EDGE + columns, EDGE), :] = edge
+    rows = columns
+    if with_edge:
+        ring[pl.ds(2 * EDGE + columns, EDGE), :] = h[:EDGE]
+        rows = columns + EDGE
+    return ring[pl.ds(EDGE - 1, rows), :] + ring[pl.ds(EDGE + 1, rows), :]
 
 
 def edge_tile(right, left):
@@ -48,12 +71,12 @@
 
     def several(number, carry):
         for n in range(unroll):
-            carry = body(number * unroll + n, carry)
+            carry = body(number * unroll + n, n, carry)
         return carry
 
     carry = lax.fori_loop(0, rounds, several, carry)
     for step in range(rounds * unroll, count):
-        carry = body(step, carry)
+        carry = body(step, step - rounds * unroll, carry)
     return carry
 
 
@@ -98,13 +121,14 @@
 
 def pack_kernel(
     section, state, bath, fields, blocks, weights,
-    to_left, to_right, table, left_weights, right_weights,
+    to_left, to_right, table,
     low, high, surface, bath_in, fields_in, blocks_in, extra, sems,
 ):
     tracers, levels, columns, lanes = state.shape
     slots = blocks.shape[0]
     many = tracers * levels
-    wide = left_weights.shape[0]
+    wide = to_left.shape[0] - 2 * many - EXTRA
+    below = pl.ds(2 * many + EXTRA, wide)
     pairs = [
         (state.at[:, :, pl.ds(0, 8)], low),
         (state.at[:, :, pl.ds(columns - 8, 8)], high),
@@ -112,8 +136,8 @@
         (bath, bath_in),
         (fields, fields_in),
         (state.at[:, 0], surface),
-        (weights.at[pl.ds(0, wide)], left_weights),
-        (weights.at[pl.ds((columns - 1) * wide, wide)], right_weights),
+        (weights.at[pl.ds(0, wide)], to_left.at[below]),
+        (weights.at[pl.ds((columns - 1) * wide, wide)], to_right.at[below]),
     ]
     copies = [pltpu.make_async_copy(src, dst, sems.at[n]) for n, (src, dst) in enumerate(pairs)]
     for copy in copies:
@@ -169,8 +193,8 @@
 def start_kernel(
     state, from_left, from_right, bath, blocks, ratios,
     q_result, rho_result, side_result, bath_result, place_result,
-    q_out, rho_out, side_out, held, bath_out, halo, near, bath_in, blocks_in, place, sems, sems_out,
-    *, count,
+    q_out, rho_out, side_out, held, bath_out, halo, near, bath_in, blocks_in, place, ring, band,
+    sems, sems_out, *, count,
 ):
     tracers, levels, columns, lanes = state.shape
     rows = columns + EDGE
@@ -235,25 +259,31 @@
 
     lookup = jnp.broadcast_to(ratios[0:1], (rows, lanes))
 
-    def side(level):
+    band[...] = band_matrix(lanes)
+
+    def side(level, slot):
         wet = level < bath_out[...]
         own = 0.5 * SCALE
         for n in range(4):
             own = jnp.where(level < near[n], 0.5 * SCALE - (n + 1), own)
         side_out[level] = own[:columns]
-        halves = []
+        masked = []
         for n in range(tracers):
             spot = (n * levels + level) * 8
             if not isinstance(level, int):
                 spot = pl.multiple_of(spot, 8)
             full = jnp.concatenate([held[n, level], halo[pl.ds(spot, 8), :]], axis=0)
-            h = jnp.where(wet, full, 0.0)
-            halves.append(own * h + neighbour_sum(h, lane))
+            masked.append(jnp.where(wet, full, 0.0))
+        along = sums_along_lanes(masked, band)
+        halves = []
+        for n, h in enumerate(masked):
+            across = sum_along_rows(h, columns, ring.at[slot, n], True)
+            halves.append(own * h + (across + along[n]))
         return halves
 
-    def deep(step, below, top):
+    def deep(step, slot, below, top):
         level = top - step
-        halves = side(level)
+        halves = side(level, slot)
         above_floor = jnp.maximum(bath_out[...] - level, 0)
         rho = jnp.take_along_axis(lookup, above_floor, axis=1, mode="promise_in_bounds")
         rho_out[level] = rho
@@ -270,10 +300,10 @@
         copies[n].wait()
         first = max(low, 2)
         top = low + size - 1
-        carry = sweep(top - first + 1, functools.partial(deep, top=top), carry, 5)
+        carry = sweep(top - first + 1, functools.partial(deep, top=top), carry, UNROLL)
         if n == 0:
             for level in (1, 0):
-                halves = side(level)
+                halves = side(level, level)
                 rho_out[level] = jnp.zeros((rows, lanes), f32)
                 for m in range(tracers):
                     q_out[m, level] = halves[m]
@@ -296,25 +326,22 @@
 
 
 def remap_kernel(
-    section, columns_in, place_from, from_left, from_right, left_weights, right_weights, weights,
-    out, picked, solved, held, held_left, held_right, place, sems,
+    columns_in, place_from, from_left, from_right, weights, own_fields,
+    out, picked, solved, held, fields_in, place, sems,
 ):
-    fields, rows, width = out.shape
+    fields, rows, width = out.shape[0] // 2, out.shape[1], out.shape[2]
     columns = rows - EDGE
     slots = weights.shape[0] // (columns * width)
-    many = from_left.shape[0] - EXTRA
     tall = slots * width
+    many = from_left.shape[0] - tall - EXTRA
     group = 8
     place_copy = pltpu.make_async_copy(place_from, place, sems.at[0])
-    edge_copies = [
-        pltpu.make_async_copy(left_weights, held_left, sems.at[1]),
-        pltpu.make_async_copy(right_weights, held_right, sems.at[2]),
-    ]
+    fields_copy = pltpu.make_async_copy(own_fields, fields_in, sems.at[1])
     copies = []
     for n in range(columns // group):
         part = pl.ds(n * group * tall, group * tall)
-        copies.append(pltpu.make_async_copy(weights.at[part], held.at[part], sems.at[3 + n]))
-    for copy in [place_copy] + copies + edge_copies:
+        copies.append(pltpu.make_async_copy(weights.at[part], held.at[part], sems.at[2 + n]))
+    for copy in [place_copy] + copies + [fields_copy]:
         copy.start()
     right = from_right[pl.ds(many, EXTRA)].astype(f32)
     left = from_left[pl.ds(many, EXTRA)].astype(f32)
@@ -343,27 +370,28 @@
         )
 
     solved[...] = jnp.zeros_like(solved)
+    below = many + EXTRA
+    one(columns, lambda k: from_right[pl.ds(below + k * width, width)])
+    one(rows - 1, lambda k: from_left[pl.ds(below + k * width, width)])
     for n in range(columns // group):
         copies[n].wait()
         for m in range(group):
             spot = n * group + m
             one(spot, lambda k: held[pl.ds((spot * slots + k) * width, width)])
-    for copy in edge_copies:
-        copy.wait()
-    one(columns, lambda k: held_right[pl.ds(k * width, width)])
-    one(rows - 1, lambda k: held_left[pl.ds(k * width, width)])
-    on_ocean = section[0] == 1
+    fields_copy.wait()
     for f in range(fields):
         out[f, pl.ds(0, columns)] = solved[pl.ds(f, columns, stride=8), :]
-        edge = solved[pl.ds(columns * 8 + f, EDGE, stride=8), :]
-        ice = edge_tile(right[2 + f : 3 + f], left[2 + f : 3 + f])
-        out[f, pl.ds(columns, EDGE)] = jnp.where(on_ocean, ice, edge)
+        out[f, pl.ds(columns, EDGE)] = solved[pl.ds(columns * 8 + f, EDGE, stride=8), :]
+        out[fields + f, pl.ds(0, columns)] = fields_in[f].astype(f32)
+        out[fields + f, pl.ds(columns, EDGE)] = edge_tile(
+            right[2 + f : 3 + f], left[2 + f : 3 + f]
+        )
 
 
 def finish_kernel(
-    section, mine, other, fields, partner_fields, bath_from, q_from, rho_from, side_from, state,
+    section, mine, other, bath_from, q_from, rho_from, side_from, state,
     surface, result,
-    q, rho, side, held, bath, sems, sems_out,
+    q, rho, side, held, bath, ring, band, sems, sems_out,
 ):
     tracers, levels, columns, lanes = state.shape
     rows = columns + EDGE
@@ -390,13 +418,9 @@
     for copy in arrivals[0]:
         copy.wait()
     on_ocean = section[0] == 1
-    lane = iota((rows, lanes), 1)
+    band[...] = band_matrix(lanes)
     flux = [jnp.where(on_ocean, other[f], mine[f]) for f in range(3)]
-    own = []
-    for f in range(3):
-        edge = jnp.where(on_ocean, mine[f, pl.ds(columns, EDGE)], other[f, pl.ds(columns, EDGE)])
-        ice = jnp.where(on_ocean, fields[f].astype(f32), partner_fields[f].astype(f32))
-        own.append(jnp.concatenate([ice, edge], axis=0))
+    own = [jnp.where(on_ocean, mine[3 + f], other[3 + f]) for f in range(3)]
     forcing = [flux[0] + own[0], flux[1] + own[1]]
     top_mix = TOP_MIX * (1.0 + flux[2] * flux[2] + own[2] * own[2])
     depth = bath[...]
@@ -425,21 +449,21 @@
         SCALE,
     )
 
-    def store_half(n, level, h):
-        q[n, level, pl.ds(0, columns)] = side[level] * h[:columns] + neighbour_sum(h, lane)[:columns]
-
-    for n in range(tracers):
-        for level in (0, 1):
-            store_half(n, level, values[n][level])
-
-    def down(step, carry, low):
+    def store_halves(level, slot, values):
+        inner = [h[:columns] for h in values]
+        along = sums_along_lanes(inner, band)
+        for n, h in enumerate(values):
+            across = sum_along_rows(h, columns, ring.at[slot, n], False)
+            q[n, level, pl.ds(0, columns)] = side[level] * inner[n] + (across + along[n])
+
+    for level in (0, 1):
+        store_halves(level, level, [values[n][level] for n in range(tracers)])
+
+    def down(step, slot, carry, low):
         level = low + step
         ratio = rho[level]
-        out = []
-        for n in range(tracers):
-            h = q[n, level] + ratio * carry[n]
-            store_half(n, level, h)
-            out.append(h)
+        out = [q[n, level] + ratio * carry[n] for n in range(tracers)]
+        store_halves(level, slot, out)
         return tuple(out)
 
     carry = tuple(values[n][1] for n in range(tracers))
@@ -448,9 +472,9 @@
             for copy in arrivals[n]:
                 copy.wait()
         first = max(low, 2)
-        carry = sweep(low + size - first, functools.partial(down, low=first), carry, 5)
-
-    def up(step, carry):
+        carry = sweep(low + size - first, functools.partial(down, low=first), carry, UNROLL)
+
+    def up(step, slot, carry):
         level = levels - 1 - step
         ratio = rho[level, pl.ds(0, columns)]
         out = []
@@ -474,7 +498,7 @@
         surface[n] = jnp.where(on_ocean, values[n][0] * unscale, other[n, pl.ds(0, columns)])
     surface[2] = jnp.where(on_ocean, top_mix[:columns], other[2, pl.ds(0, columns)])
 
-    def last(step, carry, low):
+    def last(step, slot, carry, low):
         level = low + step
         ratio = rho[level, pl.ds(0, columns)]
         wet = level < bath[pl.ds(0, columns)]
@@ -511,11 +535,6 @@
     return lax.ppermute(value, axis, [(i, (i + by) % count) for i in range(count)])
 
 
-def shift_first_section(value, by):
-    count = lax.axis_size("blk")
-    return lax.ppermute(value, ("sec", "blk"), [(i, (i + by) % count) for i in range(count)])
-
-
 def in_hbm(value):
     return pltpu.with_memory_space_constraint(value, pltpu.HBM)
 
@@ -536,7 +555,6 @@
     many = tracers * levels
 
     hbm = pl.BlockSpec(memory_space=pltpu.HBM)
-    anywhere = pl.BlockSpec(memory_space=pl.ANY)
     vmem = pl.BlockSpec(memory_space=pltpu.VMEM)
     smem = pl.BlockSpec(memory_space=pltpu.SMEM)
     shaped = jax.ShapeDtypeStruct
@@ -558,19 +576,16 @@
     )(in_hbm(blocks), in_hbm(spots))
     asked = lax.all_to_all(request, "blk", split_axis=0, concat_axis=0, tiled=True)
 
-    payload = shaped((2 * many + EXTRA, lanes), bf16)
-    edge_weights = pltpu.HBM((tall, lanes), bf16)
-    to_left, to_right, table, to_left_weights, to_right_weights = pl.pallas_call(
+    payload = shaped((2 * many + EXTRA + tall, lanes), bf16)
+    to_left, to_right, table = pl.pallas_call(
         pack_kernel,
         out_shape=(
             payload,
             payload,
             shaped((columns, 3 * lanes), bf16),
-            edge_weights,
-            edge_weights,
         ),
         in_specs=[smem] + [hbm] * 5,
-        out_specs=(vmem, vmem, vmem, hbm, hbm),
+        out_specs=(vmem, vmem, vmem),
         scratch_shapes=[
             pltpu.VMEM((tracers, levels, 8, lanes), f32),
             pltpu.VMEM((tracers, levels, 8, lanes), f32),
@@ -595,9 +610,6 @@
     )
     from_left = shift(to_right, "blk", 1)
     from_right = shift(to_left, "blk", -1)
-    left_weights = shift_first_section(to_right_weights, 1)
-    right_weights = shift_first_section(to_left_weights, -1)
-    partner_fields = lax.ppermute(fields, "sec", [(0, 1), (1, 0)])
 
     served = pl.pallas_call(
         serve_kernel,
@@ -633,6 +645,8 @@
             pltpu.VMEM(bathymetry.shape, i32),
             pltpu.VMEM(blocks.shape, i32),
             pltpu.VMEM((slots * columns, 128), i32),
+            pltpu.VMEM((UNROLL, tracers, columns + 3 * EDGE, lanes), f32),
+            pltpu.VMEM((2 * lanes, lanes), bf16),
             pltpu.SemaphoreType.DMA((pieces + 2,)),
             pltpu.SemaphoreType.DMA((3 * pieces + 2,)),
         ],
@@ -651,38 +665,35 @@
 
     mine = pl.pallas_call(
         remap_kernel,
-        out_shape=shaped((3, rows, lanes), f32),
-        in_specs=[smem, vmem, hbm, vmem, vmem, anywhere, anywhere, hbm],
+        out_shape=shaped((6, rows, lanes), f32),
+        in_specs=[vmem, hbm, vmem, vmem, hbm, hbm],
         out_specs=vmem,
         scratch_shapes=[
             pltpu.VMEM((slots, rows * 8, lanes), f32),
             pltpu.VMEM((rows * 8, lanes), f32),
             pltpu.VMEM(weights.shape, bf16),
-            pltpu.VMEM((tall, lanes), bf16),
-            pltpu.VMEM((tall, lanes), bf16),
+            pltpu.VMEM(fields.shape, bf16),
             pltpu.VMEM((slots * columns, 128), i32),
-            pltpu.SemaphoreType.DMA((3 + columns // 8,)),
+            pltpu.SemaphoreType.DMA((2 + columns // 8,)),
         ],
         compiler_params=pltpu.CompilerParams(vmem_limit_bytes=20 * MIB),
         cost_estimate=pl.CostEstimate(
             flops=16 * weights.size, bytes_accessed=2 * weights.size, transcendentals=0
         ),
     )(
-        section,
         columns_in,
         in_hbm(place),
         from_left,
         from_right,
-        left_weights,
-        right_weights,
         in_hbm(weights),
+        in_hbm(fields),
     )
     other = lax.ppermute(mine, "sec", [(0, 1), (1, 0)])
 
     surface, result = pl.pallas_call(
         finish_kernel,
         out_shape=(shaped((3, columns, lanes), f32), shaped(ocean_state.shape, f32)),
-        in_specs=[smem] + [vmem] * 4 + [hbm] * 5,
+        in_specs=[smem] + [vmem] * 2 + [hbm] * 5,
         out_specs=(vmem, hbm),
         scratch_shapes=[
             pltpu.VMEM((tracers, levels, rows, lanes), f32),
@@ -690,6 +701,8 @@
             pltpu.VMEM((levels, columns, lanes), f32),
             pltpu.VMEM(ocean_state.shape, f32),
             pltpu.VMEM((rows, lanes), i32),
+            pltpu.VMEM((UNROLL, tracers, columns + 2 * EDGE, lanes), f32),
+            pltpu.VMEM((2 * lanes, lanes), bf16),
             pltpu.SemaphoreType.DMA((pieces + 1, 4)),
             pltpu.SemaphoreType.DMA((pieces,)),
         ],
@@ -701,8 +714,6 @@
         section,
         mine,
         other,
-        fields,
-        partner_fields,
         in_hbm(bath),
         in_hbm(q),
         in_hbm(rho),

time: 67.4 us -> 50.1 us (0.74)
  starting transfers between devices: 20.6 us -> 10.7 us
  Pallas kernels: 34.3 us -> 24.9 us
  waiting for transfers between devices: 0.9 us -> 3.02 us
    ppermute x3 -> x0, starting transfers between devices: 9.93 us -> none  [the longest x2 9.44 us: shift_first_section(): lax.ppermute(value, ('sec', 'blk'), [(i, (i + by) % count) for i in range...]
    pallas_call x1, Pallas kernels: 9.13 us -> 1.53 us  [per_device(): pl.pallas_call(pack_kernel, out_shape=(payload, payload, shaped((columns,...]
    pallas_call x1, Pallas kernels: 8.83 us -> 7.13 us  [per_device(): pl.pallas_call(functools.partial(start_kernel, count=count), out_shape=(p...]
    all_to_all x1, waiting for transfers between devices: 0.01 us -> 1.55 us  [per_device(): lax.all_to_all(served, 'blk', split_axis=0, concat_axis=0, tiled=True)]
    ppermute x1, waiting for transfers between devices: 0.01 us -> 1.46 us  [per_device(): other = lax.ppermute(mine, 'sec', [(0, 1), (1, 0)])]
    ppermute x3 -> x0, waiting for transfers between devices: 0.89 us -> none  [the longest x1 0.88 us: per_device(): partner_fields = lax.ppermute(fields, 'sec', [(0, 1), (1, 0)])]
  transfers between devices with their start and end apart: 7 -> 4, of which waited for: 1 -> 2; matrix products, arithmetic and copies ran while one was open for 0% -> 0% of each run, Pallas kernels for 15% -> 16%
where the time goes in v6:
time: 50.1 us; the launch traced here: 49.8 us
  Pallas kernels  24.9 us (50%)
  starting transfers between devices  10.7 us (21%)
  blocking collectives  10.4 us (21%)
  waiting for transfers between devices  3.02 us (6%)
  between operations  0.71 us (1%)
    all_to_all x1, blocking collectives, per_device(): lax.all_to_all(request, 'blk', split_axis=0, concat_axis=0, tiled=True)  10.4 us
    pallas_call x1, Pallas kernels, per_device(): pl.pallas_call(finish_kernel, out_shape=(shaped((3, columns, lanes), f32)...  9.38 us
    pallas_call x1, Pallas kernels, per_device(): pl.pallas_call(functools.partial(start_kernel, count=count), out_shape=(p...  7.13 us
    ppermute x2, starting transfers between devices, shift(): lax.ppermute(value, axis, [(i, (i + by) % count) for i in range(count)])  7.05 us
    pallas_call x1, Pallas kernels, per_device(): pl.pallas_call(remap_kernel, out_shape=shaped((6, rows, lanes), f32), in_...  4.65 us
    all_to_all x1, starting transfers between devices, per_device(): lax.all_to_all(served, 'blk', split_axis=0, concat_axis=0, tiled=True)  3.54 us
    all_to_all x1, waiting for transfers between devices, per_device(): lax.all_to_all(served, 'blk', split_axis=0, concat_axis=0, tiled=True)  1.55 us
    pallas_call x1, Pallas kernels, per_device(): pl.pallas_call(pack_kernel, out_shape=(payload, payload, shaped((columns,...  1.53 us
  transfers between devices with their start and end apart: 4, of which 2 were waited for; matrix products, arithmetic and copies ran while one was open for 0% of the time, Pallas kernels for 16%

profile of v6, /device:TPU:0, one launch (start us, length us, event | category | flops | bytes accessed | tf_op | source)
XLA Modules:
  0.0 49.8 jit_solution(3582724291224139771)
XLA Ops:
  0.6 0.0 copy-start
  0.6 1.5 %shard_map.87 = (bf16[848,128]{1,0:T(8,128)(2,1)S(1)}, bf16[848,128]{1,0:T(8,128)(2,1)S(1)}, bf16[64,384]{1,0:T(8,128)(2,1)S(1)}) custom-call(s32[1]{0:T(128)} %bitcast.section, f32[2,80,64,128]{3,2,1,0:T(8,128)} %state.5, s32[64,128]{1,0:T(8,128)} %bath.3, bf16[3,64,128]{2,1,0:T(8,128)(2,1)} %bitcast.21, s32[4,64]{1,0:T(4,128)} %bitcast.23, ...), custom_call_target="tpu_custom_call" | custom-call | flops 1000000 | bytes 4000000 | tf_op jit(solution)/shard_map/pallas_call | solution.py:580
  2.2 3.0 %collective-permute-start = (bf16[848,128]{1,0:T(8,128)(2,1)S(1)}, bf16[848,128]{1,0:T(8,128)(2,1)S(1)}, u32[]{:S(2)}, u32[]{:S(2)}) collective-permute-start(bf16[848,128]{1,0:T(8,128)(2,1)S(1)} %get-tuple-element.13), channel_id=1, source_target_pairs={{0,1},{1,2},{2,3},{3,4},{4,5},{5,6},{6,7},{7,8},{8,9},{9,10},{10,1... | collective-permute-start | bytes 651272 | tf_op jit(solution)/shard_map/ppermute | solution.py:535
  5.2 4.1 %collective-permute-start.1 = (bf16[848,128]{1,0:T(8,128)(2,1)S(1)}, bf16[848,128]{1,0:T(8,128)(2,1)S(1)}, u32[]{:S(2)}, u32[]{:S(2)}) collective-permute-start(bf16[848,128]{1,0:T(8,128)(2,1)S(1)} %get-tuple-element.14), channel_id=1, source_target_pairs={{0,15},{1,0},{2,1},{3,2},{4,3},{5,4},{6,5},{7,6},{8,7},{9,8},{10,9... | collective-permute-start | bytes 651272 | tf_op jit(solution)/shard_map/ppermute | solution.py:535
  9.2 1.0 %shard_map.86 = s32[16,128]{1,0:T(8,128)S(1)} custom-call(s32[4,64]{1,0:T(4,128)} %bitcast.24, s32[4,64]{1,0:T(4,128)} %bitcast.26), custom_call_target="tpu_custom_call" | custom-call | flops 1000000 | bytes 100000 | tf_op jit(solution)/shard_map/pallas_call | solution.py:564
  10.3 10.4 %all_to_all.22 = s32[16,1,128]{2,1,0:T(1,128)S(1)} all-to-all(s32[16,1,128]{2,1,0:T(1,128)S(1)} %bitcast.18), channel_id=1, replica_groups=mesh['sec'=2,'blk'=16] {'blk'}, dimensions={0} | all-to-all | bytes 16384 | tf_op jit(solution)/shard_map/all_to_all | solution.py:577
  20.7 0.0 collective-permute-done.from_left
  20.7 0.0 collective-permute-done.1.from_right
  20.7 1.2 %shard_map.88 = bf16[384,384]{1,0:T(8,128)(2,1)} custom-call(s32[16,128]{1,0:T(8,128)S(1)} %bitcast.17, bf16[64,384]{1,0:T(8,128)(2,1)S(1)} %get-tuple-element.12.table, bf16[848,128]{1,0:T(8,128)(2,1)S(1)} %collective-permute-done.from_left, bf16[848,128]{1,0:T(8,128)(2,1)S(1)} %collective-permute-done.1.from_right), custom_call_target="tpu_custom_call" | custom-call | flops 10000000 | bytes 1000000 | tf_op jit(solution)/shard_map/pallas_call | solution.py:614
  21.9 3.5 %all-to-all-start.1 = ((bf16[16,24,384]{2,1,0:T(8,128)(2,1)}), bf16[16,24,384]{2,1,0:T(8,128)(2,1)S(1)}, u32[]{:S(2)}, u32[]{:S(2)}) async-start(bf16[16,24,384]{2,1,0:T(8,128)(2,1)} %bitcast.11), calls=%async_computation.1 | async-start | bytes 589824 | tf_op jit(solution)/shard_map/all_to_all | solution.py:624
  25.5 0.0 copy-done
  25.5 7.1 %shard_map.89 = (f32[2,80,72,128]{3,2,1,0:T(8,128)}, f32[80,72,128]{2,1,0:T(8,128)}, f32[80,64,128]{2,1,0:T(8,128)}, s32[72,128]{1,0:T(8,128)}, s32[256,128]{1,0:T(8,128)}) custom-call(f32[2,80,64,128]{3,2,1,0:T(8,128)} %state.5, bf16[848,128]{1,0:T(8,128)(2,1)S(1)} %collective-permute-done.from_left, ...), custom_call_target="tpu_custom_call" | custom-call | flops 44236800 | bytes 147456000 | tf_op jit(solution)/shard_map/pallas_call | solution.py:626
  32.6 1.5 %all-to-all-done.1 = bf16[16,24,384]{2,1,0:T(8,128)(2,1)S(1)} async-done(((bf16[16,24,384]{2,1,0:T(8,128)(2,1)}), bf16[16,24,384]{2,1,0:T(8,128)(2,1)S(1)}, u32[]{:S(2)}, u32[]{:S(2)}) %all-to-all-start.1) | async-done | bytes 294944 | tf_op jit(solution)/shard_map/all_to_all | solution.py:624
  34.2 4.7 %shard_map.90.mine = f32[6,72,128]{2,1,0:T(8,128)S(1)} custom-call(bf16[384,384]{1,0:T(8,128)(2,1)S(1)} %bitcast.16, s32[256,128]{1,0:T(8,128)} %get-tuple-element.15.place_from, bf16[848,128]{1,0:T(8,128)(2,1)S(1)} %collective-permute-done.from_left, bf16[848,128]{1,0:T(8,128)(2,1)S(1)} %collective-permute-done.1.from_right, bf16[32768,128]{1,0:T(8,128)(2,1)} %bitcast.20, ...), custom_call_target="tpu_custom_call" | custom-call | flops 67108864 | bytes 8388608 | tf_op jit(solution)/shard_map/pallas_call | solution.py:666
  38.8 0.1 collective-permute-start.2
  38.9 1.5 %collective-permute-done.2.other = f32[6,72,128]{2,1,0:T(8,128)S(1)} collective-permute-done((f32[6,72,128]{2,1,0:T(8,128)S(1)}, f32[6,72,128]{2,1,0:T(8,128)S(1)}, u32[]{:S(2)}, u32[]{:S(2)}) %collective-permute-start.2) | collective-permute-done | bytes 221216 | tf_op jit(solution)/shard_map/ppermute | solution.py:691
  40.4 9.4 %shard_map.91 = (f32[3,64,128]{2,1,0:T(8,128)}, f32[2,80,64,128]{3,2,1,0:T(8,128)}) custom-call(s32[1]{0:T(128)} %bitcast.section, f32[6,72,128]{2,1,0:T(8,128)S(1)} %shard_map.90.mine, f32[6,72,128]{2,1,0:T(8,128)S(1)} %collective-permute-done.2.other, s32[72,128]{1,0:T(8,128)} %get-tuple-element.16.bath_from, f32[2,80,72,128]{3,2,1,0:T(8,128)} %get-tuple-element.17.q_from, ...), custom_call_target="tpu_custom_call" | custom-call | flops 44236800 | bytes 23592960 | tf_op jit(solution)/shard_map/pallas_call | solution.py:693
  (1 shorter events, 0.0 us)
Async XLA Ops:
  0.6 24.8 %copy-start = (f32[128]{0:T(128)S(1)}, f32[128]{0:T(128)}, u32[]{:S(2)}) copy-start(f32[128]{0:T(128)} %constant.8.clone) | copy-start | bytes 1540
  2.2 18.5 %collective-permute-start = (bf16[848,128]{1,0:T(8,128)(2,1)S(1)}, bf16[848,128]{1,0:T(8,128)(2,1)S(1)}, u32[]{:S(2)}, u32[]{:S(2)}) collective-permute-start(bf16[848,128]{1,0:T(8,128)(2,1)S(1)} %get-tuple-element.13), channel_id=1, source_target_pairs={{0,1},{1,2},{2,3},{3,4},{4,5},{5,6},{6,7},{7,8},{8,9},{9,10},{10,1... | collective-permute-start | bytes 651272 | tf_op jit(solution)/shard_map/ppermute | solution.py:535
  5.2 15.5 %collective-permute-start.1 = (bf16[848,128]{1,0:T(8,128)(2,1)S(1)}, bf16[848,128]{1,0:T(8,128)(2,1)S(1)}, u32[]{:S(2)}, u32[]{:S(2)}) collective-permute-start(bf16[848,128]{1,0:T(8,128)(2,1)S(1)} %get-tuple-element.14), channel_id=1, source_target_pairs={{0,15},{1,0},{2,1},{3,2},{4,3},{5,4},{6,5},{7,6},{8,7},{9,8},{10,9... | collective-permute-start | bytes 651272 | tf_op jit(solution)/shard_map/ppermute | solution.py:535
  21.9 12.3 %all-to-all-start.1 = ((bf16[16,24,384]{2,1,0:T(8,128)(2,1)}), bf16[16,24,384]{2,1,0:T(8,128)(2,1)S(1)}, u32[]{:S(2)}, u32[]{:S(2)}) async-start(bf16[16,24,384]{2,1,0:T(8,128)(2,1)} %bitcast.11), calls=%async_computation.1 | async-start | bytes 589824 | tf_op jit(solution)/shard_map/all_to_all | solution.py:624
  38.8 1.5 %collective-permute-start.2 = (f32[6,72,128]{2,1,0:T(8,128)S(1)}, f32[6,72,128]{2,1,0:T(8,128)S(1)}, u32[]{:S(2)}, u32[]{:S(2)}) collective-permute-start(f32[6,72,128]{2,1,0:T(8,128)S(1)} %shard_map.90.mine), channel_id=1, source_target_pairs={{0,16},{16,0},{1,17},{17,1},{2,18},{18,2},{3,19},{19,3},{4,20},{20... | collective-permute-start | bytes 663560 | tf_op jit(solution)/shard_map/ppermute | solution.py:691

commit v7 on v6

--- a/solution.py
+++ b/solution.py
@@ -15,7 +15,9 @@
 SCALE = 1.0 / (0.5 * SIDE_MIX)
 
 MOST = 16
-SLOTS = 24
+SLOTS = MOST + 2
+FIELDS = 3
+PIECE = 56
 EDGE = 8
 EXTRA = 16
 UNROLL = 5
@@ -106,7 +108,9 @@
     for copy in copies:
         copy.wait()
     count, columns = request.shape[0], blocks.shape[1]
-    slot = iota((128, columns), 0)
+    place = iota((128, columns), 0)
+    field = place // SLOTS
+    slot = jnp.where(field < FIELDS, place - field * SLOTS, -1)
     here = iota((128, columns), 1)
     marks = ((slot == MOST) & (here == 0)) | ((slot == MOST + 1) & (here == columns - 1))
     asked = jnp.zeros(request.shape, f32)
@@ -116,7 +120,7 @@
         asked = asked + lax.dot_general(
             named, filled, (((1,), (1,)), ((), ())), preferred_element_type=f32
         )
-    request[...] = asked.astype(i32)
+    request[...] = asked.astype(i32) + (iota(request.shape, 1) // SLOTS) * columns
 
 
 def pack_kernel(
@@ -158,7 +162,7 @@
         own = fields_in[f]
         if f < 2:
             own = jnp.where(on_ocean, surface[f], own.astype(f32)).astype(bf16)
-        table[:, f * lanes : (f + 1) * lanes] = own
+        table[f * columns : (f + 1) * columns, :] = own
     copies[0].wait()
     copies[1].wait()
     for c in range(2):
@@ -174,9 +178,9 @@
 
 def serve_kernel(asked, table, from_left, from_right, out):
     count = asked.shape[0]
-    wanted = jnp.transpose(asked[...].astype(f32))[:SLOTS]
-    columns = table.shape[0]
-    slot = iota((SLOTS, 1), 0)
+    wanted = jnp.transpose(asked[...].astype(f32))[:PIECE]
+    height = table.shape[0]
+    slot = lax.rem(iota((PIECE, 1), 0), SLOTS)
     parts = []
     for e in range(count):
         after, before = (e + 1) % count, (e - 1) % count
@@ -185,15 +189,15 @@
             wanted[:, after : after + 1],
             jnp.where(slot == MOST + 1, wanted[:, before : before + 1], wanted[:, e : e + 1]),
         )
-        parts.append(jnp.where(iota((SLOTS, columns), 1) == spot.astype(i32), 1.0, 0.0))
+        parts.append(jnp.where(iota((PIECE, height), 1) == spot.astype(i32), 1.0, 0.0))
     chosen = jnp.concatenate(parts, axis=0).astype(bf16)
     out[...] = jnp.dot(chosen, table[...], preferred_element_type=f32).astype(bf16)
 
 
 def start_kernel(
     state, from_left, from_right, bath, blocks, ratios,
-    q_result, rho_result, side_result, bath_result, place_result,
-    q_out, rho_out, side_out, held, bath_out, halo, near, bath_in, blocks_in, place, ring, band,
+    q_result, side_result, bath_result, place_result,
+    q_out, side_out, held, bath_out, halo, near, bath_in, blocks_in, place, ring, band,
     sems, sems_out, *, count,
 ):
     tracers, levels, columns, lanes = state.shape
@@ -239,13 +243,13 @@
     bath_copy.wait()
     depth = jnp.concatenate([bath_in[...], edge.astype(i32)], axis=0)
     bath_out[...] = depth
-    send(bath_out, bath_result, 3 * len(chunks))
+    send(bath_out, bath_result, 2 * len(chunks))
     blocks_copy.wait()
     for k, (_, rank) in enumerate(ranks(blocks_in, count)):
-        arrives = blocks_in[k : k + 1, :].astype(f32) * SLOTS + rank
+        arrives = blocks_in[k : k + 1, :].astype(f32) * PIECE + rank
         spread = jnp.transpose(jnp.broadcast_to(arrives, (128, columns)))
         place[k * columns : (k + 1) * columns, :] = spread.astype(i32)
-    send(place, place_result, 3 * len(chunks) + 1)
+    send(place, place_result, 2 * len(chunks) + 1)
     lane = iota((rows, lanes), 1)
     a = pltpu.roll(depth, 1, 0)
     b = pltpu.roll(depth, rows - 1, 0)
@@ -257,7 +261,6 @@
     b, d = jnp.maximum(b, d), jnp.minimum(b, d)
     near[0], near[1], near[2], near[3] = a, jnp.maximum(b, c), jnp.minimum(b, c), d
 
-    lookup = jnp.broadcast_to(ratios[0:1], (rows, lanes))
 
     band[...] = band_matrix(lanes)
 
@@ -266,31 +269,30 @@
         own = 0.5 * SCALE
         for n in range(4):
             own = jnp.where(level < near[n], 0.5 * SCALE - (n + 1), own)
-        side_out[level] = own[:columns]
-        masked = []
+        side_out[level] = own[:columns].astype(bf16)
+        starts, masked = [], []
         for n in range(tracers):
             spot = (n * levels + level) * 8
             if not isinstance(level, int):
                 spot = pl.multiple_of(spot, 8)
             full = jnp.concatenate([held[n, level], halo[pl.ds(spot, 8), :]], axis=0)
+            starts.append(full)
             masked.append(jnp.where(wet, full, 0.0))
         along = sums_along_lanes(masked, band)
         halves = []
         for n, h in enumerate(masked):
             across = sum_along_rows(h, columns, ring.at[slot, n], True)
             halves.append(own * h + (across + along[n]))
-        return halves
+        return wet, starts, halves
 
     def deep(step, slot, below, top):
         level = top - step
-        halves = side(level, slot)
-        above_floor = jnp.maximum(bath_out[...] - level, 0)
-        rho = jnp.take_along_axis(lookup, above_floor, axis=1, mode="promise_in_bounds")
-        rho_out[level] = rho
+        wet, starts, halves = side(level, slot)
+        rho = ratio_at(ratios, bath_out[...], level)
         solved = []
         for n in range(tracers):
             q = rho * (halves[n] + below[n])
-            q_out[n, level] = q
+            q_out[n, level] = jnp.where(wet, q, starts[n])
             solved.append(q)
         return tuple(solved)
 
@@ -303,16 +305,20 @@
         carry = sweep(top - first + 1, functools.partial(deep, top=top), carry, UNROLL)
         if n == 0:
             for level in (1, 0):
-                halves = side(level, level)
-                rho_out[level] = jnp.zeros((rows, lanes), f32)
+                wet, starts, halves = side(level, level)
                 for m in range(tracers):
-                    q_out[m, level] = halves[m]
+                    q_out[m, level] = jnp.where(wet, halves[m], starts[m])
         part = pl.ds(low, size)
-        send(q_out.at[:, part], q_result.at[:, part], 3 * n)
-        send(rho_out.at[part], rho_result.at[part], 3 * n + 1)
-        send(side_out.at[part], side_result.at[part], 3 * n + 2)
+        send(q_out.at[:, part], q_result.at[:, part], 2 * n)
+        send(side_out.at[part], side_result.at[part], 2 * n + 1)
     for copy in leaving:
         copy.wait()
+
+
+def ratio_at(ratios, depth, level):
+    lookup = jnp.broadcast_to(ratios[0:1], depth.shape)
+    height = jnp.maximum(depth - level, 0)
+    return jnp.take_along_axis(lookup, height, axis=1, mode="promise_in_bounds")
 
 
 def ratios_by_height(levels, lanes):
@@ -345,21 +351,24 @@
         copy.start()
     right = from_right[pl.ds(many, EXTRA)].astype(f32)
     left = from_left[pl.ds(many, EXTRA)].astype(f32)
-    spots = iota((rows, columns_in.shape[0]), 1)
     row = iota((EDGE, 1), 0)
     picked[...] = jnp.zeros_like(picked)
     place_copy.wait()
+    wanted = []
     for k in range(slots):
         edge = jnp.where(
             row == 0,
-            right[8 + k : 9 + k, 0:1] * SLOTS + MOST,
-            jnp.where(row == EDGE - 1, left[8 + k : 9 + k, 0:1] * SLOTS + MOST + 1, -1.0),
+            right[8 + k : 9 + k, 0:1] * PIECE + MOST,
+            jnp.where(row == EDGE - 1, left[8 + k : 9 + k, 0:1] * PIECE + MOST + 1, -PIECE),
         ).astype(i32)
-        wanted = jnp.concatenate([place[k * columns : (k + 1) * columns, 0:1], edge], axis=0)
-        chosen = jnp.where(spots == wanted, 1.0, 0.0).astype(bf16)
+        wanted += [place[k * columns : (k + 1) * columns, 0:1], edge]
+    wanted = jnp.concatenate(wanted, axis=0)
+    spots = iota((slots * rows, columns_in.shape[0]), 1)
+    for f in range(fields):
+        chosen = jnp.where(spots == wanted + f * SLOTS, 1.0, 0.0).astype(bf16)
         found = jnp.dot(chosen, columns_in[...], preferred_element_type=f32)
-        for f in range(fields):
-            picked[k, pl.ds(f, rows, stride=8), :] = found[:, f * width : (f + 1) * width]
+        for k in range(slots):
+            picked[k, pl.ds(f, rows, stride=8), :] = found[k * rows : (k + 1) * rows]
 
     def one(row, table_of):
         spot = pl.ds(row * 8, 8)
@@ -389,31 +398,26 @@
 
 
 def finish_kernel(
-    section, mine, other, bath_from, q_from, rho_from, side_from, state,
-    surface, result,
-    q, rho, side, held, bath, ring, band, sems, sems_out,
+    section, mine, other, bath_from, q_from, side_from, ratios, surface, result,
+    q, rho, side, bath, ring, band, sems, sems_out,
 ):
-    tracers, levels, columns, lanes = state.shape
+    tracers, levels, columns, lanes = result.shape
     rows = columns + EDGE
     chunks = chunks_of(levels)
     bath_copy = pltpu.make_async_copy(bath_from, bath, sems.at[len(chunks), 0])
     bath_copy.start()
-    arrivals, starts = [], []
+    arrivals = []
     for n, (low, size) in enumerate(chunks):
         part = pl.ds(low, size)
         arrivals.append(
             (
                 pltpu.make_async_copy(q_from.at[:, part], q.at[:, part], sems.at[n, 0]),
-                pltpu.make_async_copy(rho_from.at[part], rho.at[part], sems.at[n, 1]),
-                pltpu.make_async_copy(side_from.at[part], side.at[part], sems.at[n, 2]),
+                pltpu.make_async_copy(side_from.at[part], side.at[part], sems.at[n, 1]),
             )
         )
-        starts.append(pltpu.make_async_copy(state.at[:, part], held.at[:, part], sems.at[n, 3]))
     for group in arrivals:
         for copy in group:
             copy.start()
-    for copy in starts:
-        copy.start()
     bath_copy.wait()
     for copy in arrivals[0]:
         copy.wait()
@@ -441,32 +445,36 @@
             values.append((surface_value, next_value))
         return values
 
+    def store_halves(level, slot, values):
+        wet = level < bath[...]
+        masked = [jnp.where(wet, h, 0.0) for h in values]
+        along = sums_along_lanes([h[:columns] for h in masked], band)
+        own = side[level].astype(f32)
+        for n, h in enumerate(masked):
+            across = sum_along_rows(h, columns, ring.at[slot, n], False)
+            half = own * h[:columns] + (across + along[n])
+            q[n, level, pl.ds(0, columns)] = jnp.where(wet[:columns], half, values[n][:columns])
+
     values = top_levels(
         rows,
         [(q[n, 0], q[n, 1]) for n in range(tracers)],
-        [q[n, 2] for n in range(tracers)],
-        rho[2],
+        [jnp.where(2 < depth, q[n, 2], 0.0) for n in range(tracers)],
+        ratio_at(ratios, depth, 2),
         SCALE,
     )
-
-    def store_halves(level, slot, values):
-        inner = [h[:columns] for h in values]
-        along = sums_along_lanes(inner, band)
-        for n, h in enumerate(values):
-            across = sum_along_rows(h, columns, ring.at[slot, n], False)
-            q[n, level, pl.ds(0, columns)] = side[level] * inner[n] + (across + along[n])
-
-    for level in (0, 1):
-        store_halves(level, level, [values[n][level] for n in range(tracers)])
+    tops = [values[n][0] for n in range(tracers)]
+    carry = tuple(jnp.where(1 < depth, values[n][1], q[n, 1]) for n in range(tracers))
+    store_halves(0, 0, tops)
+    store_halves(1, 1, carry)
 
     def down(step, slot, carry, low):
         level = low + step
-        ratio = rho[level]
+        ratio = ratio_at(ratios, bath[...], level)
+        rho[level] = ratio[:columns]
         out = [q[n, level] + ratio * carry[n] for n in range(tracers)]
         store_halves(level, slot, out)
         return tuple(out)
 
-    carry = tuple(values[n][1] for n in range(tracers))
     for n, (low, size) in enumerate(chunks):
         if n > 0:
             for copy in arrivals[n]:
@@ -476,11 +484,13 @@
 
     def up(step, slot, carry):
         level = levels - 1 - step
-        ratio = rho[level, pl.ds(0, columns)]
+        ratio = rho[level]
+        wet = level < bath[pl.ds(0, columns)]
         out = []
         for n in range(tracers):
-            value = ratio * (q[n, level, pl.ds(0, columns)] + carry[n])
-            q[n, level, pl.ds(0, columns)] = value
+            half = q[n, level, pl.ds(0, columns)]
+            value = ratio * (half + carry[n])
+            q[n, level, pl.ds(0, columns)] = jnp.where(wet, value, half)
             out.append(value)
         return tuple(out)
 
@@ -490,7 +500,7 @@
         columns,
         [(q[n, 0, pl.ds(0, columns)], q[n, 1, pl.ds(0, columns)]) for n in range(tracers)],
         carry,
-        rho[2, pl.ds(0, columns)],
+        rho[2],
         SCALE * SCALE,
     )
     unscale = 1.0 / (SCALE * SCALE)
@@ -500,30 +510,32 @@
 
     def last(step, slot, carry, low):
         level = low + step
-        ratio = rho[level, pl.ds(0, columns)]
+        ratio = rho[level]
         wet = level < bath[pl.ds(0, columns)]
         out = []
         for n in range(tracers):
             h = q[n, level, pl.ds(0, columns)] + ratio * carry[n]
-            held[n, level] = jnp.where(wet, h * unscale, held[n, level])
+            q[n, level, pl.ds(0, columns)] = jnp.where(wet, h * unscale, h)
             out.append(h)
         return tuple(out)
 
-    carry = tuple(values[n][1] for n in range(tracers))
+    wet = 1 < depth[:columns]
+    carry = []
+    for n in range(tracers):
+        start = q[n, 1, pl.ds(0, columns)]
+        q[n, 0, pl.ds(0, columns)] = values[n][0] * unscale
+        q[n, 1, pl.ds(0, columns)] = jnp.where(wet, values[n][1] * unscale, start)
+        carry.append(values[n][1])
+    carry = tuple(carry)
     leaving = []
     for n, (low, size) in enumerate(chunks):
-        starts[n].wait()
-        if n == 0:
-            for m in range(tracers):
-                held[m, 0] = values[m][0] * unscale
-                held[m, 1] = jnp.where(
-                    1 < depth[:columns], values[m][1] * unscale, held[m, 1]
-                )
         first = max(low, 2)
         carry = sweep(low + size - first, functools.partial(last, low=first), carry, 10)
         part = pl.ds(low, size)
         leaving.append(
-            pltpu.make_async_copy(held.at[:, part], result.at[:, part], sems_out.at[n])
+            pltpu.make_async_copy(
+                q.at[:, part, pl.ds(0, columns)], result.at[:, part], sems_out.at[n]
+            )
         )
         leaving[-1].start()
     for copy in leaving:
@@ -582,7 +594,7 @@
         out_shape=(
             payload,
             payload,
-            shaped((columns, 3 * lanes), bf16),
+            shaped((FIELDS * columns, lanes), bf16),
         ),
         in_specs=[smem] + [hbm] * 5,
         out_specs=(vmem, vmem, vmem),
@@ -613,7 +625,7 @@
 
     served = pl.pallas_call(
         serve_kernel,
-        out_shape=shaped((count * SLOTS, 3 * lanes), bf16),
+        out_shape=shaped((count * PIECE, lanes), bf16),
         in_specs=[vmem] * 4,
         out_specs=vmem,
         compiler_params=pltpu.CompilerParams(vmem_limit_bytes=8 * MIB),
@@ -623,21 +635,20 @@
     )(asked, table, from_left, from_right)
     columns_in = lax.all_to_all(served, "blk", split_axis=0, concat_axis=0, tiled=True)
 
-    q, rho, side, bath, place = pl.pallas_call(
+    ratios = ratios_by_height(levels, lanes)
+    q, side, bath, place = pl.pallas_call(
         functools.partial(start_kernel, count=count),
         out_shape=(
             pltpu.HBM((tracers, levels, rows, lanes), f32),
-            pltpu.HBM((levels, rows, lanes), f32),
-            pltpu.HBM((levels, columns, lanes), f32),
+            pltpu.HBM((levels, columns, lanes), bf16),
             pltpu.HBM((rows, lanes), i32),
             pltpu.HBM((slots * columns, 128), i32),
         ),
         in_specs=[hbm, vmem, vmem, hbm, hbm, vmem],
-        out_specs=(hbm,) * 5,
+        out_specs=(hbm,) * 4,
         scratch_shapes=[
             pltpu.VMEM((tracers, levels, rows, lanes), f32),
-            pltpu.VMEM((levels, rows, lanes), f32),
-            pltpu.VMEM((levels, columns, lanes), f32),
+            pltpu.VMEM((levels, columns, lanes), bf16),
             pltpu.VMEM(ocean_state.shape, f32),
             pltpu.VMEM((rows, lanes), i32),
             pltpu.VMEM((many * 8, lanes), f32),
@@ -648,7 +659,7 @@
             pltpu.VMEM((UNROLL, tracers, columns + 3 * EDGE, lanes), f32),
             pltpu.VMEM((2 * lanes, lanes), bf16),
             pltpu.SemaphoreType.DMA((pieces + 2,)),
-            pltpu.SemaphoreType.DMA((3 * pieces + 2,)),
+            pltpu.SemaphoreType.DMA((2 * pieces + 2,)),
         ],
         compiler_params=pltpu.CompilerParams(vmem_limit_bytes=28 * MIB),
         cost_estimate=pl.CostEstimate(
@@ -660,7 +671,7 @@
         from_right,
         in_hbm(bathymetry),
         in_hbm(blocks),
-        ratios_by_height(levels, lanes),
+        ratios,
     )
 
     mine = pl.pallas_call(
@@ -693,17 +704,16 @@
     surface, result = pl.pallas_call(
         finish_kernel,
         out_shape=(shaped((3, columns, lanes), f32), shaped(ocean_state.shape, f32)),
-        in_specs=[smem] + [vmem] * 2 + [hbm] * 5,
+        in_specs=[smem] + [vmem] * 2 + [hbm] * 3 + [vmem],
         out_specs=(vmem, hbm),
         scratch_shapes=[
             pltpu.VMEM((tracers, levels, rows, lanes), f32),
-            pltpu.VMEM((levels, rows, lanes), f32),
             pltpu.VMEM((levels, columns, lanes), f32),
-            pltpu.VMEM(ocean_state.shape, f32),
+            pltpu.VMEM((levels, columns, lanes), bf16),
             pltpu.VMEM((rows, lanes), i32),
             pltpu.VMEM((UNROLL, tracers, columns + 2 * EDGE, lanes), f32),
             pltpu.VMEM((2 * lanes, lanes), bf16),
-            pltpu.SemaphoreType.DMA((pieces + 1, 4)),
+            pltpu.SemaphoreType.DMA((pieces + 1, 2)),
             pltpu.SemaphoreType.DMA((pieces,)),
         ],
         compiler_params=pltpu.CompilerParams(vmem_limit_bytes=28 * MIB),
@@ -716,9 +726,8 @@
         other,
         in_hbm(bath),
         in_hbm(q),
-        in_hbm(rho),
         in_hbm(side),
-        in_hbm(ocean_state),
+        ratios,
     )
     return (surface[None], result)
 

time: 50.1 us -> 51.7 us (1.032)
  Pallas kernels: 24.9 us -> 27.1 us
  waiting for transfers between devices: 3.02 us -> 2.46 us
    pallas_call x1, Pallas kernels: 9.38 us -> 10.9 us  [per_device(): pl.pallas_call(finish_kernel, out_shape=(shaped((3, columns, lanes), f32)...]
    all_to_all x1, waiting for transfers between devices: 1.55 us -> 0.99 us  [per_device(): lax.all_to_all(served, 'blk', split_axis=0, concat_axis=0, tiled=True)]
where the time goes in v7:
time: 51.7 us; the launch traced here: 51.4 us
  Pallas kernels  27.1 us (52%)
  starting transfers between devices  10.6 us (21%)
  blocking collectives  10.4 us (20%)
  waiting for transfers between devices  2.46 us (5%)
  between operations  0.71 us (1%)
    pallas_call x1, Pallas kernels, per_device(): pl.pallas_call(finish_kernel, out_shape=(shaped((3, columns, lanes), f32)...  10.9 us
    all_to_all x1, blocking collectives, per_device(): lax.all_to_all(request, 'blk', split_axis=0, concat_axis=0, tiled=True)  10.4 us
    pallas_call x1, Pallas kernels, per_device(): pl.pallas_call(functools.partial(start_kernel, count=count), out_shape=(p...  7.29 us
    ppermute x2, starting transfers between devices, shift(): lax.ppermute(value, axis, [(i, (i + by) % count) for i in range(count)])  7.05 us
    pallas_call x1, Pallas kernels, per_device(): pl.pallas_call(remap_kernel, out_shape=shaped((6, rows, lanes), f32), in_...  5.11 us
    all_to_all x1, starting transfers between devices, per_device(): lax.all_to_all(served, 'blk', split_axis=0, concat_axis=0, tiled=True)  3.53 us
    pallas_call x1, Pallas kernels, per_device(): pl.pallas_call(pack_kernel, out_shape=(payload, payload, shaped((FIELDS *...  1.53 us
    ppermute x1, waiting for transfers between devices, per_device(): other = lax.ppermute(mine, 'sec', [(0, 1), (1, 0)])  1.46 us
  transfers between devices with their start and end apart: 4, of which 2 were waited for; matrix products, arithmetic and copies ran while one was open for 0% of the time, Pallas kernels for 16%

profile of v7, /device:TPU:0, one launch (start us, length us, event | category | flops | bytes accessed | tf_op | source)
XLA Modules:
  0.0 51.4 jit_solution(14391323274270438358)
XLA Ops:
  0.6 0.0 copy-start
  0.6 1.5 %shard_map.87 = (bf16[848,128]{1,0:T(8,128)(2,1)S(1)}, bf16[848,128]{1,0:T(8,128)(2,1)S(1)}, bf16[192,128]{1,0:T(8,128)(2,1)S(1)}) custom-call(s32[1]{0:T(128)} %bitcast.section, f32[2,80,64,128]{3,2,1,0:T(8,128)} %state.3, s32[64,128]{1,0:T(8,128)} %bath.3, bf16[3,64,128]{2,1,0:T(8,128)(2,1)} %bitcast.21, s32[4,64]{1,0:T(4,128)} %bitcast.23, ...), custom_call_target="tpu_custom_call" | custom-call | flops 1000000 | bytes 4000000 | tf_op jit(solution)/shard_map/pallas_call | solution.py:592
  2.2 3.0 %collective-permute-start = (bf16[848,128]{1,0:T(8,128)(2,1)S(1)}, bf16[848,128]{1,0:T(8,128)(2,1)S(1)}, u32[]{:S(2)}, u32[]{:S(2)}) collective-permute-start(bf16[848,128]{1,0:T(8,128)(2,1)S(1)} %get-tuple-element.12), channel_id=1, source_target_pairs={{0,1},{1,2},{2,3},{3,4},{4,5},{5,6},{6,7},{7,8},{8,9},{9,10},{10,1... | collective-permute-start | bytes 651272 | tf_op jit(solution)/shard_map/ppermute | solution.py:547
  5.2 4.1 %collective-permute-start.1 = (bf16[848,128]{1,0:T(8,128)(2,1)S(1)}, bf16[848,128]{1,0:T(8,128)(2,1)S(1)}, u32[]{:S(2)}, u32[]{:S(2)}) collective-permute-start(bf16[848,128]{1,0:T(8,128)(2,1)S(1)} %get-tuple-element.13), channel_id=1, source_target_pairs={{0,15},{1,0},{2,1},{3,2},{4,3},{5,4},{6,5},{7,6},{8,7},{9,8},{10,9... | collective-permute-start | bytes 651272 | tf_op jit(solution)/shard_map/ppermute | solution.py:547
  9.2 1.1 %shard_map.86 = s32[16,128]{1,0:T(8,128)S(1)} custom-call(s32[4,64]{1,0:T(4,128)} %bitcast.24, s32[4,64]{1,0:T(4,128)} %bitcast.26), custom_call_target="tpu_custom_call" | custom-call | flops 1000000 | bytes 100000 | tf_op jit(solution)/shard_map/pallas_call | solution.py:576
  10.3 10.4 %all_to_all.22 = s32[16,1,128]{2,1,0:T(1,128)S(1)} all-to-all(s32[16,1,128]{2,1,0:T(1,128)S(1)} %bitcast.18), channel_id=1, replica_groups=mesh['sec'=2,'blk'=16] {'blk'}, dimensions={0} | all-to-all | bytes 16384 | tf_op jit(solution)/shard_map/all_to_all | solution.py:589
  20.7 0.0 collective-permute-done.from_left
  20.7 0.0 collective-permute-done.1.from_right
  20.7 1.3 %shard_map.88 = bf16[896,128]{1,0:T(8,128)(2,1)} custom-call(s32[16,128]{1,0:T(8,128)S(1)} %bitcast.17, bf16[192,128]{1,0:T(8,128)(2,1)S(1)} %get-tuple-element.11.table, bf16[848,128]{1,0:T(8,128)(2,1)S(1)} %collective-permute-done.from_left, bf16[848,128]{1,0:T(8,128)(2,1)S(1)} %collective-permute-done.1.from_right), custom_call_target="tpu_custom_call" | custom-call | flops 10000000 | bytes 1000000 | tf_op jit(solution)/shard_map/pallas_call | solution.py:626
  22.0 3.5 %all-to-all-start.1 = ((bf16[16,56,128]{2,1,0:T(8,128)(2,1)}), bf16[16,56,128]{2,1,0:T(8,128)(2,1)S(1)}, u32[]{:S(2)}, u32[]{:S(2)}) async-start(bf16[16,56,128]{2,1,0:T(8,128)(2,1)} %bitcast.11), calls=%async_computation.1 | async-start | bytes 458752 | tf_op jit(solution)/shard_map/all_to_all | solution.py:636
  25.6 0.0 copy-done
  25.6 7.3 %shard_map.89 = (f32[2,80,72,128]{3,2,1,0:T(8,128)}, bf16[80,64,128]{2,1,0:T(8,128)(2,1)}, s32[72,128]{1,0:T(8,128)}, s32[256,128]{1,0:T(8,128)}) custom-call(f32[2,80,64,128]{3,2,1,0:T(8,128)} %state.3, bf16[848,128]{1,0:T(8,128)(2,1)S(1)} %collective-permute-done.from_left, bf16[848,128]{1,0:T(8,128)(2,1)S(1)} %collective-permute-done.1.from_right, ...), custom_call_target="tpu_custom_call" | custom-call | flops 44236800 | bytes 147456000 | tf_op jit(solution)/shard_map/pallas_call | solution.py:639
  32.9 1.0 %all-to-all-done.1 = bf16[16,56,128]{2,1,0:T(8,128)(2,1)S(1)} async-done(((bf16[16,56,128]{2,1,0:T(8,128)(2,1)}), bf16[16,56,128]{2,1,0:T(8,128)(2,1)S(1)}, u32[]{:S(2)}, u32[]{:S(2)}) %all-to-all-start.1) | async-done | bytes 229408 | tf_op jit(solution)/shard_map/all_to_all | solution.py:636
  33.9 5.1 %shard_map.90.mine = f32[6,72,128]{2,1,0:T(8,128)S(1)} custom-call(bf16[896,128]{1,0:T(8,128)(2,1)S(1)} %bitcast.16, s32[256,128]{1,0:T(8,128)} %get-tuple-element.14.place_from, bf16[848,128]{1,0:T(8,128)(2,1)S(1)} %collective-permute-done.from_left, bf16[848,128]{1,0:T(8,128)(2,1)S(1)} %collective-permute-done.1.from_right, bf16[32768,128]{1,0:T(8,128)(2,1)} %bitcast.20, ...), custom_call_target="tpu_custom_call" | custom-call | flops 67108864 | bytes 8388608 | tf_op jit(solution)/shard_map/pallas_call | solution.py:677
  39.0 0.1 collective-permute-start.2
  39.1 1.5 %collective-permute-done.2.other = f32[6,72,128]{2,1,0:T(8,128)S(1)} collective-permute-done((f32[6,72,128]{2,1,0:T(8,128)S(1)}, f32[6,72,128]{2,1,0:T(8,128)S(1)}, u32[]{:S(2)}, u32[]{:S(2)}) %collective-permute-start.2) | collective-permute-done | bytes 221216 | tf_op jit(solution)/shard_map/ppermute | solution.py:702
  40.5 10.9 %shard_map.91 = (f32[3,64,128]{2,1,0:T(8,128)}, f32[2,80,64,128]{3,2,1,0:T(8,128)}) custom-call(s32[1]{0:T(128)} %bitcast.section, f32[6,72,128]{2,1,0:T(8,128)S(1)} %shard_map.90.mine, f32[6,72,128]{2,1,0:T(8,128)S(1)} %collective-permute-done.2.other, s32[72,128]{1,0:T(8,128)} %get-tuple-element.15.bath_from, f32[2,80,72,128]{3,2,1,0:T(8,128)} %get-tuple-element.16.q_from, ...), custom_call_target="tpu_custom_call" | custom-call | flops 44236800 | bytes 23592960 | tf_op jit(solution)/shard_map/pallas_call | solution.py:704
  (1 shorter events, 0.0 us)
Async XLA Ops:
  0.6 24.9 %copy-start = (f32[128]{0:T(128)S(1)}, f32[128]{0:T(128)}, u32[]{:S(2)}) copy-start(f32[128]{0:T(128)} %constant.8.clone) | copy-start | bytes 1540
  2.2 18.6 %collective-permute-start = (bf16[848,128]{1,0:T(8,128)(2,1)S(1)}, bf16[848,128]{1,0:T(8,128)(2,1)S(1)}, u32[]{:S(2)}, u32[]{:S(2)}) collective-permute-start(bf16[848,128]{1,0:T(8,128)(2,1)S(1)} %get-tuple-element.12), channel_id=1, source_target_pairs={{0,1},{1,2},{2,3},{3,4},{4,5},{5,6},{6,7},{7,8},{8,9},{9,10},{10,1... | collective-permute-start | bytes 651272 | tf_op jit(solution)/shard_map/ppermute | solution.py:547
  5.2 15.6 %collective-permute-start.1 = (bf16[848,128]{1,0:T(8,128)(2,1)S(1)}, bf16[848,128]{1,0:T(8,128)(2,1)S(1)}, u32[]{:S(2)}, u32[]{:S(2)}) collective-permute-start(bf16[848,128]{1,0:T(8,128)(2,1)S(1)} %get-tuple-element.13), channel_id=1, source_target_pairs={{0,15},{1,0},{2,1},{3,2},{4,3},{5,4},{6,5},{7,6},{8,7},{9,8},{10,9... | collective-permute-start | bytes 651272 | tf_op jit(solution)/shard_map/ppermute | solution.py:547
  22.0 11.8 %all-to-all-start.1 = ((bf16[16,56,128]{2,1,0:T(8,128)(2,1)}), bf16[16,56,128]{2,1,0:T(8,128)(2,1)S(1)}, u32[]{:S(2)}, u32[]{:S(2)}) async-start(bf16[16,56,128]{2,1,0:T(8,128)(2,1)} %bitcast.11), calls=%async_computation.1 | async-start | bytes 458752 | tf_op jit(solution)/shard_map/all_to_all | solution.py:636
  39.0 1.5 %collective-permute-start.2 = (f32[6,72,128]{2,1,0:T(8,128)S(1)}, f32[6,72,128]{2,1,0:T(8,128)S(1)}, u32[]{:S(2)}, u32[]{:S(2)}) collective-permute-start(f32[6,72,128]{2,1,0:T(8,128)S(1)} %shard_map.90.mine), channel_id=1, source_target_pairs={{0,16},{16,0},{1,17},{17,1},{2,18},{18,2},{3,19},{19,3},{4,20},{20... | collective-permute-start | bytes 663560 | tf_op jit(solution)/shard_map/ppermute | solution.py:702

commit v8 on v7

--- a/solution.py
+++ b/solution.py
@@ -399,7 +399,7 @@
 
 def finish_kernel(
     section, mine, other, bath_from, q_from, side_from, ratios, surface, result,
-    q, rho, side, bath, ring, band, sems, sems_out,
+    q, side, bath, padded, rho, solved, done, band, sems, sems_out,
 ):
     tracers, levels, columns, lanes = result.shape
     rows = columns + EDGE
@@ -445,15 +445,11 @@
             values.append((surface_value, next_value))
         return values
 
-    def store_halves(level, slot, values):
-        wet = level < bath[...]
-        masked = [jnp.where(wet, h, 0.0) for h in values]
-        along = sums_along_lanes([h[:columns] for h in masked], band)
-        own = side[level].astype(f32)
-        for n, h in enumerate(masked):
-            across = sum_along_rows(h, columns, ring.at[slot, n], False)
-            half = own * h[:columns] + (across + along[n])
-            q[n, level, pl.ds(0, columns)] = jnp.where(wet[:columns], half, values[n][:columns])
+    def put(level, values):
+        for n, h in enumerate(values):
+            padded[n, level, pl.ds(0, EDGE)] = h[columns:]
+            padded[n, level, pl.ds(EDGE, columns)] = h[:columns]
+            padded[n, level, pl.ds(EDGE + columns, EDGE)] = h[columns:]
 
     values = top_levels(
         rows,
@@ -462,17 +458,17 @@
         ratio_at(ratios, depth, 2),
         SCALE,
     )
-    tops = [values[n][0] for n in range(tracers)]
-    carry = tuple(jnp.where(1 < depth, values[n][1], q[n, 1]) for n in range(tracers))
-    store_halves(0, 0, tops)
-    store_halves(1, 1, carry)
+    put(0, [jnp.where(0 < depth, values[n][0], 0.0) for n in range(tracers)])
+    carry = tuple(values[n][1] for n in range(tracers))
+    put(1, carry)
 
     def down(step, slot, carry, low):
         level = low + step
         ratio = ratio_at(ratios, bath[...], level)
         rho[level] = ratio[:columns]
-        out = [q[n, level] + ratio * carry[n] for n in range(tracers)]
-        store_halves(level, slot, out)
+        wet = level < bath[...]
+        out = [jnp.where(wet, q[n, level], 0.0) + ratio * carry[n] for n in range(tracers)]
+        put(level, out)
         return tuple(out)
 
     for n, (low, size) in enumerate(chunks):
@@ -482,27 +478,29 @@
         first = max(low, 2)
         carry = sweep(low + size - first, functools.partial(down, low=first), carry, UNROLL)
 
+    def halves_at(level):
+        middle = [padded[n, level, pl.ds(EDGE, columns)] for n in range(tracers)]
+        along = sums_along_lanes(middle, band)
+        own = side[level].astype(f32)
+        out = []
+        for n in range(tracers):
+            across = padded[n, level, pl.ds(EDGE - 1, columns)]
+            across = across + padded[n, level, pl.ds(EDGE + 1, columns)]
+            out.append(own * middle[n] + (across + along[n]))
+        return out
+
     def up(step, slot, carry):
         level = levels - 1 - step
         ratio = rho[level]
-        wet = level < bath[pl.ds(0, columns)]
-        out = []
+        halves = halves_at(level)
+        out = [ratio * (halves[n] + carry[n]) for n in range(tracers)]
         for n in range(tracers):
-            half = q[n, level, pl.ds(0, columns)]
-            value = ratio * (half + carry[n])
-            q[n, level, pl.ds(0, columns)] = jnp.where(wet, value, half)
-            out.append(value)
+            solved[n, level] = out[n]
         return tuple(out)
 
     zero = jnp.zeros((columns, lanes), f32)
-    carry = sweep(levels - 2, up, (zero,) * tracers, 13)
-    values = top_levels(
-        columns,
-        [(q[n, 0, pl.ds(0, columns)], q[n, 1, pl.ds(0, columns)]) for n in range(tracers)],
-        carry,
-        rho[2],
-        SCALE * SCALE,
-    )
+    carry = sweep(levels - 2, up, (zero,) * tracers, 6)
+    values = top_levels(columns, list(zip(halves_at(0), halves_at(1))), carry, rho[2], SCALE * SCALE)
     unscale = 1.0 / (SCALE * SCALE)
     for n in range(tracers):
         surface[n] = jnp.where(on_ocean, values[n][0] * unscale, other[n, pl.ds(0, columns)])
@@ -514,28 +512,23 @@
         wet = level < bath[pl.ds(0, columns)]
         out = []
         for n in range(tracers):
-            h = q[n, level, pl.ds(0, columns)] + ratio * carry[n]
-            q[n, level, pl.ds(0, columns)] = jnp.where(wet, h * unscale, h)
+            h = solved[n, level] + ratio * carry[n]
+            done[n, level] = jnp.where(wet, h * unscale, q[n, level, pl.ds(0, columns)])
             out.append(h)
         return tuple(out)
 
     wet = 1 < depth[:columns]
-    carry = []
     for n in range(tracers):
-        start = q[n, 1, pl.ds(0, columns)]
-        q[n, 0, pl.ds(0, columns)] = values[n][0] * unscale
-        q[n, 1, pl.ds(0, columns)] = jnp.where(wet, values[n][1] * unscale, start)
-        carry.append(values[n][1])
-    carry = tuple(carry)
+        done[n, 0] = values[n][0] * unscale
+        done[n, 1] = jnp.where(wet, values[n][1] * unscale, q[n, 1, pl.ds(0, columns)])
+    carry = tuple(values[n][1] for n in range(tracers))
     leaving = []
     for n, (low, size) in enumerate(chunks):
         first = max(low, 2)
         carry = sweep(low + size - first, functools.partial(last, low=first), carry, 10)
         part = pl.ds(low, size)
         leaving.append(
-            pltpu.make_async_copy(
-                q.at[:, part, pl.ds(0, columns)], result.at[:, part], sems_out.at[n]
-            )
+            pltpu.make_async_copy(done.at[:, part], result.at[:, part], sems_out.at[n])
         )
         leaving[-1].start()
     for copy in leaving:
@@ -708,15 +701,17 @@
         out_specs=(vmem, hbm),
         scratch_shapes=[
             pltpu.VMEM((tracers, levels, rows, lanes), f32),
-            pltpu.VMEM((levels, columns, lanes), f32),
             pltpu.VMEM((levels, columns, lanes), bf16),
             pltpu.VMEM((rows, lanes), i32),
-            pltpu.VMEM((UNROLL, tracers, columns + 2 * EDGE, lanes), f32),
+            pltpu.VMEM((tracers, levels, columns + 2 * EDGE, lanes), f32),
+            pltpu.VMEM((levels, columns, lanes), f32),
+            pltpu.VMEM(ocean_state.shape, f32),
+            pltpu.VMEM(ocean_state.shape, f32),
             pltpu.VMEM((2 * lanes, lanes), bf16),
             pltpu.SemaphoreType.DMA((pieces + 1, 2)),
             pltpu.SemaphoreType.DMA((pieces,)),
         ],
-        compiler_params=pltpu.CompilerParams(vmem_limit_bytes=28 * MIB),
+        compiler_params=pltpu.CompilerParams(vmem_limit_bytes=36 * MIB),
         cost_estimate=pl.CostEstimate(
             flops=60 * levels * cells, bytes_accessed=32 * levels * cells, transcendentals=0
         ),

time: 51.7 us -> 52.3 us (1.012)
  Pallas kernels: 27.1 us -> 27.8 us
    pallas_call x1, Pallas kernels: 10.9 us -> 11.5 us  [per_device(): pl.pallas_call(finish_kernel, out_shape=(shaped((3, columns, lanes), f32)...]
where the time goes in v8:
time: 52.3 us; the launch traced here: 52 us
  Pallas kernels  27.8 us (53%)
  starting transfers between devices  10.6 us (20%)
  blocking collectives  10.4 us (20%)
  waiting for transfers between devices  2.46 us (5%)
  between operations  0.71 us (1%)
    pallas_call x1, Pallas kernels, per_device(): pl.pallas_call(finish_kernel, out_shape=(shaped((3, columns, lanes), f32)...  11.5 us
    all_to_all x1, blocking collectives, per_device(): lax.all_to_all(request, 'blk', split_axis=0, concat_axis=0, tiled=True)  10.4 us
    pallas_call x1, Pallas kernels, per_device(): pl.pallas_call(functools.partial(start_kernel, count=count), out_shape=(p...  7.29 us
    ppermute x2, starting transfers between devices, shift(): lax.ppermute(value, axis, [(i, (i + by) % count) for i in range(count)])  7.05 us
    pallas_call x1, Pallas kernels, per_device(): pl.pallas_call(remap_kernel, out_shape=shaped((6, rows, lanes), f32), in_...  5.11 us
    all_to_all x1, starting transfers between devices, per_device(): lax.all_to_all(served, 'blk', split_axis=0, concat_axis=0, tiled=True)  3.53 us
    pallas_call x1, Pallas kernels, per_device(): pl.pallas_call(pack_kernel, out_shape=(payload, payload, shaped((FIELDS *...  1.53 us
    ppermute x1, waiting for transfers between devices, per_device(): other = lax.ppermute(mine, 'sec', [(0, 1), (1, 0)])  1.46 us
  transfers between devices with their start and end apart: 4, of which 2 were waited for; matrix products, arithmetic and copies ran while one was open for 0% of the time, Pallas kernels for 16%

profile of v8, /device:TPU:0, one launch (start us, length us, event | category | flops | bytes accessed | tf_op | source)
XLA Modules:
  0.0 52.0 jit_solution(17557510422918713504)
XLA Ops:
  0.6 0.0 copy-start
  0.6 1.5 %shard_map.87 = (bf16[848,128]{1,0:T(8,128)(2,1)S(1)}, bf16[848,128]{1,0:T(8,128)(2,1)S(1)}, bf16[192,128]{1,0:T(8,128)(2,1)S(1)}) custom-call(s32[1]{0:T(128)} %bitcast.section, f32[2,80,64,128]{3,2,1,0:T(8,128)} %state.3, s32[64,128]{1,0:T(8,128)} %bath.3, bf16[3,64,128]{2,1,0:T(8,128)(2,1)} %bitcast.21, s32[4,64]{1,0:T(4,128)} %bitcast.23, ...), custom_call_target="tpu_custom_call" | custom-call | flops 1000000 | bytes 4000000 | tf_op jit(solution)/shard_map/pallas_call | solution.py:585
  2.2 3.0 %collective-permute-start = (bf16[848,128]{1,0:T(8,128)(2,1)S(1)}, bf16[848,128]{1,0:T(8,128)(2,1)S(1)}, u32[]{:S(2)}, u32[]{:S(2)}) collective-permute-start(bf16[848,128]{1,0:T(8,128)(2,1)S(1)} %get-tuple-element.12), channel_id=1, source_target_pairs={{0,1},{1,2},{2,3},{3,4},{4,5},{5,6},{6,7},{7,8},{8,9},{9,10},{10,1... | collective-permute-start | bytes 651272 | tf_op jit(solution)/shard_map/ppermute | solution.py:540
  5.2 4.1 %collective-permute-start.1 = (bf16[848,128]{1,0:T(8,128)(2,1)S(1)}, bf16[848,128]{1,0:T(8,128)(2,1)S(1)}, u32[]{:S(2)}, u32[]{:S(2)}) collective-permute-start(bf16[848,128]{1,0:T(8,128)(2,1)S(1)} %get-tuple-element.13), channel_id=1, source_target_pairs={{0,15},{1,0},{2,1},{3,2},{4,3},{5,4},{6,5},{7,6},{8,7},{9,8},{10,9... | collective-permute-start | bytes 651272 | tf_op jit(solution)/shard_map/ppermute | solution.py:540
  9.2 1.1 %shard_map.86 = s32[16,128]{1,0:T(8,128)S(1)} custom-call(s32[4,64]{1,0:T(4,128)} %bitcast.24, s32[4,64]{1,0:T(4,128)} %bitcast.26), custom_call_target="tpu_custom_call" | custom-call | flops 1000000 | bytes 100000 | tf_op jit(solution)/shard_map/pallas_call | solution.py:569
  10.3 10.4 %all_to_all.22 = s32[16,1,128]{2,1,0:T(1,128)S(1)} all-to-all(s32[16,1,128]{2,1,0:T(1,128)S(1)} %bitcast.18), channel_id=1, replica_groups=mesh['sec'=2,'blk'=16] {'blk'}, dimensions={0} | all-to-all | bytes 16384 | tf_op jit(solution)/shard_map/all_to_all | solution.py:582
  20.7 0.0 collective-permute-done.from_left
  20.7 0.0 collective-permute-done.1.from_right
  20.7 1.3 %shard_map.88 = bf16[896,128]{1,0:T(8,128)(2,1)} custom-call(s32[16,128]{1,0:T(8,128)S(1)} %bitcast.17, bf16[192,128]{1,0:T(8,128)(2,1)S(1)} %get-tuple-element.11.table, bf16[848,128]{1,0:T(8,128)(2,1)S(1)} %collective-permute-done.from_left, bf16[848,128]{1,0:T(8,128)(2,1)S(1)} %collective-permute-done.1.from_right), custom_call_target="tpu_custom_call" | custom-call | flops 10000000 | bytes 1000000 | tf_op jit(solution)/shard_map/pallas_call | solution.py:619
  22.0 3.5 %all-to-all-start.1 = ((bf16[16,56,128]{2,1,0:T(8,128)(2,1)}), bf16[16,56,128]{2,1,0:T(8,128)(2,1)S(1)}, u32[]{:S(2)}, u32[]{:S(2)}) async-start(bf16[16,56,128]{2,1,0:T(8,128)(2,1)} %bitcast.11), calls=%async_computation.1 | async-start | bytes 458752 | tf_op jit(solution)/shard_map/all_to_all | solution.py:629
  25.6 0.0 copy-done
  25.6 7.3 %shard_map.89 = (f32[2,80,72,128]{3,2,1,0:T(8,128)}, bf16[80,64,128]{2,1,0:T(8,128)(2,1)}, s32[72,128]{1,0:T(8,128)}, s32[256,128]{1,0:T(8,128)}) custom-call(f32[2,80,64,128]{3,2,1,0:T(8,128)} %state.3, bf16[848,128]{1,0:T(8,128)(2,1)S(1)} %collective-permute-done.from_left, bf16[848,128]{1,0:T(8,128)(2,1)S(1)} %collective-permute-done.1.from_right, ...), custom_call_target="tpu_custom_call" | custom-call | flops 44236800 | bytes 147456000 | tf_op jit(solution)/shard_map/pallas_call | solution.py:632
  32.9 1.0 %all-to-all-done.1 = bf16[16,56,128]{2,1,0:T(8,128)(2,1)S(1)} async-done(((bf16[16,56,128]{2,1,0:T(8,128)(2,1)}), bf16[16,56,128]{2,1,0:T(8,128)(2,1)S(1)}, u32[]{:S(2)}, u32[]{:S(2)}) %all-to-all-start.1) | async-done | bytes 229408 | tf_op jit(solution)/shard_map/all_to_all | solution.py:629
  33.9 5.1 %shard_map.90.mine = f32[6,72,128]{2,1,0:T(8,128)S(1)} custom-call(bf16[896,128]{1,0:T(8,128)(2,1)S(1)} %bitcast.16, s32[256,128]{1,0:T(8,128)} %get-tuple-element.14.place_from, bf16[848,128]{1,0:T(8,128)(2,1)S(1)} %collective-permute-done.from_left, bf16[848,128]{1,0:T(8,128)(2,1)S(1)} %collective-permute-done.1.from_right, bf16[32768,128]{1,0:T(8,128)(2,1)} %bitcast.20, ...), custom_call_target="tpu_custom_call" | custom-call | flops 67108864 | bytes 8388608 | tf_op jit(solution)/shard_map/pallas_call | solution.py:670
  39.0 0.1 collective-permute-start.2
  39.1 1.5 %collective-permute-done.2.other = f32[6,72,128]{2,1,0:T(8,128)S(1)} collective-permute-done((f32[6,72,128]{2,1,0:T(8,128)S(1)}, f32[6,72,128]{2,1,0:T(8,128)S(1)}, u32[]{:S(2)}, u32[]{:S(2)}) %collective-permute-start.2) | collective-permute-done | bytes 221216 | tf_op jit(solution)/shard_map/ppermute | solution.py:695
  40.5 11.5 %shard_map.91 = (f32[3,64,128]{2,1,0:T(8,128)}, f32[2,80,64,128]{3,2,1,0:T(8,128)}) custom-call(s32[1]{0:T(128)} %bitcast.section, f32[6,72,128]{2,1,0:T(8,128)S(1)} %shard_map.90.mine, f32[6,72,128]{2,1,0:T(8,128)S(1)} %collective-permute-done.2.other, s32[72,128]{1,0:T(8,128)} %get-tuple-element.15.bath_from, f32[2,80,72,128]{3,2,1,0:T(8,128)} %get-tuple-element.16.q_from, ...), custom_call_target="tpu_custom_call" | custom-call | flops 44236800 | bytes 23592960 | tf_op jit(solution)/shard_map/pallas_call | solution.py:697
  (1 shorter events, 0.0 us)
Async XLA Ops:
  0.6 24.9 %copy-start = (f32[128]{0:T(128)S(1)}, f32[128]{0:T(128)}, u32[]{:S(2)}) copy-start(f32[128]{0:T(128)} %constant.8.clone) | copy-start | bytes 1540
  2.2 18.6 %collective-permute-start = (bf16[848,128]{1,0:T(8,128)(2,1)S(1)}, bf16[848,128]{1,0:T(8,128)(2,1)S(1)}, u32[]{:S(2)}, u32[]{:S(2)}) collective-permute-start(bf16[848,128]{1,0:T(8,128)(2,1)S(1)} %get-tuple-element.12), channel_id=1, source_target_pairs={{0,1},{1,2},{2,3},{3,4},{4,5},{5,6},{6,7},{7,8},{8,9},{9,10},{10,1... | collective-permute-start | bytes 651272 | tf_op jit(solution)/shard_map/ppermute | solution.py:540
  5.2 15.6 %collective-permute-start.1 = (bf16[848,128]{1,0:T(8,128)(2,1)S(1)}, bf16[848,128]{1,0:T(8,128)(2,1)S(1)}, u32[]{:S(2)}, u32[]{:S(2)}) collective-permute-start(bf16[848,128]{1,0:T(8,128)(2,1)S(1)} %get-tuple-element.13), channel_id=1, source_target_pairs={{0,15},{1,0},{2,1},{3,2},{4,3},{5,4},{6,5},{7,6},{8,7},{9,8},{10,9... | collective-permute-start | bytes 651272 | tf_op jit(solution)/shard_map/ppermute | solution.py:540
  22.0 11.8 %all-to-all-start.1 = ((bf16[16,56,128]{2,1,0:T(8,128)(2,1)}), bf16[16,56,128]{2,1,0:T(8,128)(2,1)S(1)}, u32[]{:S(2)}, u32[]{:S(2)}) async-start(bf16[16,56,128]{2,1,0:T(8,128)(2,1)} %bitcast.11), calls=%async_computation.1 | async-start | bytes 458752 | tf_op jit(solution)/shard_map/all_to_all | solution.py:629
  39.0 1.5 %collective-permute-start.2 = (f32[6,72,128]{2,1,0:T(8,128)S(1)}, f32[6,72,128]{2,1,0:T(8,128)S(1)}, u32[]{:S(2)}, u32[]{:S(2)}) collective-permute-start(f32[6,72,128]{2,1,0:T(8,128)S(1)} %shard_map.90.mine), channel_id=1, source_target_pairs={{0,16},{16,0},{1,17},{17,1},{2,18},{18,2},{3,19},{19,3},{4,20},{20... | collective-permute-start | bytes 663560 | tf_op jit(solution)/shard_map/ppermute | solution.py:695

commit v9 on v8

--- a/solution.py
+++ b/solution.py
@@ -1,8 +1,8 @@
 import functools
+import math
 
 import jax
 import jax.numpy as jnp
-import numpy as np
 from jax import lax
 from jax.experimental import pallas as pl
 from jax.experimental.pallas import tpu as pltpu
@@ -12,6 +12,7 @@
 SIDE_MIX = 0.2
 TOP_MIX = 1.0
 DEEP_MIX = 2.0
+FIXED = (1.0 + 2.0 * DEEP_MIX - math.sqrt(1.0 + 4.0 * DEEP_MIX)) / (2.0 * DEEP_MIX)
 SCALE = 1.0 / (0.5 * SIDE_MIX)
 
 MOST = 16
@@ -195,7 +196,7 @@
 
 
 def start_kernel(
-    state, from_left, from_right, bath, blocks, ratios,
+    state, from_left, from_right, bath, blocks,
     q_result, side_result, bath_result, place_result,
     q_out, side_out, held, bath_out, halo, near, bath_in, blocks_in, place, ring, band,
     sems, sems_out, *, count,
@@ -288,7 +289,7 @@
     def deep(step, slot, below, top):
         level = top - step
         wet, starts, halves = side(level, slot)
-        rho = ratio_at(ratios, bath_out[...], level)
+        rho = ratio_at(bath_out[...], level)
         solved = []
         for n in range(tracers):
             q = rho * (halves[n] + below[n])
@@ -315,20 +316,13 @@
         copy.wait()
 
 
-def ratio_at(ratios, depth, level):
-    lookup = jnp.broadcast_to(ratios[0:1], depth.shape)
-    height = jnp.maximum(depth - level, 0)
-    return jnp.take_along_axis(lookup, height, axis=1, mode="promise_in_bounds")
-
-
-def ratios_by_height(levels, lanes):
-    values = [0.0]
-    ratio = DEEP_MIX / (1.0 + DEEP_MIX)
-    for _ in range(levels):
-        values.append(ratio)
-        ratio = DEEP_MIX / (1.0 + DEEP_MIX + DEEP_MIX - DEEP_MIX * ratio)
-    values += [0.0] * (lanes - len(values))
-    return jnp.broadcast_to(jnp.asarray(np.array(values, np.float32)), (8, lanes))
+def ratio_at(depth, level):
+    height = depth - level
+    power = jnp.exp2((2.0 * math.log2(FIXED)) * height.astype(f32))
+    divisor = 1.0 + FIXED * power
+    inverse = pl.reciprocal(divisor, approx=True)
+    scaled = ((1.0 - FIXED * FIXED) * power) * inverse
+    return jnp.where(height > 0, FIXED + scaled * (2.0 - divisor * inverse), 0.0)
 
 
 def remap_kernel(
@@ -398,7 +392,7 @@
 
 
 def finish_kernel(
-    section, mine, other, bath_from, q_from, side_from, ratios, surface, result,
+    section, mine, other, bath_from, q_from, side_from, surface, result,
     q, side, bath, padded, rho, solved, done, band, sems, sems_out,
 ):
     tracers, levels, columns, lanes = result.shape
@@ -455,7 +449,7 @@
         rows,
         [(q[n, 0], q[n, 1]) for n in range(tracers)],
         [jnp.where(2 < depth, q[n, 2], 0.0) for n in range(tracers)],
-        ratio_at(ratios, depth, 2),
+        ratio_at(depth, 2),
         SCALE,
     )
     put(0, [jnp.where(0 < depth, values[n][0], 0.0) for n in range(tracers)])
@@ -464,7 +458,7 @@
 
     def down(step, slot, carry, low):
         level = low + step
-        ratio = ratio_at(ratios, bath[...], level)
+        ratio = ratio_at(bath[...], level)
         rho[level] = ratio[:columns]
         wet = level < bath[...]
         out = [jnp.where(wet, q[n, level], 0.0) + ratio * carry[n] for n in range(tracers)]
@@ -628,7 +622,6 @@
     )(asked, table, from_left, from_right)
     columns_in = lax.all_to_all(served, "blk", split_axis=0, concat_axis=0, tiled=True)
 
-    ratios = ratios_by_height(levels, lanes)
     q, side, bath, place = pl.pallas_call(
         functools.partial(start_kernel, count=count),
         out_shape=(
@@ -637,7 +630,7 @@
             pltpu.HBM((rows, lanes), i32),
             pltpu.HBM((slots * columns, 128), i32),
         ),
-        in_specs=[hbm, vmem, vmem, hbm, hbm, vmem],
+        in_specs=[hbm, vmem, vmem, hbm, hbm],
         out_specs=(hbm,) * 4,
         scratch_shapes=[
             pltpu.VMEM((tracers, levels, rows, lanes), f32),
@@ -664,7 +657,6 @@
         from_right,
         in_hbm(bathymetry),
         in_hbm(blocks),
-        ratios,
     )
 
     mine = pl.pallas_call(
@@ -697,7 +689,7 @@
     surface, result = pl.pallas_call(
         finish_kernel,
         out_shape=(shaped((3, columns, lanes), f32), shaped(ocean_state.shape, f32)),
-        in_specs=[smem] + [vmem] * 2 + [hbm] * 3 + [vmem],
+        in_specs=[smem] + [vmem] * 2 + [hbm] * 3,
         out_specs=(vmem, hbm),
         scratch_shapes=[
             pltpu.VMEM((tracers, levels, rows, lanes), f32),
@@ -722,7 +714,6 @@
         in_hbm(bath),
         in_hbm(q),
         in_hbm(side),
-        ratios,
     )
     return (surface[None], result)
 

time: 52.3 us -> 51.6 us (0.987)
  waiting for transfers between devices: 2.46 us -> 1.47 us
    pallas_call x1, Pallas kernels: 7.29 us -> 8.44 us  [per_device(): pl.pallas_call(functools.partial(start_kernel, count=count), out_shape=(p...]
    all_to_all x1, waiting for transfers between devices: 0.99 us -> 0.01 us  [per_device(): lax.all_to_all(served, 'blk', split_axis=0, concat_axis=0, tiled=True)]
    pallas_call x1, Pallas kernels: 11.5 us -> 10.6 us  [per_device(): pl.pallas_call(finish_kernel, out_shape=(shaped((3, columns, lanes), f32)...]
  transfers between devices with their start and end apart: 4 -> 4, of which waited for: 2 -> 1; matrix products, arithmetic and copies ran while one was open for 0% -> 0% of each run, Pallas kernels for 16% -> 19%
where the time goes in v9:
time: 51.6 us; the launch traced here: 51.3 us
  Pallas kernels  28.1 us (54%)
  starting transfers between devices  10.6 us (21%)
  blocking collectives  10.4 us (20%)
  waiting for transfers between devices  1.47 us (3%)
  between operations  0.69 us (1%)
    pallas_call x1, Pallas kernels, per_device(): pl.pallas_call(finish_kernel, out_shape=(shaped((3, columns, lanes), f32)...  10.6 us
    all_to_all x1, blocking collectives, per_device(): lax.all_to_all(request, 'blk', split_axis=0, concat_axis=0, tiled=True)  10.4 us
    pallas_call x1, Pallas kernels, per_device(): pl.pallas_call(functools.partial(start_kernel, count=count), out_shape=(p...  8.44 us
    ppermute x2, starting transfers between devices, shift(): lax.ppermute(value, axis, [(i, (i + by) % count) for i in range(count)])  7.05 us
    pallas_call x1, Pallas kernels, per_device(): pl.pallas_call(remap_kernel, out_shape=shaped((6, rows, lanes), f32), in_...  5.11 us
    all_to_all x1, starting transfers between devices, per_device(): lax.all_to_all(served, 'blk', split_axis=0, concat_axis=0, tiled=True)  3.53 us
    pallas_call x1, Pallas kernels, per_device(): pl.pallas_call(pack_kernel, out_shape=(payload, payload, shaped((FIELDS *...  1.53 us
    ppermute x1, waiting for transfers between devices, per_device(): other = lax.ppermute(mine, 'sec', [(0, 1), (1, 0)])  1.46 us
  transfers between devices with their start and end apart: 4, of which 1 were waited for; matrix products, arithmetic and copies ran while one was open for 0% of the time, Pallas kernels for 19%

profile of v9, /device:TPU:0, one launch (start us, length us, event | category | flops | bytes accessed | tf_op | source)
XLA Modules:
  0.0 51.3 jit_solution(886121052525431948)
XLA Ops:
  0.6 1.5 %shard_map.78 = (bf16[848,128]{1,0:T(8,128)(2,1)S(1)}, bf16[848,128]{1,0:T(8,128)(2,1)S(1)}, bf16[192,128]{1,0:T(8,128)(2,1)S(1)}) custom-call(s32[1]{0:T(128)} %bitcast.section, f32[2,80,64,128]{3,2,1,0:T(8,128)} %state.3, s32[64,128]{1,0:T(8,128)} %bath.3, bf16[3,64,128]{2,1,0:T(8,128)(2,1)} %bitcast.21, s32[4,64]{1,0:T(4,128)} %bitcast.23, ...), custom_call_target="tpu_custom_call" | custom-call | flops 1000000 | bytes 4000000 | tf_op jit(solution)/shard_map/pallas_call | solution.py:579
  2.2 3.0 %collective-permute-start = (bf16[848,128]{1,0:T(8,128)(2,1)S(1)}, bf16[848,128]{1,0:T(8,128)(2,1)S(1)}, u32[]{:S(2)}, u32[]{:S(2)}) collective-permute-start(bf16[848,128]{1,0:T(8,128)(2,1)S(1)} %get-tuple-element.12), channel_id=1, source_target_pairs={{0,1},{1,2},{2,3},{3,4},{4,5},{5,6},{6,7},{7,8},{8,9},{9,10},{10,1... | collective-permute-start | bytes 651272 | tf_op jit(solution)/shard_map/ppermute | solution.py:534
  5.2 4.1 %collective-permute-start.1 = (bf16[848,128]{1,0:T(8,128)(2,1)S(1)}, bf16[848,128]{1,0:T(8,128)(2,1)S(1)}, u32[]{:S(2)}, u32[]{:S(2)}) collective-permute-start(bf16[848,128]{1,0:T(8,128)(2,1)S(1)} %get-tuple-element.13), channel_id=1, source_target_pairs={{0,15},{1,0},{2,1},{3,2},{4,3},{5,4},{6,5},{7,6},{8,7},{9,8},{10,9... | collective-permute-start | bytes 651272 | tf_op jit(solution)/shard_map/ppermute | solution.py:534
  9.2 1.1 %shard_map.77 = s32[16,128]{1,0:T(8,128)S(1)} custom-call(s32[4,64]{1,0:T(4,128)} %bitcast.24, s32[4,64]{1,0:T(4,128)} %bitcast.26), custom_call_target="tpu_custom_call" | custom-call | flops 1000000 | bytes 100000 | tf_op jit(solution)/shard_map/pallas_call | solution.py:563
  10.3 10.4 %all_to_all.22 = s32[16,1,128]{2,1,0:T(1,128)S(1)} all-to-all(s32[16,1,128]{2,1,0:T(1,128)S(1)} %bitcast.18), channel_id=1, replica_groups=mesh['sec'=2,'blk'=16] {'blk'}, dimensions={0} | all-to-all | bytes 16384 | tf_op jit(solution)/shard_map/all_to_all | solution.py:576
  20.7 0.0 collective-permute-done.from_left
  20.7 0.0 collective-permute-done.1.from_right
  20.7 1.3 %shard_map.79 = bf16[896,128]{1,0:T(8,128)(2,1)} custom-call(s32[16,128]{1,0:T(8,128)S(1)} %bitcast.17, bf16[192,128]{1,0:T(8,128)(2,1)S(1)} %get-tuple-element.11.table, bf16[848,128]{1,0:T(8,128)(2,1)S(1)} %collective-permute-done.from_left, bf16[848,128]{1,0:T(8,128)(2,1)S(1)} %collective-permute-done.1.from_right), custom_call_target="tpu_custom_call" | custom-call | flops 10000000 | bytes 1000000 | tf_op jit(solution)/shard_map/pallas_call | solution.py:613
  22.0 3.5 %all-to-all-start.1 = ((bf16[16,56,128]{2,1,0:T(8,128)(2,1)}), bf16[16,56,128]{2,1,0:T(8,128)(2,1)S(1)}, u32[]{:S(2)}, u32[]{:S(2)}) async-start(bf16[16,56,128]{2,1,0:T(8,128)(2,1)} %bitcast.11), calls=%async_computation.1 | async-start | bytes 458752 | tf_op jit(solution)/shard_map/all_to_all | solution.py:623
  25.6 8.4 %shard_map.80 = (f32[2,80,72,128]{3,2,1,0:T(8,128)}, bf16[80,64,128]{2,1,0:T(8,128)(2,1)}, s32[72,128]{1,0:T(8,128)}, s32[256,128]{1,0:T(8,128)}) custom-call(f32[2,80,64,128]{3,2,1,0:T(8,128)} %state.3, bf16[848,128]{1,0:T(8,128)(2,1)S(1)} %collective-permute-done.from_left, bf16[848,128]{1,0:T(8,128)(2,1)S(1)} %collective-permute-done.1.from_right, ...), custom_call_target="tpu_custom_call" | custom-call | flops 44236800 | bytes 147456000 | tf_op jit(solution)/shard_map/pallas_call | solution.py:625
  34.0 0.0 all-to-all-done.1
  34.0 5.1 %shard_map.81.mine = f32[6,72,128]{2,1,0:T(8,128)S(1)} custom-call(bf16[896,128]{1,0:T(8,128)(2,1)S(1)} %bitcast.16, s32[256,128]{1,0:T(8,128)} %get-tuple-element.14.place_from, bf16[848,128]{1,0:T(8,128)(2,1)S(1)} %collective-permute-done.from_left, bf16[848,128]{1,0:T(8,128)(2,1)S(1)} %collective-permute-done.1.from_right, bf16[32768,128]{1,0:T(8,128)(2,1)} %bitcast.20, ...), custom_call_target="tpu_custom_call" | custom-call | flops 67108864 | bytes 8388608 | tf_op jit(solution)/shard_map/pallas_call | solution.py:662
  39.1 0.1 collective-permute-start.2
  39.2 1.5 %collective-permute-done.2.other = f32[6,72,128]{2,1,0:T(8,128)S(1)} collective-permute-done((f32[6,72,128]{2,1,0:T(8,128)S(1)}, f32[6,72,128]{2,1,0:T(8,128)S(1)}, u32[]{:S(2)}, u32[]{:S(2)}) %collective-permute-start.2) | collective-permute-done | bytes 221216 | tf_op jit(solution)/shard_map/ppermute | solution.py:687
  40.7 10.6 %shard_map.82 = (f32[3,64,128]{2,1,0:T(8,128)}, f32[2,80,64,128]{3,2,1,0:T(8,128)}) custom-call(s32[1]{0:T(128)} %bitcast.section, f32[6,72,128]{2,1,0:T(8,128)S(1)} %shard_map.81.mine, f32[6,72,128]{2,1,0:T(8,128)S(1)} %collective-permute-done.2.other, s32[72,128]{1,0:T(8,128)} %get-tuple-element.15.bath_from, f32[2,80,72,128]{3,2,1,0:T(8,128)} %get-tuple-element.16.q_from, ...), custom_call_target="tpu_custom_call" | custom-call | flops 44236800 | bytes 23592960 | tf_op jit(solution)/shard_map/pallas_call | solution.py:689
Async XLA Ops:
  2.2 18.6 %collective-permute-start = (bf16[848,128]{1,0:T(8,128)(2,1)S(1)}, bf16[848,128]{1,0:T(8,128)(2,1)S(1)}, u32[]{:S(2)}, u32[]{:S(2)}) collective-permute-start(bf16[848,128]{1,0:T(8,128)(2,1)S(1)} %get-tuple-element.12), channel_id=1, source_target_pairs={{0,1},{1,2},{2,3},{3,4},{4,5},{5,6},{6,7},{7,8},{8,9},{9,10},{10,1... | collective-permute-start | bytes 651272 | tf_op jit(solution)/shard_map/ppermute | solution.py:534
  5.2 15.6 %collective-permute-start.1 = (bf16[848,128]{1,0:T(8,128)(2,1)S(1)}, bf16[848,128]{1,0:T(8,128)(2,1)S(1)}, u32[]{:S(2)}, u32[]{:S(2)}) collective-permute-start(bf16[848,128]{1,0:T(8,128)(2,1)S(1)} %get-tuple-element.13), channel_id=1, source_target_pairs={{0,15},{1,0},{2,1},{3,2},{4,3},{5,4},{6,5},{7,6},{8,7},{9,8},{10,9... | collective-permute-start | bytes 651272 | tf_op jit(solution)/shard_map/ppermute | solution.py:534
  22.0 12.0 %all-to-all-start.1 = ((bf16[16,56,128]{2,1,0:T(8,128)(2,1)}), bf16[16,56,128]{2,1,0:T(8,128)(2,1)S(1)}, u32[]{:S(2)}, u32[]{:S(2)}) async-start(bf16[16,56,128]{2,1,0:T(8,128)(2,1)} %bitcast.11), calls=%async_computation.1 | async-start | bytes 458752 | tf_op jit(solution)/shard_map/all_to_all | solution.py:623
  39.1 1.5 %collective-permute-start.2 = (f32[6,72,128]{2,1,0:T(8,128)S(1)}, f32[6,72,128]{2,1,0:T(8,128)S(1)}, u32[]{:S(2)}, u32[]{:S(2)}) collective-permute-start(f32[6,72,128]{2,1,0:T(8,128)S(1)} %shard_map.81.mine), channel_id=1, source_target_pairs={{0,16},{16,0},{1,17},{17,1},{2,18},{18,2},{3,19},{19,3},{4,20},{20... | collective-permute-start | bytes 663560 | tf_op jit(solution)/shard_map/ppermute | solution.py:687

commit v10 on v8

--- a/solution.py
+++ b/solution.py
@@ -29,33 +29,28 @@
     return lax.broadcasted_iota(i32, shape, axis)
 
 
-def band_matrix(lanes):
-    shape = (2 * lanes, lanes)
-    apart = lax.rem(iota(shape, 0), lanes) - iota(shape, 1)
-    return jnp.where(jnp.abs(apart) == 1, 1.0, 0.0).astype(bf16)
-
-
-def sums_along_lanes(arrays, band):
-    rows = arrays[0].shape[0]
-    stacked = jnp.concatenate(arrays, axis=0)
-    head = stacked.astype(bf16)
-    tail = (stacked - head.astype(f32)).astype(bf16)
-    sums = jnp.dot(
-        jnp.concatenate([head, tail], axis=1), band[...], preferred_element_type=f32
-    )
-    return [sums[n * rows : (n + 1) * rows] for n in range(len(arrays))]
-
-
-def sum_along_rows(h, columns, ring, with_edge):
-    edge = h[columns:]
-    ring[pl.ds(0, EDGE), :] = edge
-    ring[pl.ds(EDGE, columns), :] = h[:columns]
-    ring[pl.ds(EDGE + columns, EDGE), :] = edge
-    rows = columns
-    if with_edge:
-        ring[pl.ds(2 * EDGE + columns, EDGE), :] = h[:EDGE]
-        rows = columns + EDGE
-    return ring[pl.ds(EDGE - 1, rows), :] + ring[pl.ds(EDGE + 1, rows), :]
+def adjacency(across, band, used):
+    row, other = iota(across.shape, 0), iota(across.shape, 1)
+    near = (row - other == 1) | (other - row == 1)
+    near = near | ((row == 0) & (other == used - 1)) | ((row == used - 1) & (other == 0))
+    across[...] = jnp.where(near & (row < used) & (other < used), 1.0, 0.0).astype(bf16)
+    apart = iota(band.shape, 0) - iota(band.shape, 1)
+    band[...] = jnp.where(jnp.abs(apart) == 1, 1.0, 0.0).astype(bf16)
+
+
+def rounded(h):
+    rows = -h.shape[0] % 16
+    if rows:
+        h = jnp.concatenate([h, jnp.zeros((rows, h.shape[1]), h.dtype)], axis=0)
+    return h.astype(bf16)
+
+
+def neighbour_sum(h, across, band, rows):
+    tall, lanes = h.shape
+    left = jnp.concatenate([across[pl.ds(0, rows), :], h[:rows]], axis=1)
+    gap = jnp.zeros((across.shape[1] - tall, lanes), bf16)
+    right = jnp.concatenate([h, gap, band[...]], axis=0)
+    return jnp.dot(left, right, preferred_element_type=f32)
 
 
 def edge_tile(right, left):
@@ -197,7 +192,7 @@
 def start_kernel(
     state, from_left, from_right, bath, blocks, ratios,
     q_result, side_result, bath_result, place_result,
-    q_out, side_out, held, bath_out, halo, near, bath_in, blocks_in, place, ring, band,
+    q_out, side_out, held, bath_out, halo, bath_in, blocks_in, place, across, band,
     sems, sems_out, *, count,
 ):
     tracers, levels, columns, lanes = state.shape
@@ -224,6 +219,7 @@
         copy.start()
         leaving.append(copy)
 
+    halo[...] = jnp.zeros_like(halo)
     for c in range(2):
         part = pl.ds(c * many, many)
         halo[pl.ds(c, many, stride=8), :] = from_right[part].astype(f32)
@@ -250,26 +246,10 @@
         spread = jnp.transpose(jnp.broadcast_to(arrives, (128, columns)))
         place[k * columns : (k + 1) * columns, :] = spread.astype(i32)
     send(place, place_result, 2 * len(chunks) + 1)
-    lane = iota((rows, lanes), 1)
-    a = pltpu.roll(depth, 1, 0)
-    b = pltpu.roll(depth, rows - 1, 0)
-    c = jnp.where(lane == 0, 0, pltpu.roll(depth, 1, 1))
-    d = jnp.where(lane == lanes - 1, 0, pltpu.roll(depth, lanes - 1, 1))
-    a, b = jnp.maximum(a, b), jnp.minimum(a, b)
-    c, d = jnp.maximum(c, d), jnp.minimum(c, d)
-    a, c = jnp.maximum(a, c), jnp.minimum(a, c)
-    b, d = jnp.maximum(b, d), jnp.minimum(b, d)
-    near[0], near[1], near[2], near[3] = a, jnp.maximum(b, c), jnp.minimum(b, c), d
-
-
-    band[...] = band_matrix(lanes)
-
-    def side(level, slot):
+    adjacency(across, band, rows)
+
+    def side(level):
         wet = level < bath_out[...]
-        own = 0.5 * SCALE
-        for n in range(4):
-            own = jnp.where(level < near[n], 0.5 * SCALE - (n + 1), own)
-        side_out[level] = own[:columns].astype(bf16)
         starts, masked = [], []
         for n in range(tracers):
             spot = (n * levels + level) * 8
@@ -278,16 +258,18 @@
             full = jnp.concatenate([held[n, level], halo[pl.ds(spot, 8), :]], axis=0)
             starts.append(full)
             masked.append(jnp.where(wet, full, 0.0))
-        along = sums_along_lanes(masked, band)
+        tall = across.shape[0]
+        count = neighbour_sum(rounded(jnp.where(wet, 1.0, 0.0)), across, band, tall)[:rows]
+        own = 0.5 * SCALE - count
+        side_out[level] = own[:columns].astype(bf16)
         halves = []
-        for n, h in enumerate(masked):
-            across = sum_along_rows(h, columns, ring.at[slot, n], True)
-            halves.append(own * h + (across + along[n]))
+        for h in masked:
+            halves.append(own * h + neighbour_sum(rounded(h), across, band, tall)[:rows])
         return wet, starts, halves
 
     def deep(step, slot, below, top):
         level = top - step
-        wet, starts, halves = side(level, slot)
+        wet, starts, halves = side(level)
         rho = ratio_at(ratios, bath_out[...], level)
         solved = []
         for n in range(tracers):
@@ -305,7 +287,7 @@
         carry = sweep(top - first + 1, functools.partial(deep, top=top), carry, UNROLL)
         if n == 0:
             for level in (1, 0):
-                wet, starts, halves = side(level, level)
+                wet, starts, halves = side(level)
                 for m in range(tracers):
                     q_out[m, level] = jnp.where(wet, halves[m], starts[m])
         part = pl.ds(low, size)
@@ -399,7 +381,7 @@
 
 def finish_kernel(
     section, mine, other, bath_from, q_from, side_from, ratios, surface, result,
-    q, side, bath, padded, rho, solved, done, band, sems, sems_out,
+    q, side, bath, values_at, rounded_at, rho, solved, done, across, band, sems, sems_out,
 ):
     tracers, levels, columns, lanes = result.shape
     rows = columns + EDGE
@@ -422,7 +404,7 @@
     for copy in arrivals[0]:
         copy.wait()
     on_ocean = section[0] == 1
-    band[...] = band_matrix(lanes)
+    adjacency(across, band, rows)
     flux = [jnp.where(on_ocean, other[f], mine[f]) for f in range(3)]
     own = [jnp.where(on_ocean, mine[3 + f], other[3 + f]) for f in range(3)]
     forcing = [flux[0] + own[0], flux[1] + own[1]]
@@ -447,9 +429,8 @@
 
     def put(level, values):
         for n, h in enumerate(values):
-            padded[n, level, pl.ds(0, EDGE)] = h[columns:]
-            padded[n, level, pl.ds(EDGE, columns)] = h[:columns]
-            padded[n, level, pl.ds(EDGE + columns, EDGE)] = h[columns:]
+            values_at[n, level] = h[:columns]
+            rounded_at[n, level] = rounded(h)
 
     values = top_levels(
         rows,
@@ -479,14 +460,11 @@
         carry = sweep(low + size - first, functools.partial(down, low=first), carry, UNROLL)
 
     def halves_at(level):
-        middle = [padded[n, level, pl.ds(EDGE, columns)] for n in range(tracers)]
-        along = sums_along_lanes(middle, band)
         own = side[level].astype(f32)
         out = []
         for n in range(tracers):
-            across = padded[n, level, pl.ds(EDGE - 1, columns)]
-            across = across + padded[n, level, pl.ds(EDGE + 1, columns)]
-            out.append(own * middle[n] + (across + along[n]))
+            around = neighbour_sum(rounded_at[n, level], across, band, columns)
+            out.append(own * values_at[n, level] + around)
         return out
 
     def up(step, slot, carry):
@@ -565,6 +543,7 @@
     shaped = jax.ShapeDtypeStruct
     pieces = len(chunks_of(levels))
     cells = rows * lanes
+    tall_rows = rows + -rows % 16
 
     request = pl.pallas_call(
         ask_kernel,
@@ -645,12 +624,11 @@
             pltpu.VMEM(ocean_state.shape, f32),
             pltpu.VMEM((rows, lanes), i32),
             pltpu.VMEM((many * 8, lanes), f32),
-            pltpu.VMEM((4, rows, lanes), i32),
             pltpu.VMEM(bathymetry.shape, i32),
             pltpu.VMEM(blocks.shape, i32),
             pltpu.VMEM((slots * columns, 128), i32),
-            pltpu.VMEM((UNROLL, tracers, columns + 3 * EDGE, lanes), f32),
-            pltpu.VMEM((2 * lanes, lanes), bf16),
+            pltpu.VMEM((tall_rows, lanes), bf16),
+            pltpu.VMEM((lanes, lanes), bf16),
             pltpu.SemaphoreType.DMA((pieces + 2,)),
             pltpu.SemaphoreType.DMA((2 * pieces + 2,)),
         ],
@@ -703,11 +681,13 @@
             pltpu.VMEM((tracers, levels, rows, lanes), f32),
             pltpu.VMEM((levels, columns, lanes), bf16),
             pltpu.VMEM((rows, lanes), i32),
-            pltpu.VMEM((tracers, levels, columns + 2 * EDGE, lanes), f32),
+            pltpu.VMEM(ocean_state.shape, f32),
+            pltpu.VMEM((tracers, levels, tall_rows, lanes), bf16),
             pltpu.VMEM((levels, columns, lanes), f32),
             pltpu.VMEM(ocean_state.shape, f32),
             pltpu.VMEM(ocean_state.shape, f32),
-            pltpu.VMEM((2 * lanes, lanes), bf16),
+            pltpu.VMEM((tall_rows, lanes), bf16),
+            pltpu.VMEM((lanes, lanes), bf16),
             pltpu.SemaphoreType.DMA((pieces + 1, 2)),
             pltpu.SemaphoreType.DMA((pieces,)),
         ],

time: 52.3 us -> 52.1 us (level)
  no operation moved by 1% of the time
where the time goes in v10:
time: 52.1 us; the launch traced here: 51.8 us
  Pallas kernels  27.6 us (53%)
  starting transfers between devices  10.6 us (20%)
  blocking collectives  10.4 us (20%)
  waiting for transfers between devices  2.4 us (5%)
  between operations  0.71 us (1%)
    pallas_call x1, Pallas kernels, per_device(): pl.pallas_call(finish_kernel, out_shape=(shaped((3, columns, lanes), f32)...  11.3 us
    all_to_all x1, blocking collectives, per_device(): lax.all_to_all(request, 'blk', split_axis=0, concat_axis=0, tiled=True)  10.4 us
    pallas_call x1, Pallas kernels, per_device(): pl.pallas_call(functools.partial(start_kernel, count=count), out_shape=(p...  7.35 us
    ppermute x2, starting transfers between devices, shift(): lax.ppermute(value, axis, [(i, (i + by) % count) for i in range(count)])  7.05 us
    pallas_call x1, Pallas kernels, per_device(): pl.pallas_call(remap_kernel, out_shape=shaped((6, rows, lanes), f32), in_...  5.11 us
    all_to_all x1, starting transfers between devices, per_device(): lax.all_to_all(served, 'blk', split_axis=0, concat_axis=0, tiled=True)  3.53 us
    pallas_call x1, Pallas kernels, per_device(): pl.pallas_call(pack_kernel, out_shape=(payload, payload, shaped((FIELDS *...  1.53 us
    ppermute x1, waiting for transfers between devices, per_device(): other = lax.ppermute(mine, 'sec', [(0, 1), (1, 0)])  1.46 us
  transfers between devices with their start and end apart: 4, of which 2 were waited for; matrix products, arithmetic and copies ran while one was open for 0% of the time, Pallas kernels for 16%

profile of v10, /device:TPU:0, one launch (start us, length us, event | category | flops | bytes accessed | tf_op | source)
XLA Modules:
  0.0 51.8 jit_solution(4850209349230464309)
XLA Ops:
  0.6 0.0 copy-start
  0.6 1.5 %shard_map.87 = (bf16[848,128]{1,0:T(8,128)(2,1)S(1)}, bf16[848,128]{1,0:T(8,128)(2,1)S(1)}, bf16[192,128]{1,0:T(8,128)(2,1)S(1)}) custom-call(s32[1]{0:T(128)} %bitcast.section, f32[2,80,64,128]{3,2,1,0:T(8,128)} %state.3, s32[64,128]{1,0:T(8,128)} %bath.3, bf16[3,64,128]{2,1,0:T(8,128)(2,1)} %bitcast.21, s32[4,64]{1,0:T(4,128)} %bitcast.23, ...), custom_call_target="tpu_custom_call" | custom-call | flops 1000000 | bytes 4000000 | tf_op jit(solution)/shard_map/pallas_call | solution.py:564
  2.2 3.0 %collective-permute-start = (bf16[848,128]{1,0:T(8,128)(2,1)S(1)}, bf16[848,128]{1,0:T(8,128)(2,1)S(1)}, u32[]{:S(2)}, u32[]{:S(2)}) collective-permute-start(bf16[848,128]{1,0:T(8,128)(2,1)S(1)} %get-tuple-element.12), channel_id=1, source_target_pairs={{0,1},{1,2},{2,3},{3,4},{4,5},{5,6},{6,7},{7,8},{8,9},{9,10},{10,1... | collective-permute-start | bytes 651272 | tf_op jit(solution)/shard_map/ppermute | solution.py:518
  5.2 4.1 %collective-permute-start.1 = (bf16[848,128]{1,0:T(8,128)(2,1)S(1)}, bf16[848,128]{1,0:T(8,128)(2,1)S(1)}, u32[]{:S(2)}, u32[]{:S(2)}) collective-permute-start(bf16[848,128]{1,0:T(8,128)(2,1)S(1)} %get-tuple-element.13), channel_id=1, source_target_pairs={{0,15},{1,0},{2,1},{3,2},{4,3},{5,4},{6,5},{7,6},{8,7},{9,8},{10,9... | collective-permute-start | bytes 651272 | tf_op jit(solution)/shard_map/ppermute | solution.py:518
  9.2 1.1 %shard_map.86 = s32[16,128]{1,0:T(8,128)S(1)} custom-call(s32[4,64]{1,0:T(4,128)} %bitcast.24, s32[4,64]{1,0:T(4,128)} %bitcast.26), custom_call_target="tpu_custom_call" | custom-call | flops 1000000 | bytes 100000 | tf_op jit(solution)/shard_map/pallas_call | solution.py:548
  10.3 10.4 %all_to_all.22 = s32[16,1,128]{2,1,0:T(1,128)S(1)} all-to-all(s32[16,1,128]{2,1,0:T(1,128)S(1)} %bitcast.18), channel_id=1, replica_groups=mesh['sec'=2,'blk'=16] {'blk'}, dimensions={0} | all-to-all | bytes 16384 | tf_op jit(solution)/shard_map/all_to_all | solution.py:561
  20.7 0.0 collective-permute-done.from_left
  20.7 0.0 collective-permute-done.1.from_right
  20.7 1.3 %shard_map.88 = bf16[896,128]{1,0:T(8,128)(2,1)} custom-call(s32[16,128]{1,0:T(8,128)S(1)} %bitcast.17, bf16[192,128]{1,0:T(8,128)(2,1)S(1)} %get-tuple-element.11.table, bf16[848,128]{1,0:T(8,128)(2,1)S(1)} %collective-permute-done.from_left, bf16[848,128]{1,0:T(8,128)(2,1)S(1)} %collective-permute-done.1.from_right), custom_call_target="tpu_custom_call" | custom-call | flops 10000000 | bytes 1000000 | tf_op jit(solution)/shard_map/pallas_call | solution.py:598
  22.0 3.5 %all-to-all-start.1 = ((bf16[16,56,128]{2,1,0:T(8,128)(2,1)}), bf16[16,56,128]{2,1,0:T(8,128)(2,1)S(1)}, u32[]{:S(2)}, u32[]{:S(2)}) async-start(bf16[16,56,128]{2,1,0:T(8,128)(2,1)} %bitcast.11), calls=%async_computation.1 | async-start | bytes 458752 | tf_op jit(solution)/shard_map/all_to_all | solution.py:608
  25.6 0.0 copy-done
  25.6 7.4 %shard_map.89 = (f32[2,80,72,128]{3,2,1,0:T(8,128)}, bf16[80,64,128]{2,1,0:T(8,128)(2,1)}, s32[72,128]{1,0:T(8,128)}, s32[256,128]{1,0:T(8,128)}) custom-call(f32[2,80,64,128]{3,2,1,0:T(8,128)} %state.3, bf16[848,128]{1,0:T(8,128)(2,1)S(1)} %collective-permute-done.from_left, bf16[848,128]{1,0:T(8,128)(2,1)S(1)} %collective-permute-done.1.from_right, ...), custom_call_target="tpu_custom_call" | custom-call | flops 44236800 | bytes 147456000 | tf_op jit(solution)/shard_map/pallas_call | solution.py:611
  32.9 0.9 %all-to-all-done.1 = bf16[16,56,128]{2,1,0:T(8,128)(2,1)S(1)} async-done(((bf16[16,56,128]{2,1,0:T(8,128)(2,1)}), bf16[16,56,128]{2,1,0:T(8,128)(2,1)S(1)}, u32[]{:S(2)}, u32[]{:S(2)}) %all-to-all-start.1) | async-done | bytes 229408 | tf_op jit(solution)/shard_map/all_to_all | solution.py:608
  33.9 5.1 %shard_map.90.mine = f32[6,72,128]{2,1,0:T(8,128)S(1)} custom-call(bf16[896,128]{1,0:T(8,128)(2,1)S(1)} %bitcast.16, s32[256,128]{1,0:T(8,128)} %get-tuple-element.14.place_from, bf16[848,128]{1,0:T(8,128)(2,1)S(1)} %collective-permute-done.from_left, bf16[848,128]{1,0:T(8,128)(2,1)S(1)} %collective-permute-done.1.from_right, bf16[32768,128]{1,0:T(8,128)(2,1)} %bitcast.20, ...), custom_call_target="tpu_custom_call" | custom-call | flops 67108864 | bytes 8388608 | tf_op jit(solution)/shard_map/pallas_call | solution.py:648
  39.0 0.1 collective-permute-start.2
  39.1 1.5 %collective-permute-done.2.other = f32[6,72,128]{2,1,0:T(8,128)S(1)} collective-permute-done((f32[6,72,128]{2,1,0:T(8,128)S(1)}, f32[6,72,128]{2,1,0:T(8,128)S(1)}, u32[]{:S(2)}, u32[]{:S(2)}) %collective-permute-start.2) | collective-permute-done | bytes 221216 | tf_op jit(solution)/shard_map/ppermute | solution.py:673
  40.5 11.3 %shard_map.91 = (f32[3,64,128]{2,1,0:T(8,128)}, f32[2,80,64,128]{3,2,1,0:T(8,128)}) custom-call(s32[1]{0:T(128)} %bitcast.section, f32[6,72,128]{2,1,0:T(8,128)S(1)} %shard_map.90.mine, f32[6,72,128]{2,1,0:T(8,128)S(1)} %collective-permute-done.2.other, s32[72,128]{1,0:T(8,128)} %get-tuple-element.15.bath_from, f32[2,80,72,128]{3,2,1,0:T(8,128)} %get-tuple-element.16.q_from, ...), custom_call_target="tpu_custom_call" | custom-call | flops 44236800 | bytes 23592960 | tf_op jit(solution)/shard_map/pallas_call | solution.py:675
  (1 shorter events, 0.0 us)
Async XLA Ops:
  0.6 24.9 %copy-start = (f32[128]{0:T(128)S(1)}, f32[128]{0:T(128)}, u32[]{:S(2)}) copy-start(f32[128]{0:T(128)} %constant.8.clone) | copy-start | bytes 1540
  2.2 18.6 %collective-permute-start = (bf16[848,128]{1,0:T(8,128)(2,1)S(1)}, bf16[848,128]{1,0:T(8,128)(2,1)S(1)}, u32[]{:S(2)}, u32[]{:S(2)}) collective-permute-start(bf16[848,128]{1,0:T(8,128)(2,1)S(1)} %get-tuple-element.12), channel_id=1, source_target_pairs={{0,1},{1,2},{2,3},{3,4},{4,5},{5,6},{6,7},{7,8},{8,9},{9,10},{10,1... | collective-permute-start | bytes 651272 | tf_op jit(solution)/shard_map/ppermute | solution.py:518
  5.2 15.6 %collective-permute-start.1 = (bf16[848,128]{1,0:T(8,128)(2,1)S(1)}, bf16[848,128]{1,0:T(8,128)(2,1)S(1)}, u32[]{:S(2)}, u32[]{:S(2)}) collective-permute-start(bf16[848,128]{1,0:T(8,128)(2,1)S(1)} %get-tuple-element.13), channel_id=1, source_target_pairs={{0,15},{1,0},{2,1},{3,2},{4,3},{5,4},{6,5},{7,6},{8,7},{9,8},{10,9... | collective-permute-start | bytes 651272 | tf_op jit(solution)/shard_map/ppermute | solution.py:518
  22.0 11.8 %all-to-all-start.1 = ((bf16[16,56,128]{2,1,0:T(8,128)(2,1)}), bf16[16,56,128]{2,1,0:T(8,128)(2,1)S(1)}, u32[]{:S(2)}, u32[]{:S(2)}) async-start(bf16[16,56,128]{2,1,0:T(8,128)(2,1)} %bitcast.11), calls=%async_computation.1 | async-start | bytes 458752 | tf_op jit(solution)/shard_map/all_to_all | solution.py:608
  39.0 1.5 %collective-permute-start.2 = (f32[6,72,128]{2,1,0:T(8,128)S(1)}, f32[6,72,128]{2,1,0:T(8,128)S(1)}, u32[]{:S(2)}, u32[]{:S(2)}) collective-permute-start(f32[6,72,128]{2,1,0:T(8,128)S(1)} %shard_map.90.mine), channel_id=1, source_target_pairs={{0,16},{16,0},{1,17},{17,1},{2,18},{18,2},{3,19},{19,3},{4,20},{20... | collective-permute-start | bytes 663560 | tf_op jit(solution)/shard_map/ppermute | solution.py:673

commit v11 on v10

--- a/solution.py
+++ b/solution.py
@@ -20,7 +20,6 @@
 PIECE = 56
 EDGE = 8
 EXTRA = 16
-UNROLL = 5
 MIB = 2**20
 bf16, f32, i32 = jnp.bfloat16, jnp.float32, jnp.int32
 
@@ -63,17 +62,9 @@
     return [(start, size) for start in range(0, levels, size)]
 
 
-def sweep(count, body, carry, unroll):
-    rounds = count // unroll
-
-    def several(number, carry):
-        for n in range(unroll):
-            carry = body(number * unroll + n, n, carry)
-        return carry
-
-    carry = lax.fori_loop(0, rounds, several, carry)
-    for step in range(rounds * unroll, count):
-        carry = body(step, step - rounds * unroll, carry)
+def sweep(count, body, carry):
+    for step in range(count):
+        carry = body(step, carry)
     return carry
 
 
@@ -253,8 +244,6 @@
         starts, masked = [], []
         for n in range(tracers):
             spot = (n * levels + level) * 8
-            if not isinstance(level, int):
-                spot = pl.multiple_of(spot, 8)
             full = jnp.concatenate([held[n, level], halo[pl.ds(spot, 8), :]], axis=0)
             starts.append(full)
             masked.append(jnp.where(wet, full, 0.0))
@@ -267,7 +256,7 @@
             halves.append(own * h + neighbour_sum(rounded(h), across, band, tall)[:rows])
         return wet, starts, halves
 
-    def deep(step, slot, below, top):
+    def deep(step, below, top):
         level = top - step
         wet, starts, halves = side(level)
         rho = ratio_at(ratios, bath_out[...], level)
@@ -284,7 +273,7 @@
         copies[n].wait()
         first = max(low, 2)
         top = low + size - 1
-        carry = sweep(top - first + 1, functools.partial(deep, top=top), carry, UNROLL)
+        carry = sweep(top - first + 1, functools.partial(deep, top=top), carry)
         if n == 0:
             for level in (1, 0):
                 wet, starts, halves = side(level)
@@ -443,7 +432,7 @@
     carry = tuple(values[n][1] for n in range(tracers))
     put(1, carry)
 
-    def down(step, slot, carry, low):
+    def down(step, carry, low):
         level = low + step
         ratio = ratio_at(ratios, bath[...], level)
         rho[level] = ratio[:columns]
@@ -457,7 +446,7 @@
             for copy in arrivals[n]:
                 copy.wait()
         first = max(low, 2)
-        carry = sweep(low + size - first, functools.partial(down, low=first), carry, UNROLL)
+        carry = sweep(low + size - first, functools.partial(down, low=first), carry)
 
     def halves_at(level):
         own = side[level].astype(f32)
@@ -467,7 +456,7 @@
             out.append(own * values_at[n, level] + around)
         return out
 
-    def up(step, slot, carry):
+    def up(step, carry):
         level = levels - 1 - step
         ratio = rho[level]
         halves = halves_at(level)
@@ -477,14 +466,14 @@
         return tuple(out)
 
     zero = jnp.zeros((columns, lanes), f32)
-    carry = sweep(levels - 2, up, (zero,) * tracers, 6)
+    carry = sweep(levels - 2, up, (zero,) * tracers)
     values = top_levels(columns, list(zip(halves_at(0), halves_at(1))), carry, rho[2], SCALE * SCALE)
     unscale = 1.0 / (SCALE * SCALE)
     for n in range(tracers):
         surface[n] = jnp.where(on_ocean, values[n][0] * unscale, other[n, pl.ds(0, columns)])
     surface[2] = jnp.where(on_ocean, top_mix[:columns], other[2, pl.ds(0, columns)])
 
-    def last(step, slot, carry, low):
+    def last(step, carry, low):
         level = low + step
         ratio = rho[level]
         wet = level < bath[pl.ds(0, columns)]
@@ -503,7 +492,7 @@
     leaving = []
     for n, (low, size) in enumerate(chunks):
         first = max(low, 2)
-        carry = sweep(low + size - first, functools.partial(last, low=first), carry, 10)
+        carry = sweep(low + size - first, functools.partial(last, low=first), carry)
         part = pl.ds(low, size)
         leaving.append(
             pltpu.make_async_copy(done.at[:, part], result.at[:, part], sems_out.at[n])

time: 52.1 us -> 50.5 us (0.969)
  Pallas kernels: 27.6 us -> 25 us
  waiting for transfers between devices: 2.4 us -> 3.36 us
    pallas_call x1, Pallas kernels: 11.3 us -> 9.62 us  [per_device(): pl.pallas_call(finish_kernel, out_shape=(shaped((3, columns, lanes), f32)...]
    pallas_call x1, Pallas kernels: 7.35 us -> 6.4 us  [per_device(): pl.pallas_call(functools.partial(start_kernel, count=count), out_shape=(p...]
    all_to_all x1, waiting for transfers between devices: 0.93 us -> 1.89 us  [per_device(): lax.all_to_all(served, 'blk', split_axis=0, concat_axis=0, tiled=True)]
  transfers between devices with their start and end apart: 4 -> 4, of which waited for: 2 -> 2; matrix products, arithmetic and copies ran while one was open for 0% -> 0% of each run, Pallas kernels for 16% -> 15%
where the time goes in v11:
time: 50.5 us; the launch traced here: 50.2 us
  Pallas kernels  25 us (50%)
  starting transfers between devices  10.6 us (21%)
  blocking collectives  10.4 us (21%)
  waiting for transfers between devices  3.36 us (7%)
  between operations  0.71 us (1%)
    all_to_all x1, blocking collectives, per_device(): lax.all_to_all(request, 'blk', split_axis=0, concat_axis=0, tiled=True)  10.4 us
    pallas_call x1, Pallas kernels, per_device(): pl.pallas_call(finish_kernel, out_shape=(shaped((3, columns, lanes), f32)...  9.62 us
    ppermute x2, starting transfers between devices, shift(): lax.ppermute(value, axis, [(i, (i + by) % count) for i in range(count)])  7.05 us
    pallas_call x1, Pallas kernels, per_device(): pl.pallas_call(functools.partial(start_kernel, count=count), out_shape=(p...  6.4 us
    pallas_call x1, Pallas kernels, per_device(): pl.pallas_call(remap_kernel, out_shape=shaped((6, rows, lanes), f32), in_...  5.11 us
    all_to_all x1, starting transfers between devices, per_device(): lax.all_to_all(served, 'blk', split_axis=0, concat_axis=0, tiled=True)  3.53 us
    all_to_all x1, waiting for transfers between devices, per_device(): lax.all_to_all(served, 'blk', split_axis=0, concat_axis=0, tiled=True)  1.89 us
    pallas_call x1, Pallas kernels, per_device(): pl.pallas_call(pack_kernel, out_shape=(payload, payload, shaped((FIELDS *...  1.53 us
  transfers between devices with their start and end apart: 4, of which 2 were waited for; matrix products, arithmetic and copies ran while one was open for 0% of the time, Pallas kernels for 15%

profile of v11, /device:TPU:0, one launch (start us, length us, event | category | flops | bytes accessed | tf_op | source)
XLA Modules:
  0.0 50.2 jit_solution(7484644250727093314)
XLA Ops:
  0.6 0.0 copy-start
  0.6 1.5 %shard_map.87 = (bf16[848,128]{1,0:T(8,128)(2,1)S(1)}, bf16[848,128]{1,0:T(8,128)(2,1)S(1)}, bf16[192,128]{1,0:T(8,128)(2,1)S(1)}) custom-call(s32[1]{0:T(128)} %bitcast.section, f32[2,80,64,128]{3,2,1,0:T(8,128)} %state.3, s32[64,128]{1,0:T(8,128)} %bath.3, bf16[3,64,128]{2,1,0:T(8,128)(2,1)} %bitcast.21, s32[4,64]{1,0:T(4,128)} %bitcast.23, ...), custom_call_target="tpu_custom_call" | custom-call | flops 1000000 | bytes 4000000 | tf_op jit(solution)/shard_map/pallas_call | solution.py:553
  2.2 3.0 %collective-permute-start = (bf16[848,128]{1,0:T(8,128)(2,1)S(1)}, bf16[848,128]{1,0:T(8,128)(2,1)S(1)}, u32[]{:S(2)}, u32[]{:S(2)}) collective-permute-start(bf16[848,128]{1,0:T(8,128)(2,1)S(1)} %get-tuple-element.12), channel_id=1, source_target_pairs={{0,1},{1,2},{2,3},{3,4},{4,5},{5,6},{6,7},{7,8},{8,9},{9,10},{10,1... | collective-permute-start | bytes 651272 | tf_op jit(solution)/shard_map/ppermute | solution.py:507
  5.2 4.1 %collective-permute-start.1 = (bf16[848,128]{1,0:T(8,128)(2,1)S(1)}, bf16[848,128]{1,0:T(8,128)(2,1)S(1)}, u32[]{:S(2)}, u32[]{:S(2)}) collective-permute-start(bf16[848,128]{1,0:T(8,128)(2,1)S(1)} %get-tuple-element.13), channel_id=1, source_target_pairs={{0,15},{1,0},{2,1},{3,2},{4,3},{5,4},{6,5},{7,6},{8,7},{9,8},{10,9... | collective-permute-start | bytes 651272 | tf_op jit(solution)/shard_map/ppermute | solution.py:507
  9.2 1.1 %shard_map.86 = s32[16,128]{1,0:T(8,128)S(1)} custom-call(s32[4,64]{1,0:T(4,128)} %bitcast.24, s32[4,64]{1,0:T(4,128)} %bitcast.26), custom_call_target="tpu_custom_call" | custom-call | flops 1000000 | bytes 100000 | tf_op jit(solution)/shard_map/pallas_call | solution.py:537
  10.3 10.4 %all_to_all.22 = s32[16,1,128]{2,1,0:T(1,128)S(1)} all-to-all(s32[16,1,128]{2,1,0:T(1,128)S(1)} %bitcast.18), channel_id=1, replica_groups=mesh['sec'=2,'blk'=16] {'blk'}, dimensions={0} | all-to-all | bytes 16384 | tf_op jit(solution)/shard_map/all_to_all | solution.py:550
  20.7 0.0 collective-permute-done.from_left
  20.7 0.0 collective-permute-done.1.from_right
  20.7 1.3 %shard_map.88 = bf16[896,128]{1,0:T(8,128)(2,1)} custom-call(s32[16,128]{1,0:T(8,128)S(1)} %bitcast.17, bf16[192,128]{1,0:T(8,128)(2,1)S(1)} %get-tuple-element.11.table, bf16[848,128]{1,0:T(8,128)(2,1)S(1)} %collective-permute-done.from_left, bf16[848,128]{1,0:T(8,128)(2,1)S(1)} %collective-permute-done.1.from_right), custom_call_target="tpu_custom_call" | custom-call | flops 10000000 | bytes 1000000 | tf_op jit(solution)/shard_map/pallas_call | solution.py:587
  22.0 3.5 %all-to-all-start.1 = ((bf16[16,56,128]{2,1,0:T(8,128)(2,1)}), bf16[16,56,128]{2,1,0:T(8,128)(2,1)S(1)}, u32[]{:S(2)}, u32[]{:S(2)}) async-start(bf16[16,56,128]{2,1,0:T(8,128)(2,1)} %bitcast.11), calls=%async_computation.1 | async-start | bytes 458752 | tf_op jit(solution)/shard_map/all_to_all | solution.py:597
  25.6 0.0 copy-done
  25.6 6.4 %shard_map.89 = (f32[2,80,72,128]{3,2,1,0:T(8,128)}, bf16[80,64,128]{2,1,0:T(8,128)(2,1)}, s32[72,128]{1,0:T(8,128)}, s32[256,128]{1,0:T(8,128)}) custom-call(f32[2,80,64,128]{3,2,1,0:T(8,128)} %state.3, bf16[848,128]{1,0:T(8,128)(2,1)S(1)} %collective-permute-done.from_left, bf16[848,128]{1,0:T(8,128)(2,1)S(1)} %collective-permute-done.1.from_right, ...), custom_call_target="tpu_custom_call" | custom-call | flops 44236800 | bytes 147456000 | tf_op jit(solution)/shard_map/pallas_call | solution.py:600
  32.0 1.9 %all-to-all-done.1 = bf16[16,56,128]{2,1,0:T(8,128)(2,1)S(1)} async-done(((bf16[16,56,128]{2,1,0:T(8,128)(2,1)}), bf16[16,56,128]{2,1,0:T(8,128)(2,1)S(1)}, u32[]{:S(2)}, u32[]{:S(2)}) %all-to-all-start.1) | async-done | bytes 229408 | tf_op jit(solution)/shard_map/all_to_all | solution.py:597
  33.9 5.1 %shard_map.90.mine = f32[6,72,128]{2,1,0:T(8,128)S(1)} custom-call(bf16[896,128]{1,0:T(8,128)(2,1)S(1)} %bitcast.16, s32[256,128]{1,0:T(8,128)} %get-tuple-element.14.place_from, bf16[848,128]{1,0:T(8,128)(2,1)S(1)} %collective-permute-done.from_left, bf16[848,128]{1,0:T(8,128)(2,1)S(1)} %collective-permute-done.1.from_right, bf16[32768,128]{1,0:T(8,128)(2,1)} %bitcast.20, ...), custom_call_target="tpu_custom_call" | custom-call | flops 67108864 | bytes 8388608 | tf_op jit(solution)/shard_map/pallas_call | solution.py:637
  39.0 0.1 collective-permute-start.2
  39.1 1.5 %collective-permute-done.2.other = f32[6,72,128]{2,1,0:T(8,128)S(1)} collective-permute-done((f32[6,72,128]{2,1,0:T(8,128)S(1)}, f32[6,72,128]{2,1,0:T(8,128)S(1)}, u32[]{:S(2)}, u32[]{:S(2)}) %collective-permute-start.2) | collective-permute-done | bytes 221216 | tf_op jit(solution)/shard_map/ppermute | solution.py:662
  40.5 9.6 %shard_map.91 = (f32[3,64,128]{2,1,0:T(8,128)}, f32[2,80,64,128]{3,2,1,0:T(8,128)}) custom-call(s32[1]{0:T(128)} %bitcast.section, f32[6,72,128]{2,1,0:T(8,128)S(1)} %shard_map.90.mine, f32[6,72,128]{2,1,0:T(8,128)S(1)} %collective-permute-done.2.other, s32[72,128]{1,0:T(8,128)} %get-tuple-element.15.bath_from, f32[2,80,72,128]{3,2,1,0:T(8,128)} %get-tuple-element.16.q_from, ...), custom_call_target="tpu_custom_call" | custom-call | flops 44236800 | bytes 23592960 | tf_op jit(solution)/shard_map/pallas_call | solution.py:664
  (1 shorter events, 0.0 us)
Async XLA Ops:
  0.6 24.9 %copy-start = (f32[128]{0:T(128)S(1)}, f32[128]{0:T(128)}, u32[]{:S(2)}) copy-start(f32[128]{0:T(128)} %constant.8.clone) | copy-start | bytes 1540
  2.2 18.6 %collective-permute-start = (bf16[848,128]{1,0:T(8,128)(2,1)S(1)}, bf16[848,128]{1,0:T(8,128)(2,1)S(1)}, u32[]{:S(2)}, u32[]{:S(2)}) collective-permute-start(bf16[848,128]{1,0:T(8,128)(2,1)S(1)} %get-tuple-element.12), channel_id=1, source_target_pairs={{0,1},{1,2},{2,3},{3,4},{4,5},{5,6},{6,7},{7,8},{8,9},{9,10},{10,1... | collective-permute-start | bytes 651272 | tf_op jit(solution)/shard_map/ppermute | solution.py:507
  5.2 15.6 %collective-permute-start.1 = (bf16[848,128]{1,0:T(8,128)(2,1)S(1)}, bf16[848,128]{1,0:T(8,128)(2,1)S(1)}, u32[]{:S(2)}, u32[]{:S(2)}) collective-permute-start(bf16[848,128]{1,0:T(8,128)(2,1)S(1)} %get-tuple-element.13), channel_id=1, source_target_pairs={{0,15},{1,0},{2,1},{3,2},{4,3},{5,4},{6,5},{7,6},{8,7},{9,8},{10,9... | collective-permute-start | bytes 651272 | tf_op jit(solution)/shard_map/ppermute | solution.py:507
  22.0 11.8 %all-to-all-start.1 = ((bf16[16,56,128]{2,1,0:T(8,128)(2,1)}), bf16[16,56,128]{2,1,0:T(8,128)(2,1)S(1)}, u32[]{:S(2)}, u32[]{:S(2)}) async-start(bf16[16,56,128]{2,1,0:T(8,128)(2,1)} %bitcast.11), calls=%async_computation.1 | async-start | bytes 458752 | tf_op jit(solution)/shard_map/all_to_all | solution.py:597
  39.0 1.5 %collective-permute-start.2 = (f32[6,72,128]{2,1,0:T(8,128)S(1)}, f32[6,72,128]{2,1,0:T(8,128)S(1)}, u32[]{:S(2)}, u32[]{:S(2)}) collective-permute-start(f32[6,72,128]{2,1,0:T(8,128)S(1)} %shard_map.90.mine), channel_id=1, source_target_pairs={{0,16},{16,0},{1,17},{17,1},{2,18},{18,2},{3,19},{19,3},{4,20},{20... | collective-permute-start | bytes 663560 | tf_op jit(solution)/shard_map/ppermute | solution.py:662

commit v12 on v11

--- a/solution.py
+++ b/solution.py
@@ -20,6 +20,7 @@
 PIECE = 56
 EDGE = 8
 EXTRA = 16
+IN_FLIGHT = 3
 MIB = 2**20
 bf16, f32, i32 = jnp.bfloat16, jnp.float32, jnp.int32
 
@@ -162,7 +163,7 @@
     copies[7].wait()
 
 
-def serve_kernel(asked, table, from_left, from_right, out):
+def serve_kernel(asked, table, out):
     count = asked.shape[0]
     wanted = jnp.transpose(asked[...].astype(f32))[:PIECE]
     height = table.shape[0]
@@ -201,7 +202,7 @@
     blocks_copy = pltpu.make_async_copy(blocks, blocks_in, sems.at[len(chunks) + 1])
     blocks_copy.start()
     bath_copy.start()
-    for copy in reversed(copies):
+    for copy in reversed(copies[-IN_FLIGHT:]):
         copy.start()
     leaving = []
 
@@ -271,6 +272,8 @@
     for n in reversed(range(len(chunks))):
         low, size = chunks[n]
         copies[n].wait()
+        if n >= IN_FLIGHT:
+            copies[n - IN_FLIGHT].start()
         first = max(low, 2)
         top = low + size - 1
         carry = sweep(top - first + 1, functools.partial(deep, top=top), carry)
@@ -369,29 +372,12 @@
 
 
 def finish_kernel(
-    section, mine, other, bath_from, q_from, side_from, ratios, surface, result,
-    q, side, bath, values_at, rounded_at, rho, solved, done, across, band, sems, sems_out,
+    section, mine, other, bath, q, side, ratios, surface, result,
+    values_at, rounded_at, rho, solved, done, across, band, sems_out,
 ):
     tracers, levels, columns, lanes = result.shape
     rows = columns + EDGE
     chunks = chunks_of(levels)
-    bath_copy = pltpu.make_async_copy(bath_from, bath, sems.at[len(chunks), 0])
-    bath_copy.start()
-    arrivals = []
-    for n, (low, size) in enumerate(chunks):
-        part = pl.ds(low, size)
-        arrivals.append(
-            (
-                pltpu.make_async_copy(q_from.at[:, part], q.at[:, part], sems.at[n, 0]),
-                pltpu.make_async_copy(side_from.at[part], side.at[part], sems.at[n, 1]),
-            )
-        )
-    for group in arrivals:
-        for copy in group:
-            copy.start()
-    bath_copy.wait()
-    for copy in arrivals[0]:
-        copy.wait()
     on_ocean = section[0] == 1
     adjacency(across, band, rows)
     flux = [jnp.where(on_ocean, other[f], mine[f]) for f in range(3)]
@@ -441,12 +427,7 @@
         put(level, out)
         return tuple(out)
 
-    for n, (low, size) in enumerate(chunks):
-        if n > 0:
-            for copy in arrivals[n]:
-                copy.wait()
-        first = max(low, 2)
-        carry = sweep(low + size - first, functools.partial(down, low=first), carry)
+    sweep(levels - 2, functools.partial(down, low=2), carry)
 
     def halves_at(level):
         own = side[level].astype(f32)
@@ -511,6 +492,10 @@
     return pltpu.with_memory_space_constraint(value, pltpu.HBM)
 
 
+def in_vmem(value):
+    return pltpu.with_memory_space_constraint(value, pltpu.VMEM)
+
+
 def per_device(
     surface_fields, source_blocks, source_columns, remap_weights, ocean_state, bathymetry
 ):
@@ -587,13 +572,13 @@
     served = pl.pallas_call(
         serve_kernel,
         out_shape=shaped((count * PIECE, lanes), bf16),
-        in_specs=[vmem] * 4,
+        in_specs=[vmem] * 2,
         out_specs=vmem,
         compiler_params=pltpu.CompilerParams(vmem_limit_bytes=8 * MIB),
         cost_estimate=pl.CostEstimate(
             flops=10**7, bytes_accessed=10**6, transcendentals=0
         ),
-    )(asked, table, from_left, from_right)
+    )(asked, table)
     columns_in = lax.all_to_all(served, "blk", split_axis=0, concat_axis=0, tiled=True)
 
     ratios = ratios_by_height(levels, lanes)
@@ -623,7 +608,7 @@
         ],
         compiler_params=pltpu.CompilerParams(vmem_limit_bytes=28 * MIB),
         cost_estimate=pl.CostEstimate(
-            flops=60 * levels * cells, bytes_accessed=200 * levels * cells, transcendentals=0
+            flops=60 * levels * cells, bytes_accessed=20000 * levels * cells, transcendentals=0
         ),
     )(
         in_hbm(ocean_state),
@@ -664,12 +649,9 @@
     surface, result = pl.pallas_call(
         finish_kernel,
         out_shape=(shaped((3, columns, lanes), f32), shaped(ocean_state.shape, f32)),
-        in_specs=[smem] + [vmem] * 2 + [hbm] * 3 + [vmem],
+        in_specs=[smem] + [vmem] * 6,
         out_specs=(vmem, hbm),
         scratch_shapes=[
-            pltpu.VMEM((tracers, levels, rows, lanes), f32),
-            pltpu.VMEM((levels, columns, lanes), bf16),
-            pltpu.VMEM((rows, lanes), i32),
             pltpu.VMEM(ocean_state.shape, f32),
             pltpu.VMEM((tracers, levels, tall_rows, lanes), bf16),
             pltpu.VMEM((levels, columns, lanes), f32),
@@ -677,10 +659,9 @@
             pltpu.VMEM(ocean_state.shape, f32),
             pltpu.VMEM((tall_rows, lanes), bf16),
             pltpu.VMEM((lanes, lanes), bf16),
-            pltpu.SemaphoreType.DMA((pieces + 1, 2)),
             pltpu.SemaphoreType.DMA((pieces,)),
         ],
-        compiler_params=pltpu.CompilerParams(vmem_limit_bytes=36 * MIB),
+        compiler_params=pltpu.CompilerParams(vmem_limit_bytes=26 * MIB),
         cost_estimate=pl.CostEstimate(
             flops=60 * levels * cells, bytes_accessed=32 * levels * cells, transcendentals=0
         ),
@@ -688,9 +669,9 @@
         section,
         mine,
         other,
-        in_hbm(bath),
-        in_hbm(q),
-        in_hbm(side),
+        in_vmem(bath),
+        in_vmem(q),
+        in_vmem(side),
         ratios,
     )
     return (surface[None], result)

time: 50.5 us -> 57.9 us (1.15)
  waiting for transfers between devices: 3.36 us -> 14.9 us
  blocking collectives: 10.4 us -> 0 us
  starting transfers between devices: 10.6 us -> 17.6 us
  Pallas kernels: 25 us -> 24.3 us
    all_to_all x1 -> x0, blocking collectives: 10.4 us -> none  [per_device(): lax.all_to_all(request, 'blk', split_axis=0, concat_axis=0, tiled=True)]
    all_to_all x0 -> x1, starting transfers between devices: none -> 8.32 us  [per_device(): lax.all_to_all(request, 'blk', split_axis=0, concat_axis=0, tiled=True)]
    ppermute x2, waiting for transfers between devices: 0.01 us -> 7.75 us  [shift(): lax.ppermute(value, axis, [(i, (i + by) % count) for i in range(count)])]
    all_to_all x0 -> x1, waiting for transfers between devices: none -> 5.65 us  [per_device(): lax.all_to_all(request, 'blk', split_axis=0, concat_axis=0, tiled=True)]
    all_to_all x1, waiting for transfers between devices: 1.89 us -> 0.01 us  [per_device(): lax.all_to_all(served, 'blk', split_axis=0, concat_axis=0, tiled=True)]
    pallas_call x1, Pallas kernels: 9.62 us -> 8.14 us  [per_device(): pl.pallas_call(finish_kernel, out_shape=(shaped((3, columns, lanes), f32)...]
    ppermute x2, starting transfers between devices: 7.05 us -> 5.67 us  [shift(): lax.ppermute(value, axis, [(i, (i + by) % count) for i in range(count)])]
    pallas_call x1, Pallas kernels: 1.07 us -> 1.67 us  [per_device(): pl.pallas_call(ask_kernel, out_shape=shaped((count, 128), i32), in_specs=...]
  transfers between devices with their start and end apart: 4 -> 5, of which waited for: 2 -> 4; matrix products, arithmetic and copies ran while one was open for 0% -> 0% of each run, Pallas kernels for 15% -> 14%
where the time goes in v12:
time: 57.9 us; the launch traced here: 57.5 us
  Pallas kernels  24.3 us (42%)
  starting transfers between devices  17.6 us (30%)
  waiting for transfers between devices  14.9 us (26%)
  between operations  0.74 us (1%)
    all_to_all x1, starting transfers between devices, per_device(): lax.all_to_all(request, 'blk', split_axis=0, concat_axis=0, tiled=True)  8.32 us
    pallas_call x1, Pallas kernels, per_device(): pl.pallas_call(finish_kernel, out_shape=(shaped((3, columns, lanes), f32)...  8.14 us
    ppermute x2, waiting for transfers between devices, shift(): lax.ppermute(value, axis, [(i, (i + by) % count) for i in range(count)])  7.75 us
    pallas_call x1, Pallas kernels, per_device(): pl.pallas_call(functools.partial(start_kernel, count=count), out_shape=(p...  6.43 us
    ppermute x2, starting transfers between devices, shift(): lax.ppermute(value, axis, [(i, (i + by) % count) for i in range(count)])  5.67 us
    all_to_all x1, waiting for transfers between devices, per_device(): lax.all_to_all(request, 'blk', split_axis=0, concat_axis=0, tiled=True)  5.65 us
    pallas_call x1, Pallas kernels, per_device(): pl.pallas_call(remap_kernel, out_shape=shaped((6, rows, lanes), f32), in_...  5.25 us
    all_to_all x1, starting transfers between devices, per_device(): lax.all_to_all(served, 'blk', split_axis=0, concat_axis=0, tiled=True)  3.53 us
  transfers between devices with their start and end apart: 5, of which 4 were waited for; matrix products, arithmetic and copies ran while one was open for 0% of the time, Pallas kernels for 14%

profile of v12, /device:TPU:0, one launch (start us, length us, event | category | flops | bytes accessed | tf_op | source)
XLA Modules:
  0.0 57.5 jit_solution(783842907302093570)
XLA Ops:
  0.6 1.7 %shard_map.86 = s32[16,128]{1,0:T(8,128)} custom-call(s32[4,64]{1,0:T(4,128)} %bitcast.22, s32[4,64]{1,0:T(4,128)} %bitcast.25), custom_call_target="tpu_custom_call" | custom-call | flops 1000000 | bytes 100000 | tf_op jit(solution)/shard_map/pallas_call | solution.py:522
  2.3 8.3 %all-to-all-start = ((s32[16,1,128]{2,1,0:T(1,128)}), s32[16,1,128]{2,1,0:T(1,128)S(1)}, u32[]{:S(2)}, u32[]{:S(2)}) async-start(s32[16,1,128]{2,1,0:T(1,128)} %bitcast.6), calls=%async_computation | async-start | bytes 16384 | tf_op jit(solution)/shard_map/all_to_all | solution.py:535
  10.6 0.0 copy-start.3
  10.7 1.5 %shard_map.87 = (bf16[848,128]{1,0:T(8,128)(2,1)S(1)}, bf16[848,128]{1,0:T(8,128)(2,1)S(1)}, bf16[192,128]{1,0:T(8,128)(2,1)S(1)}) custom-call(s32[1]{0:T(128)} %bitcast.section, f32[2,80,64,128]{3,2,1,0:T(8,128)} %state.3, s32[64,128]{1,0:T(8,128)} %bath.3, bf16[3,64,128]{2,1,0:T(8,128)(2,1)} %bitcast.20, s32[4,64]{1,0:T(4,128)} %bitcast.23, ...), custom_call_target="tpu_custom_call" | custom-call | flops 1000000 | bytes 4000000 | tf_op jit(solution)/shard_map/pallas_call | solution.py:538
  12.2 5.6 %all-to-all-done = s32[16,1,128]{2,1,0:T(1,128)S(1)} async-done(((s32[16,1,128]{2,1,0:T(1,128)}), s32[16,1,128]{2,1,0:T(1,128)S(1)}, u32[]{:S(2)}, u32[]{:S(2)}) %all-to-all-start) | async-done | bytes 8224 | tf_op jit(solution)/shard_map/all_to_all | solution.py:535
  17.8 1.3 %shard_map.88 = bf16[896,128]{1,0:T(8,128)(2,1)} custom-call(s32[16,128]{1,0:T(8,128)S(1)} %bitcast.17, bf16[192,128]{1,0:T(8,128)(2,1)S(1)} %get-tuple-element.11.table), custom_call_target="tpu_custom_call" | custom-call | flops 10000000 | bytes 1000000 | tf_op jit(solution)/shard_map/pallas_call | solution.py:572
  19.1 3.5 %all-to-all-start.1 = ((bf16[16,56,128]{2,1,0:T(8,128)(2,1)}), bf16[16,56,128]{2,1,0:T(8,128)(2,1)S(1)}, u32[]{:S(2)}, u32[]{:S(2)}) async-start(bf16[16,56,128]{2,1,0:T(8,128)(2,1)} %bitcast.11), calls=%async_computation.1 | async-start | bytes 458752 | tf_op jit(solution)/shard_map/all_to_all | solution.py:582
  22.7 1.8 %collective-permute-start = (bf16[848,128]{1,0:T(8,128)(2,1)S(1)}, bf16[848,128]{1,0:T(8,128)(2,1)S(1)}, u32[]{:S(2)}, u32[]{:S(2)}) collective-permute-start(bf16[848,128]{1,0:T(8,128)(2,1)S(1)} %get-tuple-element.12), channel_id=1, source_target_pairs={{0,1},{1,2},{2,3},{3,4},{4,5},{5,6},{6,7},{7,8},{8,9},{9,10},{10,1... | collective-permute-start | bytes 651272 | tf_op jit(solution)/shard_map/ppermute | solution.py:488
  24.5 3.9 %collective-permute-start.1 = (bf16[848,128]{1,0:T(8,128)(2,1)S(1)}, bf16[848,128]{1,0:T(8,128)(2,1)S(1)}, u32[]{:S(2)}, u32[]{:S(2)}) collective-permute-start(bf16[848,128]{1,0:T(8,128)(2,1)S(1)} %get-tuple-element.13), channel_id=1, source_target_pairs={{0,15},{1,0},{2,1},{3,2},{4,3},{5,4},{6,5},{7,6},{8,7},{9,8},{10,9... | collective-permute-start | bytes 651272 | tf_op jit(solution)/shard_map/ppermute | solution.py:488
  28.3 7.4 %collective-permute-done.from_left = bf16[848,128]{1,0:T(8,128)(2,1)S(1)} collective-permute-done((bf16[848,128]{1,0:T(8,128)(2,1)S(1)}, bf16[848,128]{1,0:T(8,128)(2,1)S(1)}, u32[]{:S(2)}, u32[]{:S(2)}) %collective-permute-start) | collective-permute-done | bytes 217120 | tf_op jit(solution)/shard_map/ppermute | solution.py:488
  35.7 0.4 collective-permute-done.1.from_right
  36.1 0.0 copy-done.3
  36.1 6.4 %shard_map.89 = (f32[2,80,72,128]{3,2,1,0:T(8,128)}, bf16[80,64,128]{2,1,0:T(8,128)(2,1)}, s32[72,128]{1,0:T(8,128)}, s32[256,128]{1,0:T(8,128)}) custom-call(f32[2,80,64,128]{3,2,1,0:T(8,128)} %state.3, bf16[848,128]{1,0:T(8,128)(2,1)S(1)} %collective-permute-done.from_left, bf16[848,128]{1,0:T(8,128)(2,1)S(1)} %collective-permute-done.1.from_right, ...), custom_call_target="tpu_custom_call" | custom-call | flops 44236800 | bytes 14745600000 | tf_op jit(solution)/shard_map/pallas_call | solution.py:585
  42.5 0.0 copy-start.1
  42.5 0.0 copy-start.2
  42.6 0.0 all-to-all-done.1
  42.6 0.0 copy-start
  42.6 5.3 %shard_map.90.mine = f32[6,72,128]{2,1,0:T(8,128)S(1)} custom-call(bf16[896,128]{1,0:T(8,128)(2,1)S(1)} %bitcast.16, s32[256,128]{1,0:T(8,128)} %get-tuple-element.14.place_from, bf16[848,128]{1,0:T(8,128)(2,1)S(1)} %collective-permute-done.from_left, bf16[848,128]{1,0:T(8,128)(2,1)S(1)} %collective-permute-done.1.from_right, bf16[32768,128]{1,0:T(8,128)(2,1)} %bitcast.19, ...), custom_call_target="tpu_custom_call" | custom-call | flops 67108864 | bytes 8388608 | tf_op jit(solution)/shard_map/pallas_call | solution.py:622
  47.8 0.1 collective-permute-start.2
  47.9 1.5 %collective-permute-done.2.other = f32[6,72,128]{2,1,0:T(8,128)S(1)} collective-permute-done((f32[6,72,128]{2,1,0:T(8,128)S(1)}, f32[6,72,128]{2,1,0:T(8,128)S(1)}, u32[]{:S(2)}, u32[]{:S(2)}) %collective-permute-start.2) | collective-permute-done | bytes 221216 | tf_op jit(solution)/shard_map/ppermute | solution.py:647
  49.4 0.0 copy-done.1
  49.4 0.0 copy-done.2
  49.4 0.0 copy-done
  49.4 8.1 %shard_map.91 = (f32[3,64,128]{2,1,0:T(8,128)}, f32[2,80,64,128]{3,2,1,0:T(8,128)}) custom-call(s32[1]{0:T(128)} %bitcast.section, f32[6,72,128]{2,1,0:T(8,128)S(1)} %shard_map.90.mine, f32[6,72,128]{2,1,0:T(8,128)S(1)} %collective-permute-done.2.other, s32[72,128]{1,0:T(8,128)S(1)} %copy-done.2, f32[2,80,72,128]{3,2,1,0:T(8,128)S(1)} %copy-done, ...), custom_call_target="tpu_custom_call" | custom-call | flops 44236800 | bytes 23592960 | tf_op jit(solution)/shard_map/pallas_call | solution.py:649
  (1 shorter events, 0.0 us)
Async XLA Ops:
  2.3 15.5 %all-to-all-start = ((s32[16,1,128]{2,1,0:T(1,128)}), s32[16,1,128]{2,1,0:T(1,128)S(1)}, u32[]{:S(2)}, u32[]{:S(2)}) async-start(s32[16,1,128]{2,1,0:T(1,128)} %bitcast.6), calls=%async_computation | async-start | bytes 16384 | tf_op jit(solution)/shard_map/all_to_all | solution.py:535
  10.6 25.4 %copy-start.3 = (f32[128]{0:T(128)S(1)}, f32[128]{0:T(128)}, u32[]{:S(2)}) copy-start(f32[128]{0:T(128)} %constant.8.clone) | copy-start | bytes 1540
  19.1 23.4 %all-to-all-start.1 = ((bf16[16,56,128]{2,1,0:T(8,128)(2,1)}), bf16[16,56,128]{2,1,0:T(8,128)(2,1)S(1)}, u32[]{:S(2)}, u32[]{:S(2)}) async-start(bf16[16,56,128]{2,1,0:T(8,128)(2,1)} %bitcast.11), calls=%async_computation.1 | async-start | bytes 458752 | tf_op jit(solution)/shard_map/all_to_all | solution.py:582
  22.7 13.1 %collective-permute-start = (bf16[848,128]{1,0:T(8,128)(2,1)S(1)}, bf16[848,128]{1,0:T(8,128)(2,1)S(1)}, u32[]{:S(2)}, u32[]{:S(2)}) collective-permute-start(bf16[848,128]{1,0:T(8,128)(2,1)S(1)} %get-tuple-element.12), channel_id=1, source_target_pairs={{0,1},{1,2},{2,3},{3,4},{4,5},{5,6},{6,7},{7,8},{8,9},{9,10},{10,1... | collective-permute-start | bytes 651272 | tf_op jit(solution)/shard_map/ppermute | solution.py:488
  24.5 11.6 %collective-permute-start.1 = (bf16[848,128]{1,0:T(8,128)(2,1)S(1)}, bf16[848,128]{1,0:T(8,128)(2,1)S(1)}, u32[]{:S(2)}, u32[]{:S(2)}) collective-permute-start(bf16[848,128]{1,0:T(8,128)(2,1)S(1)} %get-tuple-element.13), channel_id=1, source_target_pairs={{0,15},{1,0},{2,1},{3,2},{4,3},{5,4},{6,5},{7,6},{8,7},{9,8},{10,9... | collective-permute-start | bytes 651272 | tf_op jit(solution)/shard_map/ppermute | solution.py:488
  42.5 6.9 %copy-start.1 = (bf16[80,64,128]{2,1,0:T(8,128)(2,1)S(1)}, bf16[80,64,128]{2,1,0:T(8,128)(2,1)}, u32[]{:S(2)}) copy-start(bf16[80,64,128]{2,1,0:T(8,128)(2,1)} %get-tuple-element.17.side) | copy-start | bytes 3932164
  42.5 6.8 %copy-start.2 = (s32[72,128]{1,0:T(8,128)S(1)}, s32[72,128]{1,0:T(8,128)}, u32[]{:S(2)}) copy-start(s32[72,128]{1,0:T(8,128)} %get-tuple-element.15.bath) | copy-start | bytes 110596
  42.6 6.8 %copy-start = (f32[2,80,72,128]{3,2,1,0:T(8,128)S(1)}, f32[2,80,72,128]{3,2,1,0:T(8,128)}, u32[]{:S(2)}) copy-start(f32[2,80,72,128]{3,2,1,0:T(8,128)} %get-tuple-element.16.q) | copy-start | bytes 17694724
  47.8 1.5 %collective-permute-start.2 = (f32[6,72,128]{2,1,0:T(8,128)S(1)}, f32[6,72,128]{2,1,0:T(8,128)S(1)}, u32[]{:S(2)}, u32[]{:S(2)}) collective-permute-start(f32[6,72,128]{2,1,0:T(8,128)S(1)} %shard_map.90.mine), channel_id=1, source_target_pairs={{0,16},{16,0},{1,17},{17,1},{2,18},{18,2},{3,19},{19,3},{4,20},{20... | collective-permute-start | bytes 663560 | tf_op jit(solution)/shard_map/ppermute | solution.py:647

commit v13 on v12

--- a/solution.py
+++ b/solution.py
@@ -21,6 +21,7 @@
 EDGE = 8
 EXTRA = 16
 IN_FLIGHT = 3
+GROUP = 5
 MIB = 2**20
 bf16, f32, i32 = jnp.bfloat16, jnp.float32, jnp.int32
 
@@ -69,14 +70,14 @@
     return carry
 
 
-def ranks(blocks, count):
+def ranks(blocks, count, block_of=lambda row: row):
     slots, columns = blocks.shape
     before = jnp.where(iota((columns, columns), 0) < iota((columns, columns), 1), 1.0, 0.0)
     before = before.astype(bf16)
     used = jnp.zeros((count, 1), f32)
     result = []
     for k in range(slots):
-        owner = iota((count, columns), 0) == blocks[k : k + 1, :]
+        owner = block_of(iota((count, columns), 0)) == blocks[k : k + 1, :]
         one_hot = jnp.where(owner, 1.0, 0.0)
         earlier = used + jnp.dot(one_hot.astype(bf16), before, preferred_element_type=f32)
         rank = jnp.sum(one_hot * earlier, axis=0, keepdims=True)
@@ -101,7 +102,10 @@
     here = iota((128, columns), 1)
     marks = ((slot == MOST) & (here == 0)) | ((slot == MOST + 1) & (here == columns - 1))
     asked = jnp.zeros(request.shape, f32)
-    for k, (owner, rank) in enumerate(ranks(blocks_in, count)):
+    inner = inner_of(count)
+    outer = count // inner
+    listed = ranks(blocks_in, count, lambda row: lax.rem(row, outer) * inner + row // outer)
+    for k, (owner, rank) in enumerate(listed):
         filled = jnp.where((slot == rank.astype(i32)) | marks, 1.0, 0.0).astype(bf16)
         named = jnp.where(owner, spots_in[k : k + 1, :].astype(f32), 0.0).astype(bf16)
         asked = asked + lax.dot_general(
@@ -163,7 +167,7 @@
     copies[7].wait()
 
 
-def serve_kernel(asked, table, out):
+def serve_kernel(asked, table, from_left, from_right, out):
     count = asked.shape[0]
     wanted = jnp.transpose(asked[...].astype(f32))[:PIECE]
     height = table.shape[0]
@@ -429,26 +433,41 @@
 
     sweep(levels - 2, functools.partial(down, low=2), carry)
 
-    def halves_at(level):
-        own = side[level].astype(f32)
-        out = []
-        for n in range(tracers):
-            around = neighbour_sum(rounded_at[n, level], across, band, columns)
-            out.append(own * values_at[n, level] + around)
-        return out
-
-    def up(step, carry):
-        level = levels - 1 - step
-        ratio = rho[level]
-        halves = halves_at(level)
-        out = [ratio * (halves[n] + carry[n]) for n in range(tracers)]
-        for n in range(tracers):
-            solved[n, level] = out[n]
-        return tuple(out)
-
-    zero = jnp.zeros((columns, lanes), f32)
-    carry = sweep(levels - 2, up, (zero,) * tracers)
-    values = top_levels(columns, list(zip(halves_at(0), halves_at(1))), carry, rho[2], SCALE * SCALE)
+    def halves_at(group):
+        stacked = [rounded_at[n, level][:columns] for level in group for n in range(tracers)]
+        along = jnp.dot(
+            jnp.concatenate(stacked, axis=0), band[...], preferred_element_type=f32
+        )
+        tall = rounded_at.shape[2]
+        result = []
+        for place, level in enumerate(group):
+            side_by_side = jnp.concatenate(
+                [rounded_at[n, level] for n in range(tracers)], axis=1
+            )
+            sums = jnp.dot(
+                across[pl.ds(0, columns), pl.ds(0, tall)],
+                side_by_side,
+                preferred_element_type=f32,
+            )
+            own = side[level].astype(f32)
+            out = []
+            for n in range(tracers):
+                first = (place * tracers + n) * columns
+                around = sums[:, n * lanes : (n + 1) * lanes] + along[first : first + columns]
+                out.append(own * values_at[n, level] + around)
+            result.append(out)
+        return result
+
+    carry = [jnp.zeros((columns, lanes), f32)] * tracers
+    top = levels - 1
+    while top >= 2:
+        group = list(range(top, max(top - GROUP, 1), -1))
+        top -= len(group)
+        for level, halves in zip(group, halves_at(group)):
+            carry = [rho[level] * (halves[n] + carry[n]) for n in range(tracers)]
+            for n in range(tracers):
+                solved[n, level] = carry[n]
+    values = top_levels(columns, list(zip(*halves_at([0, 1]))), carry, rho[2], SCALE * SCALE)
     unscale = 1.0 / (SCALE * SCALE)
     for n in range(tracers):
         surface[n] = jnp.where(on_ocean, values[n][0] * unscale, other[n, pl.ds(0, columns)])
@@ -483,6 +502,24 @@
         copy.wait()
 
 
+def inner_of(count):
+    inner = 1
+    while inner * inner < count:
+        inner *= 2
+    return inner
+
+
+def exchange_requests(value, axis):
+    count = lax.axis_size(axis)
+    inner = inner_of(count)
+    outer = count // inner
+    close = [[z * inner + w for w in range(inner)] for z in range(outer)]
+    far = [[z * inner + w for z in range(outer)] for w in range(inner)]
+    value = lax.all_to_all(value, axis, 0, 0, axis_index_groups=close, tiled=True)
+    value = jnp.swapaxes(value.reshape(inner, outer, -1), 0, 1).reshape(value.shape)
+    return lax.all_to_all(value, axis, 0, 0, axis_index_groups=far, tiled=True)
+
+
 def shift(value, axis, by):
     count = lax.axis_size(axis)
     return lax.ppermute(value, axis, [(i, (i + by) % count) for i in range(count)])
@@ -532,7 +569,7 @@
         compiler_params=pltpu.CompilerParams(vmem_limit_bytes=4 * MIB),
         cost_estimate=pl.CostEstimate(flops=10**6, bytes_accessed=10**5, transcendentals=0),
     )(in_hbm(blocks), in_hbm(spots))
-    asked = lax.all_to_all(request, "blk", split_axis=0, concat_axis=0, tiled=True)
+    asked = exchange_requests(request, "blk")
 
     payload = shaped((2 * many + EXTRA + tall, lanes), bf16)
     to_left, to_right, table = pl.pallas_call(
@@ -572,13 +609,13 @@
     served = pl.pallas_call(
         serve_kernel,
         out_shape=shaped((count * PIECE, lanes), bf16),
-        in_specs=[vmem] * 2,
+        in_specs=[vmem] * 4,
         out_specs=vmem,
         compiler_params=pltpu.CompilerParams(vmem_limit_bytes=8 * MIB),
         cost_estimate=pl.CostEstimate(
             flops=10**7, bytes_accessed=10**6, transcendentals=0
         ),
-    )(asked, table)
+    )(asked, table, from_left, from_right)
     columns_in = lax.all_to_all(served, "blk", split_axis=0, concat_axis=0, tiled=True)
 
     ratios = ratios_by_height(levels, lanes)
@@ -608,7 +645,7 @@
         ],
         compiler_params=pltpu.CompilerParams(vmem_limit_bytes=28 * MIB),
         cost_estimate=pl.CostEstimate(
-            flops=60 * levels * cells, bytes_accessed=20000 * levels * cells, transcendentals=0
+            flops=60 * levels * cells, bytes_accessed=200 * levels * cells, transcendentals=0
         ),
     )(
         in_hbm(ocean_state),

time: 57.9 us -> 56.1 us (0.969)
  blocking collectives: 0 us -> 17.2 us
  waiting for transfers between devices: 14.9 us -> 3.3 us
  starting transfers between devices: 17.6 us -> 10.6 us
    all_to_all x0 -> x2, blocking collectives: none -> 17.2 us  [the longest x1 9.88 us: exchange_requests(): return lax.all_to_all(value, axis, 0, 0, axis_index_groups=far, tiled=True)]
    all_to_all x1 -> x0, starting transfers between devices: 8.32 us -> none  [per_device(): lax.all_to_all(request, 'blk', split_axis=0, concat_axis=0, tiled=True)]
    ppermute x2, waiting for transfers between devices: 7.75 us -> 0.01 us  [shift(): lax.ppermute(value, axis, [(i, (i + by) % count) for i in range(count)])]
    all_to_all x1 -> x0, waiting for transfers between devices: 5.65 us -> none  [per_device(): lax.all_to_all(request, 'blk', split_axis=0, concat_axis=0, tiled=True)]
    all_to_all x1, waiting for transfers between devices: 0.01 us -> 1.83 us  [per_device(): lax.all_to_all(served, 'blk', split_axis=0, concat_axis=0, tiled=True)]
    ppermute x2, starting transfers between devices: 5.67 us -> 7.05 us  [shift(): lax.ppermute(value, axis, [(i, (i + by) % count) for i in range(count)])]
    pallas_call x1, Pallas kernels: 1.67 us -> 1.08 us  [per_device(): pl.pallas_call(ask_kernel, out_shape=shaped((count, 128), i32), in_specs=...]
  transfers between devices with their start and end apart: 5 -> 4, of which waited for: 4 -> 2; matrix products, arithmetic and copies ran while one was open for 0% -> 0% of each run, Pallas kernels for 14% -> 13%
where the time goes in v13:
time: 56.1 us; the launch traced here: 55.7 us
  Pallas kernels  23.8 us (42%)
  blocking collectives  17.2 us (31%)
  starting transfers between devices  10.6 us (19%)
  waiting for transfers between devices  3.3 us (6%)
  between operations  0.73 us (1%)
    all_to_all x1, blocking collectives, exchange_requests(): return lax.all_to_all(value, axis, 0, 0, axis_index_groups=far, tiled=True)  9.88 us
    pallas_call x1, Pallas kernels, per_device(): pl.pallas_call(finish_kernel, out_shape=(shaped((3, columns, lanes), f32)...  8.16 us
    all_to_all x1, blocking collectives, exchange_requests(): lax.all_to_all(value, axis, 0, 0, axis_index_groups=close, tiled=True)  7.33 us
    ppermute x2, starting transfers between devices, shift(): lax.ppermute(value, axis, [(i, (i + by) % count) for i in range(count)])  7.05 us
    pallas_call x1, Pallas kernels, per_device(): pl.pallas_call(functools.partial(start_kernel, count=count), out_shape=(p...  6.44 us
    pallas_call x1, Pallas kernels, per_device(): pl.pallas_call(remap_kernel, out_shape=shaped((6, rows, lanes), f32), in_...  5.26 us
    all_to_all x1, starting transfers between devices, per_device(): lax.all_to_all(served, 'blk', split_axis=0, concat_axis=0, tiled=True)  3.53 us
    all_to_all x1, waiting for transfers between devices, per_device(): lax.all_to_all(served, 'blk', split_axis=0, concat_axis=0, tiled=True)  1.83 us
  transfers between devices with their start and end apart: 4, of which 2 were waited for; matrix products, arithmetic and copies ran while one was open for 0% of the time, Pallas kernels for 13%

profile of v13, /device:TPU:0, one launch (start us, length us, event | category | flops | bytes accessed | tf_op | source)
XLA Modules:
  0.0 55.7 jit_solution(5644343760588444147)
XLA Ops:
  0.6 0.0 copy-start.3
  0.6 1.5 %shard_map.87 = (bf16[848,128]{1,0:T(8,128)(2,1)S(1)}, bf16[848,128]{1,0:T(8,128)(2,1)S(1)}, bf16[192,128]{1,0:T(8,128)(2,1)S(1)}) custom-call(s32[1]{0:T(128)} %bitcast.section, f32[2,80,64,128]{3,2,1,0:T(8,128)} %state.3, s32[64,128]{1,0:T(8,128)} %bath.3, bf16[3,64,128]{2,1,0:T(8,128)(2,1)} %bitcast.20, s32[4,64]{1,0:T(4,128)} %bitcast.23, ...), custom_call_target="tpu_custom_call" | custom-call | flops 1000000 | bytes 4000000 | tf_op jit(solution)/shard_map/pallas_call | solution.py:575
  2.2 3.0 %collective-permute-start = (bf16[848,128]{1,0:T(8,128)(2,1)S(1)}, bf16[848,128]{1,0:T(8,128)(2,1)S(1)}, u32[]{:S(2)}, u32[]{:S(2)}) collective-permute-start(bf16[848,128]{1,0:T(8,128)(2,1)S(1)} %get-tuple-element.12), channel_id=1, source_target_pairs={{0,1},{1,2},{2,3},{3,4},{4,5},{5,6},{6,7},{7,8},{8,9},{9,10},{10,1... | collective-permute-start | bytes 651272 | tf_op jit(solution)/shard_map/ppermute | solution.py:525
  5.2 4.1 %collective-permute-start.1 = (bf16[848,128]{1,0:T(8,128)(2,1)S(1)}, bf16[848,128]{1,0:T(8,128)(2,1)S(1)}, u32[]{:S(2)}, u32[]{:S(2)}) collective-permute-start(bf16[848,128]{1,0:T(8,128)(2,1)S(1)} %get-tuple-element.13), channel_id=1, source_target_pairs={{0,15},{1,0},{2,1},{3,2},{4,3},{5,4},{6,5},{7,6},{8,7},{9,8},{10,9... | collective-permute-start | bytes 651272 | tf_op jit(solution)/shard_map/ppermute | solution.py:525
  9.2 1.1 %shard_map.86 = s32[16,128]{1,0:T(8,128)S(1)} custom-call(s32[4,64]{1,0:T(4,128)} %bitcast.24, s32[4,64]{1,0:T(4,128)} %bitcast.26), custom_call_target="tpu_custom_call" | custom-call | flops 1000000 | bytes 100000 | tf_op jit(solution)/shard_map/pallas_call | solution.py:559
  10.3 7.3 %all_to_all.28 = s32[4,4,128]{2,1,0:T(4,128)S(1)} all-to-all(s32[4,4,128]{2,1,0:T(4,128)S(1)} %bitcast.17), channel_id=1, replica_groups={{0,1,2,3},{4,5,6,7},{8,9,10,11},{12,13,14,15},{16,17,18,19},{20,21,22,2..., dimensions={0} | all-to-all | bytes 16384 | tf_op jit(solution)/shard_map/all_to_all | solution.py:518
  17.6 9.9 %all_to_all.29 = s32[4,4,128]{2,1,0:T(4,128)S(1)} all-to-all(s32[4,4,128]{2,1,0:T(4,128)S(1)} %copy.11), channel_id=1, replica_groups={{0,4,8,12},{1,5,9,13},{2,6,10,14},{3,7,11,15},{16,20,24,28},{17,21,25,2..., dimensions={0} | all-to-all | bytes 16384 | tf_op jit(solution)/shard_map/all_to_all | solution.py:520
  27.5 0.0 collective-permute-done.from_left
  27.5 0.0 collective-permute-done.1.from_right
  27.5 1.3 %shard_map.88 = bf16[896,128]{1,0:T(8,128)(2,1)} custom-call(s32[16,128]{1,0:T(8,128)S(1)} %bitcast.16, bf16[192,128]{1,0:T(8,128)(2,1)S(1)} %get-tuple-element.11.table, bf16[848,128]{1,0:T(8,128)(2,1)S(1)} %collective-permute-done.from_left, bf16[848,128]{1,0:T(8,128)(2,1)S(1)} %collective-permute-done.1.from_right), custom_call_target="tpu_custom_call" | custom-call | flops 10000000 | bytes 1000000 | tf_op jit(solution)/shard_map/pallas_call | solution.py:609
  28.8 3.5 %all-to-all-start.2 = ((bf16[16,56,128]{2,1,0:T(8,128)(2,1)}), bf16[16,56,128]{2,1,0:T(8,128)(2,1)S(1)}, u32[]{:S(2)}, u32[]{:S(2)}) async-start(bf16[16,56,128]{2,1,0:T(8,128)(2,1)} %bitcast.11), calls=%async_computation.2 | async-start | bytes 458752 | tf_op jit(solution)/shard_map/all_to_all | solution.py:619
  32.4 0.0 copy-done.3
  32.4 6.4 %shard_map.89 = (f32[2,80,72,128]{3,2,1,0:T(8,128)}, bf16[80,64,128]{2,1,0:T(8,128)(2,1)}, s32[72,128]{1,0:T(8,128)}, s32[256,128]{1,0:T(8,128)}) custom-call(f32[2,80,64,128]{3,2,1,0:T(8,128)} %state.3, bf16[848,128]{1,0:T(8,128)(2,1)S(1)} %collective-permute-done.from_left, bf16[848,128]{1,0:T(8,128)(2,1)S(1)} %collective-permute-done.1.from_right, ...), custom_call_target="tpu_custom_call" | custom-call | flops 44236800 | bytes 147456000 | tf_op jit(solution)/shard_map/pallas_call | solution.py:622
  38.8 0.0 copy-start.1
  38.8 0.0 copy-start.2
  38.9 1.8 %all-to-all-done.2 = bf16[16,56,128]{2,1,0:T(8,128)(2,1)S(1)} async-done(((bf16[16,56,128]{2,1,0:T(8,128)(2,1)}), bf16[16,56,128]{2,1,0:T(8,128)(2,1)S(1)}, u32[]{:S(2)}, u32[]{:S(2)}) %all-to-all-start.2) | async-done | bytes 229408 | tf_op jit(solution)/shard_map/all_to_all | solution.py:619
  40.7 0.0 copy-start
  40.7 5.3 %shard_map.90.mine = f32[6,72,128]{2,1,0:T(8,128)S(1)} custom-call(bf16[896,128]{1,0:T(8,128)(2,1)S(1)} %bitcast.15, s32[256,128]{1,0:T(8,128)} %get-tuple-element.14.place_from, bf16[848,128]{1,0:T(8,128)(2,1)S(1)} %collective-permute-done.from_left, bf16[848,128]{1,0:T(8,128)(2,1)S(1)} %collective-permute-done.1.from_right, bf16[32768,128]{1,0:T(8,128)(2,1)} %bitcast.19, ...), custom_call_target="tpu_custom_call" | custom-call | flops 67108864 | bytes 8388608 | tf_op jit(solution)/shard_map/pallas_call | solution.py:659
  46.0 0.1 collective-permute-start.2
  46.0 1.5 %collective-permute-done.2.other = f32[6,72,128]{2,1,0:T(8,128)S(1)} collective-permute-done((f32[6,72,128]{2,1,0:T(8,128)S(1)}, f32[6,72,128]{2,1,0:T(8,128)S(1)}, u32[]{:S(2)}, u32[]{:S(2)}) %collective-permute-start.2) | collective-permute-done | bytes 221216 | tf_op jit(solution)/shard_map/ppermute | solution.py:684
  47.5 0.0 copy-done.1
  47.5 0.0 copy-done.2
  47.5 0.0 copy-done
  47.5 8.2 %shard_map.91 = (f32[3,64,128]{2,1,0:T(8,128)}, f32[2,80,64,128]{3,2,1,0:T(8,128)}) custom-call(s32[1]{0:T(128)} %bitcast.section, f32[6,72,128]{2,1,0:T(8,128)S(1)} %shard_map.90.mine, f32[6,72,128]{2,1,0:T(8,128)S(1)} %collective-permute-done.2.other, s32[72,128]{1,0:T(8,128)S(1)} %copy-done.2, f32[2,80,72,128]{3,2,1,0:T(8,128)S(1)} %copy-done, ...), custom_call_target="tpu_custom_call" | custom-call | flops 44236800 | bytes 23592960 | tf_op jit(solution)/shard_map/pallas_call | solution.py:686
  (2 shorter events, 0.0 us)
Async XLA Ops:
  0.6 31.7 %copy-start.3 = (f32[128]{0:T(128)S(1)}, f32[128]{0:T(128)}, u32[]{:S(2)}) copy-start(f32[128]{0:T(128)} %constant.8.clone) | copy-start | bytes 1540
  2.2 25.4 %collective-permute-start = (bf16[848,128]{1,0:T(8,128)(2,1)S(1)}, bf16[848,128]{1,0:T(8,128)(2,1)S(1)}, u32[]{:S(2)}, u32[]{:S(2)}) collective-permute-start(bf16[848,128]{1,0:T(8,128)(2,1)S(1)} %get-tuple-element.12), channel_id=1, source_target_pairs={{0,1},{1,2},{2,3},{3,4},{4,5},{5,6},{6,7},{7,8},{8,9},{9,10},{10,1... | collective-permute-start | bytes 651272 | tf_op jit(solution)/shard_map/ppermute | solution.py:525
  5.2 22.4 %collective-permute-start.1 = (bf16[848,128]{1,0:T(8,128)(2,1)S(1)}, bf16[848,128]{1,0:T(8,128)(2,1)S(1)}, u32[]{:S(2)}, u32[]{:S(2)}) collective-permute-start(bf16[848,128]{1,0:T(8,128)(2,1)S(1)} %get-tuple-element.13), channel_id=1, source_target_pairs={{0,15},{1,0},{2,1},{3,2},{4,3},{5,4},{6,5},{7,6},{8,7},{9,8},{10,9... | collective-permute-start | bytes 651272 | tf_op jit(solution)/shard_map/ppermute | solution.py:525
  28.8 11.9 %all-to-all-start.2 = ((bf16[16,56,128]{2,1,0:T(8,128)(2,1)}), bf16[16,56,128]{2,1,0:T(8,128)(2,1)S(1)}, u32[]{:S(2)}, u32[]{:S(2)}) async-start(bf16[16,56,128]{2,1,0:T(8,128)(2,1)} %bitcast.11), calls=%async_computation.2 | async-start | bytes 458752 | tf_op jit(solution)/shard_map/all_to_all | solution.py:619
  38.8 8.7 %copy-start.1 = (bf16[80,64,128]{2,1,0:T(8,128)(2,1)S(1)}, bf16[80,64,128]{2,1,0:T(8,128)(2,1)}, u32[]{:S(2)}) copy-start(bf16[80,64,128]{2,1,0:T(8,128)(2,1)} %get-tuple-element.17.side) | copy-start | bytes 3932164
  38.8 8.7 %copy-start.2 = (s32[72,128]{1,0:T(8,128)S(1)}, s32[72,128]{1,0:T(8,128)}, u32[]{:S(2)}) copy-start(s32[72,128]{1,0:T(8,128)} %get-tuple-element.15.bath) | copy-start | bytes 110596
  40.7 6.8 %copy-start = (f32[2,80,72,128]{3,2,1,0:T(8,128)S(1)}, f32[2,80,72,128]{3,2,1,0:T(8,128)}, u32[]{:S(2)}) copy-start(f32[2,80,72,128]{3,2,1,0:T(8,128)} %get-tuple-element.16.q) | copy-start | bytes 17694724
  46.0 1.5 %collective-permute-start.2 = (f32[6,72,128]{2,1,0:T(8,128)S(1)}, f32[6,72,128]{2,1,0:T(8,128)S(1)}, u32[]{:S(2)}, u32[]{:S(2)}) collective-permute-start(f32[6,72,128]{2,1,0:T(8,128)S(1)} %shard_map.90.mine), channel_id=1, source_target_pairs={{0,16},{16,0},{1,17},{17,1},{2,18},{18,2},{3,19},{19,3},{4,20},{20... | collective-permute-start | bytes 663560 | tf_op jit(solution)/shard_map/ppermute | solution.py:684

commit v14 on v12

--- a/solution.py
+++ b/solution.py
@@ -163,7 +163,7 @@
     copies[7].wait()
 
 
-def serve_kernel(asked, table, out):
+def serve_kernel(asked, table, from_left, from_right, out):
     count = asked.shape[0]
     wanted = jnp.transpose(asked[...].astype(f32))[:PIECE]
     height = table.shape[0]
@@ -376,109 +376,74 @@
     values_at, rounded_at, rho, solved, done, across, band, sems_out,
 ):
     tracers, levels, columns, lanes = result.shape
-    rows = columns + EDGE
     chunks = chunks_of(levels)
     on_ocean = section[0] == 1
-    adjacency(across, band, rows)
+    adjacency(across, band, columns + EDGE)
     flux = [jnp.where(on_ocean, other[f], mine[f]) for f in range(3)]
     own = [jnp.where(on_ocean, mine[3 + f], other[3 + f]) for f in range(3)]
     forcing = [flux[0] + own[0], flux[1] + own[1]]
     top_mix = TOP_MIX * (1.0 + flux[2] * flux[2] + own[2] * own[2])
     depth = bath[...]
-
-    def top_levels(count, halves, below, rho_below, scale):
-        wet = 1 < depth[:count]
-        link = jnp.where(wet, top_mix[:count], 0.0)
-        deeper = jnp.where(2 < depth[:count], DEEP_MIX - DEEP_MIX * rho_below, 0.0)
-        second = 1.0 / (1.0 + link + deeper)
-        rho_second = link * second
-        first = 1.0 / (1.0 + link - link * rho_second)
-        values = []
-        for n in range(tracers):
-            partial = 2.0 * (halves[n][1] + below[n]) * second
-            source = 2.0 * halves[n][0] + scale * FLUX_GAIN * forcing[n][:count]
-            surface_value = (source + link * partial) * first
-            next_value = jnp.where(wet, partial, 0.0) + rho_second * surface_value
-            values.append((surface_value, next_value))
-        return values
-
-    def put(level, values):
-        for n, h in enumerate(values):
-            values_at[n, level] = h[:columns]
-            rounded_at[n, level] = rounded(h)
-
-    values = top_levels(
-        rows,
-        [(q[n, 0], q[n, 1]) for n in range(tracers)],
-        [jnp.where(2 < depth, q[n, 2], 0.0) for n in range(tracers)],
-        ratio_at(ratios, depth, 2),
-        SCALE,
-    )
-    put(0, [jnp.where(0 < depth, values[n][0], 0.0) for n in range(tracers)])
-    carry = tuple(values[n][1] for n in range(tracers))
-    put(1, carry)
-
-    def down(step, carry, low):
-        level = low + step
-        ratio = ratio_at(ratios, bath[...], level)
-        rho[level] = ratio[:columns]
-        wet = level < bath[...]
-        out = [jnp.where(wet, q[n, level], 0.0) + ratio * carry[n] for n in range(tracers)]
-        put(level, out)
-        return tuple(out)
-
-    sweep(levels - 2, functools.partial(down, low=2), carry)
-
-    def halves_at(level):
-        own = side[level].astype(f32)
-        out = []
-        for n in range(tracers):
-            around = neighbour_sum(rounded_at[n, level], across, band, columns)
-            out.append(own * values_at[n, level] + around)
-        return out
-
-    def up(step, carry):
-        level = levels - 1 - step
-        ratio = rho[level]
-        halves = halves_at(level)
-        out = [ratio * (halves[n] + carry[n]) for n in range(tracers)]
-        for n in range(tracers):
-            solved[n, level] = out[n]
-        return tuple(out)
-
-    zero = jnp.zeros((columns, lanes), f32)
-    carry = sweep(levels - 2, up, (zero,) * tracers)
-    values = top_levels(columns, list(zip(halves_at(0), halves_at(1))), carry, rho[2], SCALE * SCALE)
     unscale = 1.0 / (SCALE * SCALE)
+
+    rho[2] = ratio_at(ratios, depth, 2)
+    link = jnp.where(1 < depth, top_mix, 0.0)
+    deeper = jnp.where(2 < depth, DEEP_MIX - DEEP_MIX * rho[2], 0.0)
+    second = 1.0 / (1.0 + link + deeper)
+    rho_second = link * second
+    first = 1.0 / (1.0 + link - link * rho_second)
+
+    def top_levels(n, count, halves, below, scale):
+        partial = 2.0 * (halves[1] + below) * second[:count]
+        source = 2.0 * halves[0] + scale * FLUX_GAIN * forcing[n][:count]
+        value = (source + link[:count] * partial) * first[:count]
+        below = jnp.where(1 < depth[:count], partial, 0.0) + rho_second[:count] * value
+        return value, below
+
+    def put(n, level, h):
+        values_at[n, level] = h[:columns]
+        rounded_at[n, level] = rounded(h)
+
+    def half_at(n, level):
+        around = neighbour_sum(rounded_at[n, level], across, band, columns)
+        return side[level].astype(f32) * values_at[n, level] + around
+
+    leaving = []
     for n in range(tracers):
-        surface[n] = jnp.where(on_ocean, values[n][0] * unscale, other[n, pl.ds(0, columns)])
+        below = jnp.where(2 < depth, q[n, 2], 0.0)
+        value, carry = top_levels(n, columns + EDGE, (q[n, 0], q[n, 1]), below, SCALE)
+        put(n, 0, jnp.where(0 < depth, value, 0.0))
+        put(n, 1, carry)
+        for level in range(2, levels):
+            if n == 0 and level > 2:
+                rho[level] = ratio_at(ratios, depth, level)
+            carry = jnp.where(level < depth, q[n, level], 0.0) + rho[level] * carry
+            put(n, level, carry)
+
+        carry = jnp.zeros((columns, lanes), f32)
+        for level in range(levels - 1, 1, -1):
+            carry = rho[level, pl.ds(0, columns)] * (half_at(n, level) + carry)
+            solved[n, level] = carry
+
+        value, carry = top_levels(
+            n, columns, (half_at(n, 0), half_at(n, 1)), carry, SCALE * SCALE
+        )
+        surface[n] = jnp.where(on_ocean, value * unscale, other[n, pl.ds(0, columns)])
+        done[n, 0] = value * unscale
+        for low, size in chunks:
+            for level in range(max(low, 1), low + size):
+                if level > 1:
+                    carry = solved[n, level] + rho[level, pl.ds(0, columns)] * carry
+                start = q[n, level, pl.ds(0, columns)]
+                done[n, level] = jnp.where(level < depth[:columns], carry * unscale, start)
+            part = pl.ds(low, size)
+            leaving.append(
+                pltpu.make_async_copy(
+                    done.at[n, part], result.at[n, part], sems_out.at[len(leaving)]
+                )
+            )
+            leaving[-1].start()
     surface[2] = jnp.where(on_ocean, top_mix[:columns], other[2, pl.ds(0, columns)])
-
-    def last(step, carry, low):
-        level = low + step
-        ratio = rho[level]
-        wet = level < bath[pl.ds(0, columns)]
-        out = []
-        for n in range(tracers):
-            h = solved[n, level] + ratio * carry[n]
-            done[n, level] = jnp.where(wet, h * unscale, q[n, level, pl.ds(0, columns)])
-            out.append(h)
-        return tuple(out)
-
-    wet = 1 < depth[:columns]
-    for n in range(tracers):
-        done[n, 0] = values[n][0] * unscale
-        done[n, 1] = jnp.where(wet, values[n][1] * unscale, q[n, 1, pl.ds(0, columns)])
-    carry = tuple(values[n][1] for n in range(tracers))
-    leaving = []
-    for n, (low, size) in enumerate(chunks):
-        first = max(low, 2)
-        carry = sweep(low + size - first, functools.partial(last, low=first), carry)
-        part = pl.ds(low, size)
-        leaving.append(
-            pltpu.make_async_copy(done.at[:, part], result.at[:, part], sems_out.at[n])
-        )
-        leaving[-1].start()
     for copy in leaving:
         copy.wait()
 
@@ -572,13 +537,13 @@
     served = pl.pallas_call(
         serve_kernel,
         out_shape=shaped((count * PIECE, lanes), bf16),
-        in_specs=[vmem] * 2,
+        in_specs=[vmem] * 4,
         out_specs=vmem,
         compiler_params=pltpu.CompilerParams(vmem_limit_bytes=8 * MIB),
         cost_estimate=pl.CostEstimate(
             flops=10**7, bytes_accessed=10**6, transcendentals=0
         ),
-    )(asked, table)
+    )(asked, table, from_left, from_right)
     columns_in = lax.all_to_all(served, "blk", split_axis=0, concat_axis=0, tiled=True)
 
     ratios = ratios_by_height(levels, lanes)
@@ -608,7 +573,7 @@
         ],
         compiler_params=pltpu.CompilerParams(vmem_limit_bytes=28 * MIB),
         cost_estimate=pl.CostEstimate(
-            flops=60 * levels * cells, bytes_accessed=20000 * levels * cells, transcendentals=0
+            flops=60 * levels * cells, bytes_accessed=200 * levels * cells, transcendentals=0
         ),
     )(
         in_hbm(ocean_state),
@@ -654,12 +619,12 @@
         scratch_shapes=[
             pltpu.VMEM(ocean_state.shape, f32),
             pltpu.VMEM((tracers, levels, tall_rows, lanes), bf16),
-            pltpu.VMEM((levels, columns, lanes), f32),
+            pltpu.VMEM((levels, rows, lanes), f32),
             pltpu.VMEM(ocean_state.shape, f32),
             pltpu.VMEM(ocean_state.shape, f32),
             pltpu.VMEM((tall_rows, lanes), bf16),
             pltpu.VMEM((lanes, lanes), bf16),
-            pltpu.SemaphoreType.DMA((pieces,)),
+            pltpu.SemaphoreType.DMA((tracers * pieces,)),
         ],
         compiler_params=pltpu.CompilerParams(vmem_limit_bytes=26 * MIB),
         cost_estimate=pl.CostEstimate(

time: 57.9 us -> 49.1 us (0.85)
  waiting for transfers between devices: 14.9 us -> 3.3 us
  blocking collectives: 0 us -> 10.4 us
  starting transfers between devices: 17.6 us -> 10.6 us
  Pallas kernels: 24.3 us -> 23.5 us
    all_to_all x0 -> x1, blocking collectives: none -> 10.4 us  [per_device(): lax.all_to_all(request, 'blk', split_axis=0, concat_axis=0, tiled=True)]
    all_to_all x1 -> x0, starting transfers between devices: 8.32 us -> none  [per_device(): lax.all_to_all(request, 'blk', split_axis=0, concat_axis=0, tiled=True)]
    ppermute x2, waiting for transfers between devices: 7.75 us -> 0.01 us  [shift(): lax.ppermute(value, axis, [(i, (i + by) % count) for i in range(count)])]
    all_to_all x1 -> x0, waiting for transfers between devices: 5.65 us -> none  [per_device(): lax.all_to_all(request, 'blk', split_axis=0, concat_axis=0, tiled=True)]
    all_to_all x1, waiting for transfers between devices: 0.01 us -> 1.83 us  [per_device(): lax.all_to_all(served, 'blk', split_axis=0, concat_axis=0, tiled=True)]
    ppermute x2, starting transfers between devices: 5.67 us -> 7.05 us  [shift(): lax.ppermute(value, axis, [(i, (i + by) % count) for i in range(count)])]
    pallas_call x1, Pallas kernels: 1.67 us -> 1.07 us  [per_device(): pl.pallas_call(ask_kernel, out_shape=shaped((count, 128), i32), in_specs=...]
  transfers between devices with their start and end apart: 5 -> 4, of which waited for: 4 -> 2; matrix products, arithmetic and copies ran while one was open for 0% -> 0% of each run, Pallas kernels for 14% -> 15%
where the time goes in v14:
time: 49.1 us; the launch traced here: 48.7 us
  Pallas kernels  23.5 us (48%)
  starting transfers between devices  10.6 us (22%)
  blocking collectives  10.4 us (21%)
  waiting for transfers between devices  3.3 us (7%)
  between operations  0.73 us (1%)
    all_to_all x1, blocking collectives, per_device(): lax.all_to_all(request, 'blk', split_axis=0, concat_axis=0, tiled=True)  10.4 us
    pallas_call x1, Pallas kernels, per_device(): pl.pallas_call(finish_kernel, out_shape=(shaped((3, columns, lanes), f32)...  7.96 us
    ppermute x2, starting transfers between devices, shift(): lax.ppermute(value, axis, [(i, (i + by) % count) for i in range(count)])  7.05 us
    pallas_call x1, Pallas kernels, per_device(): pl.pallas_call(functools.partial(start_kernel, count=count), out_shape=(p...  6.43 us
    pallas_call x1, Pallas kernels, per_device(): pl.pallas_call(remap_kernel, out_shape=shaped((6, rows, lanes), f32), in_...  5.26 us
    all_to_all x1, starting transfers between devices, per_device(): lax.all_to_all(served, 'blk', split_axis=0, concat_axis=0, tiled=True)  3.53 us
    all_to_all x1, waiting for transfers between devices, per_device(): lax.all_to_all(served, 'blk', split_axis=0, concat_axis=0, tiled=True)  1.83 us
    pallas_call x1, Pallas kernels, per_device(): pl.pallas_call(pack_kernel, out_shape=(payload, payload, shaped((FIELDS *...  1.53 us
  transfers between devices with their start and end apart: 4, of which 2 were waited for; matrix products, arithmetic and copies ran while one was open for 0% of the time, Pallas kernels for 15%

profile of v14, /device:TPU:0, one launch (start us, length us, event | category | flops | bytes accessed | tf_op | source)
XLA Modules:
  0.0 48.7 jit_solution(8642043512882833372)
XLA Ops:
  0.6 0.0 copy-start.3
  0.6 1.5 %shard_map.87 = (bf16[848,128]{1,0:T(8,128)(2,1)S(1)}, bf16[848,128]{1,0:T(8,128)(2,1)S(1)}, bf16[192,128]{1,0:T(8,128)(2,1)S(1)}) custom-call(s32[1]{0:T(128)} %bitcast.section, f32[2,80,64,128]{3,2,1,0:T(8,128)} %state.3, s32[64,128]{1,0:T(8,128)} %bath.3, bf16[3,64,128]{2,1,0:T(8,128)(2,1)} %bitcast.21, s32[4,64]{1,0:T(4,128)} %bitcast.23, ...), custom_call_target="tpu_custom_call" | custom-call | flops 1000000 | bytes 4000000 | tf_op jit(solution)/shard_map/pallas_call | solution.py:503
  2.2 3.0 %collective-permute-start = (bf16[848,128]{1,0:T(8,128)(2,1)S(1)}, bf16[848,128]{1,0:T(8,128)(2,1)S(1)}, u32[]{:S(2)}, u32[]{:S(2)}) collective-permute-start(bf16[848,128]{1,0:T(8,128)(2,1)S(1)} %get-tuple-element.12), channel_id=1, source_target_pairs={{0,1},{1,2},{2,3},{3,4},{4,5},{5,6},{6,7},{7,8},{8,9},{9,10},{10,1... | collective-permute-start | bytes 651272 | tf_op jit(solution)/shard_map/ppermute | solution.py:453
  5.2 4.1 %collective-permute-start.1 = (bf16[848,128]{1,0:T(8,128)(2,1)S(1)}, bf16[848,128]{1,0:T(8,128)(2,1)S(1)}, u32[]{:S(2)}, u32[]{:S(2)}) collective-permute-start(bf16[848,128]{1,0:T(8,128)(2,1)S(1)} %get-tuple-element.13), channel_id=1, source_target_pairs={{0,15},{1,0},{2,1},{3,2},{4,3},{5,4},{6,5},{7,6},{8,7},{9,8},{10,9... | collective-permute-start | bytes 651272 | tf_op jit(solution)/shard_map/ppermute | solution.py:453
  9.2 1.1 %shard_map.86 = s32[16,128]{1,0:T(8,128)S(1)} custom-call(s32[4,64]{1,0:T(4,128)} %bitcast.24, s32[4,64]{1,0:T(4,128)} %bitcast.26), custom_call_target="tpu_custom_call" | custom-call | flops 1000000 | bytes 100000 | tf_op jit(solution)/shard_map/pallas_call | solution.py:487
  10.3 10.4 %all_to_all.22 = s32[16,1,128]{2,1,0:T(1,128)S(1)} all-to-all(s32[16,1,128]{2,1,0:T(1,128)S(1)} %bitcast.18), channel_id=1, replica_groups=mesh['sec'=2,'blk'=16] {'blk'}, dimensions={0} | all-to-all | bytes 16384 | tf_op jit(solution)/shard_map/all_to_all | solution.py:500
  20.7 0.0 collective-permute-done.from_left
  20.7 0.0 collective-permute-done.1.from_right
  20.7 1.3 %shard_map.88 = bf16[896,128]{1,0:T(8,128)(2,1)} custom-call(s32[16,128]{1,0:T(8,128)S(1)} %bitcast.17, bf16[192,128]{1,0:T(8,128)(2,1)S(1)} %get-tuple-element.11.table, bf16[848,128]{1,0:T(8,128)(2,1)S(1)} %collective-permute-done.from_left, bf16[848,128]{1,0:T(8,128)(2,1)S(1)} %collective-permute-done.1.from_right), custom_call_target="tpu_custom_call" | custom-call | flops 10000000 | bytes 1000000 | tf_op jit(solution)/shard_map/pallas_call | solution.py:537
  22.0 3.5 %all-to-all-start.1 = ((bf16[16,56,128]{2,1,0:T(8,128)(2,1)}), bf16[16,56,128]{2,1,0:T(8,128)(2,1)S(1)}, u32[]{:S(2)}, u32[]{:S(2)}) async-start(bf16[16,56,128]{2,1,0:T(8,128)(2,1)} %bitcast.11), calls=%async_computation.1 | async-start | bytes 458752 | tf_op jit(solution)/shard_map/all_to_all | solution.py:547
  25.6 0.0 copy-done.3
  25.6 6.4 %shard_map.89 = (f32[2,80,72,128]{3,2,1,0:T(8,128)}, bf16[80,64,128]{2,1,0:T(8,128)(2,1)}, s32[72,128]{1,0:T(8,128)}, s32[256,128]{1,0:T(8,128)}) custom-call(f32[2,80,64,128]{3,2,1,0:T(8,128)} %state.3, bf16[848,128]{1,0:T(8,128)(2,1)S(1)} %collective-permute-done.from_left, bf16[848,128]{1,0:T(8,128)(2,1)S(1)} %collective-permute-done.1.from_right, ...), custom_call_target="tpu_custom_call" | custom-call | flops 44236800 | bytes 147456000 | tf_op jit(solution)/shard_map/pallas_call | solution.py:550
  32.0 0.0 copy-start.1
  32.0 0.0 copy-start.2
  32.0 1.8 %all-to-all-done.1 = bf16[16,56,128]{2,1,0:T(8,128)(2,1)S(1)} async-done(((bf16[16,56,128]{2,1,0:T(8,128)(2,1)}), bf16[16,56,128]{2,1,0:T(8,128)(2,1)S(1)}, u32[]{:S(2)}, u32[]{:S(2)}) %all-to-all-start.1) | async-done | bytes 229408 | tf_op jit(solution)/shard_map/all_to_all | solution.py:547
  33.9 0.0 copy-start
  33.9 5.3 %shard_map.90.mine = f32[6,72,128]{2,1,0:T(8,128)S(1)} custom-call(bf16[896,128]{1,0:T(8,128)(2,1)S(1)} %bitcast.16, s32[256,128]{1,0:T(8,128)} %get-tuple-element.14.place_from, bf16[848,128]{1,0:T(8,128)(2,1)S(1)} %collective-permute-done.from_left, bf16[848,128]{1,0:T(8,128)(2,1)S(1)} %collective-permute-done.1.from_right, bf16[32768,128]{1,0:T(8,128)(2,1)} %bitcast.20, ...), custom_call_target="tpu_custom_call" | custom-call | flops 67108864 | bytes 8388608 | tf_op jit(solution)/shard_map/pallas_call | solution.py:587
  39.1 0.1 collective-permute-start.2
  39.2 1.5 %collective-permute-done.2.other = f32[6,72,128]{2,1,0:T(8,128)S(1)} collective-permute-done((f32[6,72,128]{2,1,0:T(8,128)S(1)}, f32[6,72,128]{2,1,0:T(8,128)S(1)}, u32[]{:S(2)}, u32[]{:S(2)}) %collective-permute-start.2) | collective-permute-done | bytes 221216 | tf_op jit(solution)/shard_map/ppermute | solution.py:612
  40.7 0.0 copy-done.1
  40.7 0.0 copy-done.2
  40.7 0.0 copy-done
  40.7 8.0 %shard_map.91 = (f32[3,64,128]{2,1,0:T(8,128)}, f32[2,80,64,128]{3,2,1,0:T(8,128)}) custom-call(s32[1]{0:T(128)} %bitcast.section, f32[6,72,128]{2,1,0:T(8,128)S(1)} %shard_map.90.mine, f32[6,72,128]{2,1,0:T(8,128)S(1)} %collective-permute-done.2.other, s32[72,128]{1,0:T(8,128)S(1)} %copy-done.2, f32[2,80,72,128]{3,2,1,0:T(8,128)S(1)} %copy-done, ...), custom_call_target="tpu_custom_call" | custom-call | flops 44236800 | bytes 23592960 | tf_op jit(solution)/shard_map/pallas_call | solution.py:614
  (1 shorter events, 0.0 us)
Async XLA Ops:
  0.6 24.9 %copy-start.3 = (f32[128]{0:T(128)S(1)}, f32[128]{0:T(128)}, u32[]{:S(2)}) copy-start(f32[128]{0:T(128)} %constant.8.clone) | copy-start | bytes 1540
  2.2 18.6 %collective-permute-start = (bf16[848,128]{1,0:T(8,128)(2,1)S(1)}, bf16[848,128]{1,0:T(8,128)(2,1)S(1)}, u32[]{:S(2)}, u32[]{:S(2)}) collective-permute-start(bf16[848,128]{1,0:T(8,128)(2,1)S(1)} %get-tuple-element.12), channel_id=1, source_target_pairs={{0,1},{1,2},{2,3},{3,4},{4,5},{5,6},{6,7},{7,8},{8,9},{9,10},{10,1... | collective-permute-start | bytes 651272 | tf_op jit(solution)/shard_map/ppermute | solution.py:453
  5.2 15.6 %collective-permute-start.1 = (bf16[848,128]{1,0:T(8,128)(2,1)S(1)}, bf16[848,128]{1,0:T(8,128)(2,1)S(1)}, u32[]{:S(2)}, u32[]{:S(2)}) collective-permute-start(bf16[848,128]{1,0:T(8,128)(2,1)S(1)} %get-tuple-element.13), channel_id=1, source_target_pairs={{0,15},{1,0},{2,1},{3,2},{4,3},{5,4},{6,5},{7,6},{8,7},{9,8},{10,9... | collective-permute-start | bytes 651272 | tf_op jit(solution)/shard_map/ppermute | solution.py:453
  22.0 11.8 %all-to-all-start.1 = ((bf16[16,56,128]{2,1,0:T(8,128)(2,1)}), bf16[16,56,128]{2,1,0:T(8,128)(2,1)S(1)}, u32[]{:S(2)}, u32[]{:S(2)}) async-start(bf16[16,56,128]{2,1,0:T(8,128)(2,1)} %bitcast.11), calls=%async_computation.1 | async-start | bytes 458752 | tf_op jit(solution)/shard_map/all_to_all | solution.py:547
  32.0 8.7 %copy-start.1 = (bf16[80,64,128]{2,1,0:T(8,128)(2,1)S(1)}, bf16[80,64,128]{2,1,0:T(8,128)(2,1)}, u32[]{:S(2)}) copy-start(bf16[80,64,128]{2,1,0:T(8,128)(2,1)} %get-tuple-element.17.side) | copy-start | bytes 3932164
  32.0 8.7 %copy-start.2 = (s32[72,128]{1,0:T(8,128)S(1)}, s32[72,128]{1,0:T(8,128)}, u32[]{:S(2)}) copy-start(s32[72,128]{1,0:T(8,128)} %get-tuple-element.15.bath) | copy-start | bytes 110596
  33.9 6.8 %copy-start = (f32[2,80,72,128]{3,2,1,0:T(8,128)S(1)}, f32[2,80,72,128]{3,2,1,0:T(8,128)}, u32[]{:S(2)}) copy-start(f32[2,80,72,128]{3,2,1,0:T(8,128)} %get-tuple-element.16.q) | copy-start | bytes 17694724
  39.1 1.5 %collective-permute-start.2 = (f32[6,72,128]{2,1,0:T(8,128)S(1)}, f32[6,72,128]{2,1,0:T(8,128)S(1)}, u32[]{:S(2)}, u32[]{:S(2)}) collective-permute-start(f32[6,72,128]{2,1,0:T(8,128)S(1)} %shard_map.90.mine), channel_id=1, source_target_pairs={{0,16},{16,0},{1,17},{17,1},{2,18},{18,2},{3,19},{19,3},{4,20},{20... | collective-permute-start | bytes 663560 | tf_op jit(solution)/shard_map/ppermute | solution.py:612

commit v15 on v14

--- a/solution.py
+++ b/solution.py
@@ -1,4 +1,5 @@
 import functools
+import math
 
 import jax
 import jax.numpy as jnp
@@ -12,6 +13,7 @@
 SIDE_MIX = 0.2
 TOP_MIX = 1.0
 DEEP_MIX = 2.0
+FIXED = (1.0 + 2.0 * DEEP_MIX - math.sqrt(1.0 + 4.0 * DEEP_MIX)) / (2.0 * DEEP_MIX)
 SCALE = 1.0 / (0.5 * SIDE_MIX)
 
 MOST = 16
@@ -85,15 +87,7 @@
     return result
 
 
-def ask_kernel(blocks, spots, request, blocks_in, spots_in, sems):
-    copies = [
-        pltpu.make_async_copy(blocks, blocks_in, sems.at[0]),
-        pltpu.make_async_copy(spots, spots_in, sems.at[1]),
-    ]
-    for copy in copies:
-        copy.start()
-    for copy in copies:
-        copy.wait()
+def ask_kernel(blocks, spots, request):
     count, columns = request.shape[0], blocks.shape[1]
     place = iota((128, columns), 0)
     field = place // SLOTS
@@ -101,9 +95,9 @@
     here = iota((128, columns), 1)
     marks = ((slot == MOST) & (here == 0)) | ((slot == MOST + 1) & (here == columns - 1))
     asked = jnp.zeros(request.shape, f32)
-    for k, (owner, rank) in enumerate(ranks(blocks_in, count)):
+    for k, (owner, rank) in enumerate(ranks(blocks, count)):
         filled = jnp.where((slot == rank.astype(i32)) | marks, 1.0, 0.0).astype(bf16)
-        named = jnp.where(owner, spots_in[k : k + 1, :].astype(f32), 0.0).astype(bf16)
+        named = jnp.where(owner, spots[k : k + 1, :].astype(f32), 0.0).astype(bf16)
         asked = asked + lax.dot_general(
             named, filled, (((1,), (1,)), ((), ())), preferred_element_type=f32
         )
@@ -111,9 +105,9 @@
 
 
 def pack_kernel(
-    section, state, bath, fields, blocks, weights,
-    to_left, to_right, table,
-    low, high, surface, bath_in, fields_in, blocks_in, extra, sems,
+    section, state, bath, fields, blocks, spots, weights,
+    to_left, to_right, table, blocks_in, spots_in,
+    low, high, surface, bath_in, fields_in, extra, sems,
 ):
     tracers, levels, columns, lanes = state.shape
     slots = blocks.shape[0]
@@ -129,6 +123,7 @@
         (state.at[:, 0], surface),
         (weights.at[pl.ds(0, wide)], to_left.at[below]),
         (weights.at[pl.ds((columns - 1) * wide, wide)], to_right.at[below]),
+        (spots, spots_in),
     ]
     copies = [pltpu.make_async_copy(src, dst, sems.at[n]) for n, (src, dst) in enumerate(pairs)]
     for copy in copies:
@@ -159,8 +154,8 @@
             to_left[part] = tiles[pl.ds(c, levels, stride=8), :].astype(bf16)
             tiles = high.at[n].reshape(levels * 8, lanes)
             to_right[part] = tiles[pl.ds(6 + c, levels, stride=8), :].astype(bf16)
-    copies[6].wait()
-    copies[7].wait()
+    for copy in copies[6:]:
+        copy.wait()
 
 
 def serve_kernel(asked, table, from_left, from_right, out):
@@ -373,7 +368,7 @@
 
 def finish_kernel(
     section, mine, other, bath, q, side, ratios, surface, result,
-    values_at, rounded_at, rho, solved, done, across, band, sems_out,
+    rho, weight, partial_at, done, across, band, sems_out,
 ):
     tracers, levels, columns, lanes = result.shape
     chunks = chunks_of(levels)
@@ -384,6 +379,7 @@
     forcing = [flux[0] + own[0], flux[1] + own[1]]
     top_mix = TOP_MIX * (1.0 + flux[2] * flux[2] + own[2] * own[2])
     depth = bath[...]
+    inner_depth = bath[pl.ds(0, columns)]
     unscale = 1.0 / (SCALE * SCALE)
 
     rho[2] = ratio_at(ratios, depth, 2)
@@ -393,49 +389,62 @@
     rho_second = link * second
     first = 1.0 / (1.0 + link - link * rho_second)
 
-    def top_levels(n, count, halves, below, scale):
-        partial = 2.0 * (halves[1] + below) * second[:count]
-        source = 2.0 * halves[0] + scale * FLUX_GAIN * forcing[n][:count]
-        value = (source + link[:count] * partial) * first[:count]
-        below = jnp.where(1 < depth[:count], partial, 0.0) + rho_second[:count] * value
-        return value, below
-
-    def put(n, level, h):
-        values_at[n, level] = h[:columns]
-        rounded_at[n, level] = rounded(h)
-
-    def half_at(n, level):
-        around = neighbour_sum(rounded_at[n, level], across, band, columns)
-        return side[level].astype(f32) * values_at[n, level] + around
+    inner_link = link[:columns]
+    top_weight = 1.0 / (1.0 + inner_link)
+    top_ratio = inner_link * top_weight
+    below_link = jnp.where(2 < inner_depth, DEEP_MIX, 0.0)
+    next_weight = 1.0 / (1.0 + top_ratio + below_link)
+    weight[1] = DEEP_MIX * next_weight
+    next_ratio = below_link * next_weight
+    x = (next_ratio - FIXED) / (next_ratio - 1.0 / FIXED)
+    base = 1.0 + DEEP_MIX - DEEP_MIX / FIXED
+    rise = DEEP_MIX * (1.0 / FIXED - FIXED)
+
+    def half_at(n, level, h):
+        around = neighbour_sum(rounded(h), across, band, columns)
+        return side[level].astype(f32) * h[:columns] + around
 
     leaving = []
     for n in range(tracers):
         below = jnp.where(2 < depth, q[n, 2], 0.0)
-        value, carry = top_levels(n, columns + EDGE, (q[n, 0], q[n, 1]), below, SCALE)
-        put(n, 0, jnp.where(0 < depth, value, 0.0))
-        put(n, 1, carry)
+        partial = 2.0 * (q[n, 1] + below) * second
+        source = 2.0 * q[n, 0] + SCALE * FLUX_GAIN * forcing[n]
+        value = (source + link * partial) * first
+        carry = jnp.where(1 < depth, partial, 0.0) + rho_second * value
+        value = jnp.where(0 < depth, value, 0.0)
+
+        source = 2.0 * half_at(n, 0, value)
+        source = source + SCALE * SCALE * FLUX_GAIN * forcing[n][:columns]
+        top_partial = source * top_weight
+        solved = (2.0 * half_at(n, 1, carry) + inner_link * top_partial) * next_weight
+        partial_at[1] = solved
         for level in range(2, levels):
-            if n == 0 and level > 2:
-                rho[level] = ratio_at(ratios, depth, level)
+            if n == 0:
+                if level > 2:
+                    rho[level] = ratio_at(ratios, depth, level)
+                linked = level + 1 < inner_depth
+                divisor = jnp.where(
+                    linked, base + DEEP_MIX + rise - (base + DEEP_MIX) * x, base + rise - base * x
+                )
+                inverse = pl.reciprocal(divisor, approx=True)
+                scaled = (DEEP_MIX - DEEP_MIX * x) * inverse
+                weight[level] = scaled * (2.0 - divisor * inverse)
+                x = (FIXED * FIXED) * x
             carry = jnp.where(level < depth, q[n, level], 0.0) + rho[level] * carry
-            put(n, level, carry)
-
-        carry = jnp.zeros((columns, lanes), f32)
-        for level in range(levels - 1, 1, -1):
-            carry = rho[level, pl.ds(0, columns)] * (half_at(n, level) + carry)
-            solved[n, level] = carry
-
-        value, carry = top_levels(
-            n, columns, (half_at(n, 0), half_at(n, 1)), carry, SCALE * SCALE
-        )
-        surface[n] = jnp.where(on_ocean, value * unscale, other[n, pl.ds(0, columns)])
-        done[n, 0] = value * unscale
-        for low, size in chunks:
-            for level in range(max(low, 1), low + size):
-                if level > 1:
-                    carry = solved[n, level] + rho[level, pl.ds(0, columns)] * carry
+            solved = weight[level] * (half_at(n, level, carry) + solved)
+            partial_at[level] = solved
+
+        value = jnp.zeros((columns, lanes), f32)
+        for low, size in reversed(chunks):
+            for level in range(low + size - 1, max(low, 1) - 1, -1):
+                wet = level < inner_depth
+                value = jnp.where(wet, partial_at[level] + weight[level] * value, 0.0)
                 start = q[n, level, pl.ds(0, columns)]
-                done[n, level] = jnp.where(level < depth[:columns], carry * unscale, start)
+                done[n, level] = jnp.where(wet, value * unscale, start)
+            if low == 0:
+                value = (top_partial + top_ratio * value) * unscale
+                done[n, 0] = value
+                surface[n] = jnp.where(on_ocean, value, other[n, pl.ds(0, columns)])
             part = pl.ds(low, size)
             leaving.append(
                 pltpu.make_async_copy(
@@ -484,40 +493,26 @@
     cells = rows * lanes
     tall_rows = rows + -rows % 16
 
-    request = pl.pallas_call(
-        ask_kernel,
-        out_shape=shaped((count, 128), i32),
-        in_specs=[hbm, hbm],
-        out_specs=vmem,
-        scratch_shapes=[
-            pltpu.VMEM(blocks.shape, i32),
-            pltpu.VMEM(spots.shape, i32),
-            pltpu.SemaphoreType.DMA((2,)),
-        ],
-        compiler_params=pltpu.CompilerParams(vmem_limit_bytes=4 * MIB),
-        cost_estimate=pl.CostEstimate(flops=10**6, bytes_accessed=10**5, transcendentals=0),
-    )(in_hbm(blocks), in_hbm(spots))
-    asked = lax.all_to_all(request, "blk", split_axis=0, concat_axis=0, tiled=True)
-
     payload = shaped((2 * many + EXTRA + tall, lanes), bf16)
-    to_left, to_right, table = pl.pallas_call(
+    to_left, to_right, table, blocks_in, spots_in = pl.pallas_call(
         pack_kernel,
         out_shape=(
             payload,
             payload,
             shaped((FIELDS * columns, lanes), bf16),
-        ),
-        in_specs=[smem] + [hbm] * 5,
-        out_specs=(vmem, vmem, vmem),
+            shaped(blocks.shape, i32),
+            shaped(spots.shape, i32),
+        ),
+        in_specs=[smem] + [hbm] * 6,
+        out_specs=(vmem,) * 5,
         scratch_shapes=[
             pltpu.VMEM((tracers, levels, 8, lanes), f32),
             pltpu.VMEM((tracers, levels, 8, lanes), f32),
             pltpu.VMEM((tracers, columns, lanes), f32),
             pltpu.VMEM(bathymetry.shape, i32),
             pltpu.VMEM(fields.shape, bf16),
-            pltpu.VMEM(blocks.shape, i32),
             pltpu.VMEM((EXTRA, lanes), f32),
-            pltpu.SemaphoreType.DMA((8,)),
+            pltpu.SemaphoreType.DMA((9,)),
         ],
         compiler_params=pltpu.CompilerParams(vmem_limit_bytes=8 * MIB),
         cost_estimate=pl.CostEstimate(
@@ -529,8 +524,18 @@
         in_hbm(bathymetry),
         in_hbm(fields),
         in_hbm(blocks),
+        in_hbm(spots),
         in_hbm(weights),
     )
+    request = pl.pallas_call(
+        ask_kernel,
+        out_shape=shaped((count, 128), i32),
+        in_specs=[vmem, vmem],
+        out_specs=vmem,
+        compiler_params=pltpu.CompilerParams(vmem_limit_bytes=4 * MIB),
+        cost_estimate=pl.CostEstimate(flops=10**6, bytes_accessed=10**5, transcendentals=0),
+    )(blocks_in, spots_in)
+    asked = lax.all_to_all(request, "blk", split_axis=0, concat_axis=0, tiled=True)
     from_left = shift(to_right, "blk", 1)
     from_right = shift(to_left, "blk", -1)
 
@@ -617,10 +622,9 @@
         in_specs=[smem] + [vmem] * 6,
         out_specs=(vmem, hbm),
         scratch_shapes=[
-            pltpu.VMEM(ocean_state.shape, f32),
-            pltpu.VMEM((tracers, levels, tall_rows, lanes), bf16),
             pltpu.VMEM((levels, rows, lanes), f32),
-            pltpu.VMEM(ocean_state.shape, f32),
+            pltpu.VMEM((levels, columns, lanes), f32),
+            pltpu.VMEM((levels, columns, lanes), f32),
             pltpu.VMEM(ocean_state.shape, f32),
             pltpu.VMEM((tall_rows, lanes), bf16),
             pltpu.VMEM((lanes, lanes), bf16),

time: 49.1 us -> 49.7 us (1.012)
  Pallas kernels: 23.5 us -> 24.2 us
    pallas_call x1, Pallas kernels: 7.96 us -> 9.4 us  [per_device(): pl.pallas_call(finish_kernel, out_shape=(shaped((3, columns, lanes), f32)...]
    pallas_call x1, Pallas kernels: 1.07 us -> 0.34 us  [per_device(): pl.pallas_call(ask_kernel, out_shape=shaped((count, 128), i32), in_specs=...]
  transfers between devices with their start and end apart: 4 -> 4, of which waited for: 2 -> 2; matrix products, arithmetic and copies ran while one was open for 0% -> 0% of each run, Pallas kernels for 15% -> 14%
where the time goes in v15:
time: 49.7 us; the launch traced here: 49.4 us
  Pallas kernels  24.2 us (49%)
  starting transfers between devices  10.6 us (21%)
  blocking collectives  10.4 us (21%)
  waiting for transfers between devices  3.32 us (7%)
  between operations  0.72 us (1%)
    all_to_all x1, blocking collectives, per_device(): lax.all_to_all(request, 'blk', split_axis=0, concat_axis=0, tiled=True)  10.4 us
    pallas_call x1, Pallas kernels, per_device(): pl.pallas_call(finish_kernel, out_shape=(shaped((3, columns, lanes), f32)...  9.4 us
    ppermute x2, starting transfers between devices, shift(): lax.ppermute(value, axis, [(i, (i + by) % count) for i in range(count)])  7.05 us
    pallas_call x1, Pallas kernels, per_device(): pl.pallas_call(functools.partial(start_kernel, count=count), out_shape=(p...  6.41 us
    pallas_call x1, Pallas kernels, per_device(): pl.pallas_call(remap_kernel, out_shape=shaped((6, rows, lanes), f32), in_...  5.26 us
    all_to_all x1, starting transfers between devices, per_device(): lax.all_to_all(served, 'blk', split_axis=0, concat_axis=0, tiled=True)  3.53 us
    all_to_all x1, waiting for transfers between devices, per_device(): lax.all_to_all(served, 'blk', split_axis=0, concat_axis=0, tiled=True)  1.86 us
    pallas_call x1, Pallas kernels, per_device(): pl.pallas_call(pack_kernel, out_shape=(payload, payload, shaped((FIELDS *...  1.54 us
  transfers between devices with their start and end apart: 4, of which 2 were waited for; matrix products, arithmetic and copies ran while one was open for 0% of the time, Pallas kernels for 14%

profile of v15, /device:TPU:0, one launch (start us, length us, event | category | flops | bytes accessed | tf_op | source)
XLA Modules:
  0.0 49.4 jit_solution(1028101086517056100)
XLA Ops:
  0.6 0.0 copy-start.3
  0.6 1.5 %shard_map.86 = (bf16[848,128]{1,0:T(8,128)(2,1)S(1)}, bf16[848,128]{1,0:T(8,128)(2,1)S(1)}, bf16[192,128]{1,0:T(8,128)(2,1)S(1)}, s32[4,64]{1,0:T(4,128)S(1)}, s32[4,64]{1,0:T(4,128)S(1)}) custom-call(s32[1]{0:T(128)} %bitcast.section, f32[2,80,64,128]{3,2,1,0:T(8,128)} %state.3, s32[64,128]{1,0:T(8,128)} %bath.3, bf16[3,64,128]{2,1,0:T(8,128)(2,1)} %bitcast.21, ...), custom_call_target="tpu_custom_call" | custom-call | flops 1000000 | bytes 4000000 | tf_op jit(solution)/shard_map/pallas_call | solution.py:497
  2.2 3.0 %collective-permute-start = (bf16[848,128]{1,0:T(8,128)(2,1)S(1)}, bf16[848,128]{1,0:T(8,128)(2,1)S(1)}, u32[]{:S(2)}, u32[]{:S(2)}) collective-permute-start(bf16[848,128]{1,0:T(8,128)(2,1)S(1)} %get-tuple-element.16), channel_id=1, source_target_pairs={{0,1},{1,2},{2,3},{3,4},{4,5},{5,6},{6,7},{7,8},{8,9},{9,10},{10,1... | collective-permute-start | bytes 651272 | tf_op jit(solution)/shard_map/ppermute | solution.py:462
  5.2 4.1 %collective-permute-start.1 = (bf16[848,128]{1,0:T(8,128)(2,1)S(1)}, bf16[848,128]{1,0:T(8,128)(2,1)S(1)}, u32[]{:S(2)}, u32[]{:S(2)}) collective-permute-start(bf16[848,128]{1,0:T(8,128)(2,1)S(1)} %get-tuple-element.17), channel_id=1, source_target_pairs={{0,15},{1,0},{2,1},{3,2},{4,3},{5,4},{6,5},{7,6},{8,7},{9,8},{10,9... | collective-permute-start | bytes 651272 | tf_op jit(solution)/shard_map/ppermute | solution.py:462
  9.2 0.3 shard_map.87
  9.6 10.4 %all_to_all.22 = s32[16,1,128]{2,1,0:T(1,128)S(1)} all-to-all(s32[16,1,128]{2,1,0:T(1,128)S(1)} %bitcast.18), channel_id=1, replica_groups=mesh['sec'=2,'blk'=16] {'blk'}, dimensions={0} | all-to-all | bytes 16384 | tf_op jit(solution)/shard_map/all_to_all | solution.py:538
  20.0 0.0 collective-permute-done.from_left
  20.0 0.0 collective-permute-done.1.from_right
  20.0 1.3 %shard_map.88 = bf16[896,128]{1,0:T(8,128)(2,1)} custom-call(s32[16,128]{1,0:T(8,128)S(1)} %bitcast.17, bf16[192,128]{1,0:T(8,128)(2,1)S(1)} %get-tuple-element.15.table, bf16[848,128]{1,0:T(8,128)(2,1)S(1)} %collective-permute-done.from_left, bf16[848,128]{1,0:T(8,128)(2,1)S(1)} %collective-permute-done.1.from_right), custom_call_target="tpu_custom_call" | custom-call | flops 10000000 | bytes 1000000 | tf_op jit(solution)/shard_map/pallas_call | solution.py:542
  21.3 3.5 %all-to-all-start.1 = ((bf16[16,56,128]{2,1,0:T(8,128)(2,1)}), bf16[16,56,128]{2,1,0:T(8,128)(2,1)S(1)}, u32[]{:S(2)}, u32[]{:S(2)}) async-start(bf16[16,56,128]{2,1,0:T(8,128)(2,1)} %bitcast.10), calls=%async_computation.1 | async-start | bytes 458752 | tf_op jit(solution)/shard_map/all_to_all | solution.py:552
  24.8 0.0 copy-done.3
  24.9 6.4 %shard_map.89 = (f32[2,80,72,128]{3,2,1,0:T(8,128)}, bf16[80,64,128]{2,1,0:T(8,128)(2,1)}, s32[72,128]{1,0:T(8,128)}, s32[256,128]{1,0:T(8,128)}) custom-call(f32[2,80,64,128]{3,2,1,0:T(8,128)} %state.3, bf16[848,128]{1,0:T(8,128)(2,1)S(1)} %collective-permute-done.from_left, bf16[848,128]{1,0:T(8,128)(2,1)S(1)} %collective-permute-done.1.from_right, ...), custom_call_target="tpu_custom_call" | custom-call | flops 44236800 | bytes 147456000 | tf_op jit(solution)/shard_map/pallas_call | solution.py:555
  31.3 0.0 copy-start.1
  31.3 0.0 copy-start.2
  31.3 1.9 %all-to-all-done.1 = bf16[16,56,128]{2,1,0:T(8,128)(2,1)S(1)} async-done(((bf16[16,56,128]{2,1,0:T(8,128)(2,1)}), bf16[16,56,128]{2,1,0:T(8,128)(2,1)S(1)}, u32[]{:S(2)}, u32[]{:S(2)}) %all-to-all-start.1) | async-done | bytes 229408 | tf_op jit(solution)/shard_map/all_to_all | solution.py:552
  33.2 0.0 copy-start
  33.2 5.3 %shard_map.90.mine = f32[6,72,128]{2,1,0:T(8,128)S(1)} custom-call(bf16[896,128]{1,0:T(8,128)(2,1)S(1)} %bitcast.16, s32[256,128]{1,0:T(8,128)} %get-tuple-element.18.place_from, bf16[848,128]{1,0:T(8,128)(2,1)S(1)} %collective-permute-done.from_left, bf16[848,128]{1,0:T(8,128)(2,1)S(1)} %collective-permute-done.1.from_right, bf16[32768,128]{1,0:T(8,128)(2,1)} %bitcast.20, ...), custom_call_target="tpu_custom_call" | custom-call | flops 67108864 | bytes 8388608 | tf_op jit(solution)/shard_map/pallas_call | solution.py:592
  38.4 0.1 collective-permute-start.2
  38.5 1.5 %collective-permute-done.2.other = f32[6,72,128]{2,1,0:T(8,128)S(1)} collective-permute-done((f32[6,72,128]{2,1,0:T(8,128)S(1)}, f32[6,72,128]{2,1,0:T(8,128)S(1)}, u32[]{:S(2)}, u32[]{:S(2)}) %collective-permute-start.2) | collective-permute-done | bytes 221216 | tf_op jit(solution)/shard_map/ppermute | solution.py:617
  40.0 0.0 copy-done.1
  40.0 0.0 copy-done.2
  40.0 0.0 copy-done
  40.0 9.4 %shard_map.91 = (f32[3,64,128]{2,1,0:T(8,128)}, f32[2,80,64,128]{3,2,1,0:T(8,128)}) custom-call(s32[1]{0:T(128)} %bitcast.section, f32[6,72,128]{2,1,0:T(8,128)S(1)} %shard_map.90.mine, f32[6,72,128]{2,1,0:T(8,128)S(1)} %collective-permute-done.2.other, s32[72,128]{1,0:T(8,128)S(1)} %copy-done.2, f32[2,80,72,128]{3,2,1,0:T(8,128)S(1)} %copy-done, ...), custom_call_target="tpu_custom_call" | custom-call | flops 44236800 | bytes 23592960 | tf_op jit(solution)/shard_map/pallas_call | solution.py:619
  (1 shorter events, 0.0 us)
Async XLA Ops:
  0.6 24.2 %copy-start.3 = (f32[128]{0:T(128)S(1)}, f32[128]{0:T(128)}, u32[]{:S(2)}) copy-start(f32[128]{0:T(128)} %constant.8.clone) | copy-start | bytes 1540
  2.2 17.8 %collective-permute-start = (bf16[848,128]{1,0:T(8,128)(2,1)S(1)}, bf16[848,128]{1,0:T(8,128)(2,1)S(1)}, u32[]{:S(2)}, u32[]{:S(2)}) collective-permute-start(bf16[848,128]{1,0:T(8,128)(2,1)S(1)} %get-tuple-element.16), channel_id=1, source_target_pairs={{0,1},{1,2},{2,3},{3,4},{4,5},{5,6},{6,7},{7,8},{8,9},{9,10},{10,1... | collective-permute-start | bytes 651272 | tf_op jit(solution)/shard_map/ppermute | solution.py:462
  5.2 14.8 %collective-permute-start.1 = (bf16[848,128]{1,0:T(8,128)(2,1)S(1)}, bf16[848,128]{1,0:T(8,128)(2,1)S(1)}, u32[]{:S(2)}, u32[]{:S(2)}) collective-permute-start(bf16[848,128]{1,0:T(8,128)(2,1)S(1)} %get-tuple-element.17), channel_id=1, source_target_pairs={{0,15},{1,0},{2,1},{3,2},{4,3},{5,4},{6,5},{7,6},{8,7},{9,8},{10,9... | collective-permute-start | bytes 651272 | tf_op jit(solution)/shard_map/ppermute | solution.py:462
  21.3 11.8 %all-to-all-start.1 = ((bf16[16,56,128]{2,1,0:T(8,128)(2,1)}), bf16[16,56,128]{2,1,0:T(8,128)(2,1)S(1)}, u32[]{:S(2)}, u32[]{:S(2)}) async-start(bf16[16,56,128]{2,1,0:T(8,128)(2,1)} %bitcast.10), calls=%async_computation.1 | async-start | bytes 458752 | tf_op jit(solution)/shard_map/all_to_all | solution.py:552
  31.3 8.7 %copy-start.1 = (bf16[80,64,128]{2,1,0:T(8,128)(2,1)S(1)}, bf16[80,64,128]{2,1,0:T(8,128)(2,1)}, u32[]{:S(2)}) copy-start(bf16[80,64,128]{2,1,0:T(8,128)(2,1)} %get-tuple-element.21.side) | copy-start | bytes 3932164
  31.3 8.7 %copy-start.2 = (s32[72,128]{1,0:T(8,128)S(1)}, s32[72,128]{1,0:T(8,128)}, u32[]{:S(2)}) copy-start(s32[72,128]{1,0:T(8,128)} %get-tuple-element.19.bath) | copy-start | bytes 110596
  33.2 6.8 %copy-start = (f32[2,80,72,128]{3,2,1,0:T(8,128)S(1)}, f32[2,80,72,128]{3,2,1,0:T(8,128)}, u32[]{:S(2)}) copy-start(f32[2,80,72,128]{3,2,1,0:T(8,128)} %get-tuple-element.20.q) | copy-start | bytes 17694724
  38.4 1.5 %collective-permute-start.2 = (f32[6,72,128]{2,1,0:T(8,128)S(1)}, f32[6,72,128]{2,1,0:T(8,128)S(1)}, u32[]{:S(2)}, u32[]{:S(2)}) collective-permute-start(f32[6,72,128]{2,1,0:T(8,128)S(1)} %shard_map.90.mine), channel_id=1, source_target_pairs={{0,16},{16,0},{1,17},{17,1},{2,18},{18,2},{3,19},{19,3},{4,20},{20... | collective-permute-start | bytes 663560 | tf_op jit(solution)/shard_map/ppermute | solution.py:617

commit v16 on v14

--- a/solution.py
+++ b/solution.py
@@ -85,15 +85,7 @@
     return result
 
 
-def ask_kernel(blocks, spots, request, blocks_in, spots_in, sems):
-    copies = [
-        pltpu.make_async_copy(blocks, blocks_in, sems.at[0]),
-        pltpu.make_async_copy(spots, spots_in, sems.at[1]),
-    ]
-    for copy in copies:
-        copy.start()
-    for copy in copies:
-        copy.wait()
+def ask_kernel(blocks, spots, request):
     count, columns = request.shape[0], blocks.shape[1]
     place = iota((128, columns), 0)
     field = place // SLOTS
@@ -101,9 +93,9 @@
     here = iota((128, columns), 1)
     marks = ((slot == MOST) & (here == 0)) | ((slot == MOST + 1) & (here == columns - 1))
     asked = jnp.zeros(request.shape, f32)
-    for k, (owner, rank) in enumerate(ranks(blocks_in, count)):
+    for k, (owner, rank) in enumerate(ranks(blocks, count)):
         filled = jnp.where((slot == rank.astype(i32)) | marks, 1.0, 0.0).astype(bf16)
-        named = jnp.where(owner, spots_in[k : k + 1, :].astype(f32), 0.0).astype(bf16)
+        named = jnp.where(owner, spots[k : k + 1, :].astype(f32), 0.0).astype(bf16)
         asked = asked + lax.dot_general(
             named, filled, (((1,), (1,)), ((), ())), preferred_element_type=f32
         )
@@ -111,9 +103,9 @@
 
 
 def pack_kernel(
-    section, state, bath, fields, blocks, weights,
-    to_left, to_right, table,
-    low, high, surface, bath_in, fields_in, blocks_in, extra, sems,
+    section, state, bath, fields, blocks, spots, weights,
+    to_left, to_right, table, blocks_in, spots_in,
+    low, high, surface, bath_in, fields_in, extra, sems,
 ):
     tracers, levels, columns, lanes = state.shape
     slots = blocks.shape[0]
@@ -129,6 +121,7 @@
         (state.at[:, 0], surface),
         (weights.at[pl.ds(0, wide)], to_left.at[below]),
         (weights.at[pl.ds((columns - 1) * wide, wide)], to_right.at[below]),
+        (spots, spots_in),
     ]
     copies = [pltpu.make_async_copy(src, dst, sems.at[n]) for n, (src, dst) in enumerate(pairs)]
     for copy in copies:
@@ -159,24 +152,25 @@
             to_left[part] = tiles[pl.ds(c, levels, stride=8), :].astype(bf16)
             tiles = high.at[n].reshape(levels * 8, lanes)
             to_right[part] = tiles[pl.ds(6 + c, levels, stride=8), :].astype(bf16)
-    copies[6].wait()
-    copies[7].wait()
+    for copy in copies[6:]:
+        copy.wait()
 
 
 def serve_kernel(asked, table, from_left, from_right, out):
     count = asked.shape[0]
-    wanted = jnp.transpose(asked[...].astype(f32))[:PIECE]
     height = table.shape[0]
-    slot = lax.rem(iota((PIECE, 1), 0), SLOTS)
+    request = asked[...].astype(f32)
+    slot = lax.rem(iota(request.shape, 1), SLOTS)
+    request = jnp.where(
+        slot == MOST,
+        pltpu.roll(request, count - 1, 0),
+        jnp.where(slot == MOST + 1, pltpu.roll(request, 1, 0), request),
+    )
+    wanted = jnp.transpose(request)[:PIECE].astype(i32)
     parts = []
     for e in range(count):
-        after, before = (e + 1) % count, (e - 1) % count
-        spot = jnp.where(
-            slot == MOST,
-            wanted[:, after : after + 1],
-            jnp.where(slot == MOST + 1, wanted[:, before : before + 1], wanted[:, e : e + 1]),
-        )
-        parts.append(jnp.where(iota((PIECE, height), 1) == spot.astype(i32), 1.0, 0.0))
+        here = iota((PIECE, height), 1) == wanted[:, e : e + 1]
+        parts.append(jnp.where(here, 1.0, 0.0))
     chosen = jnp.concatenate(parts, axis=0).astype(bf16)
     out[...] = jnp.dot(chosen, table[...], preferred_element_type=f32).astype(bf16)
 
@@ -321,7 +315,7 @@
     for n in range(columns // group):
         part = pl.ds(n * group * tall, group * tall)
         copies.append(pltpu.make_async_copy(weights.at[part], held.at[part], sems.at[2 + n]))
-    for copy in [place_copy] + copies + [fields_copy]:
+    for copy in [place_copy, fields_copy] + copies[:IN_FLIGHT]:
         copy.start()
     right = from_right[pl.ds(many, EXTRA)].astype(f32)
     left = from_left[pl.ds(many, EXTRA)].astype(f32)
@@ -358,6 +352,8 @@
     one(rows - 1, lambda k: from_left[pl.ds(below + k * width, width)])
     for n in range(columns // group):
         copies[n].wait()
+        if n + IN_FLIGHT < len(copies):
+            copies[n + IN_FLIGHT].start()
         for m in range(group):
             spot = n * group + m
             one(spot, lambda k: held[pl.ds((spot * slots + k) * width, width)])
@@ -484,40 +480,26 @@
     cells = rows * lanes
     tall_rows = rows + -rows % 16
 
-    request = pl.pallas_call(
-        ask_kernel,
-        out_shape=shaped((count, 128), i32),
-        in_specs=[hbm, hbm],
-        out_specs=vmem,
-        scratch_shapes=[
-            pltpu.VMEM(blocks.shape, i32),
-            pltpu.VMEM(spots.shape, i32),
-            pltpu.SemaphoreType.DMA((2,)),
-        ],
-        compiler_params=pltpu.CompilerParams(vmem_limit_bytes=4 * MIB),
-        cost_estimate=pl.CostEstimate(flops=10**6, bytes_accessed=10**5, transcendentals=0),
-    )(in_hbm(blocks), in_hbm(spots))
-    asked = lax.all_to_all(request, "blk", split_axis=0, concat_axis=0, tiled=True)
-
     payload = shaped((2 * many + EXTRA + tall, lanes), bf16)
-    to_left, to_right, table = pl.pallas_call(
+    to_left, to_right, table, blocks_in, spots_in = pl.pallas_call(
         pack_kernel,
         out_shape=(
             payload,
             payload,
             shaped((FIELDS * columns, lanes), bf16),
-        ),
-        in_specs=[smem] + [hbm] * 5,
-        out_specs=(vmem, vmem, vmem),
+            shaped(blocks.shape, i32),
+            shaped(spots.shape, i32),
+        ),
+        in_specs=[smem] + [hbm] * 6,
+        out_specs=(vmem,) * 5,
         scratch_shapes=[
             pltpu.VMEM((tracers, levels, 8, lanes), f32),
             pltpu.VMEM((tracers, levels, 8, lanes), f32),
             pltpu.VMEM((tracers, columns, lanes), f32),
             pltpu.VMEM(bathymetry.shape, i32),
             pltpu.VMEM(fields.shape, bf16),
-            pltpu.VMEM(blocks.shape, i32),
             pltpu.VMEM((EXTRA, lanes), f32),
-            pltpu.SemaphoreType.DMA((8,)),
+            pltpu.SemaphoreType.DMA((9,)),
         ],
         compiler_params=pltpu.CompilerParams(vmem_limit_bytes=8 * MIB),
         cost_estimate=pl.CostEstimate(
@@ -529,8 +511,18 @@
         in_hbm(bathymetry),
         in_hbm(fields),
         in_hbm(blocks),
+        in_hbm(spots),
         in_hbm(weights),
     )
+    request = pl.pallas_call(
+        ask_kernel,
+        out_shape=shaped((count, 128), i32),
+        in_specs=[vmem, vmem],
+        out_specs=vmem,
+        compiler_params=pltpu.CompilerParams(vmem_limit_bytes=4 * MIB),
+        cost_estimate=pl.CostEstimate(flops=10**6, bytes_accessed=10**5, transcendentals=0),
+    )(blocks_in, spots_in)
+    asked = lax.all_to_all(request, "blk", split_axis=0, concat_axis=0, tiled=True)
     from_left = shift(to_right, "blk", 1)
     from_right = shift(to_left, "blk", -1)
 

time: 49.1 us -> 48.8 us (level)
    pallas_call x1, Pallas kernels: 1.07 us -> 0.34 us  [per_device(): pl.pallas_call(ask_kernel, out_shape=shaped((count, 128), i32), in_specs=...]
    pallas_call x1, Pallas kernels: 5.26 us -> 5.9 us  [per_device(): pl.pallas_call(remap_kernel, out_shape=shaped((6, rows, lanes), f32), in_...]
  transfers between devices with their start and end apart: 4 -> 4, of which waited for: 2 -> 2; matrix products, arithmetic and copies ran while one was open for 0% -> 0% of each run, Pallas kernels for 15% -> 14%
where the time goes in v16:
time: 48.8 us; the launch traced here: 48.5 us
  Pallas kernels  23.3 us (48%)
  starting transfers between devices  10.6 us (22%)
  blocking collectives  10.4 us (21%)
  waiting for transfers between devices  3.32 us (7%)
  between operations  0.72 us (1%)
    all_to_all x1, blocking collectives, per_device(): lax.all_to_all(request, 'blk', split_axis=0, concat_axis=0, tiled=True)  10.4 us
    pallas_call x1, Pallas kernels, per_device(): pl.pallas_call(finish_kernel, out_shape=(shaped((3, columns, lanes), f32)...  7.96 us
    ppermute x2, starting transfers between devices, shift(): lax.ppermute(value, axis, [(i, (i + by) % count) for i in range(count)])  7.05 us
    pallas_call x1, Pallas kernels, per_device(): pl.pallas_call(functools.partial(start_kernel, count=count), out_shape=(p...  6.41 us
    pallas_call x1, Pallas kernels, per_device(): pl.pallas_call(remap_kernel, out_shape=shaped((6, rows, lanes), f32), in_...  5.9 us
    all_to_all x1, starting transfers between devices, per_device(): lax.all_to_all(served, 'blk', split_axis=0, concat_axis=0, tiled=True)  3.53 us
    all_to_all x1, waiting for transfers between devices, per_device(): lax.all_to_all(served, 'blk', split_axis=0, concat_axis=0, tiled=True)  1.86 us
    pallas_call x1, Pallas kernels, per_device(): pl.pallas_call(pack_kernel, out_shape=(payload, payload, shaped((FIELDS *...  1.54 us
  transfers between devices with their start and end apart: 4, of which 2 were waited for; matrix products, arithmetic and copies ran while one was open for 0% of the time, Pallas kernels for 14%

profile of v16, /device:TPU:0, one launch (start us, length us, event | category | flops | bytes accessed | tf_op | source)
XLA Modules:
  0.0 48.5 jit_solution(514731547844129978)
XLA Ops:
  0.6 0.0 copy-start.3
  0.6 1.5 %shard_map.86 = (bf16[848,128]{1,0:T(8,128)(2,1)S(1)}, bf16[848,128]{1,0:T(8,128)(2,1)S(1)}, bf16[192,128]{1,0:T(8,128)(2,1)S(1)}, s32[4,64]{1,0:T(4,128)S(1)}, s32[4,64]{1,0:T(4,128)S(1)}) custom-call(s32[1]{0:T(128)} %bitcast.section, f32[2,80,64,128]{3,2,1,0:T(8,128)} %state.3, s32[64,128]{1,0:T(8,128)} %bath.3, bf16[3,64,128]{2,1,0:T(8,128)(2,1)} %bitcast.21, ...), custom_call_target="tpu_custom_call" | custom-call | flops 1000000 | bytes 4000000 | tf_op jit(solution)/shard_map/pallas_call | solution.py:484
  2.2 3.0 %collective-permute-start = (bf16[848,128]{1,0:T(8,128)(2,1)S(1)}, bf16[848,128]{1,0:T(8,128)(2,1)S(1)}, u32[]{:S(2)}, u32[]{:S(2)}) collective-permute-start(bf16[848,128]{1,0:T(8,128)(2,1)S(1)} %get-tuple-element.16), channel_id=1, source_target_pairs={{0,1},{1,2},{2,3},{3,4},{4,5},{5,6},{6,7},{7,8},{8,9},{9,10},{10,1... | collective-permute-start | bytes 651272 | tf_op jit(solution)/shard_map/ppermute | solution.py:449
  5.2 4.1 %collective-permute-start.1 = (bf16[848,128]{1,0:T(8,128)(2,1)S(1)}, bf16[848,128]{1,0:T(8,128)(2,1)S(1)}, u32[]{:S(2)}, u32[]{:S(2)}) collective-permute-start(bf16[848,128]{1,0:T(8,128)(2,1)S(1)} %get-tuple-element.17), channel_id=1, source_target_pairs={{0,15},{1,0},{2,1},{3,2},{4,3},{5,4},{6,5},{7,6},{8,7},{9,8},{10,9... | collective-permute-start | bytes 651272 | tf_op jit(solution)/shard_map/ppermute | solution.py:449
  9.2 0.3 shard_map.87
  9.6 10.4 %all_to_all.22 = s32[16,1,128]{2,1,0:T(1,128)S(1)} all-to-all(s32[16,1,128]{2,1,0:T(1,128)S(1)} %bitcast.18), channel_id=1, replica_groups=mesh['sec'=2,'blk'=16] {'blk'}, dimensions={0} | all-to-all | bytes 16384 | tf_op jit(solution)/shard_map/all_to_all | solution.py:525
  20.0 0.0 collective-permute-done.from_left
  20.0 0.0 collective-permute-done.1.from_right
  20.0 1.2 %shard_map.88 = bf16[896,128]{1,0:T(8,128)(2,1)} custom-call(s32[16,128]{1,0:T(8,128)S(1)} %bitcast.17, bf16[192,128]{1,0:T(8,128)(2,1)S(1)} %get-tuple-element.15.table, bf16[848,128]{1,0:T(8,128)(2,1)S(1)} %collective-permute-done.from_left, bf16[848,128]{1,0:T(8,128)(2,1)S(1)} %collective-permute-done.1.from_right), custom_call_target="tpu_custom_call" | custom-call | flops 10000000 | bytes 1000000 | tf_op jit(solution)/shard_map/pallas_call | solution.py:529
  21.2 3.5 %all-to-all-start.1 = ((bf16[16,56,128]{2,1,0:T(8,128)(2,1)}), bf16[16,56,128]{2,1,0:T(8,128)(2,1)S(1)}, u32[]{:S(2)}, u32[]{:S(2)}) async-start(bf16[16,56,128]{2,1,0:T(8,128)(2,1)} %bitcast.10), calls=%async_computation.1 | async-start | bytes 458752 | tf_op jit(solution)/shard_map/all_to_all | solution.py:539
  24.7 0.0 copy-done.3
  24.7 6.4 %shard_map.89 = (f32[2,80,72,128]{3,2,1,0:T(8,128)}, bf16[80,64,128]{2,1,0:T(8,128)(2,1)}, s32[72,128]{1,0:T(8,128)}, s32[256,128]{1,0:T(8,128)}) custom-call(f32[2,80,64,128]{3,2,1,0:T(8,128)} %state.3, bf16[848,128]{1,0:T(8,128)(2,1)S(1)} %collective-permute-done.from_left, bf16[848,128]{1,0:T(8,128)(2,1)S(1)} %collective-permute-done.1.from_right, ...), custom_call_target="tpu_custom_call" | custom-call | flops 44236800 | bytes 147456000 | tf_op jit(solution)/shard_map/pallas_call | solution.py:542
  31.2 0.0 copy-start.1
  31.2 0.0 copy-start.2
  31.2 1.9 %all-to-all-done.1 = bf16[16,56,128]{2,1,0:T(8,128)(2,1)S(1)} async-done(((bf16[16,56,128]{2,1,0:T(8,128)(2,1)}), bf16[16,56,128]{2,1,0:T(8,128)(2,1)S(1)}, u32[]{:S(2)}, u32[]{:S(2)}) %all-to-all-start.1) | async-done | bytes 229408 | tf_op jit(solution)/shard_map/all_to_all | solution.py:539
  33.0 0.0 copy-start
  33.0 5.9 %shard_map.90.mine = f32[6,72,128]{2,1,0:T(8,128)S(1)} custom-call(bf16[896,128]{1,0:T(8,128)(2,1)S(1)} %bitcast.16, s32[256,128]{1,0:T(8,128)} %get-tuple-element.18.place_from, bf16[848,128]{1,0:T(8,128)(2,1)S(1)} %collective-permute-done.from_left, bf16[848,128]{1,0:T(8,128)(2,1)S(1)} %collective-permute-done.1.from_right, bf16[32768,128]{1,0:T(8,128)(2,1)} %bitcast.20, ...), custom_call_target="tpu_custom_call" | custom-call | flops 67108864 | bytes 8388608 | tf_op jit(solution)/shard_map/pallas_call | solution.py:579
  38.9 0.1 collective-permute-start.2
  39.0 1.5 %collective-permute-done.2.other = f32[6,72,128]{2,1,0:T(8,128)S(1)} collective-permute-done((f32[6,72,128]{2,1,0:T(8,128)S(1)}, f32[6,72,128]{2,1,0:T(8,128)S(1)}, u32[]{:S(2)}, u32[]{:S(2)}) %collective-permute-start.2) | collective-permute-done | bytes 221216 | tf_op jit(solution)/shard_map/ppermute | solution.py:604
  40.5 0.0 copy-done.1
  40.5 0.0 copy-done.2
  40.5 0.0 copy-done
  40.5 8.0 %shard_map.91 = (f32[3,64,128]{2,1,0:T(8,128)}, f32[2,80,64,128]{3,2,1,0:T(8,128)}) custom-call(s32[1]{0:T(128)} %bitcast.section, f32[6,72,128]{2,1,0:T(8,128)S(1)} %shard_map.90.mine, f32[6,72,128]{2,1,0:T(8,128)S(1)} %collective-permute-done.2.other, s32[72,128]{1,0:T(8,128)S(1)} %copy-done.2, f32[2,80,72,128]{3,2,1,0:T(8,128)S(1)} %copy-done, ...), custom_call_target="tpu_custom_call" | custom-call | flops 44236800 | bytes 23592960 | tf_op jit(solution)/shard_map/pallas_call | solution.py:606
  (1 shorter events, 0.0 us)
Async XLA Ops:
  0.6 24.1 %copy-start.3 = (f32[128]{0:T(128)S(1)}, f32[128]{0:T(128)}, u32[]{:S(2)}) copy-start(f32[128]{0:T(128)} %constant.8.clone) | copy-start | bytes 1540
  2.2 17.8 %collective-permute-start = (bf16[848,128]{1,0:T(8,128)(2,1)S(1)}, bf16[848,128]{1,0:T(8,128)(2,1)S(1)}, u32[]{:S(2)}, u32[]{:S(2)}) collective-permute-start(bf16[848,128]{1,0:T(8,128)(2,1)S(1)} %get-tuple-element.16), channel_id=1, source_target_pairs={{0,1},{1,2},{2,3},{3,4},{4,5},{5,6},{6,7},{7,8},{8,9},{9,10},{10,1... | collective-permute-start | bytes 651272 | tf_op jit(solution)/shard_map/ppermute | solution.py:449
  5.2 14.8 %collective-permute-start.1 = (bf16[848,128]{1,0:T(8,128)(2,1)S(1)}, bf16[848,128]{1,0:T(8,128)(2,1)S(1)}, u32[]{:S(2)}, u32[]{:S(2)}) collective-permute-start(bf16[848,128]{1,0:T(8,128)(2,1)S(1)} %get-tuple-element.17), channel_id=1, source_target_pairs={{0,15},{1,0},{2,1},{3,2},{4,3},{5,4},{6,5},{7,6},{8,7},{9,8},{10,9... | collective-permute-start | bytes 651272 | tf_op jit(solution)/shard_map/ppermute | solution.py:449
  21.2 11.8 %all-to-all-start.1 = ((bf16[16,56,128]{2,1,0:T(8,128)(2,1)}), bf16[16,56,128]{2,1,0:T(8,128)(2,1)S(1)}, u32[]{:S(2)}, u32[]{:S(2)}) async-start(bf16[16,56,128]{2,1,0:T(8,128)(2,1)} %bitcast.10), calls=%async_computation.1 | async-start | bytes 458752 | tf_op jit(solution)/shard_map/all_to_all | solution.py:539
  31.2 9.3 %copy-start.1 = (bf16[80,64,128]{2,1,0:T(8,128)(2,1)S(1)}, bf16[80,64,128]{2,1,0:T(8,128)(2,1)}, u32[]{:S(2)}) copy-start(bf16[80,64,128]{2,1,0:T(8,128)(2,1)} %get-tuple-element.21.side) | copy-start | bytes 3932164
  31.2 9.3 %copy-start.2 = (s32[72,128]{1,0:T(8,128)S(1)}, s32[72,128]{1,0:T(8,128)}, u32[]{:S(2)}) copy-start(s32[72,128]{1,0:T(8,128)} %get-tuple-element.19.bath) | copy-start | bytes 110596
  33.0 7.5 %copy-start = (f32[2,80,72,128]{3,2,1,0:T(8,128)S(1)}, f32[2,80,72,128]{3,2,1,0:T(8,128)}, u32[]{:S(2)}) copy-start(f32[2,80,72,128]{3,2,1,0:T(8,128)} %get-tuple-element.20.q) | copy-start | bytes 17694724
  38.9 1.5 %collective-permute-start.2 = (f32[6,72,128]{2,1,0:T(8,128)S(1)}, f32[6,72,128]{2,1,0:T(8,128)S(1)}, u32[]{:S(2)}, u32[]{:S(2)}) collective-permute-start(f32[6,72,128]{2,1,0:T(8,128)S(1)} %shard_map.90.mine), channel_id=1, source_target_pairs={{0,16},{16,0},{1,17},{17,1},{2,18},{18,2},{3,19},{19,3},{4,20},{20... | collective-permute-start | bytes 663560 | tf_op jit(solution)/shard_map/ppermute | solution.py:604

commit v17 on v16

--- a/solution.py
+++ b/solution.py
@@ -20,7 +20,6 @@
 PIECE = 56
 EDGE = 8
 EXTRA = 16
-IN_FLIGHT = 3
 MIB = 2**20
 bf16, f32, i32 = jnp.bfloat16, jnp.float32, jnp.int32
 
@@ -177,8 +176,8 @@
 
 def start_kernel(
     state, from_left, from_right, bath, blocks, ratios,
-    q_result, side_result, bath_result, place_result,
-    q_out, side_out, held, bath_out, halo, bath_in, blocks_in, place, across, band,
+    q_result, rho_result, side_result, bath_result, place_result,
+    q_out, rho_out, side_out, held, bath_out, halo, bath_in, blocks_in, place, across, band,
     sems, sems_out, *, count,
 ):
     tracers, levels, columns, lanes = state.shape
@@ -196,7 +195,7 @@
     blocks_copy = pltpu.make_async_copy(blocks, blocks_in, sems.at[len(chunks) + 1])
     blocks_copy.start()
     bath_copy.start()
-    for copy in reversed(copies[-IN_FLIGHT:]):
+    for copy in reversed(copies):
         copy.start()
     leaving = []
 
@@ -225,22 +224,21 @@
     bath_copy.wait()
     depth = jnp.concatenate([bath_in[...], edge.astype(i32)], axis=0)
     bath_out[...] = depth
-    send(bath_out, bath_result, 2 * len(chunks))
+    send(bath_out, bath_result, 3 * len(chunks))
     blocks_copy.wait()
     for k, (_, rank) in enumerate(ranks(blocks_in, count)):
         arrives = blocks_in[k : k + 1, :].astype(f32) * PIECE + rank
         spread = jnp.transpose(jnp.broadcast_to(arrives, (128, columns)))
         place[k * columns : (k + 1) * columns, :] = spread.astype(i32)
-    send(place, place_result, 2 * len(chunks) + 1)
+    send(place, place_result, 3 * len(chunks) + 1)
     adjacency(across, band, rows)
 
     def side(level):
         wet = level < bath_out[...]
-        starts, masked = [], []
+        masked = []
         for n in range(tracers):
             spot = (n * levels + level) * 8
             full = jnp.concatenate([held[n, level], halo[pl.ds(spot, 8), :]], axis=0)
-            starts.append(full)
             masked.append(jnp.where(wet, full, 0.0))
         tall = across.shape[0]
         count = neighbour_sum(rounded(jnp.where(wet, 1.0, 0.0)), across, band, tall)[:rows]
@@ -249,16 +247,17 @@
         halves = []
         for h in masked:
             halves.append(own * h + neighbour_sum(rounded(h), across, band, tall)[:rows])
-        return wet, starts, halves
+        return halves
 
     def deep(step, below, top):
         level = top - step
-        wet, starts, halves = side(level)
+        halves = side(level)
         rho = ratio_at(ratios, bath_out[...], level)
+        rho_out[level] = rho
         solved = []
         for n in range(tracers):
             q = rho * (halves[n] + below[n])
-            q_out[n, level] = jnp.where(wet, q, starts[n])
+            q_out[n, level] = q
             solved.append(q)
         return tuple(solved)
 
@@ -266,19 +265,19 @@
     for n in reversed(range(len(chunks))):
         low, size = chunks[n]
         copies[n].wait()
-        if n >= IN_FLIGHT:
-            copies[n - IN_FLIGHT].start()
         first = max(low, 2)
         top = low + size - 1
         carry = sweep(top - first + 1, functools.partial(deep, top=top), carry)
         if n == 0:
             for level in (1, 0):
-                wet, starts, halves = side(level)
+                halves = side(level)
+                rho_out[level] = jnp.zeros((rows, lanes), f32)
                 for m in range(tracers):
-                    q_out[m, level] = jnp.where(wet, halves[m], starts[m])
+                    q_out[m, level] = halves[m]
         part = pl.ds(low, size)
-        send(q_out.at[:, part], q_result.at[:, part], 2 * n)
-        send(side_out.at[part], side_result.at[part], 2 * n + 1)
+        send(q_out.at[:, part], q_result.at[:, part], 3 * n)
+        send(rho_out.at[part], rho_result.at[part], 3 * n + 1)
+        send(side_out.at[part], side_result.at[part], 3 * n + 2)
     for copy in leaving:
         copy.wait()
 
@@ -308,14 +307,14 @@
     slots = weights.shape[0] // (columns * width)
     tall = slots * width
     many = from_left.shape[0] - tall - EXTRA
-    group = 8
+    group = 4
     place_copy = pltpu.make_async_copy(place_from, place, sems.at[0])
     fields_copy = pltpu.make_async_copy(own_fields, fields_in, sems.at[1])
     copies = []
     for n in range(columns // group):
         part = pl.ds(n * group * tall, group * tall)
         copies.append(pltpu.make_async_copy(weights.at[part], held.at[part], sems.at[2 + n]))
-    for copy in [place_copy, fields_copy] + copies[:IN_FLIGHT]:
+    for copy in [place_copy] + copies + [fields_copy]:
         copy.start()
     right = from_right[pl.ds(many, EXTRA)].astype(f32)
     left = from_left[pl.ds(many, EXTRA)].astype(f32)
@@ -352,8 +351,6 @@
     one(rows - 1, lambda k: from_left[pl.ds(below + k * width, width)])
     for n in range(columns // group):
         copies[n].wait()
-        if n + IN_FLIGHT < len(copies):
-            copies[n + IN_FLIGHT].start()
         for m in range(group):
             spot = n * group + m
             one(spot, lambda k: held[pl.ds((spot * slots + k) * width, width)])
@@ -368,11 +365,21 @@
 
 
 def finish_kernel(
-    section, mine, other, bath, q, side, ratios, surface, result,
-    values_at, rounded_at, rho, solved, done, across, band, sems_out,
+    section, mine, other, bath, q, rho, side, state, surface, result,
+    values_at, rounded_at, solved, done, across, band, sems, sems_out,
 ):
     tracers, levels, columns, lanes = result.shape
     chunks = chunks_of(levels)
+    starts = []
+    for n in range(tracers):
+        for low, size in chunks:
+            part = pl.ds(low, size)
+            starts.append(
+                pltpu.make_async_copy(
+                    state.at[n, part], done.at[n, part], sems.at[len(starts)]
+                )
+            )
+            starts[-1].start()
     on_ocean = section[0] == 1
     adjacency(across, band, columns + EDGE)
     flux = [jnp.where(on_ocean, other[f], mine[f]) for f in range(3)]
@@ -382,7 +389,6 @@
     depth = bath[...]
     unscale = 1.0 / (SCALE * SCALE)
 
-    rho[2] = ratio_at(ratios, depth, 2)
     link = jnp.where(1 < depth, top_mix, 0.0)
     deeper = jnp.where(2 < depth, DEEP_MIX - DEEP_MIX * rho[2], 0.0)
     second = 1.0 / (1.0 + link + deeper)
@@ -406,14 +412,11 @@
 
     leaving = []
     for n in range(tracers):
-        below = jnp.where(2 < depth, q[n, 2], 0.0)
-        value, carry = top_levels(n, columns + EDGE, (q[n, 0], q[n, 1]), below, SCALE)
+        value, carry = top_levels(n, columns + EDGE, (q[n, 0], q[n, 1]), q[n, 2], SCALE)
         put(n, 0, jnp.where(0 < depth, value, 0.0))
         put(n, 1, carry)
         for level in range(2, levels):
-            if n == 0 and level > 2:
-                rho[level] = ratio_at(ratios, depth, level)
-            carry = jnp.where(level < depth, q[n, level], 0.0) + rho[level] * carry
+            carry = q[n, level] + rho[level] * carry
             put(n, level, carry)
 
         carry = jnp.zeros((columns, lanes), f32)
@@ -425,13 +428,15 @@
             n, columns, (half_at(n, 0), half_at(n, 1)), carry, SCALE * SCALE
         )
         surface[n] = jnp.where(on_ocean, value * unscale, other[n, pl.ds(0, columns)])
+        for copy in starts[n * len(chunks) : (n + 1) * len(chunks)]:
+            copy.wait()
         done[n, 0] = value * unscale
         for low, size in chunks:
             for level in range(max(low, 1), low + size):
                 if level > 1:
                     carry = solved[n, level] + rho[level, pl.ds(0, columns)] * carry
-                start = q[n, level, pl.ds(0, columns)]
-                done[n, level] = jnp.where(level < depth[:columns], carry * unscale, start)
+                wet = level < depth[:columns]
+                done[n, level] = jnp.where(wet, carry * unscale, done[n, level])
             part = pl.ds(low, size)
             leaving.append(
                 pltpu.make_async_copy(
@@ -539,18 +544,20 @@
     columns_in = lax.all_to_all(served, "blk", split_axis=0, concat_axis=0, tiled=True)
 
     ratios = ratios_by_height(levels, lanes)
-    q, side, bath, place = pl.pallas_call(
+    q, rho, side, bath, place = pl.pallas_call(
         functools.partial(start_kernel, count=count),
         out_shape=(
             pltpu.HBM((tracers, levels, rows, lanes), f32),
+            pltpu.HBM((levels, rows, lanes), f32),
             pltpu.HBM((levels, columns, lanes), bf16),
             pltpu.HBM((rows, lanes), i32),
             pltpu.HBM((slots * columns, 128), i32),
         ),
         in_specs=[hbm, vmem, vmem, hbm, hbm, vmem],
-        out_specs=(hbm,) * 4,
+        out_specs=(hbm,) * 5,
         scratch_shapes=[
             pltpu.VMEM((tracers, levels, rows, lanes), f32),
+            pltpu.VMEM((levels, rows, lanes), f32),
             pltpu.VMEM((levels, columns, lanes), bf16),
             pltpu.VMEM(ocean_state.shape, f32),
             pltpu.VMEM((rows, lanes), i32),
@@ -561,7 +568,7 @@
             pltpu.VMEM((tall_rows, lanes), bf16),
             pltpu.VMEM((lanes, lanes), bf16),
             pltpu.SemaphoreType.DMA((pieces + 2,)),
-            pltpu.SemaphoreType.DMA((2 * pieces + 2,)),
+            pltpu.SemaphoreType.DMA((3 * pieces + 2,)),
         ],
         compiler_params=pltpu.CompilerParams(vmem_limit_bytes=28 * MIB),
         cost_estimate=pl.CostEstimate(
@@ -587,7 +594,7 @@
             pltpu.VMEM(weights.shape, bf16),
             pltpu.VMEM(fields.shape, bf16),
             pltpu.VMEM((slots * columns, 128), i32),
-            pltpu.SemaphoreType.DMA((2 + columns // 8,)),
+            pltpu.SemaphoreType.DMA((2 + columns // 4,)),
         ],
         compiler_params=pltpu.CompilerParams(vmem_limit_bytes=20 * MIB),
         cost_estimate=pl.CostEstimate(
@@ -606,16 +613,16 @@
     surface, result = pl.pallas_call(
         finish_kernel,
         out_shape=(shaped((3, columns, lanes), f32), shaped(ocean_state.shape, f32)),
-        in_specs=[smem] + [vmem] * 6,
+        in_specs=[smem] + [vmem] * 6 + [hbm],
         out_specs=(vmem, hbm),
         scratch_shapes=[
             pltpu.VMEM(ocean_state.shape, f32),
             pltpu.VMEM((tracers, levels, tall_rows, lanes), bf16),
-            pltpu.VMEM((levels, rows, lanes), f32),
             pltpu.VMEM(ocean_state.shape, f32),
             pltpu.VMEM(ocean_state.shape, f32),
             pltpu.VMEM((tall_rows, lanes), bf16),
             pltpu.VMEM((lanes, lanes), bf16),
+            pltpu.SemaphoreType.DMA((tracers * pieces,)),
             pltpu.SemaphoreType.DMA((tracers * pieces,)),
         ],
         compiler_params=pltpu.CompilerParams(vmem_limit_bytes=26 * MIB),
@@ -628,8 +635,9 @@
         other,
         in_vmem(bath),
         in_vmem(q),
+        in_vmem(rho),
         in_vmem(side),
-        ratios,
+        in_hbm(ocean_state),
     )
     return (surface[None], result)
 

time: 48.8 us -> 51.7 us (1.059)
  local copies, waits for them, and re-layouts: 0.03 us -> 1.34 us
  Pallas kernels: 23.3 us -> 24.2 us
  starting transfers between devices: 10.6 us -> 11.3 us
    pallas_call x1, Pallas kernels: 5.9 us -> 7.4 us  [per_device(): pl.pallas_call(remap_kernel, out_shape=shaped((6, rows, lanes), f32), in_...]
    unnamed x8 -> x10, local copies, waits for them, and re-layouts: 0.02 us -> 1.33 us
    all_to_all x1, starting transfers between devices: 3.53 us -> 4.18 us  [per_device(): lax.all_to_all(served, 'blk', split_axis=0, concat_axis=0, tiled=True)]
    pallas_call x1, Pallas kernels: 7.96 us -> 7.39 us  [per_device(): pl.pallas_call(finish_kernel, out_shape=(shaped((3, columns, lanes), f32)...]
  transfers between devices with their start and end apart: 4 -> 4, of which waited for: 2 -> 2; matrix products, arithmetic and copies ran while one was open for 0% -> 0% of each run, Pallas kernels for 14% -> 13%
where the time goes in v17:
time: 51.7 us; the launch traced here: 51.4 us
  Pallas kernels  24.2 us (47%)
  starting transfers between devices  11.3 us (22%)
  blocking collectives  10.4 us (20%)
  waiting for transfers between devices  3.39 us (7%)
  local copies, waits for them, and re-layouts  1.34 us (3%)
  between operations  0.73 us (1%)
    all_to_all x1, blocking collectives, per_device(): lax.all_to_all(request, 'blk', split_axis=0, concat_axis=0, tiled=True)  10.4 us
    pallas_call x1, Pallas kernels, per_device(): pl.pallas_call(remap_kernel, out_shape=shaped((6, rows, lanes), f32), in_...  7.4 us
    pallas_call x1, Pallas kernels, per_device(): pl.pallas_call(finish_kernel, out_shape=(shaped((3, columns, lanes), f32)...  7.39 us
    ppermute x2, starting transfers between devices, shift(): lax.ppermute(value, axis, [(i, (i + by) % count) for i in range(count)])  7.05 us
    pallas_call x1, Pallas kernels, per_device(): pl.pallas_call(functools.partial(start_kernel, count=count), out_shape=(p...  6.39 us
    all_to_all x1, starting transfers between devices, per_device(): lax.all_to_all(served, 'blk', split_axis=0, concat_axis=0, tiled=True)  4.18 us
    all_to_all x1, waiting for transfers between devices, per_device(): lax.all_to_all(served, 'blk', split_axis=0, concat_axis=0, tiled=True)  1.92 us
    pallas_call x1, Pallas kernels, per_device(): pl.pallas_call(pack_kernel, out_shape=(payload, payload, shaped((FIELDS *...  1.54 us
  transfers between devices with their start and end apart: 4, of which 2 were waited for; matrix products, arithmetic and copies ran while one was open for 0% of the time, Pallas kernels for 13%

profile of v17, /device:TPU:0, one launch (start us, length us, event | category | flops | bytes accessed | tf_op | source)
XLA Modules:
  0.0 51.4 jit_solution(3867492641022131502)
XLA Ops:
  0.6 0.0 copy-start.4
  0.6 1.5 %shard_map.86 = (bf16[848,128]{1,0:T(8,128)(2,1)S(1)}, bf16[848,128]{1,0:T(8,128)(2,1)S(1)}, bf16[192,128]{1,0:T(8,128)(2,1)S(1)}, s32[4,64]{1,0:T(4,128)S(1)}, s32[4,64]{1,0:T(4,128)S(1)}) custom-call(s32[1]{0:T(128)} %bitcast.section, f32[2,80,64,128]{3,2,1,0:T(8,128)} %state.5, s32[64,128]{1,0:T(8,128)} %bath.3, bf16[3,64,128]{2,1,0:T(8,128)(2,1)} %bitcast.20, ...), custom_call_target="tpu_custom_call" | custom-call | flops 1000000 | bytes 4000000 | tf_op jit(solution)/shard_map/pallas_call | solution.py:489
  2.2 3.0 %collective-permute-start = (bf16[848,128]{1,0:T(8,128)(2,1)S(1)}, bf16[848,128]{1,0:T(8,128)(2,1)S(1)}, u32[]{:S(2)}, u32[]{:S(2)}) collective-permute-start(bf16[848,128]{1,0:T(8,128)(2,1)S(1)} %get-tuple-element.17), channel_id=1, source_target_pairs={{0,1},{1,2},{2,3},{3,4},{4,5},{5,6},{6,7},{7,8},{8,9},{9,10},{10,1... | collective-permute-start | bytes 651272 | tf_op jit(solution)/shard_map/ppermute | solution.py:454
  5.2 4.1 %collective-permute-start.1 = (bf16[848,128]{1,0:T(8,128)(2,1)S(1)}, bf16[848,128]{1,0:T(8,128)(2,1)S(1)}, u32[]{:S(2)}, u32[]{:S(2)}) collective-permute-start(bf16[848,128]{1,0:T(8,128)(2,1)S(1)} %get-tuple-element.18), channel_id=1, source_target_pairs={{0,15},{1,0},{2,1},{3,2},{4,3},{5,4},{6,5},{7,6},{8,7},{9,8},{10,9... | collective-permute-start | bytes 651272 | tf_op jit(solution)/shard_map/ppermute | solution.py:454
  9.2 0.3 shard_map.87
  9.6 10.4 %all_to_all.22 = s32[16,1,128]{2,1,0:T(1,128)S(1)} all-to-all(s32[16,1,128]{2,1,0:T(1,128)S(1)} %bitcast.17), channel_id=1, replica_groups=mesh['sec'=2,'blk'=16] {'blk'}, dimensions={0} | all-to-all | bytes 16384 | tf_op jit(solution)/shard_map/all_to_all | solution.py:530
  20.0 0.0 collective-permute-done.from_left
  20.0 0.0 collective-permute-done.1.from_right
  20.0 1.2 %shard_map.88 = bf16[896,128]{1,0:T(8,128)(2,1)} custom-call(s32[16,128]{1,0:T(8,128)S(1)} %bitcast.16, bf16[192,128]{1,0:T(8,128)(2,1)S(1)} %get-tuple-element.16.table, bf16[848,128]{1,0:T(8,128)(2,1)S(1)} %collective-permute-done.from_left, bf16[848,128]{1,0:T(8,128)(2,1)S(1)} %collective-permute-done.1.from_right), custom_call_target="tpu_custom_call" | custom-call | flops 10000000 | bytes 1000000 | tf_op jit(solution)/shard_map/pallas_call | solution.py:534
  21.2 4.2 %all-to-all-start.1 = ((bf16[16,56,128]{2,1,0:T(8,128)(2,1)}), bf16[16,56,128]{2,1,0:T(8,128)(2,1)}, u32[]{:S(2)}, u32[]{:S(2)}) async-start(bf16[16,56,128]{2,1,0:T(8,128)(2,1)} %bitcast.10), calls=%async_computation.1 | async-start | bytes 458752 | tf_op jit(solution)/shard_map/all_to_all | solution.py:544
  25.4 0.0 copy-done.4
  25.4 6.4 %shard_map.89 = (f32[2,80,72,128]{3,2,1,0:T(8,128)}, f32[80,72,128]{2,1,0:T(8,128)}, bf16[80,64,128]{2,1,0:T(8,128)(2,1)}, s32[72,128]{1,0:T(8,128)}, s32[256,128]{1,0:T(8,128)}) custom-call(f32[2,80,64,128]{3,2,1,0:T(8,128)} %state.5, bf16[848,128]{1,0:T(8,128)(2,1)S(1)} %collective-permute-done.from_left, ...), custom_call_target="tpu_custom_call" | custom-call | flops 44236800 | bytes 147456000 | tf_op jit(solution)/shard_map/pallas_call | solution.py:547
  31.8 0.0 copy-start.1
  31.8 0.0 copy-start.3
  31.8 1.9 %all-to-all-done.1 = bf16[16,56,128]{2,1,0:T(8,128)(2,1)} async-done(((bf16[16,56,128]{2,1,0:T(8,128)(2,1)}), bf16[16,56,128]{2,1,0:T(8,128)(2,1)}, u32[]{:S(2)}, u32[]{:S(2)}) %all-to-all-start.1) | async-done | bytes 229408 | tf_op jit(solution)/shard_map/all_to_all | solution.py:544
  33.7 0.0 copy-start
  33.7 7.4 %shard_map.90.mine = f32[6,72,128]{2,1,0:T(8,128)S(1)} custom-call(bf16[896,128]{1,0:T(8,128)(2,1)} %bitcast.11.columns_in, s32[256,128]{1,0:T(8,128)} %get-tuple-element.19.place_from, bf16[848,128]{1,0:T(8,128)(2,1)S(1)} %collective-permute-done.from_left, bf16[848,128]{1,0:T(8,128)(2,1)S(1)} %collective-permute-done.1.from_right, ...), custom_call_target="tpu_custom_call" | custom-call | flops 67108864 | bytes 8388608 | tf_op jit(solution)/shard_map/pallas_call | solution.py:586
  41.1 0.1 collective-permute-start.2
  41.2 1.5 %collective-permute-done.2.other = f32[6,72,128]{2,1,0:T(8,128)S(1)} collective-permute-done((f32[6,72,128]{2,1,0:T(8,128)S(1)}, f32[6,72,128]{2,1,0:T(8,128)S(1)}, u32[]{:S(2)}, u32[]{:S(2)}) %collective-permute-start.2) | collective-permute-done | bytes 221216 | tf_op jit(solution)/shard_map/ppermute | solution.py:611
  42.7 0.0 copy-done.1
  42.7 0.0 copy-done.3
  42.7 0.0 copy-done
  42.7 0.0 copy-start.2
  42.7 1.3 %copy-done.2 = bf16[80,64,128]{2,1,0:T(8,128)(2,1)S(1)} copy-done((bf16[80,64,128]{2,1,0:T(8,128)(2,1)S(1)}, bf16[80,64,128]{2,1,0:T(8,128)(2,1)}, u32[]{:S(2)}) %copy-start.2) | copy-done | bytes 1310744
  44.0 7.4 %shard_map.91 = (f32[3,64,128]{2,1,0:T(8,128)}, f32[2,80,64,128]{3,2,1,0:T(8,128)}) custom-call(s32[1]{0:T(128)} %bitcast.section, f32[6,72,128]{2,1,0:T(8,128)S(1)} %shard_map.90.mine, f32[6,72,128]{2,1,0:T(8,128)S(1)} %collective-permute-done.2.other, s32[72,128]{1,0:T(8,128)S(1)} %copy-done.3, f32[2,80,72,128]{3,2,1,0:T(8,128)S(1)} %copy-done, ...), custom_call_target="tpu_custom_call" | custom-call | flops 44236800 | bytes 23592960 | tf_op jit(solution)/shard_map/pallas_call | solution.py:613
  (1 shorter events, 0.0 us)
Async XLA Ops:
  0.6 24.7 %copy-start.4 = (f32[128]{0:T(128)S(1)}, f32[128]{0:T(128)}, u32[]{:S(2)}) copy-start(f32[128]{0:T(128)} %constant.8.clone) | copy-start | bytes 1540
  2.2 17.8 %collective-permute-start = (bf16[848,128]{1,0:T(8,128)(2,1)S(1)}, bf16[848,128]{1,0:T(8,128)(2,1)S(1)}, u32[]{:S(2)}, u32[]{:S(2)}) collective-permute-start(bf16[848,128]{1,0:T(8,128)(2,1)S(1)} %get-tuple-element.17), channel_id=1, source_target_pairs={{0,1},{1,2},{2,3},{3,4},{4,5},{5,6},{6,7},{7,8},{8,9},{9,10},{10,1... | collective-permute-start | bytes 651272 | tf_op jit(solution)/shard_map/ppermute | solution.py:454
  5.2 14.8 %collective-permute-start.1 = (bf16[848,128]{1,0:T(8,128)(2,1)S(1)}, bf16[848,128]{1,0:T(8,128)(2,1)S(1)}, u32[]{:S(2)}, u32[]{:S(2)}) collective-permute-start(bf16[848,128]{1,0:T(8,128)(2,1)S(1)} %get-tuple-element.18), channel_id=1, source_target_pairs={{0,15},{1,0},{2,1},{3,2},{4,3},{5,4},{6,5},{7,6},{8,7},{9,8},{10,9... | collective-permute-start | bytes 651272 | tf_op jit(solution)/shard_map/ppermute | solution.py:454
  21.2 12.6 %all-to-all-start.1 = ((bf16[16,56,128]{2,1,0:T(8,128)(2,1)}), bf16[16,56,128]{2,1,0:T(8,128)(2,1)}, u32[]{:S(2)}, u32[]{:S(2)}) async-start(bf16[16,56,128]{2,1,0:T(8,128)(2,1)} %bitcast.10), calls=%async_computation.1 | async-start | bytes 458752 | tf_op jit(solution)/shard_map/all_to_all | solution.py:544
  31.8 10.9 %copy-start.1 = (f32[80,72,128]{2,1,0:T(8,128)S(1)}, f32[80,72,128]{2,1,0:T(8,128)}, u32[]{:S(2)}) copy-start(f32[80,72,128]{2,1,0:T(8,128)} %get-tuple-element.22.rho) | copy-start | bytes 8847364
  31.8 10.9 %copy-start.3 = (s32[72,128]{1,0:T(8,128)S(1)}, s32[72,128]{1,0:T(8,128)}, u32[]{:S(2)}) copy-start(s32[72,128]{1,0:T(8,128)} %get-tuple-element.20.bath) | copy-start | bytes 110596
  33.7 9.0 %copy-start = (f32[2,80,72,128]{3,2,1,0:T(8,128)S(1)}, f32[2,80,72,128]{3,2,1,0:T(8,128)}, u32[]{:S(2)}) copy-start(f32[2,80,72,128]{3,2,1,0:T(8,128)} %get-tuple-element.21.q) | copy-start | bytes 17694724
  41.1 1.5 %collective-permute-start.2 = (f32[6,72,128]{2,1,0:T(8,128)S(1)}, f32[6,72,128]{2,1,0:T(8,128)S(1)}, u32[]{:S(2)}, u32[]{:S(2)}) collective-permute-start(f32[6,72,128]{2,1,0:T(8,128)S(1)} %shard_map.90.mine), channel_id=1, source_target_pairs={{0,16},{16,0},{1,17},{17,1},{2,18},{18,2},{3,19},{19,3},{4,20},{20... | collective-permute-start | bytes 663560 | tf_op jit(solution)/shard_map/ppermute | solution.py:611
  42.7 1.3 %copy-start.2 = (bf16[80,64,128]{2,1,0:T(8,128)(2,1)S(1)}, bf16[80,64,128]{2,1,0:T(8,128)(2,1)}, u32[]{:S(2)}) copy-start(bf16[80,64,128]{2,1,0:T(8,128)(2,1)} %get-tuple-element.23.side) | copy-start | bytes 3932164

commit v18 on v17

--- a/solution.py
+++ b/solution.py
@@ -176,8 +176,8 @@
 
 def start_kernel(
     state, from_left, from_right, bath, blocks, ratios,
-    q_result, rho_result, side_result, bath_result, place_result,
-    q_out, rho_out, side_out, held, bath_out, halo, bath_in, blocks_in, place, across, band,
+    q_result, side_result, bath_result, place_result,
+    q_out, side_out, held, bath_out, halo, bath_in, blocks_in, place, across, band,
     sems, sems_out, *, count,
 ):
     tracers, levels, columns, lanes = state.shape
@@ -224,13 +224,13 @@
     bath_copy.wait()
     depth = jnp.concatenate([bath_in[...], edge.astype(i32)], axis=0)
     bath_out[...] = depth
-    send(bath_out, bath_result, 3 * len(chunks))
+    send(bath_out, bath_result, 2 * len(chunks))
     blocks_copy.wait()
     for k, (_, rank) in enumerate(ranks(blocks_in, count)):
         arrives = blocks_in[k : k + 1, :].astype(f32) * PIECE + rank
         spread = jnp.transpose(jnp.broadcast_to(arrives, (128, columns)))
         place[k * columns : (k + 1) * columns, :] = spread.astype(i32)
-    send(place, place_result, 3 * len(chunks) + 1)
+    send(place, place_result, 2 * len(chunks) + 1)
     adjacency(across, band, rows)
 
     def side(level):
@@ -253,7 +253,6 @@
         level = top - step
         halves = side(level)
         rho = ratio_at(ratios, bath_out[...], level)
-        rho_out[level] = rho
         solved = []
         for n in range(tracers):
             q = rho * (halves[n] + below[n])
@@ -271,13 +270,11 @@
         if n == 0:
             for level in (1, 0):
                 halves = side(level)
-                rho_out[level] = jnp.zeros((rows, lanes), f32)
                 for m in range(tracers):
                     q_out[m, level] = halves[m]
         part = pl.ds(low, size)
-        send(q_out.at[:, part], q_result.at[:, part], 3 * n)
-        send(rho_out.at[part], rho_result.at[part], 3 * n + 1)
-        send(side_out.at[part], side_result.at[part], 3 * n + 2)
+        send(q_out.at[:, part], q_result.at[:, part], 2 * n)
+        send(side_out.at[part], side_result.at[part], 2 * n + 1)
     for copy in leaving:
         copy.wait()
 
@@ -307,7 +304,7 @@
     slots = weights.shape[0] // (columns * width)
     tall = slots * width
     many = from_left.shape[0] - tall - EXTRA
-    group = 4
+    group = 8
     place_copy = pltpu.make_async_copy(place_from, place, sems.at[0])
     fields_copy = pltpu.make_async_copy(own_fields, fields_in, sems.at[1])
     copies = []
@@ -365,8 +362,8 @@
 
 
 def finish_kernel(
-    section, mine, other, bath, q, rho, side, state, surface, result,
-    values_at, rounded_at, solved, done, across, band, sems, sems_out,
+    section, mine, other, bath, q, side, ratios, state, surface, result,
+    values_at, rounded_at, rho, solved, done, across, band, sems, sems_out,
 ):
     tracers, levels, columns, lanes = result.shape
     chunks = chunks_of(levels)
@@ -389,6 +386,7 @@
     depth = bath[...]
     unscale = 1.0 / (SCALE * SCALE)
 
+    rho[2] = ratio_at(ratios, depth, 2)
     link = jnp.where(1 < depth, top_mix, 0.0)
     deeper = jnp.where(2 < depth, DEEP_MIX - DEEP_MIX * rho[2], 0.0)
     second = 1.0 / (1.0 + link + deeper)
@@ -416,6 +414,8 @@
         put(n, 0, jnp.where(0 < depth, value, 0.0))
         put(n, 1, carry)
         for level in range(2, levels):
+            if n == 0 and level > 2:
+                rho[level] = ratio_at(ratios, depth, level)
             carry = q[n, level] + rho[level] * carry
             put(n, level, carry)
 
@@ -544,20 +544,18 @@
     columns_in = lax.all_to_all(served, "blk", split_axis=0, concat_axis=0, tiled=True)
 
     ratios = ratios_by_height(levels, lanes)
-    q, rho, side, bath, place = pl.pallas_call(
+    q, side, bath, place = pl.pallas_call(
         functools.partial(start_kernel, count=count),
         out_shape=(
             pltpu.HBM((tracers, levels, rows, lanes), f32),
-            pltpu.HBM((levels, rows, lanes), f32),
             pltpu.HBM((levels, columns, lanes), bf16),
             pltpu.HBM((rows, lanes), i32),
             pltpu.HBM((slots * columns, 128), i32),
         ),
         in_specs=[hbm, vmem, vmem, hbm, hbm, vmem],
-        out_specs=(hbm,) * 5,
+        out_specs=(hbm,) * 4,
         scratch_shapes=[
             pltpu.VMEM((tracers, levels, rows, lanes), f32),
-            pltpu.VMEM((levels, rows, lanes), f32),
             pltpu.VMEM((levels, columns, lanes), bf16),
             pltpu.VMEM(ocean_state.shape, f32),
             pltpu.VMEM((rows, lanes), i32),
@@ -568,7 +566,7 @@
             pltpu.VMEM((tall_rows, lanes), bf16),
             pltpu.VMEM((lanes, lanes), bf16),
             pltpu.SemaphoreType.DMA((pieces + 2,)),
-            pltpu.SemaphoreType.DMA((3 * pieces + 2,)),
+            pltpu.SemaphoreType.DMA((2 * pieces + 2,)),
         ],
         compiler_params=pltpu.CompilerParams(vmem_limit_bytes=28 * MIB),
         cost_estimate=pl.CostEstimate(
@@ -594,7 +592,7 @@
             pltpu.VMEM(weights.shape, bf16),
             pltpu.VMEM(fields.shape, bf16),
             pltpu.VMEM((slots * columns, 128), i32),
-            pltpu.SemaphoreType.DMA((2 + columns // 4,)),
+            pltpu.SemaphoreType.DMA((2 + columns // 8,)),
         ],
         compiler_params=pltpu.CompilerParams(vmem_limit_bytes=20 * MIB),
         cost_estimate=pl.CostEstimate(
@@ -618,6 +616,7 @@
         scratch_shapes=[
             pltpu.VMEM(ocean_state.shape, f32),
             pltpu.VMEM((tracers, levels, tall_rows, lanes), bf16),
+            pltpu.VMEM((levels, rows, lanes), f32),
             pltpu.VMEM(ocean_state.shape, f32),
             pltpu.VMEM(ocean_state.shape, f32),
             pltpu.VMEM((tall_rows, lanes), bf16),
@@ -635,8 +634,8 @@
         other,
         in_vmem(bath),
         in_vmem(q),
-        in_vmem(rho),
         in_vmem(side),
+        ratios,
         in_hbm(ocean_state),
     )
     return (surface[None], result)

time: 51.7 us -> 48.4 us (0.936)
  Pallas kernels: 24.2 us -> 22.7 us
  local copies, waits for them, and re-layouts: 1.34 us -> 0.03 us
  starting transfers between devices: 11.3 us -> 10.6 us
    pallas_call x1, Pallas kernels: 7.4 us -> 5.26 us  [per_device(): pl.pallas_call(remap_kernel, out_shape=shaped((6, rows, lanes), f32), in_...]
    unnamed x10 -> x8, local copies, waits for them, and re-layouts: 1.33 us -> 0.02 us
    pallas_call x1, Pallas kernels: 7.39 us -> 8.22 us  [per_device(): pl.pallas_call(finish_kernel, out_shape=(shaped((3, columns, lanes), f32)...]
    all_to_all x1, starting transfers between devices: 4.18 us -> 3.53 us  [per_device(): lax.all_to_all(served, 'blk', split_axis=0, concat_axis=0, tiled=True)]
  transfers between devices with their start and end apart: 4 -> 4, of which waited for: 2 -> 2; matrix products, arithmetic and copies ran while one was open for 0% -> 0% of each run, Pallas kernels for 13% -> 14%
where the time goes in v18:
time: 48.4 us; the launch traced here: 48.1 us
  Pallas kernels  22.7 us (47%)
  starting transfers between devices  10.6 us (22%)
  blocking collectives  10.4 us (21%)
  waiting for transfers between devices  3.51 us (7%)
  between operations  0.72 us (1%)
    all_to_all x1, blocking collectives, per_device(): lax.all_to_all(request, 'blk', split_axis=0, concat_axis=0, tiled=True)  10.4 us
    pallas_call x1, Pallas kernels, per_device(): pl.pallas_call(finish_kernel, out_shape=(shaped((3, columns, lanes), f32)...  8.22 us
    ppermute x2, starting transfers between devices, shift(): lax.ppermute(value, axis, [(i, (i + by) % count) for i in range(count)])  7.05 us
    pallas_call x1, Pallas kernels, per_device(): pl.pallas_call(functools.partial(start_kernel, count=count), out_shape=(p...  6.22 us
    pallas_call x1, Pallas kernels, per_device(): pl.pallas_call(remap_kernel, out_shape=shaped((6, rows, lanes), f32), in_...  5.26 us
    all_to_all x1, starting transfers between devices, per_device(): lax.all_to_all(served, 'blk', split_axis=0, concat_axis=0, tiled=True)  3.53 us
    all_to_all x1, waiting for transfers between devices, per_device(): lax.all_to_all(served, 'blk', split_axis=0, concat_axis=0, tiled=True)  2.04 us
    pallas_call x1, Pallas kernels, per_device(): pl.pallas_call(pack_kernel, out_shape=(payload, payload, shaped((FIELDS *...  1.54 us
  transfers between devices with their start and end apart: 4, of which 2 were waited for; matrix products, arithmetic and copies ran while one was open for 0% of the time, Pallas kernels for 14%

profile of v18, /device:TPU:0, one launch (start us, length us, event | category | flops | bytes accessed | tf_op | source)
XLA Modules:
  0.0 48.1 jit_solution(2231799684293682572)
XLA Ops:
  0.6 0.0 copy-start.3
  0.6 1.5 %shard_map.86 = (bf16[848,128]{1,0:T(8,128)(2,1)S(1)}, bf16[848,128]{1,0:T(8,128)(2,1)S(1)}, bf16[192,128]{1,0:T(8,128)(2,1)S(1)}, s32[4,64]{1,0:T(4,128)S(1)}, s32[4,64]{1,0:T(4,128)S(1)}) custom-call(s32[1]{0:T(128)} %bitcast.section, f32[2,80,64,128]{3,2,1,0:T(8,128)} %state.5, s32[64,128]{1,0:T(8,128)} %bath.3, bf16[3,64,128]{2,1,0:T(8,128)(2,1)} %bitcast.21, ...), custom_call_target="tpu_custom_call" | custom-call | flops 1000000 | bytes 4000000 | tf_op jit(solution)/shard_map/pallas_call | solution.py:489
  2.2 3.0 %collective-permute-start = (bf16[848,128]{1,0:T(8,128)(2,1)S(1)}, bf16[848,128]{1,0:T(8,128)(2,1)S(1)}, u32[]{:S(2)}, u32[]{:S(2)}) collective-permute-start(bf16[848,128]{1,0:T(8,128)(2,1)S(1)} %get-tuple-element.16), channel_id=1, source_target_pairs={{0,1},{1,2},{2,3},{3,4},{4,5},{5,6},{6,7},{7,8},{8,9},{9,10},{10,1... | collective-permute-start | bytes 651272 | tf_op jit(solution)/shard_map/ppermute | solution.py:454
  5.2 4.1 %collective-permute-start.1 = (bf16[848,128]{1,0:T(8,128)(2,1)S(1)}, bf16[848,128]{1,0:T(8,128)(2,1)S(1)}, u32[]{:S(2)}, u32[]{:S(2)}) collective-permute-start(bf16[848,128]{1,0:T(8,128)(2,1)S(1)} %get-tuple-element.17), channel_id=1, source_target_pairs={{0,15},{1,0},{2,1},{3,2},{4,3},{5,4},{6,5},{7,6},{8,7},{9,8},{10,9... | collective-permute-start | bytes 651272 | tf_op jit(solution)/shard_map/ppermute | solution.py:454
  9.2 0.3 shard_map.87
  9.6 10.4 %all_to_all.22 = s32[16,1,128]{2,1,0:T(1,128)S(1)} all-to-all(s32[16,1,128]{2,1,0:T(1,128)S(1)} %bitcast.18), channel_id=1, replica_groups=mesh['sec'=2,'blk'=16] {'blk'}, dimensions={0} | all-to-all | bytes 16384 | tf_op jit(solution)/shard_map/all_to_all | solution.py:530
  20.0 0.0 collective-permute-done.from_left
  20.0 0.0 collective-permute-done.1.from_right
  20.0 1.2 %shard_map.88 = bf16[896,128]{1,0:T(8,128)(2,1)} custom-call(s32[16,128]{1,0:T(8,128)S(1)} %bitcast.17, bf16[192,128]{1,0:T(8,128)(2,1)S(1)} %get-tuple-element.15.table, bf16[848,128]{1,0:T(8,128)(2,1)S(1)} %collective-permute-done.from_left, bf16[848,128]{1,0:T(8,128)(2,1)S(1)} %collective-permute-done.1.from_right), custom_call_target="tpu_custom_call" | custom-call | flops 10000000 | bytes 1000000 | tf_op jit(solution)/shard_map/pallas_call | solution.py:534
  21.2 3.5 %all-to-all-start.1 = ((bf16[16,56,128]{2,1,0:T(8,128)(2,1)}), bf16[16,56,128]{2,1,0:T(8,128)(2,1)S(1)}, u32[]{:S(2)}, u32[]{:S(2)}) async-start(bf16[16,56,128]{2,1,0:T(8,128)(2,1)} %bitcast.10), calls=%async_computation.1 | async-start | bytes 458752 | tf_op jit(solution)/shard_map/all_to_all | solution.py:544
  24.7 0.0 copy-done.3
  24.7 6.2 %shard_map.89 = (f32[2,80,72,128]{3,2,1,0:T(8,128)}, bf16[80,64,128]{2,1,0:T(8,128)(2,1)}, s32[72,128]{1,0:T(8,128)}, s32[256,128]{1,0:T(8,128)}) custom-call(f32[2,80,64,128]{3,2,1,0:T(8,128)} %state.5, bf16[848,128]{1,0:T(8,128)(2,1)S(1)} %collective-permute-done.from_left, bf16[848,128]{1,0:T(8,128)(2,1)S(1)} %collective-permute-done.1.from_right, ...), custom_call_target="tpu_custom_call" | custom-call | flops 44236800 | bytes 147456000 | tf_op jit(solution)/shard_map/pallas_call | solution.py:547
  31.0 0.0 copy-start.1
  31.0 0.0 copy-start.2
  31.0 2.0 %all-to-all-done.1 = bf16[16,56,128]{2,1,0:T(8,128)(2,1)S(1)} async-done(((bf16[16,56,128]{2,1,0:T(8,128)(2,1)}), bf16[16,56,128]{2,1,0:T(8,128)(2,1)S(1)}, u32[]{:S(2)}, u32[]{:S(2)}) %all-to-all-start.1) | async-done | bytes 229408 | tf_op jit(solution)/shard_map/all_to_all | solution.py:544
  33.0 0.0 copy-start
  33.0 5.3 %shard_map.90.mine = f32[6,72,128]{2,1,0:T(8,128)S(1)} custom-call(bf16[896,128]{1,0:T(8,128)(2,1)S(1)} %bitcast.16, s32[256,128]{1,0:T(8,128)} %get-tuple-element.18.place_from, bf16[848,128]{1,0:T(8,128)(2,1)S(1)} %collective-permute-done.from_left, bf16[848,128]{1,0:T(8,128)(2,1)S(1)} %collective-permute-done.1.from_right, bf16[32768,128]{1,0:T(8,128)(2,1)} %bitcast.20, ...), custom_call_target="tpu_custom_call" | custom-call | flops 67108864 | bytes 8388608 | tf_op jit(solution)/shard_map/pallas_call | solution.py:584
  38.3 0.1 collective-permute-start.2
  38.4 1.5 %collective-permute-done.2.other = f32[6,72,128]{2,1,0:T(8,128)S(1)} collective-permute-done((f32[6,72,128]{2,1,0:T(8,128)S(1)}, f32[6,72,128]{2,1,0:T(8,128)S(1)}, u32[]{:S(2)}, u32[]{:S(2)}) %collective-permute-start.2) | collective-permute-done | bytes 221216 | tf_op jit(solution)/shard_map/ppermute | solution.py:609
  39.8 0.0 copy-done.1
  39.8 0.0 copy-done.2
  39.8 0.0 copy-done
  39.9 8.2 %shard_map.91 = (f32[3,64,128]{2,1,0:T(8,128)}, f32[2,80,64,128]{3,2,1,0:T(8,128)}) custom-call(s32[1]{0:T(128)} %bitcast.section, f32[6,72,128]{2,1,0:T(8,128)S(1)} %shard_map.90.mine, f32[6,72,128]{2,1,0:T(8,128)S(1)} %collective-permute-done.2.other, s32[72,128]{1,0:T(8,128)S(1)} %copy-done.2, f32[2,80,72,128]{3,2,1,0:T(8,128)S(1)} %copy-done, ...), custom_call_target="tpu_custom_call" | custom-call | flops 44236800 | bytes 23592960 | tf_op jit(solution)/shard_map/pallas_call | solution.py:611
  (1 shorter events, 0.0 us)
Async XLA Ops:
  0.6 24.1 %copy-start.3 = (f32[128]{0:T(128)S(1)}, f32[128]{0:T(128)}, u32[]{:S(2)}) copy-start(f32[128]{0:T(128)} %constant.8.clone) | copy-start | bytes 1540
  2.2 17.8 %collective-permute-start = (bf16[848,128]{1,0:T(8,128)(2,1)S(1)}, bf16[848,128]{1,0:T(8,128)(2,1)S(1)}, u32[]{:S(2)}, u32[]{:S(2)}) collective-permute-start(bf16[848,128]{1,0:T(8,128)(2,1)S(1)} %get-tuple-element.16), channel_id=1, source_target_pairs={{0,1},{1,2},{2,3},{3,4},{4,5},{5,6},{6,7},{7,8},{8,9},{9,10},{10,1... | collective-permute-start | bytes 651272 | tf_op jit(solution)/shard_map/ppermute | solution.py:454
  5.2 14.8 %collective-permute-start.1 = (bf16[848,128]{1,0:T(8,128)(2,1)S(1)}, bf16[848,128]{1,0:T(8,128)(2,1)S(1)}, u32[]{:S(2)}, u32[]{:S(2)}) collective-permute-start(bf16[848,128]{1,0:T(8,128)(2,1)S(1)} %get-tuple-element.17), channel_id=1, source_target_pairs={{0,15},{1,0},{2,1},{3,2},{4,3},{5,4},{6,5},{7,6},{8,7},{9,8},{10,9... | collective-permute-start | bytes 651272 | tf_op jit(solution)/shard_map/ppermute | solution.py:454
  21.2 11.8 %all-to-all-start.1 = ((bf16[16,56,128]{2,1,0:T(8,128)(2,1)}), bf16[16,56,128]{2,1,0:T(8,128)(2,1)S(1)}, u32[]{:S(2)}, u32[]{:S(2)}) async-start(bf16[16,56,128]{2,1,0:T(8,128)(2,1)} %bitcast.10), calls=%async_computation.1 | async-start | bytes 458752 | tf_op jit(solution)/shard_map/all_to_all | solution.py:544
  31.0 8.9 %copy-start.1 = (bf16[80,64,128]{2,1,0:T(8,128)(2,1)S(1)}, bf16[80,64,128]{2,1,0:T(8,128)(2,1)}, u32[]{:S(2)}) copy-start(bf16[80,64,128]{2,1,0:T(8,128)(2,1)} %get-tuple-element.21.side) | copy-start | bytes 3932164
  31.0 8.9 %copy-start.2 = (s32[72,128]{1,0:T(8,128)S(1)}, s32[72,128]{1,0:T(8,128)}, u32[]{:S(2)}) copy-start(s32[72,128]{1,0:T(8,128)} %get-tuple-element.19.bath) | copy-start | bytes 110596
  33.0 6.8 %copy-start = (f32[2,80,72,128]{3,2,1,0:T(8,128)S(1)}, f32[2,80,72,128]{3,2,1,0:T(8,128)}, u32[]{:S(2)}) copy-start(f32[2,80,72,128]{3,2,1,0:T(8,128)} %get-tuple-element.20.q) | copy-start | bytes 17694724
  38.3 1.5 %collective-permute-start.2 = (f32[6,72,128]{2,1,0:T(8,128)S(1)}, f32[6,72,128]{2,1,0:T(8,128)S(1)}, u32[]{:S(2)}, u32[]{:S(2)}) collective-permute-start(f32[6,72,128]{2,1,0:T(8,128)S(1)} %shard_map.90.mine), channel_id=1, source_target_pairs={{0,16},{16,0},{1,17},{17,1},{2,18},{18,2},{3,19},{19,3},{4,20},{20... | collective-permute-start | bytes 663560 | tf_op jit(solution)/shard_map/ppermute | solution.py:609

commit v19 on v18

--- a/solution.py
+++ b/solution.py
@@ -1,4 +1,5 @@
 import functools
+import math
 
 import jax
 import jax.numpy as jnp
@@ -12,6 +13,7 @@
 SIDE_MIX = 0.2
 TOP_MIX = 1.0
 DEEP_MIX = 2.0
+FIXED = (1.0 + 2.0 * DEEP_MIX - math.sqrt(1.0 + 4.0 * DEEP_MIX)) / (2.0 * DEEP_MIX)
 SCALE = 1.0 / (0.5 * SIDE_MIX)
 
 MOST = 16
@@ -295,6 +297,15 @@
     return jnp.broadcast_to(jnp.asarray(np.array(values, np.float32)), (8, lanes))
 
 
+def ratio_in_closed_form(depth, level):
+    height = depth - level
+    power = jnp.exp2((2.0 * math.log2(FIXED)) * height.astype(f32))
+    divisor = 1.0 + FIXED * power
+    inverse = pl.reciprocal(divisor, approx=True)
+    scaled = ((1.0 - FIXED * FIXED) * power) * inverse
+    return jnp.where(height > 0, FIXED + scaled * (2.0 - divisor * inverse), 0.0)
+
+
 def remap_kernel(
     columns_in, place_from, from_left, from_right, weights, own_fields,
     out, picked, solved, held, fields_in, place, sems,
@@ -362,7 +373,7 @@
 
 
 def finish_kernel(
-    section, mine, other, bath, q, side, ratios, state, surface, result,
+    section, mine, other, bath, q, side, state, surface, result,
     values_at, rounded_at, rho, solved, done, across, band, sems, sems_out,
 ):
     tracers, levels, columns, lanes = result.shape
@@ -386,7 +397,7 @@
     depth = bath[...]
     unscale = 1.0 / (SCALE * SCALE)
 
-    rho[2] = ratio_at(ratios, depth, 2)
+    rho[2] = ratio_in_closed_form(depth, 2)
     link = jnp.where(1 < depth, top_mix, 0.0)
     deeper = jnp.where(2 < depth, DEEP_MIX - DEEP_MIX * rho[2], 0.0)
     second = 1.0 / (1.0 + link + deeper)
@@ -415,7 +426,7 @@
         put(n, 1, carry)
         for level in range(2, levels):
             if n == 0 and level > 2:
-                rho[level] = ratio_at(ratios, depth, level)
+                rho[level] = ratio_in_closed_form(depth, level)
             carry = q[n, level] + rho[level] * carry
             put(n, level, carry)
 
@@ -611,7 +622,7 @@
     surface, result = pl.pallas_call(
         finish_kernel,
         out_shape=(shaped((3, columns, lanes), f32), shaped(ocean_state.shape, f32)),
-        in_specs=[smem] + [vmem] * 6 + [hbm],
+        in_specs=[smem] + [vmem] * 5 + [hbm],
         out_specs=(vmem, hbm),
         scratch_shapes=[
             pltpu.VMEM(ocean_state.shape, f32),
@@ -635,7 +646,6 @@
         in_vmem(bath),
         in_vmem(q),
         in_vmem(side),
-        ratios,
         in_hbm(ocean_state),
     )
     return (surface[None], result)

time: 48.4 us -> 48.6 us (level)
  no operation moved by 1% of the time
where the time goes in v19:
time: 48.6 us; the launch traced here: 48.3 us
  Pallas kernels  22.9 us (47%)
  starting transfers between devices  10.6 us (22%)
  blocking collectives  10.4 us (21%)
  waiting for transfers between devices  3.51 us (7%)
  between operations  0.72 us (1%)
    all_to_all x1, blocking collectives, per_device(): lax.all_to_all(request, 'blk', split_axis=0, concat_axis=0, tiled=True)  10.4 us
    pallas_call x1, Pallas kernels, per_device(): pl.pallas_call(finish_kernel, out_shape=(shaped((3, columns, lanes), f32)...  8.4 us
    ppermute x2, starting transfers between devices, shift(): lax.ppermute(value, axis, [(i, (i + by) % count) for i in range(count)])  7.05 us
    pallas_call x1, Pallas kernels, per_device(): pl.pallas_call(functools.partial(start_kernel, count=count), out_shape=(p...  6.22 us
    pallas_call x1, Pallas kernels, per_device(): pl.pallas_call(remap_kernel, out_shape=shaped((6, rows, lanes), f32), in_...  5.26 us
    all_to_all x1, starting transfers between devices, per_device(): lax.all_to_all(served, 'blk', split_axis=0, concat_axis=0, tiled=True)  3.53 us
    all_to_all x1, waiting for transfers between devices, per_device(): lax.all_to_all(served, 'blk', split_axis=0, concat_axis=0, tiled=True)  2.04 us
    pallas_call x1, Pallas kernels, per_device(): pl.pallas_call(pack_kernel, out_shape=(payload, payload, shaped((FIELDS *...  1.54 us
  transfers between devices with their start and end apart: 4, of which 2 were waited for; matrix products, arithmetic and copies ran while one was open for 0% of the time, Pallas kernels for 14%

profile of v19, /device:TPU:0, one launch (start us, length us, event | category | flops | bytes accessed | tf_op | source)
XLA Modules:
  0.0 48.3 jit_solution(14754180889587533882)
XLA Ops:
  0.6 0.0 copy-start.3
  0.6 1.5 %shard_map.86 = (bf16[848,128]{1,0:T(8,128)(2,1)S(1)}, bf16[848,128]{1,0:T(8,128)(2,1)S(1)}, bf16[192,128]{1,0:T(8,128)(2,1)S(1)}, s32[4,64]{1,0:T(4,128)S(1)}, s32[4,64]{1,0:T(4,128)S(1)}) custom-call(s32[1]{0:T(128)} %bitcast.section, f32[2,80,64,128]{3,2,1,0:T(8,128)} %state.5, s32[64,128]{1,0:T(8,128)} %bath.3, bf16[3,64,128]{2,1,0:T(8,128)(2,1)} %bitcast.21, ...), custom_call_target="tpu_custom_call" | custom-call | flops 1000000 | bytes 4000000 | tf_op jit(solution)/shard_map/pallas_call | solution.py:500
  2.2 3.0 %collective-permute-start = (bf16[848,128]{1,0:T(8,128)(2,1)S(1)}, bf16[848,128]{1,0:T(8,128)(2,1)S(1)}, u32[]{:S(2)}, u32[]{:S(2)}) collective-permute-start(bf16[848,128]{1,0:T(8,128)(2,1)S(1)} %get-tuple-element.16), channel_id=1, source_target_pairs={{0,1},{1,2},{2,3},{3,4},{4,5},{5,6},{6,7},{7,8},{8,9},{9,10},{10,1... | collective-permute-start | bytes 651272 | tf_op jit(solution)/shard_map/ppermute | solution.py:465
  5.2 4.1 %collective-permute-start.1 = (bf16[848,128]{1,0:T(8,128)(2,1)S(1)}, bf16[848,128]{1,0:T(8,128)(2,1)S(1)}, u32[]{:S(2)}, u32[]{:S(2)}) collective-permute-start(bf16[848,128]{1,0:T(8,128)(2,1)S(1)} %get-tuple-element.17), channel_id=1, source_target_pairs={{0,15},{1,0},{2,1},{3,2},{4,3},{5,4},{6,5},{7,6},{8,7},{9,8},{10,9... | collective-permute-start | bytes 651272 | tf_op jit(solution)/shard_map/ppermute | solution.py:465
  9.2 0.3 shard_map.87
  9.6 10.4 %all_to_all.22 = s32[16,1,128]{2,1,0:T(1,128)S(1)} all-to-all(s32[16,1,128]{2,1,0:T(1,128)S(1)} %bitcast.18), channel_id=1, replica_groups=mesh['sec'=2,'blk'=16] {'blk'}, dimensions={0} | all-to-all | bytes 16384 | tf_op jit(solution)/shard_map/all_to_all | solution.py:541
  20.0 0.0 collective-permute-done.from_left
  20.0 0.0 collective-permute-done.1.from_right
  20.0 1.2 %shard_map.88 = bf16[896,128]{1,0:T(8,128)(2,1)} custom-call(s32[16,128]{1,0:T(8,128)S(1)} %bitcast.17, bf16[192,128]{1,0:T(8,128)(2,1)S(1)} %get-tuple-element.15.table, bf16[848,128]{1,0:T(8,128)(2,1)S(1)} %collective-permute-done.from_left, bf16[848,128]{1,0:T(8,128)(2,1)S(1)} %collective-permute-done.1.from_right), custom_call_target="tpu_custom_call" | custom-call | flops 10000000 | bytes 1000000 | tf_op jit(solution)/shard_map/pallas_call | solution.py:545
  21.2 3.5 %all-to-all-start.1 = ((bf16[16,56,128]{2,1,0:T(8,128)(2,1)}), bf16[16,56,128]{2,1,0:T(8,128)(2,1)S(1)}, u32[]{:S(2)}, u32[]{:S(2)}) async-start(bf16[16,56,128]{2,1,0:T(8,128)(2,1)} %bitcast.10), calls=%async_computation.1 | async-start | bytes 458752 | tf_op jit(solution)/shard_map/all_to_all | solution.py:555
  24.7 0.0 copy-done.3
  24.7 6.2 %shard_map.89 = (f32[2,80,72,128]{3,2,1,0:T(8,128)}, bf16[80,64,128]{2,1,0:T(8,128)(2,1)}, s32[72,128]{1,0:T(8,128)}, s32[256,128]{1,0:T(8,128)}) custom-call(f32[2,80,64,128]{3,2,1,0:T(8,128)} %state.5, bf16[848,128]{1,0:T(8,128)(2,1)S(1)} %collective-permute-done.from_left, bf16[848,128]{1,0:T(8,128)(2,1)S(1)} %collective-permute-done.1.from_right, ...), custom_call_target="tpu_custom_call" | custom-call | flops 44236800 | bytes 147456000 | tf_op jit(solution)/shard_map/pallas_call | solution.py:558
  31.0 0.0 copy-start.1
  31.0 0.0 copy-start.2
  31.0 2.0 %all-to-all-done.1 = bf16[16,56,128]{2,1,0:T(8,128)(2,1)S(1)} async-done(((bf16[16,56,128]{2,1,0:T(8,128)(2,1)}), bf16[16,56,128]{2,1,0:T(8,128)(2,1)S(1)}, u32[]{:S(2)}, u32[]{:S(2)}) %all-to-all-start.1) | async-done | bytes 229408 | tf_op jit(solution)/shard_map/all_to_all | solution.py:555
  33.0 0.0 copy-start
  33.0 5.3 %shard_map.90.mine = f32[6,72,128]{2,1,0:T(8,128)S(1)} custom-call(bf16[896,128]{1,0:T(8,128)(2,1)S(1)} %bitcast.16, s32[256,128]{1,0:T(8,128)} %get-tuple-element.18.place_from, bf16[848,128]{1,0:T(8,128)(2,1)S(1)} %collective-permute-done.from_left, bf16[848,128]{1,0:T(8,128)(2,1)S(1)} %collective-permute-done.1.from_right, bf16[32768,128]{1,0:T(8,128)(2,1)} %bitcast.20, ...), custom_call_target="tpu_custom_call" | custom-call | flops 67108864 | bytes 8388608 | tf_op jit(solution)/shard_map/pallas_call | solution.py:595
  38.3 0.1 collective-permute-start.2
  38.4 1.5 %collective-permute-done.2.other = f32[6,72,128]{2,1,0:T(8,128)S(1)} collective-permute-done((f32[6,72,128]{2,1,0:T(8,128)S(1)}, f32[6,72,128]{2,1,0:T(8,128)S(1)}, u32[]{:S(2)}, u32[]{:S(2)}) %collective-permute-start.2) | collective-permute-done | bytes 221216 | tf_op jit(solution)/shard_map/ppermute | solution.py:620
  39.8 0.0 copy-done.1
  39.8 0.0 copy-done.2
  39.8 0.0 copy-done
  39.9 8.4 %shard_map.91 = (f32[3,64,128]{2,1,0:T(8,128)}, f32[2,80,64,128]{3,2,1,0:T(8,128)}) custom-call(s32[1]{0:T(128)} %bitcast.section, f32[6,72,128]{2,1,0:T(8,128)S(1)} %shard_map.90.mine, f32[6,72,128]{2,1,0:T(8,128)S(1)} %collective-permute-done.2.other, s32[72,128]{1,0:T(8,128)S(1)} %copy-done.2, f32[2,80,72,128]{3,2,1,0:T(8,128)S(1)} %copy-done, ...), custom_call_target="tpu_custom_call" | custom-call | flops 44236800 | bytes 23592960 | tf_op jit(solution)/shard_map/pallas_call | solution.py:622
  (1 shorter events, 0.0 us)
Async XLA Ops:
  0.6 24.1 %copy-start.3 = (f32[128]{0:T(128)S(1)}, f32[128]{0:T(128)}, u32[]{:S(2)}) copy-start(f32[128]{0:T(128)} %constant.8.clone) | copy-start | bytes 1540
  2.2 17.8 %collective-permute-start = (bf16[848,128]{1,0:T(8,128)(2,1)S(1)}, bf16[848,128]{1,0:T(8,128)(2,1)S(1)}, u32[]{:S(2)}, u32[]{:S(2)}) collective-permute-start(bf16[848,128]{1,0:T(8,128)(2,1)S(1)} %get-tuple-element.16), channel_id=1, source_target_pairs={{0,1},{1,2},{2,3},{3,4},{4,5},{5,6},{6,7},{7,8},{8,9},{9,10},{10,1... | collective-permute-start | bytes 651272 | tf_op jit(solution)/shard_map/ppermute | solution.py:465
  5.2 14.8 %collective-permute-start.1 = (bf16[848,128]{1,0:T(8,128)(2,1)S(1)}, bf16[848,128]{1,0:T(8,128)(2,1)S(1)}, u32[]{:S(2)}, u32[]{:S(2)}) collective-permute-start(bf16[848,128]{1,0:T(8,128)(2,1)S(1)} %get-tuple-element.17), channel_id=1, source_target_pairs={{0,15},{1,0},{2,1},{3,2},{4,3},{5,4},{6,5},{7,6},{8,7},{9,8},{10,9... | collective-permute-start | bytes 651272 | tf_op jit(solution)/shard_map/ppermute | solution.py:465
  21.2 11.8 %all-to-all-start.1 = ((bf16[16,56,128]{2,1,0:T(8,128)(2,1)}), bf16[16,56,128]{2,1,0:T(8,128)(2,1)S(1)}, u32[]{:S(2)}, u32[]{:S(2)}) async-start(bf16[16,56,128]{2,1,0:T(8,128)(2,1)} %bitcast.10), calls=%async_computation.1 | async-start | bytes 458752 | tf_op jit(solution)/shard_map/all_to_all | solution.py:555
  31.0 8.9 %copy-start.1 = (bf16[80,64,128]{2,1,0:T(8,128)(2,1)S(1)}, bf16[80,64,128]{2,1,0:T(8,128)(2,1)}, u32[]{:S(2)}) copy-start(bf16[80,64,128]{2,1,0:T(8,128)(2,1)} %get-tuple-element.21.side) | copy-start | bytes 3932164
  31.0 8.9 %copy-start.2 = (s32[72,128]{1,0:T(8,128)S(1)}, s32[72,128]{1,0:T(8,128)}, u32[]{:S(2)}) copy-start(s32[72,128]{1,0:T(8,128)} %get-tuple-element.19.bath) | copy-start | bytes 110596
  33.0 6.8 %copy-start = (f32[2,80,72,128]{3,2,1,0:T(8,128)S(1)}, f32[2,80,72,128]{3,2,1,0:T(8,128)}, u32[]{:S(2)}) copy-start(f32[2,80,72,128]{3,2,1,0:T(8,128)} %get-tuple-element.20.q) | copy-start | bytes 17694724
  38.3 1.5 %collective-permute-start.2 = (f32[6,72,128]{2,1,0:T(8,128)S(1)}, f32[6,72,128]{2,1,0:T(8,128)S(1)}, u32[]{:S(2)}, u32[]{:S(2)}) collective-permute-start(f32[6,72,128]{2,1,0:T(8,128)S(1)} %shard_map.90.mine), channel_id=1, source_target_pairs={{0,16},{16,0},{1,17},{17,1},{2,18},{18,2},{3,19},{19,3},{4,20},{20... | collective-permute-start | bytes 663560 | tf_op jit(solution)/shard_map/ppermute | solution.py:620
